TPU v7x, 32 devices: a whole 2x2x4 slice. The times are simulated.
32 devices in a mesh: groups: 2 (over x), expert: 16 (over z, y, core).
Axes of the slice: x: 2, y: 2, z: 4, core: 2. Of those that a mesh axis runs over, the one named last changes fastest.
Arguments:
- tokens: bfloat16 [512, 7168], P(('groups', 'expert')), parts along dimension 0, may hold values from -6 to 6
- scales: float32 [512, 56], P(('groups', 'expert')), parts along dimension 0, may hold values from 0.25 to 4
- routes: int32 [512, 2], P(('groups', 'expert')), parts along dimension 0, may hold values from 0 to 3, all different within a row; in each aligned block of 16 rows (0 to 15, 16 to 31, ...) at most 12 rows name the same one
- gate_codes: int32 [512, 2], P(('groups', 'expert')), parts along dimension 0, may hold values from 1 to 65535
- w_gate: bfloat16 [16, 7168, 256], P('expert'), may hold values from -0.0625 to 0.0625
- w_up: bfloat16 [16, 7168, 256], P('expert'), may hold values from -0.0625 to 0.0625
- w_down: bfloat16 [16, 256, 7168], P('expert'), may hold values from -0.1875 to 0.1875
Outputs:
- mixed: bfloat16 [512, 7168], P(('groups', 'expert')), parts along dimension 0
There are 2 independent parts, one for each index of `groups`. A program takes and returns all parts, laid end to end along the dimension named above; an argument that names none is the same for every part. Nothing has to cross between parts.
Inputs may be any that keep to these rules, and one draw needn't show every extreme that they name: `routes`: each row names 2 different experts. In each aligned block of 16 rows (the rows of one device) no expert is named by more than 12 rows, a bound that some block reaches.
All inputs are finite; a program needn't handle non-finite values.
Results may differ from a plain program's by a relative error of at most 0.0079.
Values may be sent and summed in bfloat16 or wider, within the bound.
No kernel may reach another device: no remote copies, remote signals or barrier semaphores. Data moves between devices by JAX's collectives and lax.ppermute only.
A program may use at most 128 MiB of HBM per device.

v0:
```python
import jax
import jax.numpy as jnp
from jax import lax
from jax.sharding import PartitionSpec as P

SHARDS = 4


def dequantize(codes, factors):
    shape = codes.shape
    blocks = (
        codes.astype(jnp.float32).reshape(shape[:-1] + (shape[-1] // 128, 128)) * factors[..., None]
    )
    return blocks.reshape(shape).astype(jnp.bfloat16)


def expert_partial(slot_rows, w_gate, w_up, w_down):
    gate_proj = jnp.einsum("ncd,df->ncf", slot_rows, w_gate[0], preferred_element_type=jnp.float32)
    upward = jnp.einsum("ncd,df->ncf", slot_rows, w_up[0], preferred_element_type=jnp.float32)
    hidden = (jax.nn.silu(gate_proj) * upward).astype(jnp.bfloat16)
    return jnp.einsum("ncf,fd->ncd", hidden, w_down[0], preferred_element_type=jnp.float32).astype(
        jnp.bfloat16
    )


def shards(tokens, scales, routes, gate_codes, w_gate, w_up, w_down):
    tok_rows, features = tokens.shape
    picks_per = routes.shape[1]
    devices = lax.axis_size("expert")
    experts = devices // SHARDS
    capacity = 3 * tok_rows * picks_per // (2 * experts)
    chosen = routes.reshape(-1)
    onehot = (chosen[:, None] == jnp.arange(experts, dtype=jnp.int32)[None, :]).astype(jnp.int32)
    position = jnp.sum((jnp.cumsum(onehot, 0) - onehot) * onehot, axis=1)
    slot_index = chosen * capacity + position
    owner_row = (
        jnp.full((experts * capacity,), tok_rows, jnp.int32)
        .at[slot_index]
        .set(jnp.arange(tok_rows * picks_per, dtype=jnp.int32) // picks_per)
    )
    values = dequantize(tokens, scales)
    packed = jnp.take(values, owner_row, axis=0, mode="fill", fill_value=0).reshape(
        experts, capacity, features
    )
    outgoing = jnp.broadcast_to(packed[:, None], (experts, SHARDS, capacity, features)).reshape(
        devices, capacity, features
    )
    partial_value = expert_partial(
        lax.all_to_all(outgoing, "expert", split_axis=0, concat_axis=0, tiled=True),
        w_gate,
        w_up,
        w_down,
    )
    returned = lax.all_to_all(partial_value, "expert", split_axis=0, concat_axis=0, tiled=True)
    summed = jnp.sum(
        returned.reshape(experts, SHARDS, capacity, features).astype(jnp.float32), axis=1
    )
    answers_all = summed.astype(jnp.bfloat16).reshape(experts * capacity, features)
    answers = jnp.take(answers_all, slot_index, axis=0)
    weights = gate_codes.astype(jnp.float32) / 65536.0
    mixed = jnp.sum(
        answers.reshape(tok_rows, picks_per, features).astype(jnp.float32) * weights[:, :, None],
        axis=1,
    )
    return mixed.astype(jnp.bfloat16)


def solution(mesh):
    in_specs = (
        P(("groups", "expert"), None),
        P(("groups", "expert"), None),
        P(("groups", "expert"), None),
        P(("groups", "expert"), None),
        P("expert", None, None),
        P("expert", None, None),
        P("expert", None, None),
    )
    out_specs = P(("groups", "expert"), None)
    return jax.shard_map(shards, mesh=mesh, in_specs=in_specs, out_specs=out_specs, check_vma=False)
```

profile of v0, /device:TPU:15, one launch (start us, length us, event | category | flops | bytes accessed | tf_op | source)
XLA Modules:
  0.0 195.1 jit_solution(9751285146290558599)
XLA Ops:
  0.0 0.8 copy.24
  0.8 0.7 broadcast_multiply_fusion
  1.4 0.1 reshape.77
  1.5 0.1 fusion.13
  1.6 0.1 reduce_window_sum.11
  1.7 0.2 select_reduce_fusion
  1.8 0.1 copy.27
  1.9 0.1 mul.51
  2.0 0.7 scatter_custom_fusion
  2.8 0.9 mul.52
  3.6 1.0 fusion.11
  4.7 1.0 gather_fusion
  5.7 0.2 gather.13
  5.8 0.1 broadcast_in_dim.38
  5.9 0.1 broadcast_select_fusion
  6.1 0.4 broadcast_in_dim.42
  6.5 0.0 copy-start.3
  6.5 87.6 %all_to_all.10 = bf16[16,12,7168]{2,1,0:T(8,128)(2,1)S(1)} all-to-all(bf16[16,12,7168]{2,1,0:T(8,128)(2,1)S(1)} %bitcast.32), channel_id=1, replica_groups=mesh['groups'=2,'expert'=16] {'expert'}, dimensions={0} | all-to-all | bytes 5505024 | tf_op jit(solution)/shard_map/all_to_all | solution.py:49
  94.1 0.0 copy-done.3
  94.1 0.0 copy-start.4
  94.1 1.1 fusion.3
  95.3 0.9 copy-done.4
  96.2 0.0 copy-start
  96.2 1.1 fusion.8
  97.3 0.9 copy-done
  98.2 0.9 convolution_convert_fusion
  99.1 3.4 %copy.29 = bf16[16,12,7168]{2,1,0:T(8,128)(2,1)} copy(bf16[16,12,7168]{2,0,1:T(8,128)(2,1)S(1)} %convolution_convert_fusion) | data formatting | bytes 5505024 | tf_op jit(solution)/shard_map/convert_element_type | solution.py:21
  102.5 0.0 copy-start.1
  102.5 0.0 copy-start.2
  102.5 5.4 %all-to-all-start.1 = ((bf16[16,12,7168]{2,1,0:T(8,128)(2,1)}), bf16[16,12,7168]{2,1,0:T(8,128)(2,1)}, u32[]{:S(2)}, u32[]{:S(2)}) async-start(bf16[16,12,7168]{2,1,0:T(8,128)(2,1)} %copy.29), calls=%async_computation.1 | async-start | bytes 7340032 | tf_op jit(solution)/shard_map/all_to_all | solution.py:54
  107.9 0.1 reduce_sum.35
  108.0 0.1 copy.25
  108.1 0.0 copy-done.1
  108.1 0.1 copy.26
  108.2 0.0 copy-done.2
  108.2 0.1 copy.32
  108.3 80.8 %all-to-all-done.1 = bf16[16,12,7168]{2,1,0:T(8,128)(2,1)} async-done(((bf16[16,12,7168]{2,1,0:T(8,128)(2,1)}), bf16[16,12,7168]{2,1,0:T(8,128)(2,1)}, u32[]{:S(2)}, u32[]{:S(2)}) %all-to-all-start.1) | async-done | bytes 2752544 | tf_op jit(solution)/shard_map/all_to_all | solution.py:54
  189.1 2.7 %bitcast_reduce_fusion = bf16[4,12,7168]{2,1,0:T(8,128)(2,1)S(1)} fusion(bf16[16,12,7168]{2,1,0:T(8,128)(2,1)} %all-to-all-done.1), kind=kLoop, calls=%fused_computation.4 | loop fusion | flops 1032192 | bytes 3440640 | tf_op jit(solution)/shard_map/reduce_sum | solution.py:55
  191.8 0.2 reshape.80
  192.0 0.8 gather_fusion.1
  192.8 0.2 gather.15
  193.0 2.1 %multiply_reduce_fusion = bf16[16,7168]{1,0:T(8,128)(2,1)} fusion(bf16[16,2,7168]{2,1,0:T(2,128)(2,1)S(1)} %gather.15, pred[16,2]{1,0:T(8,128)(4,1)S(1)} %copy.26, f32[16,2]{1,0:T(8,128)S(1)} %copy.32), kind=kLoop, calls=%fused_computation.12 | loop fusion | flops 802816 | bytes 688288 | tf_op jit(solution)/shard_map/reduce_sum | solution.py:61
  (8 shorter events, 0.1 us)
Async XLA Ops:
  6.5 87.6 %copy-start.3 = (bf16[1,7168,256]{2,1,0:T(8,128)(2,1)S(1)}, bf16[1,7168,256]{2,1,0:T(8,128)(2,1)}, u32[]{:S(2)}) copy-start(bf16[1,7168,256]{2,1,0:T(8,128)(2,1)} %param.11) | copy-start | bytes 11010052
  94.1 2.0 %copy-start.4 = (bf16[1,7168,256]{2,1,0:T(8,128)(2,1)S(1)}, bf16[1,7168,256]{2,1,0:T(8,128)(2,1)}, u32[]{:S(2)}) copy-start(bf16[1,7168,256]{2,1,0:T(8,128)(2,1)} %param.12) | copy-start | bytes 11010052
  96.2 2.0 %copy-start = (bf16[1,256,7168]{2,1,0:T(8,128)(2,1)S(1)}, bf16[1,256,7168]{2,1,0:T(8,128)(2,1)}, u32[]{:S(2)}) copy-start(bf16[1,256,7168]{2,1,0:T(8,128)(2,1)} %param.13) | copy-start | bytes 11010052
  102.5 5.5 %copy-start.1 = (s32[16,2]{0,1:T(2,128)S(1)}, s32[16,2]{0,1:T(2,128)}, u32[]{:S(2)}) copy-start(s32[16,2]{0,1:T(2,128)} %param.9) | copy-start | bytes 388
  102.5 5.7 %copy-start.2 = (s32[16,2]{0,1:T(2,128)S(1)}, s32[16,2]{0,1:T(2,128)}, u32[]{:S(2)}) copy-start(s32[16,2]{0,1:T(2,128)} %param.10) | copy-start | bytes 388
  102.5 86.6 %all-to-all-start.1 = ((bf16[16,12,7168]{2,1,0:T(8,128)(2,1)}), bf16[16,12,7168]{2,1,0:T(8,128)(2,1)}, u32[]{:S(2)}, u32[]{:S(2)}) async-start(bf16[16,12,7168]{2,1,0:T(8,128)(2,1)} %copy.29), calls=%async_computation.1 | async-start | bytes 7340032 | tf_op jit(solution)/shard_map/all_to_all | solution.py:54
where the time goes:
time: 196 us; the launch traced here: 195 us
  blocking collectives  87.6 us (45%)
  waiting for transfers between devices  80.8 us (41%)
  local copies, waits for them, and re-layouts  10.9 us (6%)
  other arithmetic  7.01 us (4%)
  starting transfers between devices  5.37 us (3%)
  matrix products  3.18 us (2%)
    all_to_all x1, blocking collectives, shards(): lax.all_to_all(outgoing, 'expert', split_axis=0, concat_axis=0, tiled=True)  87.6 us
    all_to_all x1, waiting for transfers between devices, shards(): lax.all_to_all(partial_value, 'expert', split_axis=0, concat_axis=0, tile...  80.8 us
    all_to_all x1, starting transfers between devices, shards(): lax.all_to_all(partial_value, 'expert', split_axis=0, concat_axis=0, tile...  5.37 us
  transfers between devices with their start and end apart: 1, of which 1 were waited for; matrix products, arithmetic and copies ran while one was open for 0% of the time, Pallas kernels for 0%

commit v1 on v0

v1 whole, which is shorter than its diff:
```python
import jax
import jax.numpy as jnp
from jax import lax
from jax.sharding import PartitionSpec as P

SHARDS = 4


def dequantize(codes, factors):
    shape = codes.shape
    blocks = (
        codes.astype(jnp.float32).reshape(shape[:-1] + (shape[-1] // 128, 128)) * factors[..., None]
    )
    return blocks.reshape(shape).astype(jnp.bfloat16)


def shards(tokens, scales, routes, gate_codes, w_gate, w_up, w_down):
    devices = lax.axis_size("expert")
    experts = devices // SHARDS
    values = dequantize(tokens, scales)
    weights = gate_codes.astype(jnp.float32) / 65536.0
    named = routes[:, :, None] == jnp.arange(experts, dtype=jnp.int32)[None, None, :]
    table = jnp.sum(jnp.where(named, weights[:, :, None], 0.0), axis=1)
    all_values = lax.all_gather(values, "expert", axis=0, tiled=True)
    all_table = lax.all_gather(table, "expert", axis=0, tiled=True)
    mine = lax.axis_index("expert") // SHARDS
    row_weight = lax.dynamic_slice_in_dim(all_table, mine, 1, axis=1)
    gate_proj = jnp.dot(all_values, w_gate[0], preferred_element_type=jnp.float32)
    upward = jnp.dot(all_values, w_up[0], preferred_element_type=jnp.float32)
    hidden = (jax.nn.silu(gate_proj) * upward).astype(jnp.bfloat16)
    part = jnp.dot(hidden, w_down[0], preferred_element_type=jnp.float32) * row_weight
    return lax.psum_scatter(part.astype(jnp.bfloat16), "expert", scatter_dimension=0, tiled=True)


def solution(mesh):
    in_specs = (
        P(("groups", "expert"), None),
        P(("groups", "expert"), None),
        P(("groups", "expert"), None),
        P(("groups", "expert"), None),
        P("expert", None, None),
        P("expert", None, None),
        P("expert", None, None),
    )
    out_specs = P(("groups", "expert"), None)
    return jax.shard_map(shards, mesh=mesh, in_specs=in_specs, out_specs=out_specs, check_vma=False)
```

time: 196 us -> 149 us (0.76)
  the two profiles are of different devices: /device:TPU:15 before, /device:TPU:0 now
where the time goes in v1:
time: 149 us
  waiting for transfers between devices  93.7 us (63%)
  blocking collectives  23.4 us (16%)
  matrix products  14.3 us (10%)
  between operations  13.4 us (9%)
  other arithmetic  3.09 us (2%)
    reduce_scatter x1, waiting for transfers between devices, shards(): lax.psum_scatter(part.astype(jnp.bfloat16), 'expert', scatter_dimension=0...  67.8 us
    all_gather x1, waiting for transfers between devices, shards(): all_values = lax.all_gather(values, 'expert', axis=0, tiled=True)  25.8 us
    all_gather x1, blocking collectives, shards(): all_table = lax.all_gather(table, 'expert', axis=0, tiled=True)  23.4 us
    dot_general x1, matrix products, shards(): jnp.dot(hidden, w_down[0], preferred_element_type=jnp.float32) * row_weight  10 us
    dot_general x1, matrix products, shards(): jnp.dot(all_values, w_gate[0], preferred_element_type=jnp.float32)  4.26 us
  transfers between devices with their start and end apart: 2, of which 2 were waited for; matrix products, arithmetic and copies ran while one was open for 1% of the time, Pallas kernels for 0%

profile of v1, /device:TPU:0, one launch (start us, length us, event | category | flops | bytes accessed | tf_op | source)
XLA Modules:
  0.0 148.9 jit_solution(11251124536335342272)
XLA Ops:
  6.5 0.0 all-gather.3.cloned.1.call-start
  6.5 0.9 mul.28
  7.4 1.7 %fusion.14 = bf16[16,7168]{1,0:T(8,128)(2,1)} fusion(f32[2,8,56,128]{3,2,1,0:T(8,128)S(1)} %bitcast.26, bf16[16,7168]{1,0:T(8,128)(2,1)} %param.7), kind=kLoop, calls=%fused_computation.10 | loop fusion | flops 344064 | bytes 917504 | tf_op jit(solution)/shard_map/convert_element_type | solution.py:14
  9.1 0.0 all-gather.3.cloned.1.call-update
  9.2 0.0 reduce-scatter.2.cloned.1.call-start
  9.2 0.7 convert_multiply_fusion
  9.9 0.7 select_reduce_fusion
  10.6 23.4 %all-gather = f32[16,16,4]{1,2,0:T(4,128)S(1)} all-gather(f32[1,16,4]{1,2,0:T(4,128)S(1)} %bitcast.27), channel_id=1, replica_groups=mesh['groups'=2,'expert'=16] {'expert'}, dimensions={0}, use_global_device_ids=true | all-gather | bytes 4352 | tf_op jit(solution)/shard_map/all_gather | solution.py:25
  34.0 0.1 reshape.7
  34.1 25.8 %all-gather.3.cloned.1.call-done = bf16[256,7168]{1,0:T(8,128)(2,1)} async-done(((bf16[16,7168]{1,0:T(8,128)(2,1)}), bf16[256,7168]{1,0:T(8,128)(2,1)}) %all-gather.3.cloned.1.call-update) | async-done | bytes 3670032 | tf_op jit(solution)/shard_map/all_gather | solution.py:24
  59.9 4.3 %fusion.4 = f32[256,256]{1,0:T(8,128)S(1)} fusion(bf16[256,7168]{1,0:T(8,128)(2,1)} %all-gather.3.cloned.1.call-done, bf16[1,7168,256]{2,1,0:T(8,128)(2,1)} %param.11), kind=kOutput, calls=%fused_computation.5 | convolution fusion | flops 939524096 | bytes 7602176 | tf_op jit(solution)/shard_map/dot_general | solution.py:28
  64.2 10.0 %fusion = bf16[256,7168]{1,0:T(8,128)(2,1)} fusion(bf16[1,256,7168]{2,1,0:T(8,128)(2,1)} %param.13, f32[256]{0:T(256)S(1)} %bitcast.28, bf16[256,7168]{1,0:T(8,128)(2,1)} %all-gather.3.cloned.1.call-done, bf16[1,7168,256]{2,1,0:T(8,128)(2,1)} %param.12, f32[256,256]{1,0:T(8,128)S(1)} %fusion.4), kind=kOutput, calls=%fused_computation.1 | convolution fusion | flops 1883111424 | bytes 14943232 | tf_op jit(solution)/shard_map/dot_general | solution.py:31
  74.2 0.0 reduce-scatter.2.cloned.1.call-update
  74.2 67.8 %reduce-scatter.2.cloned.1.call-done = bf16[16,7168]{1,0:T(8,128)(2,1)} async-done(((bf16[256,7168]{1,0:T(8,128)(2,1)}), bf16[16,7168]{1,0:T(8,128)(2,1)}) %reduce-scatter.2.cloned.1.call-update) | async-done | bytes 229392 | tf_op jit(solution)/shard_map/reduce_scatter | solution.py:32
  (2 shorter events, 0.0 us)
Async XLA Ops:
  6.5 53.4 %all-gather.3.cloned.1.call-start = ((), (), s32[]{:S(2)}) async-start(), calls=%async_computation.1 | async-start | bytes 3899392 | tf_op jit(solution)/shard_map/all_gather | solution.py:24
  9.2 132.9 %reduce-scatter.2.cloned.1.call-start = ((), (), s32[]{:S(2)}) async-start(), calls=%async_computation.2 | async-start | bytes 3899392 | tf_op jit(solution)/shard_map/reduce_scatter | solution.py:32
Sparse Core Ops, SparseCore 0:
  9.6 50.2 all-gather.2
  74.4 67.6 reduce-scatter.1

commit v2 on v1

v2 whole, which is shorter than its diff:
```python
import functools

import jax
import jax.numpy as jnp
from jax import lax
from jax.experimental import pallas as pl
from jax.experimental.pallas import tpu as pltpu
from jax.sharding import PartitionSpec as P

SHARDS = 4
QUARTERS = 4
VMEM_BYTES = 48 * 1024 * 1024


def zero_one(condition):
    return jnp.where(condition, 1.0, 0.0).astype(jnp.bfloat16)


def exact_dot(left, right):
    return jnp.dot(left, right, preferred_element_type=jnp.float32)


def pack_kernel(capacity, planes, tok_ref, scale_ref, route_ref, *rest):
    outs, quarters_ref = rest[:planes], rest[planes]
    rows, features = tok_ref.shape
    width = features // QUARTERS
    for block in range(features // 128):
        quarter, at = divmod(block * 128, width)
        codes = tok_ref[:, block * 128 : (block + 1) * 128].astype(jnp.float32)
        factors = scale_ref[:, block : block + 1]
        quarters_ref[quarter * rows : (quarter + 1) * rows, at : at + 128] = (
            codes * factors
        ).astype(jnp.bfloat16)
    plane = lax.axis_index("expert") // SHARDS
    offsets = (route_ref[...] ^ plane).astype(jnp.float32).astype(jnp.bfloat16)
    columns = QUARTERS * rows
    picks = offsets.shape[1]
    copies = zero_one(
        lax.broadcasted_iota(jnp.int32, (rows, columns), 1) % rows
        == lax.broadcasted_iota(jnp.int32, (rows, columns), 0)
    )
    turned = lax.dot_general(
        offsets, copies, (((0,), (0,)), ((), ())), preferred_element_type=jnp.float32
    )
    numbers = lax.broadcasted_iota(jnp.int32, (planes, columns), 0).astype(jnp.float32)
    named = jnp.zeros((planes, columns), jnp.float32)
    for pick in range(picks):
        named = named + jnp.where(turned[pick : pick + 1, :] == numbers, 1.0, 0.0)
    first = lax.broadcasted_iota(jnp.int32, (columns, columns), 0)
    second = lax.broadcasted_iota(jnp.int32, (columns, columns), 1)
    before = zero_one((first // rows == second // rows) & (first < second))
    position = exact_dot(named.astype(jnp.bfloat16), before)
    slot_row = lax.broadcasted_iota(jnp.int32, (QUARTERS * capacity, columns), 0)
    slot_col = lax.broadcasted_iota(jnp.int32, (QUARTERS * capacity, columns), 1)
    same_quarter = slot_row // capacity == slot_col // rows
    slot = (slot_row % capacity).astype(jnp.float32)
    values = quarters_ref[...]
    for offset in range(planes):
        pick_out = zero_one(
            same_quarter
            & (named[offset : offset + 1, :] > 0.5)
            & (position[offset : offset + 1, :] == slot)
        )
        outs[offset][...] = exact_dot(pick_out, values).astype(jnp.bfloat16)


def order_matrix(capacity, turned):
    size = SHARDS * QUARTERS * capacity
    row = lax.broadcasted_iota(jnp.int32, (size, size), 1 if turned else 0)
    col = lax.broadcasted_iota(jnp.int32, (size, size), 0 if turned else 1)
    quarter, block, slot = row // (SHARDS * capacity), (row // capacity) % SHARDS, row % capacity
    return zero_one(col == (block * QUARTERS + quarter) * capacity + slot)


def expert_kernel(capacity, planes, *refs):
    blocks = refs[: planes * SHARDS]
    gate_ref, up_ref, down_ref = refs[planes * SHARDS : planes * SHARDS + 3]
    outs = refs[planes * SHARDS + 3 : planes * SHARDS + 3 + 2 * planes]
    rows_ref, part_ref = refs[planes * SHARDS + 3 + 2 * planes :]
    group = SHARDS * capacity
    width = blocks[0].shape[1]
    order = order_matrix(capacity, False)
    for offset in range(planes):
        held = jnp.concatenate(
            [blocks[offset * SHARDS + member][...] for member in range(SHARDS)], axis=0
        )
        sorted_rows = exact_dot(order, held).astype(jnp.bfloat16)
        for quarter in range(QUARTERS):
            rows_ref[quarter, offset * group : (offset + 1) * group, :] = sorted_rows[
                quarter * group : (quarter + 1) * group, :
            ]
    gate = jnp.zeros((planes * group, gate_ref.shape[2]), jnp.float32)
    upward = jnp.zeros((planes * group, gate_ref.shape[2]), jnp.float32)
    for quarter in range(QUARTERS):
        span = slice(quarter * width, (quarter + 1) * width)
        gate = gate + exact_dot(rows_ref[quarter], gate_ref[0, span, :])
        upward = upward + exact_dot(rows_ref[quarter], up_ref[0, span, :])
    hidden = (gate / (1.0 + jnp.exp(-gate)) * upward).astype(jnp.bfloat16)
    for quarter in range(QUARTERS):
        span = slice(quarter * width, (quarter + 1) * width)
        part_ref[quarter] = exact_dot(hidden, down_ref[0, :, span]).astype(jnp.bfloat16)
    back = order_matrix(capacity, True)
    half = QUARTERS * SHARDS * capacity // 2
    for offset in range(planes):
        held = jnp.concatenate(
            [
                part_ref[quarter, offset * group : (offset + 1) * group, :]
                for quarter in range(QUARTERS)
            ],
            axis=0,
        )
        answer = exact_dot(back, held).astype(jnp.bfloat16)
        outs[2 * offset][...] = answer[:half]
        outs[2 * offset + 1][...] = answer[half:]


def mix_kernel(capacity, planes, route_ref, code_ref, *refs):
    returned, out_ref = refs[:planes], refs[planes]
    rows, picks = route_ref.shape
    width = returned[0].shape[1]
    tall = QUARTERS * rows
    plane = lax.axis_index("expert") // SHARDS
    offsets = (route_ref[...] ^ plane).astype(jnp.float32).astype(jnp.bfloat16)
    copies = zero_one(
        lax.broadcasted_iota(jnp.int32, (tall, rows), 0) % rows
        == lax.broadcasted_iota(jnp.int32, (tall, rows), 1)
    )
    offsets = exact_dot(copies, offsets)
    weights = code_ref[...].astype(jnp.float32) / 65536.0
    weights = jnp.concatenate([weights] * QUARTERS, axis=0)
    numbers = lax.broadcasted_iota(jnp.int32, (tall, planes), 1).astype(jnp.float32)
    named = jnp.zeros((tall, planes), jnp.float32)
    factors = jnp.zeros((tall, planes), jnp.float32)
    for pick in range(picks):
        here = offsets[:, pick : pick + 1] == numbers
        named = named + jnp.where(here, 1.0, 0.0)
        factors = factors + jnp.where(here, weights[:, pick : pick + 1], 0.0)
    first = lax.broadcasted_iota(jnp.int32, (tall, tall), 0)
    second = lax.broadcasted_iota(jnp.int32, (tall, tall), 1)
    before = zero_one((first // rows == second // rows) & (second < first))
    position = exact_dot(before, named.astype(jnp.bfloat16))
    slot_row = lax.broadcasted_iota(jnp.int32, (tall, QUARTERS * capacity), 0)
    slot_col = lax.broadcasted_iota(jnp.int32, (tall, QUARTERS * capacity), 1)
    same_quarter = slot_row // rows == slot_col // capacity
    slot = (slot_col % capacity).astype(jnp.float32)
    total = jnp.zeros((tall, width), jnp.float32)
    for offset in range(planes):
        take = zero_one(
            same_quarter
            & (named[:, offset : offset + 1] > 0.5)
            & (position[:, offset : offset + 1] == slot)
        )
        total = total + factors[:, offset : offset + 1] * exact_dot(take, returned[offset][...])
    total = total.astype(jnp.bfloat16)
    for quarter in range(QUARTERS):
        out_ref[:, quarter * width : (quarter + 1) * width] = total[
            quarter * rows : (quarter + 1) * rows, :
        ]


def shards(tokens, scales, routes, gate_codes, w_gate, w_up, w_down):
    tok_rows, features = tokens.shape
    picks_per = routes.shape[1]
    devices = lax.axis_size("expert")
    planes = devices // SHARDS
    capacity = 3 * tok_rows * picks_per // (2 * planes)
    width = features // QUARTERS
    tall = QUARTERS * capacity
    vmem = pl.BlockSpec(memory_space=pltpu.VMEM)
    params = pltpu.CompilerParams(vmem_limit_bytes=VMEM_BYTES)

    def partner(array, distance):
        return lax.ppermute(array, "expert", [(i, i ^ distance) for i in range(devices)])

    block = jax.ShapeDtypeStruct((tall, width), jnp.bfloat16)
    packed = pl.pallas_call(
        functools.partial(pack_kernel, capacity, planes),
        out_shape=[block] * planes,
        in_specs=[vmem] * 3,
        out_specs=[vmem] * planes,
        scratch_shapes=[pltpu.VMEM((QUARTERS * tok_rows, width), jnp.bfloat16)],
        compiler_params=params,
    )(tokens, scales, routes)

    gathered = []
    for offset in range(planes):
        own = packed[0] if offset == 0 else partner(packed[offset], offset * SHARDS)
        across = partner(own, 2)
        gathered += [own, across, partner(own, 1), partner(across, 1)]

    pair = jax.ShapeDtypeStruct((2 * tall, width), jnp.bfloat16)
    parts = pl.pallas_call(
        functools.partial(expert_kernel, capacity, planes),
        out_shape=[pair] * (2 * planes),
        in_specs=[vmem] * (planes * SHARDS + 3),
        out_specs=[vmem] * (2 * planes),
        scratch_shapes=[
            pltpu.VMEM((QUARTERS, planes * SHARDS * capacity, width), jnp.bfloat16),
            pltpu.VMEM((QUARTERS, planes * SHARDS * capacity, width), jnp.bfloat16),
        ],
        compiler_params=params,
    )(*gathered, w_gate, w_up, w_down)

    returned = []
    for offset in range(planes):
        kept, arrived = parts[2 * offset], partner(parts[2 * offset + 1], 1)
        kept, arrived = kept.astype(jnp.float32), arrived.astype(jnp.float32)
        across = partner((kept[tall:] + arrived[tall:]).astype(jnp.bfloat16), 2)
        answer = (kept[:tall] + arrived[:tall] + across.astype(jnp.float32)).astype(jnp.bfloat16)
        returned.append(answer if offset == 0 else partner(answer, offset * SHARDS))

    return pl.pallas_call(
        functools.partial(mix_kernel, capacity, planes),
        out_shape=jax.ShapeDtypeStruct((tok_rows, features), jnp.bfloat16),
        in_specs=[vmem] * (planes + 2),
        out_specs=vmem,
        compiler_params=params,
    )(routes, gate_codes, *returned)


def solution(mesh):
    in_specs = (
        P(("groups", "expert"), None),
        P(("groups", "expert"), None),
        P(("groups", "expert"), None),
        P(("groups", "expert"), None),
        P("expert", None, None),
        P("expert", None, None),
        P("expert", None, None),
    )
    out_specs = P(("groups", "expert"), None)
    return jax.shard_map(shards, mesh=mesh, in_specs=in_specs, out_specs=out_specs, check_vma=False)
```

time: 149 us -> 70.5 us (0.47)
  waiting for transfers between devices: 93.7 us -> 30.3 us
  starting transfers between devices: 0.04 us -> 26.4 us
  blocking collectives: 23.4 us -> 0 us
  matrix products: 14.3 us -> 0 us
  between operations: 13.4 us -> 0.12 us
  Pallas kernels: 0 us -> 10.2 us
  other arithmetic: 3.09 us -> 0.74 us
  local copies, waits for them, and re-layouts: 0.97 us -> 2.48 us
    reduce_scatter x1 -> x0, waiting for transfers between devices: 67.8 us -> none  [shards(): lax.psum_scatter(part.astype(jnp.bfloat16), 'expert', scatter_dimension=0...]
    ppermute x0 -> x26, waiting for transfers between devices: none -> 30.3 us  [partner(): lax.ppermute(array, 'expert', [(i, i ^ distance) for i in range(devices)])]
    ppermute x0 -> x26, starting transfers between devices: none -> 26.4 us  [partner(): lax.ppermute(array, 'expert', [(i, i ^ distance) for i in range(devices)])]
    all_gather x1 -> x0, waiting for transfers between devices: 25.8 us -> none  [shards(): all_values = lax.all_gather(values, 'expert', axis=0, tiled=True)]
    all_gather x1 -> x0, blocking collectives: 23.4 us -> none  [shards(): all_table = lax.all_gather(table, 'expert', axis=0, tiled=True)]
    dot_general x2 -> x0, matrix products: 14.3 us -> none  [the longest x1 10 us: shards(): jnp.dot(hidden, w_down[0], preferred_element_type=jnp.float32) * row_weight]
    pallas_call x0 -> x3, Pallas kernels: none -> 10.2 us  [the longest x1 8.1 us: shards(): pl.pallas_call(functools.partial(expert_kernel, capacity, planes), out_sh...]
    unnamed x1 -> x8, local copies, waits for them, and re-layouts: 0.09 us -> 2.48 us
  transfers between devices with their start and end apart: 2 -> 26, of which waited for: 2 -> 12; matrix products, arithmetic and copies ran while one was open for 1% -> 1% of each run, Pallas kernels for 0% -> 0%
where the time goes in v2:
time: 70.5 us; the launch traced here: 70.3 us
  waiting for transfers between devices  30.3 us (43%)
  starting transfers between devices  26.4 us (37%)
  Pallas kernels  10.2 us (14%)
  local copies, waits for them, and re-layouts  2.48 us (4%)
  other arithmetic  0.74 us (1%)
    ppermute x26, waiting for transfers between devices, partner(): lax.ppermute(array, 'expert', [(i, i ^ distance) for i in range(devices)])  30.3 us
    ppermute x26, starting transfers between devices, partner(): lax.ppermute(array, 'expert', [(i, i ^ distance) for i in range(devices)])  26.4 us
    pallas_call x1, Pallas kernels, shards(): pl.pallas_call(functools.partial(expert_kernel, capacity, planes), out_sh...  8.1 us
    unnamed x8, local copies, waits for them, and re-layouts  2.48 us
    pallas_call x1, Pallas kernels, shards(): pl.pallas_call(functools.partial(mix_kernel, capacity, planes), out_shape...  1.47 us
  transfers between devices with their start and end apart: 26, of which 12 were waited for; matrix products, arithmetic and copies ran while one was open for 1% of the time, Pallas kernels for 0%

profile of v2, /device:TPU:0, one launch (start us, length us, event | category | flops | bytes accessed | tf_op | source)
XLA Modules:
  0.0 70.3 jit_solution(12633195363563481639)
XLA Ops:
  0.0 0.8 %copy.9.route_ref = s32[16,2]{1,0:T(8,128)S(1)} copy(s32[16,2]{0,1:T(2,128)} %param.9) | data formatting | bytes 256 | tf_op args[2]
  0.8 0.9 %copy-done = bf16[16,7168]{1,0:T(8,128)(2,1)S(1)} copy-done((bf16[16,7168]{1,0:T(8,128)(2,1)S(1)}, bf16[16,7168]{1,0:T(8,128)(2,1)}, u32[]{:S(2)}) %copy-start) | copy-done | bytes 229400
  1.7 0.7 copy-done.1
  2.4 0.6 shard_map.73
  3.0 4.1 %collective-permute-start.7 = (bf16[48,1792]{1,0:T(8,128)(2,1)S(1)}, bf16[48,1792]{1,0:T(8,128)(2,1)S(1)}, u32[]{:S(2)}, u32[]{:S(2)}) collective-permute-start(bf16[48,1792]{1,0:T(8,128)(2,1)S(1)} %get-tuple-element.19), channel_id=1, source_target_pairs={{0,8},{1,9},{2,10},{3,11},{4,12},{5,13},{6,14},{7,15},{8,0},{9,1},... | collective-permute-start | bytes 516104 | tf_op jit(solution)/shard_map/ppermute | solution.py:173
  7.1 1.3 %collective-permute-start.11 = (bf16[48,1792]{1,0:T(8,128)(2,1)S(1)}, bf16[48,1792]{1,0:T(8,128)(2,1)S(1)}, u32[]{:S(2)}, u32[]{:S(2)}) collective-permute-start(bf16[48,1792]{1,0:T(8,128)(2,1)S(1)} %get-tuple-element.20), channel_id=1, source_target_pairs={{0,12},{1,13},{2,14},{3,15},{4,8},{5,9},{6,10},{7,11},{8,4},{9,5},... | collective-permute-start | bytes 516104 | tf_op jit(solution)/shard_map/ppermute | solution.py:173
  8.5 0.2 collective-permute-start.3
  8.7 1.5 %collective-permute-start = (bf16[48,1792]{1,0:T(8,128)(2,1)S(1)}, bf16[48,1792]{1,0:T(8,128)(2,1)S(1)}, u32[]{:S(2)}, u32[]{:S(2)}) collective-permute-start(bf16[48,1792]{1,0:T(8,128)(2,1)S(1)} %get-tuple-element.17.refs_0_), channel_id=1, source_target_pairs={{0,2},{1,3},{2,0},{3,1},{4,6},{5,7},{6,4},{7,5},{8,10},{9,11},{10,... | collective-permute-start | bytes 516104 | tf_op jit(solution)/shard_map/ppermute | solution.py:173
  10.2 0.0 collective-permute-start.1
  10.2 9.5 %collective-permute-done.7.refs_8_ = bf16[48,1792]{1,0:T(8,128)(2,1)S(1)} collective-permute-done((bf16[48,1792]{1,0:T(8,128)(2,1)S(1)}, bf16[48,1792]{1,0:T(8,128)(2,1)S(1)}, u32[]{:S(2)}, u32[]{:S(2)}) %collective-permute-start.7) | collective-permute-done | bytes 172064 | tf_op jit(solution)/shard_map/ppermute | solution.py:173
  19.7 1.9 %collective-permute-start.8 = (bf16[48,1792]{1,0:T(8,128)(2,1)S(1)}, bf16[48,1792]{1,0:T(8,128)(2,1)S(1)}, u32[]{:S(2)}, u32[]{:S(2)}) collective-permute-start(bf16[48,1792]{1,0:T(8,128)(2,1)S(1)} %collective-permute-done.7.refs_8_), channel_id=1, source_target_pairs={{0,2},{1,3},{2,0},{3,1},{4,6},{5,7},{6,4},{7,5},{8,10},{9,11},{10,... | collective-permute-start | bytes 516104 | tf_op jit(solution)/shard_map/ppermute | solution.py:173
  21.6 0.0 collective-permute-done.11.refs_12_
  21.6 0.2 collective-permute-start.12
  21.8 0.0 collective-permute-done.3.refs_4_
  21.8 1.9 %collective-permute-start.4 = (bf16[48,1792]{1,0:T(8,128)(2,1)S(1)}, bf16[48,1792]{1,0:T(8,128)(2,1)S(1)}, u32[]{:S(2)}, u32[]{:S(2)}) collective-permute-start(bf16[48,1792]{1,0:T(8,128)(2,1)S(1)} %collective-permute-done.3.refs_4_), channel_id=1, source_target_pairs={{0,2},{1,3},{2,0},{3,1},{4,6},{5,7},{6,4},{7,5},{8,10},{9,11},{10,... | collective-permute-start | bytes 516104 | tf_op jit(solution)/shard_map/ppermute | solution.py:173
  23.6 0.0 collective-permute-done.refs_1_
  23.7 0.0 collective-permute-start.2
  23.7 0.0 collective-permute-done.1.refs_2_
  23.7 0.5 collective-permute-start.13
  24.2 2.9 %collective-permute-done.8.refs_9_ = bf16[48,1792]{1,0:T(8,128)(2,1)S(1)} collective-permute-done((bf16[48,1792]{1,0:T(8,128)(2,1)S(1)}, bf16[48,1792]{1,0:T(8,128)(2,1)S(1)}, u32[]{:S(2)}, u32[]{:S(2)}) %collective-permute-start.8) | collective-permute-done | bytes 172064 | tf_op jit(solution)/shard_map/ppermute | solution.py:173
  27.1 0.0 collective-permute-start.5
  27.1 2.9 %collective-permute-done.12.refs_13_ = bf16[48,1792]{1,0:T(8,128)(2,1)S(1)} collective-permute-done((bf16[48,1792]{1,0:T(8,128)(2,1)S(1)}, bf16[48,1792]{1,0:T(8,128)(2,1)S(1)}, u32[]{:S(2)}, u32[]{:S(2)}) %collective-permute-start.12) | collective-permute-done | bytes 172064 | tf_op jit(solution)/shard_map/ppermute | solution.py:173
  30.0 0.0 collective-permute-start.9
  30.0 1.8 %collective-permute-done.4.refs_5_ = bf16[48,1792]{1,0:T(8,128)(2,1)S(1)} collective-permute-done((bf16[48,1792]{1,0:T(8,128)(2,1)S(1)}, bf16[48,1792]{1,0:T(8,128)(2,1)S(1)}, u32[]{:S(2)}, u32[]{:S(2)}) %collective-permute-start.4) | collective-permute-done | bytes 172064 | tf_op jit(solution)/shard_map/ppermute | solution.py:173
  31.9 0.0 collective-permute-start.10
  31.9 0.0 collective-permute-done.2.refs_3_
  31.9 0.5 collective-permute-start.14
  32.4 0.0 collective-permute-done.13.refs_14_
  32.4 0.1 collective-permute-start.6
  32.4 0.0 collective-permute-done.5.refs_6_
  32.4 0.0 collective-permute-done.9.refs_10_
  32.4 0.8 %collective-permute-done.10.refs_11_ = bf16[48,1792]{1,0:T(8,128)(2,1)S(1)} collective-permute-done((bf16[48,1792]{1,0:T(8,128)(2,1)S(1)}, bf16[48,1792]{1,0:T(8,128)(2,1)S(1)}, u32[]{:S(2)}, u32[]{:S(2)}) %collective-permute-start.10) | collective-permute-done | bytes 172064 | tf_op jit(solution)/shard_map/ppermute | solution.py:173
  33.3 0.2 collective-permute-done.14.refs_15_
  33.5 0.3 collective-permute-done.6.refs_7_
  33.8 8.1 %shard_map.74 = (bf16[96,1792]{1,0:T(8,128)(2,1)S(1)}, bf16[96,1792]{1,0:T(8,128)(2,1)S(1)}, bf16[96,1792]{1,0:T(8,128)(2,1)S(1)}, bf16[96,1792]{1,0:T(8,128)(2,...) custom-call(bf16[48,1792]{1,0:T(8,128)(2,1)S(1)} %get-tuple-element., ...), custom_call_target="tpu_custom_call" | custom-call | tf_op jit(solution)/shard_map/pallas_call | solution.py:192
  41.9 0.3 collective-permute-start.23
  42.2 0.0 copy-done.2
  42.2 0.1 copy.10.code_ref
  42.3 0.3 collective-permute-start.20
  42.7 0.3 collective-permute-start.17
  43.1 0.3 collective-permute-start.15
  43.5 0.2 collective-permute-done.23
  43.7 1.3 %collective-permute-start.24 = (bf16[48,1792]{1,0:T(8,128)(2,1)S(1)}, bf16[48,1792]{1,0:T(8,128)(2,1)S(1)}, u32[]{:S(2)}, u32[]{:S(2)}) collective-permute-start(bf16[48,1792]{1,0:T(8,128)(2,1)S(1)} %fusion), channel_id=1, source_target_pairs={{0,2},{1,3},{2,0},{3,1},{4,6},{5,7},{6,4},{7,5},{8,10},{9,11},{10,... | collective-permute-start | bytes 516104 | tf_op jit(solution)/shard_map/ppermute | solution.py:173
  45.0 0.0 collective-permute-done.20
  45.1 0.8 %collective-permute-start.21 = (bf16[48,1792]{1,0:T(8,128)(2,1)S(1)}, bf16[48,1792]{1,0:T(8,128)(2,1)S(1)}, u32[]{:S(2)}, u32[]{:S(2)}) collective-permute-start(bf16[48,1792]{1,0:T(8,128)(2,1)S(1)} %fusion.3), channel_id=1, source_target_pairs={{0,2},{1,3},{2,0},{3,1},{4,6},{5,7},{6,4},{7,5},{8,10},{9,11},{10,... | collective-permute-start | bytes 516104 | tf_op jit(solution)/shard_map/ppermute | solution.py:173
  46.0 0.0 collective-permute-done.17
  46.0 1.3 %collective-permute-start.18 = (bf16[48,1792]{1,0:T(8,128)(2,1)S(1)}, bf16[48,1792]{1,0:T(8,128)(2,1)S(1)}, u32[]{:S(2)}, u32[]{:S(2)}) collective-permute-start(bf16[48,1792]{1,0:T(8,128)(2,1)S(1)} %fusion.6), channel_id=1, source_target_pairs={{0,2},{1,3},{2,0},{3,1},{4,6},{5,7},{6,4},{7,5},{8,10},{9,11},{10,... | collective-permute-start | bytes 516104 | tf_op jit(solution)/shard_map/ppermute | solution.py:173
  47.4 0.0 collective-permute-done.15
  47.4 0.1 fusion.9
  47.5 0.8 %collective-permute-start.16 = (bf16[48,1792]{1,0:T(8,128)(2,1)S(1)}, bf16[48,1792]{1,0:T(8,128)(2,1)S(1)}, u32[]{:S(2)}, u32[]{:S(2)}) collective-permute-start(bf16[48,1792]{1,0:T(8,128)(2,1)S(1)} %fusion.9), channel_id=1, source_target_pairs={{0,2},{1,3},{2,0},{3,1},{4,6},{5,7},{6,4},{7,5},{8,10},{9,11},{10,... | collective-permute-start | bytes 516104 | tf_op jit(solution)/shard_map/ppermute | solution.py:173
  48.3 2.6 %collective-permute-done.24 = bf16[48,1792]{1,0:T(8,128)(2,1)S(1)} collective-permute-done((bf16[48,1792]{1,0:T(8,128)(2,1)S(1)}, bf16[48,1792]{1,0:T(8,128)(2,1)S(1)}, u32[]{:S(2)}, u32[]{:S(2)}) %collective-permute-start.24) | collective-permute-done | bytes 172064 | tf_op jit(solution)/shard_map/ppermute | solution.py:173
  51.0 0.1 fusion.2
  51.0 4.3 %collective-permute-start.25 = (bf16[48,1792]{1,0:T(8,128)(2,1)S(1)}, bf16[48,1792]{1,0:T(8,128)(2,1)S(1)}, u32[]{:S(2)}, u32[]{:S(2)}) collective-permute-start(bf16[48,1792]{1,0:T(8,128)(2,1)S(1)} %fusion.2), channel_id=1, source_target_pairs={{0,12},{1,13},{2,14},{3,15},{4,8},{5,9},{6,10},{7,11},{8,4},{9,5},... | collective-permute-start | bytes 516104 | tf_op jit(solution)/shard_map/ppermute | solution.py:173
  55.4 0.0 collective-permute-done.21
  55.4 2.7 %collective-permute-start.22 = (bf16[48,1792]{1,0:T(8,128)(2,1)S(1)}, bf16[48,1792]{1,0:T(8,128)(2,1)S(1)}, u32[]{:S(2)}, u32[]{:S(2)}) collective-permute-start(bf16[48,1792]{1,0:T(8,128)(2,1)S(1)} %fusion.5), channel_id=1, source_target_pairs={{0,8},{1,9},{2,10},{3,11},{4,12},{5,13},{6,14},{7,15},{8,0},{9,1},... | collective-permute-start | bytes 516104 | tf_op jit(solution)/shard_map/ppermute | solution.py:173
  58.2 0.2 collective-permute-done.18
  58.3 0.1 fusion.8
  58.4 1.5 %collective-permute-start.19 = (bf16[48,1792]{1,0:T(8,128)(2,1)S(1)}, bf16[48,1792]{1,0:T(8,128)(2,1)S(1)}, u32[]{:S(2)}, u32[]{:S(2)}) collective-permute-start(bf16[48,1792]{1,0:T(8,128)(2,1)S(1)} %fusion.8), channel_id=1, source_target_pairs={{0,4},{1,5},{2,6},{3,7},{4,0},{5,1},{6,2},{7,3},{8,12},{9,13},{10,... | collective-permute-start | bytes 516104 | tf_op jit(solution)/shard_map/ppermute | solution.py:173
  59.9 1.4 %collective-permute-done.16 = bf16[48,1792]{1,0:T(8,128)(2,1)S(1)} collective-permute-done((bf16[48,1792]{1,0:T(8,128)(2,1)S(1)}, bf16[48,1792]{1,0:T(8,128)(2,1)S(1)}, u32[]{:S(2)}, u32[]{:S(2)}) %collective-permute-start.16) | collective-permute-done | bytes 172064 | tf_op jit(solution)/shard_map/ppermute | solution.py:173
  61.4 0.1 fusion.11.refs_0_
  61.4 0.0 collective-permute-done.25.refs_3_
  61.4 7.4 %collective-permute-done.22.refs_2_ = bf16[48,1792]{1,0:T(8,128)(2,1)S(1)} collective-permute-done((bf16[48,1792]{1,0:T(8,128)(2,1)S(1)}, bf16[48,1792]{1,0:T(8,128)(2,1)S(1)}, u32[]{:S(2)}, u32[]{:S(2)}) %collective-permute-start.22) | collective-permute-done | bytes 172064 | tf_op jit(solution)/shard_map/ppermute | solution.py:173
  68.8 0.0 collective-permute-done.19.refs_1_
  68.8 1.5 %shard_map.75 = bf16[16,7168]{1,0:T(8,128)(2,1)} custom-call(s32[16,2]{1,0:T(8,128)S(1)} %copy.9.route_ref, s32[16,2]{1,0:T(8,128)S(1)} %copy.10.code_ref, bf16[48,1792]{1,0:T(8,128)(2,1)S(1)} %fusion.11.refs_0_, bf16[48,1792]{1,0:T(8,128)(2,1)S(1)} %collective-permute-done.19.refs_1_, bf16[48,1792]{1,0:T(8,128)(2,1)S(1)} %collective-permute-done.22.refs_2_, ...), custom_call_target="tpu_custom_call" | custom-call | tf_op jit(solution)/shard_map/pallas_call | solution.py:212
  (15 shorter events, 0.5 us)
Async XLA Ops:
  0.8 0.9 %copy-start = (bf16[16,7168]{1,0:T(8,128)(2,1)S(1)}, bf16[16,7168]{1,0:T(8,128)(2,1)}, u32[]{:S(2)}) copy-start(bf16[16,7168]{1,0:T(8,128)(2,1)} %tok_ref.1) | copy-start | bytes 688132
  1.7 0.7 copy-start.1
  3.0 16.7 %collective-permute-start.7 = (bf16[48,1792]{1,0:T(8,128)(2,1)S(1)}, bf16[48,1792]{1,0:T(8,128)(2,1)S(1)}, u32[]{:S(2)}, u32[]{:S(2)}) collective-permute-start(bf16[48,1792]{1,0:T(8,128)(2,1)S(1)} %get-tuple-element.19), channel_id=1, source_target_pairs={{0,8},{1,9},{2,10},{3,11},{4,12},{5,13},{6,14},{7,15},{8,0},{9,1},... | collective-permute-start | bytes 516104 | tf_op jit(solution)/shard_map/ppermute | solution.py:173
  7.1 14.5 %collective-permute-start.11 = (bf16[48,1792]{1,0:T(8,128)(2,1)S(1)}, bf16[48,1792]{1,0:T(8,128)(2,1)S(1)}, u32[]{:S(2)}, u32[]{:S(2)}) collective-permute-start(bf16[48,1792]{1,0:T(8,128)(2,1)S(1)} %get-tuple-element.20), channel_id=1, source_target_pairs={{0,12},{1,13},{2,14},{3,15},{4,8},{5,9},{6,10},{7,11},{8,4},{9,5},... | collective-permute-start | bytes 516104 | tf_op jit(solution)/shard_map/ppermute | solution.py:173
  8.5 13.3 %collective-permute-start.3 = (bf16[48,1792]{1,0:T(8,128)(2,1)S(1)}, bf16[48,1792]{1,0:T(8,128)(2,1)S(1)}, u32[]{:S(2)}, u32[]{:S(2)}) collective-permute-start(bf16[48,1792]{1,0:T(8,128)(2,1)S(1)} %get-tuple-element.18), channel_id=1, source_target_pairs={{0,4},{1,5},{2,6},{3,7},{4,0},{5,1},{6,2},{7,3},{8,12},{9,13},{10,... | collective-permute-start | bytes 516104 | tf_op jit(solution)/shard_map/ppermute | solution.py:173
  8.7 33.5 %copy-start.2 = (s32[16,2]{0,1:T(2,128)S(1)}, s32[16,2]{0,1:T(2,128)}, u32[]{:S(2)}) copy-start(s32[16,2]{0,1:T(2,128)} %param.10) | copy-start | bytes 388
  8.7 14.9 %collective-permute-start = (bf16[48,1792]{1,0:T(8,128)(2,1)S(1)}, bf16[48,1792]{1,0:T(8,128)(2,1)S(1)}, u32[]{:S(2)}, u32[]{:S(2)}) collective-permute-start(bf16[48,1792]{1,0:T(8,128)(2,1)S(1)} %get-tuple-element.17.refs_0_), channel_id=1, source_target_pairs={{0,2},{1,3},{2,0},{3,1},{4,6},{5,7},{6,4},{7,5},{8,10},{9,11},{10,... | collective-permute-start | bytes 516104 | tf_op jit(solution)/shard_map/ppermute | solution.py:173
  10.2 13.4 %collective-permute-start.1 = (bf16[48,1792]{1,0:T(8,128)(2,1)S(1)}, bf16[48,1792]{1,0:T(8,128)(2,1)S(1)}, u32[]{:S(2)}, u32[]{:S(2)}) collective-permute-start(bf16[48,1792]{1,0:T(8,128)(2,1)S(1)} %get-tuple-element.17.refs_0_), channel_id=1, source_target_pairs={{0,1},{1,0},{2,3},{3,2},{4,5},{5,4},{6,7},{7,6},{8,9},{9,8},{10,11... | collective-permute-start | bytes 516104 | tf_op jit(solution)/shard_map/ppermute | solution.py:173
  19.7 7.3 %collective-permute-start.8 = (bf16[48,1792]{1,0:T(8,128)(2,1)S(1)}, bf16[48,1792]{1,0:T(8,128)(2,1)S(1)}, u32[]{:S(2)}, u32[]{:S(2)}) collective-permute-start(bf16[48,1792]{1,0:T(8,128)(2,1)S(1)} %collective-permute-done.7.refs_8_), channel_id=1, source_target_pairs={{0,2},{1,3},{2,0},{3,1},{4,6},{5,7},{6,4},{7,5},{8,10},{9,11},{10,... | collective-permute-start | bytes 516104 | tf_op jit(solution)/shard_map/ppermute | solution.py:173
  21.6 8.4 %collective-permute-start.12 = (bf16[48,1792]{1,0:T(8,128)(2,1)S(1)}, bf16[48,1792]{1,0:T(8,128)(2,1)S(1)}, u32[]{:S(2)}, u32[]{:S(2)}) collective-permute-start(bf16[48,1792]{1,0:T(8,128)(2,1)S(1)} %collective-permute-done.11.refs_12_), channel_id=1, source_target_pairs={{0,2},{1,3},{2,0},{3,1},{4,6},{5,7},{6,4},{7,5},{8,10},{9,11},{10,... | collective-permute-start | bytes 516104 | tf_op jit(solution)/shard_map/ppermute | solution.py:173
  21.8 10.1 %collective-permute-start.4 = (bf16[48,1792]{1,0:T(8,128)(2,1)S(1)}, bf16[48,1792]{1,0:T(8,128)(2,1)S(1)}, u32[]{:S(2)}, u32[]{:S(2)}) collective-permute-start(bf16[48,1792]{1,0:T(8,128)(2,1)S(1)} %collective-permute-done.3.refs_4_), channel_id=1, source_target_pairs={{0,2},{1,3},{2,0},{3,1},{4,6},{5,7},{6,4},{7,5},{8,10},{9,11},{10,... | collective-permute-start | bytes 516104 | tf_op jit(solution)/shard_map/ppermute | solution.py:173
  23.7 8.2 %collective-permute-start.2 = (bf16[48,1792]{1,0:T(8,128)(2,1)S(1)}, bf16[48,1792]{1,0:T(8,128)(2,1)S(1)}, u32[]{:S(2)}, u32[]{:S(2)}) collective-permute-start(bf16[48,1792]{1,0:T(8,128)(2,1)S(1)} %collective-permute-done.refs_1_), channel_id=1, source_target_pairs={{0,1},{1,0},{2,3},{3,2},{4,5},{5,4},{6,7},{7,6},{8,9},{9,8},{10,11... | collective-permute-start | bytes 516104 | tf_op jit(solution)/shard_map/ppermute | solution.py:173
  23.7 8.7 %collective-permute-start.13 = (bf16[48,1792]{1,0:T(8,128)(2,1)S(1)}, bf16[48,1792]{1,0:T(8,128)(2,1)S(1)}, u32[]{:S(2)}, u32[]{:S(2)}) collective-permute-start(bf16[48,1792]{1,0:T(8,128)(2,1)S(1)} %collective-permute-done.11.refs_12_), channel_id=1, source_target_pairs={{0,1},{1,0},{2,3},{3,2},{4,5},{5,4},{6,7},{7,6},{8,9},{9,8},{10,11... | collective-permute-start | bytes 516104 | tf_op jit(solution)/shard_map/ppermute | solution.py:173
  27.1 5.4 %collective-permute-start.5 = (bf16[48,1792]{1,0:T(8,128)(2,1)S(1)}, bf16[48,1792]{1,0:T(8,128)(2,1)S(1)}, u32[]{:S(2)}, u32[]{:S(2)}) collective-permute-start(bf16[48,1792]{1,0:T(8,128)(2,1)S(1)} %collective-permute-done.3.refs_4_), channel_id=1, source_target_pairs={{0,1},{1,0},{2,3},{3,2},{4,5},{5,4},{6,7},{7,6},{8,9},{9,8},{10,11... | collective-permute-start | bytes 516104 | tf_op jit(solution)/shard_map/ppermute | solution.py:173
  30.0 2.4 %collective-permute-start.9 = (bf16[48,1792]{1,0:T(8,128)(2,1)S(1)}, bf16[48,1792]{1,0:T(8,128)(2,1)S(1)}, u32[]{:S(2)}, u32[]{:S(2)}) collective-permute-start(bf16[48,1792]{1,0:T(8,128)(2,1)S(1)} %collective-permute-done.7.refs_8_), channel_id=1, source_target_pairs={{0,1},{1,0},{2,3},{3,2},{4,5},{5,4},{6,7},{7,6},{8,9},{9,8},{10,11... | collective-permute-start | bytes 516104 | tf_op jit(solution)/shard_map/ppermute | solution.py:173
  31.9 1.4 %collective-permute-start.10 = (bf16[48,1792]{1,0:T(8,128)(2,1)S(1)}, bf16[48,1792]{1,0:T(8,128)(2,1)S(1)}, u32[]{:S(2)}, u32[]{:S(2)}) collective-permute-start(bf16[48,1792]{1,0:T(8,128)(2,1)S(1)} %collective-permute-done.8.refs_9_), channel_id=1, source_target_pairs={{0,1},{1,0},{2,3},{3,2},{4,5},{5,4},{6,7},{7,6},{8,9},{9,8},{10,11... | collective-permute-start | bytes 516104 | tf_op jit(solution)/shard_map/ppermute | solution.py:173
  31.9 1.6 %collective-permute-start.14 = (bf16[48,1792]{1,0:T(8,128)(2,1)S(1)}, bf16[48,1792]{1,0:T(8,128)(2,1)S(1)}, u32[]{:S(2)}, u32[]{:S(2)}) collective-permute-start(bf16[48,1792]{1,0:T(8,128)(2,1)S(1)} %collective-permute-done.12.refs_13_), channel_id=1, source_target_pairs={{0,1},{1,0},{2,3},{3,2},{4,5},{5,4},{6,7},{7,6},{8,9},{9,8},{10,11... | collective-permute-start | bytes 516104 | tf_op jit(solution)/shard_map/ppermute | solution.py:173
  32.4 1.4 %collective-permute-start.6 = (bf16[48,1792]{1,0:T(8,128)(2,1)S(1)}, bf16[48,1792]{1,0:T(8,128)(2,1)S(1)}, u32[]{:S(2)}, u32[]{:S(2)}) collective-permute-start(bf16[48,1792]{1,0:T(8,128)(2,1)S(1)} %collective-permute-done.4.refs_5_), channel_id=1, source_target_pairs={{0,1},{1,0},{2,3},{3,2},{4,5},{5,4},{6,7},{7,6},{8,9},{9,8},{10,11... | collective-permute-start | bytes 516104 | tf_op jit(solution)/shard_map/ppermute | solution.py:173
  41.9 1.7 %collective-permute-start.23 = (bf16[96,1792]{1,0:T(8,128)(2,1)S(1)}, bf16[96,1792]{1,0:T(8,128)(2,1)S(1)}, u32[]{:S(2)}, u32[]{:S(2)}) collective-permute-start(bf16[96,1792]{1,0:T(8,128)(2,1)S(1)} %get-tuple-element.28), channel_id=1, source_target_pairs={{0,1},{1,0},{2,3},{3,2},{4,5},{5,4},{6,7},{7,6},{8,9},{9,8},{10,11... | collective-permute-start | bytes 1032200 | tf_op jit(solution)/shard_map/ppermute | solution.py:173
  42.3 2.7 %collective-permute-start.20 = (bf16[96,1792]{1,0:T(8,128)(2,1)S(1)}, bf16[96,1792]{1,0:T(8,128)(2,1)S(1)}, u32[]{:S(2)}, u32[]{:S(2)}) collective-permute-start(bf16[96,1792]{1,0:T(8,128)(2,1)S(1)} %get-tuple-element.26), channel_id=1, source_target_pairs={{0,1},{1,0},{2,3},{3,2},{4,5},{5,4},{6,7},{7,6},{8,9},{9,8},{10,11... | collective-permute-start | bytes 1032200 | tf_op jit(solution)/shard_map/ppermute | solution.py:173
  42.7 3.2 %collective-permute-start.17 = (bf16[96,1792]{1,0:T(8,128)(2,1)S(1)}, bf16[96,1792]{1,0:T(8,128)(2,1)S(1)}, u32[]{:S(2)}, u32[]{:S(2)}) collective-permute-start(bf16[96,1792]{1,0:T(8,128)(2,1)S(1)} %get-tuple-element.24), channel_id=1, source_target_pairs={{0,1},{1,0},{2,3},{3,2},{4,5},{5,4},{6,7},{7,6},{8,9},{9,8},{10,11... | collective-permute-start | bytes 1032200 | tf_op jit(solution)/shard_map/ppermute | solution.py:173
  43.1 4.3 %collective-permute-start.15 = (bf16[96,1792]{1,0:T(8,128)(2,1)S(1)}, bf16[96,1792]{1,0:T(8,128)(2,1)S(1)}, u32[]{:S(2)}, u32[]{:S(2)}) collective-permute-start(bf16[96,1792]{1,0:T(8,128)(2,1)S(1)} %get-tuple-element.22), channel_id=1, source_target_pairs={{0,1},{1,0},{2,3},{3,2},{4,5},{5,4},{6,7},{7,6},{8,9},{9,8},{10,11... | collective-permute-start | bytes 1032200 | tf_op jit(solution)/shard_map/ppermute | solution.py:173
  43.7 7.3 %collective-permute-start.24 = (bf16[48,1792]{1,0:T(8,128)(2,1)S(1)}, bf16[48,1792]{1,0:T(8,128)(2,1)S(1)}, u32[]{:S(2)}, u32[]{:S(2)}) collective-permute-start(bf16[48,1792]{1,0:T(8,128)(2,1)S(1)} %fusion), channel_id=1, source_target_pairs={{0,2},{1,3},{2,0},{3,1},{4,6},{5,7},{6,4},{7,5},{8,10},{9,11},{10,... | collective-permute-start | bytes 516104 | tf_op jit(solution)/shard_map/ppermute | solution.py:173
  45.1 10.2 %collective-permute-start.21 = (bf16[48,1792]{1,0:T(8,128)(2,1)S(1)}, bf16[48,1792]{1,0:T(8,128)(2,1)S(1)}, u32[]{:S(2)}, u32[]{:S(2)}) collective-permute-start(bf16[48,1792]{1,0:T(8,128)(2,1)S(1)} %fusion.3), channel_id=1, source_target_pairs={{0,2},{1,3},{2,0},{3,1},{4,6},{5,7},{6,4},{7,5},{8,10},{9,11},{10,... | collective-permute-start | bytes 516104 | tf_op jit(solution)/shard_map/ppermute | solution.py:173
  46.0 12.3 %collective-permute-start.18 = (bf16[48,1792]{1,0:T(8,128)(2,1)S(1)}, bf16[48,1792]{1,0:T(8,128)(2,1)S(1)}, u32[]{:S(2)}, u32[]{:S(2)}) collective-permute-start(bf16[48,1792]{1,0:T(8,128)(2,1)S(1)} %fusion.6), channel_id=1, source_target_pairs={{0,2},{1,3},{2,0},{3,1},{4,6},{5,7},{6,4},{7,5},{8,10},{9,11},{10,... | collective-permute-start | bytes 516104 | tf_op jit(solution)/shard_map/ppermute | solution.py:173
  47.5 13.9 %collective-permute-start.16 = (bf16[48,1792]{1,0:T(8,128)(2,1)S(1)}, bf16[48,1792]{1,0:T(8,128)(2,1)S(1)}, u32[]{:S(2)}, u32[]{:S(2)}) collective-permute-start(bf16[48,1792]{1,0:T(8,128)(2,1)S(1)} %fusion.9), channel_id=1, source_target_pairs={{0,2},{1,3},{2,0},{3,1},{4,6},{5,7},{6,4},{7,5},{8,10},{9,11},{10,... | collective-permute-start | bytes 516104 | tf_op jit(solution)/shard_map/ppermute | solution.py:173
  51.0 10.4 %collective-permute-start.25 = (bf16[48,1792]{1,0:T(8,128)(2,1)S(1)}, bf16[48,1792]{1,0:T(8,128)(2,1)S(1)}, u32[]{:S(2)}, u32[]{:S(2)}) collective-permute-start(bf16[48,1792]{1,0:T(8,128)(2,1)S(1)} %fusion.2), channel_id=1, source_target_pairs={{0,12},{1,13},{2,14},{3,15},{4,8},{5,9},{6,10},{7,11},{8,4},{9,5},... | collective-permute-start | bytes 516104 | tf_op jit(solution)/shard_map/ppermute | solution.py:173
  55.4 13.4 %collective-permute-start.22 = (bf16[48,1792]{1,0:T(8,128)(2,1)S(1)}, bf16[48,1792]{1,0:T(8,128)(2,1)S(1)}, u32[]{:S(2)}, u32[]{:S(2)}) collective-permute-start(bf16[48,1792]{1,0:T(8,128)(2,1)S(1)} %fusion.5), channel_id=1, source_target_pairs={{0,8},{1,9},{2,10},{3,11},{4,12},{5,13},{6,14},{7,15},{8,0},{9,1},... | collective-permute-start | bytes 516104 | tf_op jit(solution)/shard_map/ppermute | solution.py:173
  58.4 10.4 %collective-permute-start.19 = (bf16[48,1792]{1,0:T(8,128)(2,1)S(1)}, bf16[48,1792]{1,0:T(8,128)(2,1)S(1)}, u32[]{:S(2)}, u32[]{:S(2)}) collective-permute-start(bf16[48,1792]{1,0:T(8,128)(2,1)S(1)} %fusion.8), channel_id=1, source_target_pairs={{0,4},{1,5},{2,6},{3,7},{4,0},{5,1},{6,2},{7,3},{8,12},{9,13},{10,... | collective-permute-start | bytes 516104 | tf_op jit(solution)/shard_map/ppermute | solution.py:173

commit v3 on v2

v3 whole, which is shorter than its diff:
```python
import functools

import jax
import jax.numpy as jnp
from jax import lax
from jax.experimental import pallas as pl
from jax.experimental.pallas import tpu as pltpu
from jax.sharding import PartitionSpec as P

SHARDS = 4
QUARTERS = 4
VMEM_BYTES = 16 * 1024 * 1024
PACK_VMEM_BYTES = 48 * 1024 * 1024
LOAD_VMEM_BYTES = 40 * 1024 * 1024


def zero_one(condition):
    return jnp.where(condition, 1.0, 0.0).astype(jnp.bfloat16)


def exact_dot(left, right):
    return jnp.dot(left, right, preferred_element_type=jnp.float32)


def pack_kernel(capacity, planes, tok_hbm, scale_hbm, route_ref, *rest):
    outs = rest[:planes]
    quarters_ref, tok_ref, scale_ref, tok_sem, scale_sem = rest[planes:]
    tok_copy = pltpu.make_async_copy(tok_hbm, tok_ref, tok_sem)
    scale_copy = pltpu.make_async_copy(scale_hbm, scale_ref, scale_sem)
    tok_copy.start()
    scale_copy.start()
    rows, features = tok_ref.shape
    width = features // QUARTERS
    plane = lax.axis_index("expert") // SHARDS
    offsets = (route_ref[...] ^ plane).astype(jnp.float32).astype(jnp.bfloat16)
    columns = QUARTERS * rows
    picks = offsets.shape[0]
    copies = zero_one(
        lax.broadcasted_iota(jnp.int32, (rows, columns), 1) % rows
        == lax.broadcasted_iota(jnp.int32, (rows, columns), 0)
    )
    turned = exact_dot(offsets, copies)
    numbers = lax.broadcasted_iota(jnp.int32, (planes, columns), 0).astype(jnp.float32)
    named = jnp.zeros((planes, columns), jnp.float32)
    for pick in range(picks):
        named = named + jnp.where(turned[pick : pick + 1, :] == numbers, 1.0, 0.0)
    first = lax.broadcasted_iota(jnp.int32, (columns, columns), 0)
    second = lax.broadcasted_iota(jnp.int32, (columns, columns), 1)
    before = zero_one((first // rows == second // rows) & (first < second))
    position = exact_dot(named.astype(jnp.bfloat16), before)
    slot_row = lax.broadcasted_iota(jnp.int32, (QUARTERS * capacity, columns), 0)
    slot_col = lax.broadcasted_iota(jnp.int32, (QUARTERS * capacity, columns), 1)
    same_quarter = slot_row // capacity == slot_col // rows
    slot = (slot_row % capacity).astype(jnp.float32)
    tok_copy.wait()
    scale_copy.wait()
    for block in range(features // 128):
        quarter, at = divmod(block * 128, width)
        codes = tok_ref[:, block * 128 : (block + 1) * 128].astype(jnp.float32)
        factors = scale_ref[:, block : block + 1]
        quarters_ref[quarter * rows : (quarter + 1) * rows, at : at + 128] = (
            codes * factors
        ).astype(jnp.bfloat16)
    values = quarters_ref[...]
    for offset in range(planes):
        pick_out = zero_one(
            same_quarter
            & (named[offset : offset + 1, :] > 0.5)
            & (position[offset : offset + 1, :] == slot)
        )
        outs[offset][...] = exact_dot(pick_out, values).astype(jnp.bfloat16)


def order_matrix(capacity, turned):
    size = SHARDS * QUARTERS * capacity
    row = lax.broadcasted_iota(jnp.int32, (size, size), 1 if turned else 0)
    col = lax.broadcasted_iota(jnp.int32, (size, size), 0 if turned else 1)
    quarter, block, slot = row // (SHARDS * capacity), (row // capacity) % SHARDS, row % capacity
    return zero_one(col == (block * QUARTERS + quarter) * capacity + slot)


def expert_kernel(capacity, offsets, load, *refs):
    count = offsets * SHARDS
    blocks = refs[:count]
    group, tall = SHARDS * capacity, QUARTERS * capacity
    width = blocks[0].shape[1]
    spans = [slice(quarter * width, (quarter + 1) * width) for quarter in range(QUARTERS)]
    waits = []
    if load:
        given = refs[count : count + 3]
        kept_ref, sent_ref, gate_ref, up_ref, down_ref, rows_ref, part_ref, sems = refs[count + 3 :]
        for span in spans:
            for part in (0, 1):
                here = (slice(None), span, slice(None))
                waits.append((given[part].at[here], (gate_ref, up_ref)[part].at[here]))
        for span in spans:
            here = (slice(None), slice(None), span)
            waits.append((given[2].at[here], down_ref.at[here]))
        waits = [
            pltpu.make_async_copy(source, target, sems.at[index])
            for index, (source, target) in enumerate(waits)
        ]
        for copy in waits:
            copy.start()
    else:
        gate_ref, up_ref, down_ref, unused, kept_ref, sent_ref, rows_ref, part_ref = refs[count:]
    order = order_matrix(capacity, False)
    for offset in range(offsets):
        held = jnp.concatenate(
            [blocks[offset * SHARDS + member][...] for member in range(SHARDS)], axis=0
        )
        sorted_rows = exact_dot(order, held).astype(jnp.bfloat16)
        for quarter in range(QUARTERS):
            rows_ref[quarter, offset * group : (offset + 1) * group, :] = sorted_rows[
                quarter * group : (quarter + 1) * group, :
            ]
    gate = jnp.zeros((offsets * group, gate_ref.shape[2]), jnp.float32)
    upward = jnp.zeros((offsets * group, gate_ref.shape[2]), jnp.float32)
    for quarter, span in enumerate(spans):
        if load:
            waits[2 * quarter].wait()
            waits[2 * quarter + 1].wait()
        gate = gate + exact_dot(rows_ref[quarter], gate_ref[0, span, :])
        upward = upward + exact_dot(rows_ref[quarter], up_ref[0, span, :])
    hidden = (gate / (1.0 + jnp.exp(-gate)) * upward).astype(jnp.bfloat16)
    for quarter, span in enumerate(spans):
        if load:
            waits[2 * QUARTERS + quarter].wait()
        part_ref[quarter] = exact_dot(hidden, down_ref[0, :, span]).astype(jnp.bfloat16)
    back = order_matrix(capacity, True)
    for offset in range(offsets):
        held = jnp.concatenate(
            [
                part_ref[quarter, offset * group : (offset + 1) * group, :]
                for quarter in range(QUARTERS)
            ],
            axis=0,
        )
        answer = exact_dot(back, held).astype(jnp.bfloat16)
        for member in range(SHARDS):
            out_ref = sent_ref if member >= 2 else kept_ref
            at = (member % 2 * offsets + offset) * tall
            out_ref[at : at + tall, :] = answer[member * tall : (member + 1) * tall, :]


def mix_kernel(capacity, planes, route_ref, code_ref, *refs):
    returned, out_ref = refs[:planes], refs[planes]
    picks, rows = route_ref.shape
    width = out_ref.shape[1] // QUARTERS
    tall = QUARTERS * rows
    plane = lax.axis_index("expert") // SHARDS
    copies = zero_one(
        lax.broadcasted_iota(jnp.int32, (tall, rows), 0) % rows
        == lax.broadcasted_iota(jnp.int32, (tall, rows), 1)
    )

    def turned(numbers):
        numbers = numbers.astype(jnp.float32).astype(jnp.bfloat16)
        return lax.dot_general(
            copies, numbers, (((1,), (1,)), ((), ())), preferred_element_type=jnp.float32
        )

    offsets = turned(route_ref[...] ^ plane)
    codes = code_ref[...]
    weights = (turned(codes // 256) * 256.0 + turned(codes % 256)) / 65536.0
    numbers = lax.broadcasted_iota(jnp.int32, (tall, planes), 1).astype(jnp.float32)
    named = jnp.zeros((tall, planes), jnp.float32)
    factors = jnp.zeros((tall, planes), jnp.float32)
    for pick in range(picks):
        here = offsets[:, pick : pick + 1] == numbers
        named = named + jnp.where(here, 1.0, 0.0)
        factors = factors + jnp.where(here, weights[:, pick : pick + 1], 0.0)
    first = lax.broadcasted_iota(jnp.int32, (tall, tall), 0)
    second = lax.broadcasted_iota(jnp.int32, (tall, tall), 1)
    before = zero_one((first // rows == second // rows) & (second < first))
    position = exact_dot(before, named.astype(jnp.bfloat16))
    slot_row = lax.broadcasted_iota(jnp.int32, (tall, QUARTERS * capacity), 0)
    slot_col = lax.broadcasted_iota(jnp.int32, (tall, QUARTERS * capacity), 1)
    same_quarter = slot_row // rows == slot_col // capacity
    slot = (slot_col % capacity).astype(jnp.float32)
    total = jnp.zeros((tall, width), jnp.float32)
    for offset in range(planes):
        take = zero_one(
            same_quarter
            & (named[:, offset : offset + 1] > 0.5)
            & (position[:, offset : offset + 1] == slot)
        )
        total = total + factors[:, offset : offset + 1] * exact_dot(take, returned[offset][...])
    total = total.astype(jnp.bfloat16)
    for quarter in range(QUARTERS):
        out_ref[:, quarter * width : (quarter + 1) * width] = total[
            quarter * rows : (quarter + 1) * rows, :
        ]


def shards(tokens, scales, routes, gate_codes, w_gate, w_up, w_down):
    tok_rows, features = tokens.shape
    picks_per = routes.shape[1]
    devices = lax.axis_size("expert")
    planes = devices // SHARDS
    capacity = 3 * tok_rows * picks_per // (2 * planes)
    width = features // QUARTERS
    tall = QUARTERS * capacity
    vmem = pl.BlockSpec(memory_space=pltpu.VMEM)
    hbm = pl.BlockSpec(memory_space=pl.ANY)
    anywhere = pl.BlockSpec(memory_space=pl.ANY)
    params = pltpu.CompilerParams(vmem_limit_bytes=VMEM_BYTES)
    pack_params = pltpu.CompilerParams(vmem_limit_bytes=PACK_VMEM_BYTES)
    load_params = pltpu.CompilerParams(vmem_limit_bytes=LOAD_VMEM_BYTES)

    def partner(array, distance):
        return lax.ppermute(array, "expert", [(i, i ^ distance) for i in range(devices)])

    block = jax.ShapeDtypeStruct((tall, width), jnp.bfloat16)
    packed = pl.pallas_call(
        functools.partial(pack_kernel, capacity, planes),
        out_shape=[block] * planes,
        in_specs=[hbm] * 2 + [vmem],
        out_specs=[vmem] * planes,
        scratch_shapes=[
            pltpu.VMEM((QUARTERS * tok_rows, width), jnp.bfloat16),
            pltpu.VMEM(tokens.shape, tokens.dtype),
            pltpu.VMEM(scales.shape, scales.dtype),
            pltpu.SemaphoreType.DMA,
            pltpu.SemaphoreType.DMA,
        ],
        compiler_params=pack_params,
    )(tokens, scales, routes.T)

    groups = ((0, planes // 2), (planes // 2, 3 * planes // 4), (3 * planes // 4, planes))
    arriving = [packed[0]] + [partner(packed[at], at * SHARDS) for at in range(1, planes)]
    returned = []
    weights, kept = (w_gate, w_up, w_down), None
    for start, stop in groups:
        gathered = []
        for offset in range(start, stop):
            own = arriving[offset]
            across = partner(own, 2)
            gathered += [own, across, partner(own, 1), partner(across, 1)]
        offsets = stop - start
        rows = offsets * SHARDS * capacity
        load = start == 0
        half = jax.ShapeDtypeStruct((2 * offsets * tall, width), jnp.bfloat16)
        scratch = [pltpu.VMEM((QUARTERS, rows, width), jnp.bfloat16)] * 2
        held = [jax.ShapeDtypeStruct(array.shape, array.dtype) for array in weights]
        kept, sent, *loaded = pl.pallas_call(
            functools.partial(expert_kernel, capacity, offsets, load),
            out_shape=[half] * 2 + (held if load else []),
            in_specs=[vmem] * (offsets * SHARDS) + ([hbm] * 3 if load else [vmem] * 3 + [anywhere]),
            out_specs=[vmem] * (5 if load else 2),
            scratch_shapes=scratch + ([pltpu.SemaphoreType.DMA((3 * QUARTERS,))] if load else []),
            compiler_params=load_params if load else params,
            cost_estimate=pl.CostEstimate(
                flops=6 * rows * features * w_gate.shape[2], bytes_accessed=0, transcendentals=0
            ),
        )(*gathered, *weights, *([] if load else [kept]))
        weights = loaded if load else weights
        if load:
            last = groups[-1][0]
            *arriving[last:], kept = lax.optimization_barrier((*arriving[last:], kept))
        arrived = partner(sent, 1).astype(jnp.float32)
        mine = kept.astype(jnp.float32)
        middle = offsets * tall
        across = partner((mine[middle:] + arrived[middle:]).astype(jnp.bfloat16), 2)
        answer = mine[:middle] + arrived[:middle] + across.astype(jnp.float32)
        answer = answer.astype(jnp.bfloat16)
        for offset in range(start, stop):
            piece = answer[(offset - start) * tall : (offset - start + 1) * tall]
            returned.append(piece if offset == 0 else partner(piece, offset * SHARDS))

    return pl.pallas_call(
        functools.partial(mix_kernel, capacity, planes),
        out_shape=jax.ShapeDtypeStruct((tok_rows, features), jnp.bfloat16),
        in_specs=[vmem] * (planes + 2),
        out_specs=vmem,
        compiler_params=params,
    )(routes.T, gate_codes.T, *returned)


def solution(mesh):
    in_specs = (
        P(("groups", "expert"), None),
        P(("groups", "expert"), None),
        P(("groups", "expert"), None),
        P(("groups", "expert"), None),
        P("expert", None, None),
        P("expert", None, None),
        P("expert", None, None),
    )
    out_specs = P(("groups", "expert"), None)
    return jax.shard_map(shards, mesh=mesh, in_specs=in_specs, out_specs=out_specs, check_vma=False)
```

time: 70.5 us -> 69.1 us (0.980)
  waiting for transfers between devices: 30.3 us -> 26.2 us
  Pallas kernels: 10.2 us -> 12.5 us
    ppermute x26 -> x24, waiting for transfers between devices: 30.3 us -> 26.2 us  [partner(): lax.ppermute(array, 'expert', [(i, i ^ distance) for i in range(devices)])]
    pallas_call x1 -> x3, Pallas kernels: 8.1 us -> 9.91 us  [shards(): pl.pallas_call(functools.partial(expert_kernel, capacity, offsets, load),...]
    ppermute x26 -> x24, starting transfers between devices: 26.4 us -> 27 us  [partner(): lax.ppermute(array, 'expert', [(i, i ^ distance) for i in range(devices)])]
    unnamed x8 -> x10, local copies, waits for them, and re-layouts: 2.48 us -> 2.32 us
  transfers between devices with their start and end apart: 26 -> 24, of which waited for: 12 -> 11; matrix products, arithmetic and copies ran while one was open for 1% -> 1% of each run, Pallas kernels for 0% -> 11%
where the time goes in v3:
time: 69.1 us; the launch traced here: 68.9 us
  starting transfers between devices  27 us (39%)
  waiting for transfers between devices  26.2 us (38%)
  Pallas kernels  12.5 us (18%)
  local copies, waits for them, and re-layouts  2.35 us (3%)
  other arithmetic  0.71 us (1%)
    ppermute x24, starting transfers between devices, partner(): lax.ppermute(array, 'expert', [(i, i ^ distance) for i in range(devices)])  27 us
    ppermute x24, waiting for transfers between devices, partner(): lax.ppermute(array, 'expert', [(i, i ^ distance) for i in range(devices)])  26.2 us
    pallas_call x3, Pallas kernels, shards(): pl.pallas_call(functools.partial(expert_kernel, capacity, offsets, load),...  9.91 us
    unnamed x10, local copies, waits for them, and re-layouts  2.32 us
    pallas_call x1, Pallas kernels, shards(): pl.pallas_call(functools.partial(mix_kernel, capacity, planes), out_shape...  1.48 us
  transfers between devices with their start and end apart: 24, of which 11 were waited for; matrix products, arithmetic and copies ran while one was open for 1% of the time, Pallas kernels for 11%

profile of v3, /device:TPU:0, one launch (start us, length us, event | category | flops | bytes accessed | tf_op | source)
XLA Modules:
  0.0 68.9 jit_solution(15116577533692810084)
XLA Ops:
  0.0 0.9 %copy-done = bf16[16,7168]{1,0:T(8,128)(2,1)S(1)} copy-done((bf16[16,7168]{1,0:T(8,128)(2,1)S(1)}, bf16[16,7168]{1,0:T(8,128)(2,1)}, u32[]{:S(2)}) %copy-start) | copy-done | bytes 229400
  0.9 0.7 %copy-done.1 = f32[16,56]{1,0:T(8,128)S(1)} copy-done((f32[16,56]{1,0:T(8,128)S(1)}, f32[16,56]{1,0:T(8,128)}, u32[]{:S(2)}) %copy-start.1) | copy-done | bytes 3608
  1.6 0.7 copy-done.2
  2.3 1.1 %shard_map.73 = (bf16[48,1792]{1,0:T(8,128)(2,1)S(1)}, bf16[48,1792]{1,0:T(8,128)(2,1)S(1)}, bf16[48,1792]{1,0:T(8,128)(2,1)S(1)}, bf16[48,1792]{1,0:T(8,128)(2,1)S(1)}) custom-call(bf16[16,7168]{1,0:T(8,128)(2,1)S(1)} %copy-done, f32[16,56]{1,0:T(8,128)S(1)} %copy-done.1, s32[2,16]{1,0:T(2,128)S(1)} %bitcast.2), custom_call_target="tpu_custom_call" | custom-call | tf_op jit(solution)/shard_map/pallas_call | solution.py:215
  3.5 3.1 %collective-permute-start.4 = (bf16[48,1792]{1,0:T(8,128)(2,1)S(1)}, bf16[48,1792]{1,0:T(8,128)(2,1)S(1)}, u32[]{:S(2)}, u32[]{:S(2)}) collective-permute-start(bf16[48,1792]{1,0:T(8,128)(2,1)S(1)} %get-tuple-element.22), channel_id=1, source_target_pairs={{0,4},{1,5},{2,6},{3,7},{4,0},{5,1},{6,2},{7,3},{8,12},{9,13},{10,... | collective-permute-start | bytes 516104 | tf_op jit(solution)/shard_map/ppermute | solution.py:212
  6.5 1.5 %collective-permute-start.1 = (bf16[48,1792]{1,0:T(8,128)(2,1)S(1)}, bf16[48,1792]{1,0:T(8,128)(2,1)S(1)}, u32[]{:S(2)}, u32[]{:S(2)}) collective-permute-start(bf16[48,1792]{1,0:T(8,128)(2,1)S(1)} %get-tuple-element.21.refs_0_), channel_id=1, source_target_pairs={{0,2},{1,3},{2,0},{3,1},{4,6},{5,7},{6,4},{7,5},{8,10},{9,11},{10,... | collective-permute-start | bytes 516104 | tf_op jit(solution)/shard_map/ppermute | solution.py:212
  8.1 2.6 %collective-permute-start.11 = (bf16[48,1792]{1,0:T(8,128)(2,1)S(1)}, bf16[48,1792]{1,0:T(8,128)(2,1)S(1)}, u32[]{:S(2)}, u32[]{:S(2)}) collective-permute-start(bf16[48,1792]{1,0:T(8,128)(2,1)S(1)} %get-tuple-element.26), channel_id=1, source_target_pairs={{0,8},{1,9},{2,10},{3,11},{4,12},{5,13},{6,14},{7,15},{8,0},{9,1},... | collective-permute-start | bytes 516104 | tf_op jit(solution)/shard_map/ppermute | solution.py:212
  10.7 0.3 collective-permute-done.4.refs_4_
  10.9 5.0 %collective-permute-start.5 = (bf16[48,1792]{1,0:T(8,128)(2,1)S(1)}, bf16[48,1792]{1,0:T(8,128)(2,1)S(1)}, u32[]{:S(2)}, u32[]{:S(2)}) collective-permute-start(bf16[48,1792]{1,0:T(8,128)(2,1)S(1)} %collective-permute-done.4.refs_4_), channel_id=1, source_target_pairs={{0,2},{1,3},{2,0},{3,1},{4,6},{5,7},{6,4},{7,5},{8,10},{9,11},{10,... | collective-permute-start | bytes 516104 | tf_op jit(solution)/shard_map/ppermute | solution.py:212
  15.9 0.0 collective-permute-start.2
  16.0 0.0 collective-permute-done.1.refs_1_
  16.0 0.5 collective-permute-start.3
  16.5 1.8 %collective-permute-done.11.refs_0_ = bf16[48,1792]{1,0:T(8,128)(2,1)S(1)} collective-permute-done((bf16[48,1792]{1,0:T(8,128)(2,1)S(1)}, bf16[48,1792]{1,0:T(8,128)(2,1)S(1)}, u32[]{:S(2)}, u32[]{:S(2)}) %collective-permute-start.11) | collective-permute-done | bytes 172064 | tf_op jit(solution)/shard_map/ppermute | solution.py:212
  18.2 0.5 collective-permute-start.12
  18.8 0.0 collective-permute-start.6
  18.8 1.9 %collective-permute-done.5.refs_5_ = bf16[48,1792]{1,0:T(8,128)(2,1)S(1)} collective-permute-done((bf16[48,1792]{1,0:T(8,128)(2,1)S(1)}, bf16[48,1792]{1,0:T(8,128)(2,1)S(1)}, u32[]{:S(2)}, u32[]{:S(2)}) %collective-permute-start.5) | collective-permute-done | bytes 172064 | tf_op jit(solution)/shard_map/ppermute | solution.py:212
  20.6 0.0 collective-permute-start.7
  20.6 0.0 collective-permute-done.2.refs_2_
  20.6 2.1 %collective-permute-start = (bf16[48,1792]{1,0:T(8,128)(2,1)S(1)}, bf16[48,1792]{1,0:T(8,128)(2,1)S(1)}, u32[]{:S(2)}, u32[]{:S(2)}) collective-permute-start(bf16[48,1792]{1,0:T(8,128)(2,1)S(1)} %get-tuple-element.20), channel_id=1, source_target_pairs={{0,12},{1,13},{2,14},{3,15},{4,8},{5,9},{6,10},{7,11},{8,4},{9,5},... | collective-permute-start | bytes 516104 | tf_op jit(solution)/shard_map/ppermute | solution.py:212
  22.7 0.0 collective-permute-done.3.refs_3_
  22.7 0.2 collective-permute-start.13
  22.9 0.7 %collective-permute-done.12.refs_1_ = bf16[48,1792]{1,0:T(8,128)(2,1)S(1)} collective-permute-done((bf16[48,1792]{1,0:T(8,128)(2,1)S(1)}, bf16[48,1792]{1,0:T(8,128)(2,1)S(1)}, u32[]{:S(2)}, u32[]{:S(2)}) %collective-permute-start.12) | collective-permute-done | bytes 172064 | tf_op jit(solution)/shard_map/ppermute | solution.py:212
  23.6 0.0 collective-permute-start.14
  23.6 0.0 collective-permute-done.6.refs_6_
  23.6 0.0 collective-permute-done.7.refs_7_
  23.7 5.3 %shard_map.74 = (bf16[192,1792]{1,0:T(8,128)(2,1)S(1)}, bf16[192,1792]{1,0:T(8,128)(2,1)S(1)}, bf16[1,7168,256]{2,1,0:T(8,128)(2,1)S(1)}, bf16[1,7168,256]{2,1,0:T(8,128)(2,1)S(1)}, bf16[1,256,7168]{2,1,0:T(8,128)(2,1)S(1)}) custom-call(bf16[48,1792]{1,0:T(8,128)(2,1)S(1)} %get-tuple-element.21.refs_0_, bf16[48,1792]{1,0:T(8,128)(2,1)S(1)} %collective-permute-done.1.refs_1_, ...), custom_call_target="tpu_custom_call" | custom-call | flops 1056964608 | tf_op jit(solution)/shard_map/pallas_call | solution.py:246
  29.0 0.3 collective-permute-done.refs_0_
  29.3 0.0 collective-permute-done.13.refs_2_
  29.3 0.0 collective-permute-done.14.refs_3_
  29.3 2.3 %shard_map.75 = (bf16[96,1792]{1,0:T(8,128)(2,1)S(1)}, bf16[96,1792]{1,0:T(8,128)(2,1)S(1)}) custom-call(bf16[48,1792]{1,0:T(8,128)(2,1)S(1)} %collective-permute-done.11.refs_0_, bf16[48,1792]{1,0:T(8,128)(2,1)S(1)} %collective-permute-done.12.refs_1_, bf16[48,1792]{1,0:T(8,128)(2,1)S(1)} %collective-permute-done.13.refs_2_, ...), custom_call_target="tpu_custom_call" | custom-call | flops 528482304 | tf_op jit(solution)/shard_map/pallas_call | solution.py:246
  31.6 0.3 collective-permute-start.15
  31.9 2.4 %collective-permute-start.18 = (bf16[48,1792]{1,0:T(8,128)(2,1)S(1)}, bf16[48,1792]{1,0:T(8,128)(2,1)S(1)}, u32[]{:S(2)}, u32[]{:S(2)}) collective-permute-start(bf16[48,1792]{1,0:T(8,128)(2,1)S(1)} %collective-permute-done.refs_0_), channel_id=1, source_target_pairs={{0,2},{1,3},{2,0},{3,1},{4,6},{5,7},{6,4},{7,5},{8,10},{9,11},{10,... | collective-permute-start | bytes 516104 | tf_op jit(solution)/shard_map/ppermute | solution.py:212
  34.2 0.2 collective-permute-start.19
  34.5 4.8 %collective-permute-done.18.refs_1_ = bf16[48,1792]{1,0:T(8,128)(2,1)S(1)} collective-permute-done((bf16[48,1792]{1,0:T(8,128)(2,1)S(1)}, bf16[48,1792]{1,0:T(8,128)(2,1)S(1)}, u32[]{:S(2)}, u32[]{:S(2)}) %collective-permute-start.18) | collective-permute-done | bytes 172064 | tf_op jit(solution)/shard_map/ppermute | solution.py:212
  39.2 0.0 collective-permute-start.20
  39.2 0.0 collective-permute-done.15
  39.3 1.8 %collective-permute-start.16 = (bf16[48,1792]{1,0:T(8,128)(2,1)S(1)}, bf16[48,1792]{1,0:T(8,128)(2,1)S(1)}, u32[]{:S(2)}, u32[]{:S(2)}) collective-permute-start(bf16[48,1792]{1,0:T(8,128)(2,1)S(1)} %fusion.6), channel_id=1, source_target_pairs={{0,2},{1,3},{2,0},{3,1},{4,6},{5,7},{6,4},{7,5},{8,10},{9,11},{10,... | collective-permute-start | bytes 516104 | tf_op jit(solution)/shard_map/ppermute | solution.py:212
  41.1 0.1 convert_element_type.45
  41.2 0.3 collective-permute-start.8
  41.5 0.0 collective-permute-done.19.refs_2_
  41.5 0.0 collective-permute-done.20.refs_3_
  41.5 2.3 %shard_map.76 = (bf16[96,1792]{1,0:T(8,128)(2,1)S(1)}, bf16[96,1792]{1,0:T(8,128)(2,1)S(1)}) custom-call(bf16[48,1792]{1,0:T(8,128)(2,1)S(1)} %collective-permute-done.refs_0_, bf16[48,1792]{1,0:T(8,128)(2,1)S(1)} %collective-permute-done.18.refs_1_, bf16[48,1792]{1,0:T(8,128)(2,1)S(1)} %collective-permute-done.19.refs_2_, ...), custom_call_target="tpu_custom_call" | custom-call | flops 528482304 | tf_op jit(solution)/shard_map/pallas_call | solution.py:246
  43.8 0.3 collective-permute-start.21
  44.2 2.0 %collective-permute-done.16 = bf16[48,1792]{1,0:T(8,128)(2,1)S(1)} collective-permute-done((bf16[48,1792]{1,0:T(8,128)(2,1)S(1)}, bf16[48,1792]{1,0:T(8,128)(2,1)S(1)}, u32[]{:S(2)}, u32[]{:S(2)}) %collective-permute-start.16) | collective-permute-done | bytes 172064 | tf_op jit(solution)/shard_map/ppermute | solution.py:212
  46.2 2.2 %collective-permute-start.17 = (bf16[48,1792]{1,0:T(8,128)(2,1)S(1)}, bf16[48,1792]{1,0:T(8,128)(2,1)S(1)}, u32[]{:S(2)}, u32[]{:S(2)}) collective-permute-start(bf16[48,1792]{1,0:T(8,128)(2,1)S(1)} %fusion.8), channel_id=1, source_target_pairs={{0,8},{1,9},{2,10},{3,11},{4,12},{5,13},{6,14},{7,15},{8,0},{9,1},... | collective-permute-start | bytes 516104 | tf_op jit(solution)/shard_map/ppermute | solution.py:212
  48.5 0.0 collective-permute-done.21
  48.5 0.1 fusion.3
  48.6 0.0 copy-start.4
  48.6 1.8 %collective-permute-start.22 = (bf16[48,1792]{1,0:T(8,128)(2,1)S(1)}, bf16[48,1792]{1,0:T(8,128)(2,1)S(1)}, u32[]{:S(2)}, u32[]{:S(2)}) collective-permute-start(bf16[48,1792]{1,0:T(8,128)(2,1)S(1)} %fusion.3), channel_id=1, source_target_pairs={{0,2},{1,3},{2,0},{3,1},{4,6},{5,7},{6,4},{7,5},{8,10},{9,11},{10,... | collective-permute-start | bytes 516104 | tf_op jit(solution)/shard_map/ppermute | solution.py:212
  50.4 0.0 collective-permute-done.8
  50.4 0.1 convert_element_type.46
  50.5 0.1 fusion
  50.6 0.4 collective-permute-start.9
  50.9 5.0 %collective-permute-done.22 = bf16[48,1792]{1,0:T(8,128)(2,1)S(1)} collective-permute-done((bf16[48,1792]{1,0:T(8,128)(2,1)S(1)}, bf16[48,1792]{1,0:T(8,128)(2,1)S(1)}, u32[]{:S(2)}, u32[]{:S(2)}) %collective-permute-start.22) | collective-permute-done | bytes 172064 | tf_op jit(solution)/shard_map/ppermute | solution.py:212
  56.0 0.1 fusion.5
  56.0 1.2 %collective-permute-start.23 = (bf16[48,1792]{1,0:T(8,128)(2,1)S(1)}, bf16[48,1792]{1,0:T(8,128)(2,1)S(1)}, u32[]{:S(2)}, u32[]{:S(2)}) collective-permute-start(bf16[48,1792]{1,0:T(8,128)(2,1)S(1)} %fusion.5), channel_id=1, source_target_pairs={{0,12},{1,13},{2,14},{3,15},{4,8},{5,9},{6,10},{7,11},{8,4},{9,5},... | collective-permute-start | bytes 516104 | tf_op jit(solution)/shard_map/ppermute | solution.py:212
  57.3 4.5 %collective-permute-done.9 = bf16[96,1792]{1,0:T(8,128)(2,1)S(1)} collective-permute-done((bf16[96,1792]{1,0:T(8,128)(2,1)S(1)}, bf16[96,1792]{1,0:T(8,128)(2,1)S(1)}, u32[]{:S(2)}, u32[]{:S(2)}) %collective-permute-start.9) | collective-permute-done | bytes 344096 | tf_op jit(solution)/shard_map/ppermute | solution.py:212
  61.8 0.1 fusion.2
  61.9 0.5 collective-permute-start.10
  62.4 0.0 collective-permute-done.17.refs_2_
  62.4 1.0 %collective-permute-done.23.refs_3_ = bf16[48,1792]{1,0:T(8,128)(2,1)S(1)} collective-permute-done((bf16[48,1792]{1,0:T(8,128)(2,1)S(1)}, bf16[48,1792]{1,0:T(8,128)(2,1)S(1)}, u32[]{:S(2)}, u32[]{:S(2)}) %collective-permute-start.23) | collective-permute-done | bytes 172064 | tf_op jit(solution)/shard_map/ppermute | solution.py:212
  63.4 3.9 %collective-permute-done.10.refs_1_ = bf16[48,1792]{1,0:T(8,128)(2,1)S(1)} collective-permute-done((bf16[48,1792]{1,0:T(8,128)(2,1)S(1)}, bf16[48,1792]{1,0:T(8,128)(2,1)S(1)}, u32[]{:S(2)}, u32[]{:S(2)}) %collective-permute-start.10) | collective-permute-done | bytes 172064 | tf_op jit(solution)/shard_map/ppermute | solution.py:212
  67.4 0.0 copy-done.3
  67.4 1.5 %shard_map.77 = bf16[16,7168]{1,0:T(8,128)(2,1)} custom-call(s32[2,16]{1,0:T(2,128)S(1)} %bitcast.3, s32[2,16]{1,0:T(2,128)S(1)} %bitcast.4, bf16[48,1792]{1,0:T(8,128)(2,1)S(1)} %get-tuple-element.36.refs_0_, bf16[48,1792]{1,0:T(8,128)(2,1)S(1)} %collective-permute-done.10.refs_1_, bf16[48,1792]{1,0:T(8,128)(2,1)S(1)} %collective-permute-done.17.refs_2_, ...), custom_call_target="tpu_custom_call" | custom-call | tf_op jit(solution)/shard_map/pallas_call | solution.py:271
  (12 shorter events, 0.3 us)
Async XLA Ops:
  0.0 0.9 %copy-start = (bf16[16,7168]{1,0:T(8,128)(2,1)S(1)}, bf16[16,7168]{1,0:T(8,128)(2,1)}, u32[]{:S(2)}) copy-start(bf16[16,7168]{1,0:T(8,128)(2,1)} %tok_hbm.1) | copy-start | bytes 688132
  0.9 0.7 %copy-start.1 = (f32[16,56]{1,0:T(8,128)S(1)}, f32[16,56]{1,0:T(8,128)}, u32[]{:S(2)}) copy-start(f32[16,56]{1,0:T(8,128)} %scale_hbm.1) | copy-start | bytes 10756
  1.6 0.7 copy-start.2
  3.5 7.5 %collective-permute-start.4 = (bf16[48,1792]{1,0:T(8,128)(2,1)S(1)}, bf16[48,1792]{1,0:T(8,128)(2,1)S(1)}, u32[]{:S(2)}, u32[]{:S(2)}) collective-permute-start(bf16[48,1792]{1,0:T(8,128)(2,1)S(1)} %get-tuple-element.22), channel_id=1, source_target_pairs={{0,4},{1,5},{2,6},{3,7},{4,0},{5,1},{6,2},{7,3},{8,12},{9,13},{10,... | collective-permute-start | bytes 516104 | tf_op jit(solution)/shard_map/ppermute | solution.py:212
  6.5 9.4 %collective-permute-start.1 = (bf16[48,1792]{1,0:T(8,128)(2,1)S(1)}, bf16[48,1792]{1,0:T(8,128)(2,1)S(1)}, u32[]{:S(2)}, u32[]{:S(2)}) collective-permute-start(bf16[48,1792]{1,0:T(8,128)(2,1)S(1)} %get-tuple-element.21.refs_0_), channel_id=1, source_target_pairs={{0,2},{1,3},{2,0},{3,1},{4,6},{5,7},{6,4},{7,5},{8,10},{9,11},{10,... | collective-permute-start | bytes 516104 | tf_op jit(solution)/shard_map/ppermute | solution.py:212
  8.1 10.2 %collective-permute-start.11 = (bf16[48,1792]{1,0:T(8,128)(2,1)S(1)}, bf16[48,1792]{1,0:T(8,128)(2,1)S(1)}, u32[]{:S(2)}, u32[]{:S(2)}) collective-permute-start(bf16[48,1792]{1,0:T(8,128)(2,1)S(1)} %get-tuple-element.26), channel_id=1, source_target_pairs={{0,8},{1,9},{2,10},{3,11},{4,12},{5,13},{6,14},{7,15},{8,0},{9,1},... | collective-permute-start | bytes 516104 | tf_op jit(solution)/shard_map/ppermute | solution.py:212
  10.9 9.7 %collective-permute-start.5 = (bf16[48,1792]{1,0:T(8,128)(2,1)S(1)}, bf16[48,1792]{1,0:T(8,128)(2,1)S(1)}, u32[]{:S(2)}, u32[]{:S(2)}) collective-permute-start(bf16[48,1792]{1,0:T(8,128)(2,1)S(1)} %collective-permute-done.4.refs_4_), channel_id=1, source_target_pairs={{0,2},{1,3},{2,0},{3,1},{4,6},{5,7},{6,4},{7,5},{8,10},{9,11},{10,... | collective-permute-start | bytes 516104 | tf_op jit(solution)/shard_map/ppermute | solution.py:212
  15.9 4.7 %collective-permute-start.2 = (bf16[48,1792]{1,0:T(8,128)(2,1)S(1)}, bf16[48,1792]{1,0:T(8,128)(2,1)S(1)}, u32[]{:S(2)}, u32[]{:S(2)}) collective-permute-start(bf16[48,1792]{1,0:T(8,128)(2,1)S(1)} %get-tuple-element.21.refs_0_), channel_id=1, source_target_pairs={{0,1},{1,0},{2,3},{3,2},{4,5},{5,4},{6,7},{7,6},{8,9},{9,8},{10,11... | collective-permute-start | bytes 516104 | tf_op jit(solution)/shard_map/ppermute | solution.py:212
  16.0 6.8 %collective-permute-start.3 = (bf16[48,1792]{1,0:T(8,128)(2,1)S(1)}, bf16[48,1792]{1,0:T(8,128)(2,1)S(1)}, u32[]{:S(2)}, u32[]{:S(2)}) collective-permute-start(bf16[48,1792]{1,0:T(8,128)(2,1)S(1)} %collective-permute-done.1.refs_1_), channel_id=1, source_target_pairs={{0,1},{1,0},{2,3},{3,2},{4,5},{5,4},{6,7},{7,6},{8,9},{9,8},{10,11... | collective-permute-start | bytes 516104 | tf_op jit(solution)/shard_map/ppermute | solution.py:212
  18.2 5.4 %collective-permute-start.12 = (bf16[48,1792]{1,0:T(8,128)(2,1)S(1)}, bf16[48,1792]{1,0:T(8,128)(2,1)S(1)}, u32[]{:S(2)}, u32[]{:S(2)}) collective-permute-start(bf16[48,1792]{1,0:T(8,128)(2,1)S(1)} %collective-permute-done.11.refs_0_), channel_id=1, source_target_pairs={{0,2},{1,3},{2,0},{3,1},{4,6},{5,7},{6,4},{7,5},{8,10},{9,11},{10,... | collective-permute-start | bytes 516104 | tf_op jit(solution)/shard_map/ppermute | solution.py:212
  18.8 4.9 %collective-permute-start.6 = (bf16[48,1792]{1,0:T(8,128)(2,1)S(1)}, bf16[48,1792]{1,0:T(8,128)(2,1)S(1)}, u32[]{:S(2)}, u32[]{:S(2)}) collective-permute-start(bf16[48,1792]{1,0:T(8,128)(2,1)S(1)} %collective-permute-done.4.refs_4_), channel_id=1, source_target_pairs={{0,1},{1,0},{2,3},{3,2},{4,5},{5,4},{6,7},{7,6},{8,9},{9,8},{10,11... | collective-permute-start | bytes 516104 | tf_op jit(solution)/shard_map/ppermute | solution.py:212
  20.6 3.0 %collective-permute-start.7 = (bf16[48,1792]{1,0:T(8,128)(2,1)S(1)}, bf16[48,1792]{1,0:T(8,128)(2,1)S(1)}, u32[]{:S(2)}, u32[]{:S(2)}) collective-permute-start(bf16[48,1792]{1,0:T(8,128)(2,1)S(1)} %collective-permute-done.5.refs_5_), channel_id=1, source_target_pairs={{0,1},{1,0},{2,3},{3,2},{4,5},{5,4},{6,7},{7,6},{8,9},{9,8},{10,11... | collective-permute-start | bytes 516104 | tf_op jit(solution)/shard_map/ppermute | solution.py:212
  20.6 8.7 %collective-permute-start = (bf16[48,1792]{1,0:T(8,128)(2,1)S(1)}, bf16[48,1792]{1,0:T(8,128)(2,1)S(1)}, u32[]{:S(2)}, u32[]{:S(2)}) collective-permute-start(bf16[48,1792]{1,0:T(8,128)(2,1)S(1)} %get-tuple-element.20), channel_id=1, source_target_pairs={{0,12},{1,13},{2,14},{3,15},{4,8},{5,9},{6,10},{7,11},{8,4},{9,5},... | collective-permute-start | bytes 516104 | tf_op jit(solution)/shard_map/ppermute | solution.py:212
  22.7 6.6 %collective-permute-start.13 = (bf16[48,1792]{1,0:T(8,128)(2,1)S(1)}, bf16[48,1792]{1,0:T(8,128)(2,1)S(1)}, u32[]{:S(2)}, u32[]{:S(2)}) collective-permute-start(bf16[48,1792]{1,0:T(8,128)(2,1)S(1)} %collective-permute-done.11.refs_0_), channel_id=1, source_target_pairs={{0,1},{1,0},{2,3},{3,2},{4,5},{5,4},{6,7},{7,6},{8,9},{9,8},{10,11... | collective-permute-start | bytes 516104 | tf_op jit(solution)/shard_map/ppermute | solution.py:212
  23.6 5.7 %collective-permute-start.14 = (bf16[48,1792]{1,0:T(8,128)(2,1)S(1)}, bf16[48,1792]{1,0:T(8,128)(2,1)S(1)}, u32[]{:S(2)}, u32[]{:S(2)}) collective-permute-start(bf16[48,1792]{1,0:T(8,128)(2,1)S(1)} %collective-permute-done.12.refs_1_), channel_id=1, source_target_pairs={{0,1},{1,0},{2,3},{3,2},{4,5},{5,4},{6,7},{7,6},{8,9},{9,8},{10,11... | collective-permute-start | bytes 516104 | tf_op jit(solution)/shard_map/ppermute | solution.py:212
  31.6 7.6 %collective-permute-start.15 = (bf16[96,1792]{1,0:T(8,128)(2,1)S(1)}, bf16[96,1792]{1,0:T(8,128)(2,1)S(1)}, u32[]{:S(2)}, u32[]{:S(2)}) collective-permute-start(bf16[96,1792]{1,0:T(8,128)(2,1)S(1)} %get-tuple-element.31), channel_id=1, source_target_pairs={{0,1},{1,0},{2,3},{3,2},{4,5},{5,4},{6,7},{7,6},{8,9},{9,8},{10,11... | collective-permute-start | bytes 1032200 | tf_op jit(solution)/shard_map/ppermute | solution.py:212
  31.9 7.3 %collective-permute-start.18 = (bf16[48,1792]{1,0:T(8,128)(2,1)S(1)}, bf16[48,1792]{1,0:T(8,128)(2,1)S(1)}, u32[]{:S(2)}, u32[]{:S(2)}) collective-permute-start(bf16[48,1792]{1,0:T(8,128)(2,1)S(1)} %collective-permute-done.refs_0_), channel_id=1, source_target_pairs={{0,2},{1,3},{2,0},{3,1},{4,6},{5,7},{6,4},{7,5},{8,10},{9,11},{10,... | collective-permute-start | bytes 516104 | tf_op jit(solution)/shard_map/ppermute | solution.py:212
  34.2 7.3 %collective-permute-start.19 = (bf16[48,1792]{1,0:T(8,128)(2,1)S(1)}, bf16[48,1792]{1,0:T(8,128)(2,1)S(1)}, u32[]{:S(2)}, u32[]{:S(2)}) collective-permute-start(bf16[48,1792]{1,0:T(8,128)(2,1)S(1)} %collective-permute-done.refs_0_), channel_id=1, source_target_pairs={{0,1},{1,0},{2,3},{3,2},{4,5},{5,4},{6,7},{7,6},{8,9},{9,8},{10,11... | collective-permute-start | bytes 516104 | tf_op jit(solution)/shard_map/ppermute | solution.py:212
  39.2 2.3 %collective-permute-start.20 = (bf16[48,1792]{1,0:T(8,128)(2,1)S(1)}, bf16[48,1792]{1,0:T(8,128)(2,1)S(1)}, u32[]{:S(2)}, u32[]{:S(2)}) collective-permute-start(bf16[48,1792]{1,0:T(8,128)(2,1)S(1)} %collective-permute-done.18.refs_1_), channel_id=1, source_target_pairs={{0,1},{1,0},{2,3},{3,2},{4,5},{5,4},{6,7},{7,6},{8,9},{9,8},{10,11... | collective-permute-start | bytes 516104 | tf_op jit(solution)/shard_map/ppermute | solution.py:212
  39.3 6.9 %collective-permute-start.16 = (bf16[48,1792]{1,0:T(8,128)(2,1)S(1)}, bf16[48,1792]{1,0:T(8,128)(2,1)S(1)}, u32[]{:S(2)}, u32[]{:S(2)}) collective-permute-start(bf16[48,1792]{1,0:T(8,128)(2,1)S(1)} %fusion.6), channel_id=1, source_target_pairs={{0,2},{1,3},{2,0},{3,1},{4,6},{5,7},{6,4},{7,5},{8,10},{9,11},{10,... | collective-permute-start | bytes 516104 | tf_op jit(solution)/shard_map/ppermute | solution.py:212
  41.2 9.2 %collective-permute-start.8 = (bf16[192,1792]{1,0:T(8,128)(2,1)S(1)}, bf16[192,1792]{1,0:T(8,128)(2,1)S(1)}, u32[]{:S(2)}, u32[]{:S(2)}) collective-permute-start(bf16[192,1792]{1,0:T(8,128)(2,1)S(1)} %get-tuple-element.25), channel_id=1, source_target_pairs={{0,1},{1,0},{2,3},{3,2},{4,5},{5,4},{6,7},{7,6},{8,9},{9,8},{10,11... | collective-permute-start | bytes 2064392 | tf_op jit(solution)/shard_map/ppermute | solution.py:212
  43.8 4.6 %collective-permute-start.21 = (bf16[96,1792]{1,0:T(8,128)(2,1)S(1)}, bf16[96,1792]{1,0:T(8,128)(2,1)S(1)}, u32[]{:S(2)}, u32[]{:S(2)}) collective-permute-start(bf16[96,1792]{1,0:T(8,128)(2,1)S(1)} %get-tuple-element.34), channel_id=1, source_target_pairs={{0,1},{1,0},{2,3},{3,2},{4,5},{5,4},{6,7},{7,6},{8,9},{9,8},{10,11... | collective-permute-start | bytes 1032200 | tf_op jit(solution)/shard_map/ppermute | solution.py:212
  46.2 16.2 %collective-permute-start.17 = (bf16[48,1792]{1,0:T(8,128)(2,1)S(1)}, bf16[48,1792]{1,0:T(8,128)(2,1)S(1)}, u32[]{:S(2)}, u32[]{:S(2)}) collective-permute-start(bf16[48,1792]{1,0:T(8,128)(2,1)S(1)} %fusion.8), channel_id=1, source_target_pairs={{0,8},{1,9},{2,10},{3,11},{4,12},{5,13},{6,14},{7,15},{8,0},{9,1},... | collective-permute-start | bytes 516104 | tf_op jit(solution)/shard_map/ppermute | solution.py:212
  48.6 18.8 %copy-start.3 = (s32[16,2]{0,1:T(2,128)S(1)}, s32[16,2]{0,1:T(2,128)}, u32[]{:S(2)}) copy-start(s32[16,2]{0,1:T(2,128)} %param.9) | copy-start | bytes 388
  48.6 18.8 %copy-start.4 = (s32[16,2]{0,1:T(2,128)S(1)}, s32[16,2]{0,1:T(2,128)}, u32[]{:S(2)}) copy-start(s32[16,2]{0,1:T(2,128)} %param.10) | copy-start | bytes 388
  48.6 7.4 %collective-permute-start.22 = (bf16[48,1792]{1,0:T(8,128)(2,1)S(1)}, bf16[48,1792]{1,0:T(8,128)(2,1)S(1)}, u32[]{:S(2)}, u32[]{:S(2)}) collective-permute-start(bf16[48,1792]{1,0:T(8,128)(2,1)S(1)} %fusion.3), channel_id=1, source_target_pairs={{0,2},{1,3},{2,0},{3,1},{4,6},{5,7},{6,4},{7,5},{8,10},{9,11},{10,... | collective-permute-start | bytes 516104 | tf_op jit(solution)/shard_map/ppermute | solution.py:212
  50.6 11.2 %collective-permute-start.9 = (bf16[96,1792]{1,0:T(8,128)(2,1)S(1)}, bf16[96,1792]{1,0:T(8,128)(2,1)S(1)}, u32[]{:S(2)}, u32[]{:S(2)}) collective-permute-start(bf16[96,1792]{1,0:T(8,128)(2,1)S(1)} %fusion), channel_id=1, source_target_pairs={{0,2},{1,3},{2,0},{3,1},{4,6},{5,7},{6,4},{7,5},{8,10},{9,11},{10,... | collective-permute-start | bytes 1032200 | tf_op jit(solution)/shard_map/ppermute | solution.py:212
  56.0 7.4 %collective-permute-start.23 = (bf16[48,1792]{1,0:T(8,128)(2,1)S(1)}, bf16[48,1792]{1,0:T(8,128)(2,1)S(1)}, u32[]{:S(2)}, u32[]{:S(2)}) collective-permute-start(bf16[48,1792]{1,0:T(8,128)(2,1)S(1)} %fusion.5), channel_id=1, source_target_pairs={{0,12},{1,13},{2,14},{3,15},{4,8},{5,9},{6,10},{7,11},{8,4},{9,5},... | collective-permute-start | bytes 516104 | tf_op jit(solution)/shard_map/ppermute | solution.py:212
  61.9 5.5 %collective-permute-start.10 = (bf16[48,1792]{1,0:T(8,128)(2,1)S(1)}, bf16[48,1792]{1,0:T(8,128)(2,1)S(1)}, u32[]{:S(2)}, u32[]{:S(2)}) collective-permute-start(bf16[48,1792]{1,0:T(8,128)(2,1)S(1)} %get-tuple-element.35), channel_id=1, source_target_pairs={{0,4},{1,5},{2,6},{3,7},{4,0},{5,1},{6,2},{7,3},{8,12},{9,13},{10,... | collective-permute-start | bytes 516104 | tf_op jit(solution)/shard_map/ppermute | solution.py:212

commit v4 on v3

--- a/solution.py
+++ b/solution.py
@@ -16,6 +16,10 @@
 
 def zero_one(condition):
     return jnp.where(condition, 1.0, 0.0).astype(jnp.bfloat16)
+
+
+def after(array, *others):
+    return lax.optimization_barrier((array, *others))[0]
 
 
 def exact_dot(left, right):
@@ -79,35 +83,30 @@
     return zero_one(col == (block * QUARTERS + quarter) * capacity + slot)
 
 
-def expert_kernel(capacity, offsets, load, *refs):
-    count = offsets * SHARDS
+def load_kernel(gate_hbm, up_hbm, down_hbm, unused, gate_ref, up_ref, down_ref, sems):
+    copies = [
+        pltpu.make_async_copy(source, target, sems.at[index])
+        for index, (source, target) in enumerate(
+            ((gate_hbm, gate_ref), (up_hbm, up_ref), (down_hbm, down_ref))
+        )
+    ]
+    for copy in copies:
+        copy.start()
+    for copy in copies:
+        copy.wait()
+
+
+def expert_kernel(capacity, offsets, *refs):
+    count = 2 * offsets
     blocks = refs[:count]
+    gate_ref, up_ref, down_ref, kept_ref, sent_ref, rows_ref, part_ref = refs[count:]
     group, tall = SHARDS * capacity, QUARTERS * capacity
     width = blocks[0].shape[1]
     spans = [slice(quarter * width, (quarter + 1) * width) for quarter in range(QUARTERS)]
-    waits = []
-    if load:
-        given = refs[count : count + 3]
-        kept_ref, sent_ref, gate_ref, up_ref, down_ref, rows_ref, part_ref, sems = refs[count + 3 :]
-        for span in spans:
-            for part in (0, 1):
-                here = (slice(None), span, slice(None))
-                waits.append((given[part].at[here], (gate_ref, up_ref)[part].at[here]))
-        for span in spans:
-            here = (slice(None), slice(None), span)
-            waits.append((given[2].at[here], down_ref.at[here]))
-        waits = [
-            pltpu.make_async_copy(source, target, sems.at[index])
-            for index, (source, target) in enumerate(waits)
-        ]
-        for copy in waits:
-            copy.start()
-    else:
-        gate_ref, up_ref, down_ref, unused, kept_ref, sent_ref, rows_ref, part_ref = refs[count:]
     order = order_matrix(capacity, False)
     for offset in range(offsets):
         held = jnp.concatenate(
-            [blocks[offset * SHARDS + member][...] for member in range(SHARDS)], axis=0
+            [blocks[2 * offset][...], blocks[2 * offset + 1][...]], axis=0
         )
         sorted_rows = exact_dot(order, held).astype(jnp.bfloat16)
         for quarter in range(QUARTERS):
@@ -117,15 +116,10 @@
     gate = jnp.zeros((offsets * group, gate_ref.shape[2]), jnp.float32)
     upward = jnp.zeros((offsets * group, gate_ref.shape[2]), jnp.float32)
     for quarter, span in enumerate(spans):
-        if load:
-            waits[2 * quarter].wait()
-            waits[2 * quarter + 1].wait()
         gate = gate + exact_dot(rows_ref[quarter], gate_ref[0, span, :])
         upward = upward + exact_dot(rows_ref[quarter], up_ref[0, span, :])
     hidden = (gate / (1.0 + jnp.exp(-gate)) * upward).astype(jnp.bfloat16)
     for quarter, span in enumerate(spans):
-        if load:
-            waits[2 * QUARTERS + quarter].wait()
         part_ref[quarter] = exact_dot(hidden, down_ref[0, :, span]).astype(jnp.bfloat16)
     back = order_matrix(capacity, True)
     for offset in range(offsets):
@@ -203,7 +197,6 @@
     tall = QUARTERS * capacity
     vmem = pl.BlockSpec(memory_space=pltpu.VMEM)
     hbm = pl.BlockSpec(memory_space=pl.ANY)
-    anywhere = pl.BlockSpec(memory_space=pl.ANY)
     params = pltpu.CompilerParams(vmem_limit_bytes=VMEM_BYTES)
     pack_params = pltpu.CompilerParams(vmem_limit_bytes=PACK_VMEM_BYTES)
     load_params = pltpu.CompilerParams(vmem_limit_bytes=LOAD_VMEM_BYTES)
@@ -227,46 +220,103 @@
         compiler_params=pack_params,
     )(tokens, scales, routes.T)
 
-    groups = ((0, planes // 2), (planes // 2, 3 * planes // 4), (3 * planes // 4, planes))
-    arriving = [packed[0]] + [partner(packed[at], at * SHARDS) for at in range(1, planes)]
-    returned = []
-    weights, kept = (w_gate, w_up, w_down), None
-    for start, stop in groups:
-        gathered = []
-        for offset in range(start, stop):
-            own = arriving[offset]
-            across = partner(own, 2)
-            gathered += [own, across, partner(own, 1), partner(across, 1)]
+    weights = pl.pallas_call(
+        load_kernel,
+        out_shape=[jax.ShapeDtypeStruct(w.shape, w.dtype) for w in (w_gate, w_up, w_down)],
+        in_specs=[hbm] * 4,
+        out_specs=[vmem] * 3,
+        scratch_shapes=[pltpu.SemaphoreType.DMA((3,))],
+        compiler_params=load_params,
+    )(w_gate, w_up, w_down, packed[0])
+
+    def expert(start, stop, held, weights):
         offsets = stop - start
         rows = offsets * SHARDS * capacity
-        load = start == 0
         half = jax.ShapeDtypeStruct((2 * offsets * tall, width), jnp.bfloat16)
-        scratch = [pltpu.VMEM((QUARTERS, rows, width), jnp.bfloat16)] * 2
-        held = [jax.ShapeDtypeStruct(array.shape, array.dtype) for array in weights]
-        kept, sent, *loaded = pl.pallas_call(
-            functools.partial(expert_kernel, capacity, offsets, load),
-            out_shape=[half] * 2 + (held if load else []),
-            in_specs=[vmem] * (offsets * SHARDS) + ([hbm] * 3 if load else [vmem] * 3 + [anywhere]),
-            out_specs=[vmem] * (5 if load else 2),
-            scratch_shapes=scratch + ([pltpu.SemaphoreType.DMA((3 * QUARTERS,))] if load else []),
-            compiler_params=load_params if load else params,
+        return pl.pallas_call(
+            functools.partial(expert_kernel, capacity, offsets),
+            out_shape=[half] * 2,
+            in_specs=[vmem] * (offsets * 2 + 3),
+            out_specs=[vmem] * 2,
+            scratch_shapes=[pltpu.VMEM((QUARTERS, rows, width), jnp.bfloat16)] * 2,
+            compiler_params=params,
             cost_estimate=pl.CostEstimate(
-                flops=6 * rows * features * w_gate.shape[2], bytes_accessed=0, transcendentals=0
+                flops=6 * rows * features * w_gate.shape[2],
+                bytes_accessed=0,
+                transcendentals=0,
             ),
-        )(*gathered, *weights, *([] if load else [kept]))
-        weights = loaded if load else weights
-        if load:
-            last = groups[-1][0]
-            *arriving[last:], kept = lax.optimization_barrier((*arriving[last:], kept))
-        arrived = partner(sent, 1).astype(jnp.float32)
-        mine = kept.astype(jnp.float32)
+        )(*held, *weights)
+
+    def across(array):
+        return partner(array, 2)
+
+    def along(array, offset):
+        return array if offset == 0 else partner(array, offset * SHARDS)
+
+    def fold(kept, arrived, offsets):
         middle = offsets * tall
-        across = partner((mine[middle:] + arrived[middle:]).astype(jnp.bfloat16), 2)
-        answer = mine[:middle] + arrived[:middle] + across.astype(jnp.float32)
-        answer = answer.astype(jnp.bfloat16)
-        for offset in range(start, stop):
-            piece = answer[(offset - start) * tall : (offset - start + 1) * tall]
-            returned.append(piece if offset == 0 else partner(piece, offset * SHARDS))
+        kept, arrived = kept.astype(jnp.float32), arrived.astype(jnp.float32)
+        leaving = (kept[middle:] + arrived[middle:]).astype(jnp.bfloat16)
+        return leaving, kept[:middle] + arrived[:middle]
+
+    def pair(own, other):
+        both = jnp.concatenate([own, other], axis=0)
+        return [both, partner(both, 1)]
+
+    half, late = planes // 2, 3 * planes // 4
+    first, second, third = range(half), range(half, late), range(late, planes)
+    arrive, cross, held, returned = {}, {}, {}, {}
+
+    def take(table, places):
+        return [table[at] for at in places]
+
+    for at in list(second) + list(first):
+        arrive[at] = along(packed[at], at)
+    cross[0] = across(arrive[0])
+    for at in first:
+        if at:
+            arrive[at] = after(arrive[at], *weights)
+            cross[at] = across(arrive[at])
+    for at in third:
+        arrive[at] = along(after(packed[at], *take(arrive, second)), at)
+    for at in second:
+        cross[at] = across(after(arrive[at], cross[0]))
+    for at in second:
+        held[at] = pair(arrive[at], cross[at])
+    held2 = sum(take(held, second), [])
+    kept2, sent2 = expert(half, late, held2, weights)
+    for at in first:
+        held[at] = pair(arrive[at], cross[at])
+    held1 = sum(take(held, first), [])
+    held1[0] = after(held1[0], kept2)
+    kept1, sent1 = expert(0, half, held1, weights)
+    back2 = partner(sent2, 1)
+    leave2, stay2 = fold(kept2, back2, len(second))
+    for at in third:
+        cross[at] = across(arrive[at])
+    home2 = across(leave2)
+    for at in third:
+        held[at] = pair(arrive[at], cross[at])
+    held3 = sum(take(held, third), [])
+    held3[0] = after(held3[0], kept1, leave2)
+    kept3, sent3 = expert(late, planes, held3, weights)
+    back1 = partner(sent1, 1)
+    leave1, stay1 = fold(kept1, back1, len(first))
+    home1 = across(leave1)
+    back3 = partner(sent3, 1)
+    leave3, stay3 = fold(kept3, back3, len(third))
+    home3 = across(leave3)
+    answer2 = (stay2 + home2.astype(jnp.float32)).astype(jnp.bfloat16)
+    for index, at in enumerate(second):
+        returned[at] = along(answer2[index * tall : (index + 1) * tall], at)
+    answer1 = (stay1 + home1.astype(jnp.float32)).astype(jnp.bfloat16)
+    for index, at in enumerate(first):
+        returned[at] = along(answer1[index * tall : (index + 1) * tall], at)
+    answer3 = (stay3 + home3.astype(jnp.float32)).astype(jnp.bfloat16)
+    answer3 = after(answer3, *take(returned, second))
+    for index, at in enumerate(third):
+        returned[at] = along(answer3[index * tall : (index + 1) * tall], at)
+    returned = [returned[at] for at in range(planes)]
 
     return pl.pallas_call(
         functools.partial(mix_kernel, capacity, planes),

time: 69.1 us -> 66.7 us (0.965)
  starting transfers between devices: 27 us -> 22 us
  Pallas kernels: 12.5 us -> 14.2 us
  waiting for transfers between devices: 26.2 us -> 26.9 us
    ppermute x24 -> x20, starting transfers between devices: 27 us -> 22 us  [partner(): lax.ppermute(array, 'expert', [(i, i ^ distance) for i in range(devices)])]
    pallas_call x3 -> x4, Pallas kernels: 9.91 us -> 11.6 us  [the longest x3 7.39 us: expert(): pl.pallas_call(functools.partial(expert_kernel, capacity, offsets), out_s...]
    ppermute x24 -> x20, waiting for transfers between devices: 26.2 us -> 26.9 us  [partner(): lax.ppermute(array, 'expert', [(i, i ^ distance) for i in range(devices)])]
    unnamed x10 -> x14, local copies, waits for them, and re-layouts: 2.32 us -> 2.37 us
  transfers between devices with their start and end apart: 24 -> 20, of which waited for: 11 -> 9; matrix products, arithmetic and copies ran while one was open for 1% -> 1% of each run, Pallas kernels for 11% -> 17%
where the time goes in v4:
time: 66.7 us; the launch traced here: 66.5 us
  waiting for transfers between devices  26.9 us (40%)
  starting transfers between devices  22 us (33%)
  Pallas kernels  14.2 us (21%)
  local copies, waits for them, and re-layouts  2.45 us (4%)
  other arithmetic  0.72 us (1%)
    ppermute x20, waiting for transfers between devices, partner(): lax.ppermute(array, 'expert', [(i, i ^ distance) for i in range(devices)])  26.9 us
    ppermute x20, starting transfers between devices, partner(): lax.ppermute(array, 'expert', [(i, i ^ distance) for i in range(devices)])  22 us
    pallas_call x3, Pallas kernels, expert(): pl.pallas_call(functools.partial(expert_kernel, capacity, offsets), out_s...  7.39 us
    pallas_call x1, Pallas kernels, shards(): pl.pallas_call(load_kernel, out_shape=[jax.ShapeDtypeStruct(w.shape, w.dt...  4.23 us
    unnamed x14, local copies, waits for them, and re-layouts  2.37 us
    pallas_call x1, Pallas kernels, shards(): pl.pallas_call(functools.partial(mix_kernel, capacity, planes), out_shape...  1.48 us
  transfers between devices with their start and end apart: 20, of which 9 were waited for; matrix products, arithmetic and copies ran while one was open for 1% of the time, Pallas kernels for 17%

profile of v4, /device:TPU:0, one launch (start us, length us, event | category | flops | bytes accessed | tf_op | source)
XLA Modules:
  0.0 66.5 jit_solution(9925026550831959984)
XLA Ops:
  0.0 0.0 copy-start
  0.0 0.9 %copy-done = bf16[16,7168]{1,0:T(8,128)(2,1)S(1)} copy-done((bf16[16,7168]{1,0:T(8,128)(2,1)S(1)}, bf16[16,7168]{1,0:T(8,128)(2,1)}, u32[]{:S(2)}) %copy-start) | copy-done | bytes 229400
  0.9 0.0 copy-start.1
  0.9 0.7 %copy-done.1 = f32[16,56]{1,0:T(8,128)S(1)} copy-done((f32[16,56]{1,0:T(8,128)S(1)}, f32[16,56]{1,0:T(8,128)}, u32[]{:S(2)}) %copy-start.1) | copy-done | bytes 3608
  1.6 0.0 copy-start.2
  1.6 0.7 %copy-done.2 = s32[16,2]{0,1:T(2,128)S(1)} copy-done((s32[16,2]{0,1:T(2,128)S(1)}, s32[16,2]{0,1:T(2,128)}, u32[]{:S(2)}) %copy-start.2) | copy-done | bytes 152
  2.3 1.1 %shard_map.73 = (bf16[48,1792]{1,0:T(8,128)(2,1)S(1)}, bf16[48,1792]{1,0:T(8,128)(2,1)S(1)}, bf16[48,1792]{1,0:T(8,128)(2,1)S(1)}, bf16[48,1792]{1,0:T(8,128)(2,1)S(1)}) custom-call(bf16[16,7168]{1,0:T(8,128)(2,1)S(1)} %copy-done, f32[16,56]{1,0:T(8,128)S(1)} %copy-done.1, s32[2,16]{1,0:T(2,128)S(1)} %bitcast.2), custom_call_target="tpu_custom_call" | custom-call | tf_op jit(solution)/shard_map/pallas_call | solution.py:208
  3.5 4.1 %collective-permute-start.1 = (bf16[48,1792]{1,0:T(8,128)(2,1)S(1)}, bf16[48,1792]{1,0:T(8,128)(2,1)S(1)}, u32[]{:S(2)}, u32[]{:S(2)}) collective-permute-start(bf16[48,1792]{1,0:T(8,128)(2,1)S(1)} %get-tuple-element.25), channel_id=1, source_target_pairs={{0,8},{1,9},{2,10},{3,11},{4,12},{5,13},{6,14},{7,15},{8,0},{9,1},... | collective-permute-start | bytes 516104 | tf_op jit(solution)/shard_map/ppermute | solution.py:205
  7.6 1.6 %collective-permute-start.5 = (bf16[48,1792]{1,0:T(8,128)(2,1)S(1)}, bf16[48,1792]{1,0:T(8,128)(2,1)S(1)}, u32[]{:S(2)}, u32[]{:S(2)}) collective-permute-start(bf16[48,1792]{1,0:T(8,128)(2,1)S(1)} %get-tuple-element.32), channel_id=1, source_target_pairs={{0,4},{1,5},{2,6},{3,7},{4,0},{5,1},{6,2},{7,3},{8,12},{9,13},{10,... | collective-permute-start | bytes 516104 | tf_op jit(solution)/shard_map/ppermute | solution.py:205
  9.1 1.5 %collective-permute-start = (bf16[48,1792]{1,0:T(8,128)(2,1)S(1)}, bf16[48,1792]{1,0:T(8,128)(2,1)S(1)}, u32[]{:S(2)}, u32[]{:S(2)}) collective-permute-start(bf16[48,1792]{1,0:T(8,128)(2,1)S(1)} %get-tuple-element.24.unused), channel_id=1, source_target_pairs={{0,2},{1,3},{2,0},{3,1},{4,6},{5,7},{6,4},{7,5},{8,10},{9,11},{10,... | collective-permute-start | bytes 516104 | tf_op jit(solution)/shard_map/ppermute | solution.py:205
  10.7 4.2 %shard_map.74 = (bf16[1,7168,256]{2,1,0:T(8,128)(2,1)S(1)}, bf16[1,7168,256]{2,1,0:T(8,128)(2,1)S(1)}, bf16[1,256,7168]{2,1,0:T(8,128)(2,1)S(1)}) custom-call(bf16[1,7168,256]{2,1,0:T(8,128)(2,1)} %gate_hbm.1, bf16[1,7168,256]{2,1,0:T(8,128)(2,1)} %up_hbm.1, bf16[1,256,7168]{2,1,0:T(8,128)(2,1)} %down_hbm.1, bf16[48,1792]{1,0:T(8,128)(2,1)S(1)} %get-tuple-element.24.unused), custom_call_target="tpu_custom_call" | custom-call | tf_op jit(solution)/shard_map/pallas_call | solution.py:223
  14.9 0.8 %collective-permute-done.1 = bf16[48,1792]{1,0:T(8,128)(2,1)S(1)} collective-permute-done((bf16[48,1792]{1,0:T(8,128)(2,1)S(1)}, bf16[48,1792]{1,0:T(8,128)(2,1)S(1)}, u32[]{:S(2)}, u32[]{:S(2)}) %collective-permute-start.1) | collective-permute-done | bytes 172064 | tf_op jit(solution)/shard_map/ppermute | solution.py:205
  15.7 3.4 %collective-permute-start.14 = (bf16[48,1792]{1,0:T(8,128)(2,1)S(1)}, bf16[48,1792]{1,0:T(8,128)(2,1)S(1)}, u32[]{:S(2)}, u32[]{:S(2)}) collective-permute-start(bf16[48,1792]{1,0:T(8,128)(2,1)S(1)} %get-tuple-element.38), channel_id=1, source_target_pairs={{0,12},{1,13},{2,14},{3,15},{4,8},{5,9},{6,10},{7,11},{8,4},{9,5},... | collective-permute-start | bytes 516104 | tf_op jit(solution)/shard_map/ppermute | solution.py:205
  19.2 0.0 collective-permute-done
  19.2 1.5 %collective-permute-start.2 = (bf16[48,1792]{1,0:T(8,128)(2,1)S(1)}, bf16[48,1792]{1,0:T(8,128)(2,1)S(1)}, u32[]{:S(2)}, u32[]{:S(2)}) collective-permute-start(bf16[48,1792]{1,0:T(8,128)(2,1)S(1)} %collective-permute-done.1), channel_id=1, source_target_pairs={{0,2},{1,3},{2,0},{3,1},{4,6},{5,7},{6,4},{7,5},{8,10},{9,11},{10,... | collective-permute-start | bytes 516104 | tf_op jit(solution)/shard_map/ppermute | solution.py:205
  20.7 0.1 collective-permute-start.4
  20.8 0.0 collective-permute-done.5
  20.8 0.6 collective-permute-start.6
  21.4 5.1 %collective-permute-done.2 = bf16[48,1792]{1,0:T(8,128)(2,1)S(1)} collective-permute-done((bf16[48,1792]{1,0:T(8,128)(2,1)S(1)}, bf16[48,1792]{1,0:T(8,128)(2,1)S(1)}, u32[]{:S(2)}, u32[]{:S(2)}) %collective-permute-start.2) | collective-permute-done | bytes 172064 | tf_op jit(solution)/shard_map/ppermute | solution.py:205
  26.5 0.1 collective-permute-start.3
  26.6 2.3 %collective-permute-done.6 = bf16[48,1792]{1,0:T(8,128)(2,1)S(1)} collective-permute-done((bf16[48,1792]{1,0:T(8,128)(2,1)S(1)}, bf16[48,1792]{1,0:T(8,128)(2,1)S(1)}, u32[]{:S(2)}, u32[]{:S(2)}) %collective-permute-start.6) | collective-permute-done | bytes 172064 | tf_op jit(solution)/shard_map/ppermute | solution.py:205
  28.9 0.1 collective-permute-start.7
  29.0 0.0 collective-permute-done.14
  29.0 1.6 %collective-permute-start.15 = (bf16[48,1792]{1,0:T(8,128)(2,1)S(1)}, bf16[48,1792]{1,0:T(8,128)(2,1)S(1)}, u32[]{:S(2)}, u32[]{:S(2)}) collective-permute-start(bf16[48,1792]{1,0:T(8,128)(2,1)S(1)} %collective-permute-done.14), channel_id=1, source_target_pairs={{0,2},{1,3},{2,0},{3,1},{4,6},{5,7},{6,4},{7,5},{8,10},{9,11},{10,... | collective-permute-start | bytes 516104 | tf_op jit(solution)/shard_map/ppermute | solution.py:205
  30.6 0.0 collective-permute-done.3.refs_1_
  30.6 2.3 %shard_map.75 = (bf16[96,1792]{1,0:T(8,128)(2,1)S(1)}, bf16[96,1792]{1,0:T(8,128)(2,1)S(1)}) custom-call(bf16[96,1792]{1,0:T(8,128)(2,1)S(1)} %constant_dynamic-update-slice_fusion.2.refs_0_, bf16[96,1792]{1,0:T(8,128)(2,1)S(1)} %collective-permute-done.3.refs_1_, bf16[1,7168,256]{2,1,0:T(8,128)(2,1)S(1)} %get-tuple-element.27.refs_2_.refs_4_, ...), custom_call_target="tpu_custom_call" | custom-call | flops 528482304 | tf_op jit(solution)/shard_map/pallas_call | solution.py:236
  32.9 0.2 collective-permute-start.11
  33.1 2.7 %collective-permute-done.15 = bf16[48,1792]{1,0:T(8,128)(2,1)S(1)} collective-permute-done((bf16[48,1792]{1,0:T(8,128)(2,1)S(1)}, bf16[48,1792]{1,0:T(8,128)(2,1)S(1)}, u32[]{:S(2)}, u32[]{:S(2)}) %collective-permute-start.15) | collective-permute-done | bytes 172064 | tf_op jit(solution)/shard_map/ppermute | solution.py:205
  35.8 0.1 collective-permute-start.16
  35.9 0.0 collective-permute-done.11
  36.0 1.6 %collective-permute-start.12 = (bf16[48,1792]{1,0:T(8,128)(2,1)S(1)}, bf16[48,1792]{1,0:T(8,128)(2,1)S(1)}, u32[]{:S(2)}, u32[]{:S(2)}) collective-permute-start(bf16[48,1792]{1,0:T(8,128)(2,1)S(1)} %fusion.6), channel_id=1, source_target_pairs={{0,2},{1,3},{2,0},{3,1},{4,6},{5,7},{6,4},{7,5},{8,10},{9,11},{10,... | collective-permute-start | bytes 516104 | tf_op jit(solution)/shard_map/ppermute | solution.py:205
  37.6 0.0 collective-permute-done.4.refs_1_
  37.6 0.0 collective-permute-done.7.refs_3_
  37.6 2.8 %shard_map.76 = (bf16[192,1792]{1,0:T(8,128)(2,1)S(1)}, bf16[192,1792]{1,0:T(8,128)(2,1)S(1)}) custom-call(bf16[96,1792]{1,0:T(8,128)(2,1)S(1)} %constant_dynamic-update-slice_fusion.refs_0_, bf16[96,1792]{1,0:T(8,128)(2,1)S(1)} %collective-permute-done.4.refs_1_, bf16[96,1792]{1,0:T(8,128)(2,1)S(1)} %constant_dynamic-update-slice_fusion.4.refs_2_, ...), custom_call_target="tpu_custom_call" | custom-call | flops 1056964608 | tf_op jit(solution)/shard_map/pallas_call | solution.py:236
  40.4 0.3 collective-permute-start.8
  40.7 0.1 convert_element_type.45
  40.8 0.0 collective-permute-done.16.refs_1_
  40.8 2.3 %shard_map.77 = (bf16[96,1792]{1,0:T(8,128)(2,1)S(1)}, bf16[96,1792]{1,0:T(8,128)(2,1)S(1)}) custom-call(bf16[96,1792]{1,0:T(8,128)(2,1)S(1)} %constant_dynamic-update-slice_fusion.6.refs_0_, bf16[96,1792]{1,0:T(8,128)(2,1)S(1)} %collective-permute-done.16.refs_1_, bf16[1,7168,256]{2,1,0:T(8,128)(2,1)S(1)} %get-tuple-element.27.refs_2_.refs_4_, ...), custom_call_target="tpu_custom_call" | custom-call | flops 528482304 | tf_op jit(solution)/shard_map/pallas_call | solution.py:236
  43.1 0.4 collective-permute-start.17
  43.5 0.0 collective-permute-done.12
  43.5 0.1 fusion.8
  43.6 0.1 collective-permute-start.13
  43.6 1.2 %collective-permute-done.17 = bf16[96,1792]{1,0:T(8,128)(2,1)S(1)} collective-permute-done((bf16[96,1792]{1,0:T(8,128)(2,1)S(1)}, bf16[96,1792]{1,0:T(8,128)(2,1)S(1)}, u32[]{:S(2)}, u32[]{:S(2)}) %collective-permute-start.17) | collective-permute-done | bytes 344096 | tf_op jit(solution)/shard_map/ppermute | solution.py:205
  44.9 0.1 fusion.3
  45.0 0.0 copy-start.3
  45.0 0.0 copy-start.4
  45.0 0.6 collective-permute-start.18
  45.6 0.0 collective-permute-done.8
  45.6 0.1 convert_element_type.46
  45.6 0.1 fusion
  45.7 1.6 %collective-permute-start.9 = (bf16[96,1792]{1,0:T(8,128)(2,1)S(1)}, bf16[96,1792]{1,0:T(8,128)(2,1)S(1)}, u32[]{:S(2)}, u32[]{:S(2)}) collective-permute-start(bf16[96,1792]{1,0:T(8,128)(2,1)S(1)} %fusion), channel_id=1, source_target_pairs={{0,2},{1,3},{2,0},{3,1},{4,6},{5,7},{6,4},{7,5},{8,10},{9,11},{10,... | collective-permute-start | bytes 1032200 | tf_op jit(solution)/shard_map/ppermute | solution.py:205
  47.3 4.9 %collective-permute-done.18 = bf16[48,1792]{1,0:T(8,128)(2,1)S(1)} collective-permute-done((bf16[48,1792]{1,0:T(8,128)(2,1)S(1)}, bf16[48,1792]{1,0:T(8,128)(2,1)S(1)}, u32[]{:S(2)}, u32[]{:S(2)}) %collective-permute-start.18) | collective-permute-done | bytes 172064 | tf_op jit(solution)/shard_map/ppermute | solution.py:205
  52.2 0.1 fusion.5
  52.3 0.0 collective-permute-done.13.refs_2_
  52.3 2.6 %collective-permute-start.19 = (bf16[48,1792]{1,0:T(8,128)(2,1)S(1)}, bf16[48,1792]{1,0:T(8,128)(2,1)S(1)}, u32[]{:S(2)}, u32[]{:S(2)}) collective-permute-start(bf16[48,1792]{1,0:T(8,128)(2,1)S(1)} %fusion.5), channel_id=1, source_target_pairs={{0,12},{1,13},{2,14},{3,15},{4,8},{5,9},{6,10},{7,11},{8,4},{9,5},... | collective-permute-start | bytes 516104 | tf_op jit(solution)/shard_map/ppermute | solution.py:205
  55.0 4.0 %collective-permute-done.9 = bf16[96,1792]{1,0:T(8,128)(2,1)S(1)} collective-permute-done((bf16[96,1792]{1,0:T(8,128)(2,1)S(1)}, bf16[96,1792]{1,0:T(8,128)(2,1)S(1)}, u32[]{:S(2)}, u32[]{:S(2)}) %collective-permute-start.9) | collective-permute-done | bytes 344096 | tf_op jit(solution)/shard_map/ppermute | solution.py:205
  59.0 0.1 fusion.2
  59.1 0.1 collective-permute-start.10
  59.2 1.4 %collective-permute-done.19.refs_3_ = bf16[48,1792]{1,0:T(8,128)(2,1)S(1)} collective-permute-done((bf16[48,1792]{1,0:T(8,128)(2,1)S(1)}, bf16[48,1792]{1,0:T(8,128)(2,1)S(1)}, u32[]{:S(2)}, u32[]{:S(2)}) %collective-permute-start.19) | collective-permute-done | bytes 172064 | tf_op jit(solution)/shard_map/ppermute | solution.py:205
  60.6 4.4 %collective-permute-done.10.refs_1_ = bf16[48,1792]{1,0:T(8,128)(2,1)S(1)} collective-permute-done((bf16[48,1792]{1,0:T(8,128)(2,1)S(1)}, bf16[48,1792]{1,0:T(8,128)(2,1)S(1)}, u32[]{:S(2)}, u32[]{:S(2)}) %collective-permute-start.10) | collective-permute-done | bytes 172064 | tf_op jit(solution)/shard_map/ppermute | solution.py:205
  65.0 0.0 copy-done.3
  65.0 0.0 copy-done.4
  65.0 1.5 %shard_map.78 = bf16[16,7168]{1,0:T(8,128)(2,1)} custom-call(s32[2,16]{1,0:T(2,128)S(1)} %bitcast.3, s32[2,16]{1,0:T(2,128)S(1)} %bitcast.4, bf16[48,1792]{1,0:T(8,128)(2,1)S(1)} %get-tuple-element.44.refs_0_, bf16[48,1792]{1,0:T(8,128)(2,1)S(1)} %collective-permute-done.10.refs_1_, bf16[48,1792]{1,0:T(8,128)(2,1)S(1)} %collective-permute-done.13.refs_2_, ...), custom_call_target="tpu_custom_call" | custom-call | tf_op jit(solution)/shard_map/pallas_call | solution.py:321
  (14 shorter events, 0.3 us)
Async XLA Ops:
  0.0 0.9 %copy-start = (bf16[16,7168]{1,0:T(8,128)(2,1)S(1)}, bf16[16,7168]{1,0:T(8,128)(2,1)}, u32[]{:S(2)}) copy-start(bf16[16,7168]{1,0:T(8,128)(2,1)} %tok_hbm.1) | copy-start | bytes 688132
  0.9 0.7 %copy-start.1 = (f32[16,56]{1,0:T(8,128)S(1)}, f32[16,56]{1,0:T(8,128)}, u32[]{:S(2)}) copy-start(f32[16,56]{1,0:T(8,128)} %scale_hbm.1) | copy-start | bytes 10756
  1.6 0.7 %copy-start.2 = (s32[16,2]{0,1:T(2,128)S(1)}, s32[16,2]{0,1:T(2,128)}, u32[]{:S(2)}) copy-start(s32[16,2]{0,1:T(2,128)} %param.9) | copy-start | bytes 388
  3.5 12.3 %collective-permute-start.1 = (bf16[48,1792]{1,0:T(8,128)(2,1)S(1)}, bf16[48,1792]{1,0:T(8,128)(2,1)S(1)}, u32[]{:S(2)}, u32[]{:S(2)}) collective-permute-start(bf16[48,1792]{1,0:T(8,128)(2,1)S(1)} %get-tuple-element.25), channel_id=1, source_target_pairs={{0,8},{1,9},{2,10},{3,11},{4,12},{5,13},{6,14},{7,15},{8,0},{9,1},... | collective-permute-start | bytes 516104 | tf_op jit(solution)/shard_map/ppermute | solution.py:205
  7.6 13.2 %collective-permute-start.5 = (bf16[48,1792]{1,0:T(8,128)(2,1)S(1)}, bf16[48,1792]{1,0:T(8,128)(2,1)S(1)}, u32[]{:S(2)}, u32[]{:S(2)}) collective-permute-start(bf16[48,1792]{1,0:T(8,128)(2,1)S(1)} %get-tuple-element.32), channel_id=1, source_target_pairs={{0,4},{1,5},{2,6},{3,7},{4,0},{5,1},{6,2},{7,3},{8,12},{9,13},{10,... | collective-permute-start | bytes 516104 | tf_op jit(solution)/shard_map/ppermute | solution.py:205
  9.1 10.0 %collective-permute-start = (bf16[48,1792]{1,0:T(8,128)(2,1)S(1)}, bf16[48,1792]{1,0:T(8,128)(2,1)S(1)}, u32[]{:S(2)}, u32[]{:S(2)}) collective-permute-start(bf16[48,1792]{1,0:T(8,128)(2,1)S(1)} %get-tuple-element.24.unused), channel_id=1, source_target_pairs={{0,2},{1,3},{2,0},{3,1},{4,6},{5,7},{6,4},{7,5},{8,10},{9,11},{10,... | collective-permute-start | bytes 516104 | tf_op jit(solution)/shard_map/ppermute | solution.py:205
  15.7 13.2 %collective-permute-start.14 = (bf16[48,1792]{1,0:T(8,128)(2,1)S(1)}, bf16[48,1792]{1,0:T(8,128)(2,1)S(1)}, u32[]{:S(2)}, u32[]{:S(2)}) collective-permute-start(bf16[48,1792]{1,0:T(8,128)(2,1)S(1)} %get-tuple-element.38), channel_id=1, source_target_pairs={{0,12},{1,13},{2,14},{3,15},{4,8},{5,9},{6,10},{7,11},{8,4},{9,5},... | collective-permute-start | bytes 516104 | tf_op jit(solution)/shard_map/ppermute | solution.py:205
  19.2 7.3 %collective-permute-start.2 = (bf16[48,1792]{1,0:T(8,128)(2,1)S(1)}, bf16[48,1792]{1,0:T(8,128)(2,1)S(1)}, u32[]{:S(2)}, u32[]{:S(2)}) collective-permute-start(bf16[48,1792]{1,0:T(8,128)(2,1)S(1)} %collective-permute-done.1), channel_id=1, source_target_pairs={{0,2},{1,3},{2,0},{3,1},{4,6},{5,7},{6,4},{7,5},{8,10},{9,11},{10,... | collective-permute-start | bytes 516104 | tf_op jit(solution)/shard_map/ppermute | solution.py:205
  20.7 16.9 %collective-permute-start.4 = (bf16[96,1792]{1,0:T(8,128)(2,1)S(1)}, bf16[96,1792]{1,0:T(8,128)(2,1)S(1)}, u32[]{:S(2)}, u32[]{:S(2)}) collective-permute-start(bf16[96,1792]{1,0:T(8,128)(2,1)S(1)} %constant_dynamic-update-slice_fusion.refs_0_), channel_id=1, source_target_pairs={{0,1},{1,0},{2,3},{3,2},{4,5},{5,4},{6,7},{7,6},{8,9},{9,8},{10,11... | collective-permute-start | bytes 1032200 | tf_op jit(solution)/shard_map/ppermute | solution.py:205
  20.8 8.1 %collective-permute-start.6 = (bf16[48,1792]{1,0:T(8,128)(2,1)S(1)}, bf16[48,1792]{1,0:T(8,128)(2,1)S(1)}, u32[]{:S(2)}, u32[]{:S(2)}) collective-permute-start(bf16[48,1792]{1,0:T(8,128)(2,1)S(1)} %collective-permute-done.5), channel_id=1, source_target_pairs={{0,2},{1,3},{2,0},{3,1},{4,6},{5,7},{6,4},{7,5},{8,10},{9,11},{10,... | collective-permute-start | bytes 516104 | tf_op jit(solution)/shard_map/ppermute | solution.py:205
  26.5 4.1 %collective-permute-start.3 = (bf16[96,1792]{1,0:T(8,128)(2,1)S(1)}, bf16[96,1792]{1,0:T(8,128)(2,1)S(1)}, u32[]{:S(2)}, u32[]{:S(2)}) collective-permute-start(bf16[96,1792]{1,0:T(8,128)(2,1)S(1)} %constant_dynamic-update-slice_fusion.2.refs_0_), channel_id=1, source_target_pairs={{0,1},{1,0},{2,3},{3,2},{4,5},{5,4},{6,7},{7,6},{8,9},{9,8},{10,11... | collective-permute-start | bytes 1032200 | tf_op jit(solution)/shard_map/ppermute | solution.py:205
  28.9 8.7 %collective-permute-start.7 = (bf16[96,1792]{1,0:T(8,128)(2,1)S(1)}, bf16[96,1792]{1,0:T(8,128)(2,1)S(1)}, u32[]{:S(2)}, u32[]{:S(2)}) collective-permute-start(bf16[96,1792]{1,0:T(8,128)(2,1)S(1)} %constant_dynamic-update-slice_fusion.4.refs_2_), channel_id=1, source_target_pairs={{0,1},{1,0},{2,3},{3,2},{4,5},{5,4},{6,7},{7,6},{8,9},{9,8},{10,11... | collective-permute-start | bytes 1032200 | tf_op jit(solution)/shard_map/ppermute | solution.py:205
  29.0 6.8 %collective-permute-start.15 = (bf16[48,1792]{1,0:T(8,128)(2,1)S(1)}, bf16[48,1792]{1,0:T(8,128)(2,1)S(1)}, u32[]{:S(2)}, u32[]{:S(2)}) collective-permute-start(bf16[48,1792]{1,0:T(8,128)(2,1)S(1)} %collective-permute-done.14), channel_id=1, source_target_pairs={{0,2},{1,3},{2,0},{3,1},{4,6},{5,7},{6,4},{7,5},{8,10},{9,11},{10,... | collective-permute-start | bytes 516104 | tf_op jit(solution)/shard_map/ppermute | solution.py:205
  32.9 3.1 %collective-permute-start.11 = (bf16[96,1792]{1,0:T(8,128)(2,1)S(1)}, bf16[96,1792]{1,0:T(8,128)(2,1)S(1)}, u32[]{:S(2)}, u32[]{:S(2)}) collective-permute-start(bf16[96,1792]{1,0:T(8,128)(2,1)S(1)} %get-tuple-element.36), channel_id=1, source_target_pairs={{0,1},{1,0},{2,3},{3,2},{4,5},{5,4},{6,7},{7,6},{8,9},{9,8},{10,11... | collective-permute-start | bytes 1032200 | tf_op jit(solution)/shard_map/ppermute | solution.py:205
  35.8 5.0 %collective-permute-start.16 = (bf16[96,1792]{1,0:T(8,128)(2,1)S(1)}, bf16[96,1792]{1,0:T(8,128)(2,1)S(1)}, u32[]{:S(2)}, u32[]{:S(2)}) collective-permute-start(bf16[96,1792]{1,0:T(8,128)(2,1)S(1)} %constant_dynamic-update-slice_fusion.6.refs_0_), channel_id=1, source_target_pairs={{0,1},{1,0},{2,3},{3,2},{4,5},{5,4},{6,7},{7,6},{8,9},{9,8},{10,11... | collective-permute-start | bytes 1032200 | tf_op jit(solution)/shard_map/ppermute | solution.py:205
  36.0 7.5 %collective-permute-start.12 = (bf16[48,1792]{1,0:T(8,128)(2,1)S(1)}, bf16[48,1792]{1,0:T(8,128)(2,1)S(1)}, u32[]{:S(2)}, u32[]{:S(2)}) collective-permute-start(bf16[48,1792]{1,0:T(8,128)(2,1)S(1)} %fusion.6), channel_id=1, source_target_pairs={{0,2},{1,3},{2,0},{3,1},{4,6},{5,7},{6,4},{7,5},{8,10},{9,11},{10,... | collective-permute-start | bytes 516104 | tf_op jit(solution)/shard_map/ppermute | solution.py:205
  40.4 5.1 %collective-permute-start.8 = (bf16[192,1792]{1,0:T(8,128)(2,1)S(1)}, bf16[192,1792]{1,0:T(8,128)(2,1)S(1)}, u32[]{:S(2)}, u32[]{:S(2)}) collective-permute-start(bf16[192,1792]{1,0:T(8,128)(2,1)S(1)} %get-tuple-element.35), channel_id=1, source_target_pairs={{0,1},{1,0},{2,3},{3,2},{4,5},{5,4},{6,7},{7,6},{8,9},{9,8},{10,11... | collective-permute-start | bytes 2064392 | tf_op jit(solution)/shard_map/ppermute | solution.py:205
  43.1 1.7 %collective-permute-start.17 = (bf16[96,1792]{1,0:T(8,128)(2,1)S(1)}, bf16[96,1792]{1,0:T(8,128)(2,1)S(1)}, u32[]{:S(2)}, u32[]{:S(2)}) collective-permute-start(bf16[96,1792]{1,0:T(8,128)(2,1)S(1)} %get-tuple-element.41), channel_id=1, source_target_pairs={{0,1},{1,0},{2,3},{3,2},{4,5},{5,4},{6,7},{7,6},{8,9},{9,8},{10,11... | collective-permute-start | bytes 1032200 | tf_op jit(solution)/shard_map/ppermute | solution.py:205
  43.6 8.8 %collective-permute-start.13 = (bf16[48,1792]{1,0:T(8,128)(2,1)S(1)}, bf16[48,1792]{1,0:T(8,128)(2,1)S(1)}, u32[]{:S(2)}, u32[]{:S(2)}) collective-permute-start(bf16[48,1792]{1,0:T(8,128)(2,1)S(1)} %fusion.8), channel_id=1, source_target_pairs={{0,8},{1,9},{2,10},{3,11},{4,12},{5,13},{6,14},{7,15},{8,0},{9,1},... | collective-permute-start | bytes 516104 | tf_op jit(solution)/shard_map/ppermute | solution.py:205
  45.0 20.0 %copy-start.3 = (s32[16,2]{0,1:T(2,128)S(1)}, s32[16,2]{0,1:T(2,128)}, u32[]{:S(2)}) copy-start(s32[16,2]{0,1:T(2,128)} %param.9) | copy-start | bytes 388
  45.0 20.0 %copy-start.4 = (s32[16,2]{0,1:T(2,128)S(1)}, s32[16,2]{0,1:T(2,128)}, u32[]{:S(2)}) copy-start(s32[16,2]{0,1:T(2,128)} %param.10) | copy-start | bytes 388
  45.0 7.3 %collective-permute-start.18 = (bf16[48,1792]{1,0:T(8,128)(2,1)S(1)}, bf16[48,1792]{1,0:T(8,128)(2,1)S(1)}, u32[]{:S(2)}, u32[]{:S(2)}) collective-permute-start(bf16[48,1792]{1,0:T(8,128)(2,1)S(1)} %fusion.3), channel_id=1, source_target_pairs={{0,2},{1,3},{2,0},{3,1},{4,6},{5,7},{6,4},{7,5},{8,10},{9,11},{10,... | collective-permute-start | bytes 516104 | tf_op jit(solution)/shard_map/ppermute | solution.py:205
  45.7 13.3 %collective-permute-start.9 = (bf16[96,1792]{1,0:T(8,128)(2,1)S(1)}, bf16[96,1792]{1,0:T(8,128)(2,1)S(1)}, u32[]{:S(2)}, u32[]{:S(2)}) collective-permute-start(bf16[96,1792]{1,0:T(8,128)(2,1)S(1)} %fusion), channel_id=1, source_target_pairs={{0,2},{1,3},{2,0},{3,1},{4,6},{5,7},{6,4},{7,5},{8,10},{9,11},{10,... | collective-permute-start | bytes 1032200 | tf_op jit(solution)/shard_map/ppermute | solution.py:205
  52.3 8.2 %collective-permute-start.19 = (bf16[48,1792]{1,0:T(8,128)(2,1)S(1)}, bf16[48,1792]{1,0:T(8,128)(2,1)S(1)}, u32[]{:S(2)}, u32[]{:S(2)}) collective-permute-start(bf16[48,1792]{1,0:T(8,128)(2,1)S(1)} %fusion.5), channel_id=1, source_target_pairs={{0,12},{1,13},{2,14},{3,15},{4,8},{5,9},{6,10},{7,11},{8,4},{9,5},... | collective-permute-start | bytes 516104 | tf_op jit(solution)/shard_map/ppermute | solution.py:205
  59.1 5.9 %collective-permute-start.10 = (bf16[48,1792]{1,0:T(8,128)(2,1)S(1)}, bf16[48,1792]{1,0:T(8,128)(2,1)S(1)}, u32[]{:S(2)}, u32[]{:S(2)}) collective-permute-start(bf16[48,1792]{1,0:T(8,128)(2,1)S(1)} %get-tuple-element.43), channel_id=1, source_target_pairs={{0,4},{1,5},{2,6},{3,7},{4,0},{5,1},{6,2},{7,3},{8,12},{9,13},{10,... | collective-permute-start | bytes 516104 | tf_op jit(solution)/shard_map/ppermute | solution.py:205

commit v5 on v4

--- a/solution.py
+++ b/solution.py
@@ -9,6 +9,21 @@
 
 SHARDS = 4
 QUARTERS = 4
+GROUPS = ("own+near", "mid", "far")
+SPLIT = ("c mid", "c near",)
+ORDER = {
+    "z far": ("y own",),
+    "expert far": ("rc mid",),
+    "rz far": ("z mid",),
+    "c own": ("c near",),
+    "c mid": ("y mid",),
+    "rz mid": ("rc far", "c mid", "z near",),
+    "c far": ("z near",),
+    "ry own+near": ("y near",),
+    "y far": ("z near",),
+    "expert mid": ("c mid",),
+    "c near": ("y mid", "load all",),
+}
 VMEM_BYTES = 16 * 1024 * 1024
 PACK_VMEM_BYTES = 48 * 1024 * 1024
 LOAD_VMEM_BYTES = 40 * 1024 * 1024
@@ -220,17 +235,7 @@
         compiler_params=pack_params,
     )(tokens, scales, routes.T)
 
-    weights = pl.pallas_call(
-        load_kernel,
-        out_shape=[jax.ShapeDtypeStruct(w.shape, w.dtype) for w in (w_gate, w_up, w_down)],
-        in_specs=[hbm] * 4,
-        out_specs=[vmem] * 3,
-        scratch_shapes=[pltpu.SemaphoreType.DMA((3,))],
-        compiler_params=load_params,
-    )(w_gate, w_up, w_down, packed[0])
-
-    def expert(start, stop, held, weights):
-        offsets = stop - start
+    def expert(offsets, held, weights):
         rows = offsets * SHARDS * capacity
         half = jax.ShapeDtypeStruct((2 * offsets * tall, width), jnp.bfloat16)
         return pl.pallas_call(
@@ -247,11 +252,15 @@
             ),
         )(*held, *weights)
 
-    def across(array):
-        return partner(array, 2)
-
-    def along(array, offset):
-        return array if offset == 0 else partner(array, offset * SHARDS)
+    def load(gate):
+        return pl.pallas_call(
+            load_kernel,
+            out_shape=[jax.ShapeDtypeStruct(w.shape, w.dtype) for w in (w_gate, w_up, w_down)],
+            in_specs=[hbm] * 4,
+            out_specs=[vmem] * 3,
+            scratch_shapes=[pltpu.SemaphoreType.DMA((3,))],
+            compiler_params=load_params,
+        )(w_gate, w_up, w_down, gate)
 
     def fold(kept, arrived, offsets):
         middle = offsets * tall
@@ -259,63 +268,81 @@
         leaving = (kept[middle:] + arrived[middle:]).astype(jnp.bfloat16)
         return leaving, kept[:middle] + arrived[:middle]
 
-    def pair(own, other):
-        both = jnp.concatenate([own, other], axis=0)
-        return [both, partner(both, 1)]
-
     half, late = planes // 2, 3 * planes // 4
-    first, second, third = range(half), range(half, late), range(late, planes)
-    arrive, cross, held, returned = {}, {}, {}, {}
-
-    def take(table, places):
-        return [table[at] for at in places]
-
-    for at in list(second) + list(first):
-        arrive[at] = along(packed[at], at)
-    cross[0] = across(arrive[0])
-    for at in first:
-        if at:
-            arrive[at] = after(arrive[at], *weights)
-            cross[at] = across(arrive[at])
-    for at in third:
-        arrive[at] = along(after(packed[at], *take(arrive, second)), at)
-    for at in second:
-        cross[at] = across(after(arrive[at], cross[0]))
-    for at in second:
-        held[at] = pair(arrive[at], cross[at])
-    held2 = sum(take(held, second), [])
-    kept2, sent2 = expert(half, late, held2, weights)
-    for at in first:
-        held[at] = pair(arrive[at], cross[at])
-    held1 = sum(take(held, first), [])
-    held1[0] = after(held1[0], kept2)
-    kept1, sent1 = expert(0, half, held1, weights)
-    back2 = partner(sent2, 1)
-    leave2, stay2 = fold(kept2, back2, len(second))
-    for at in third:
-        cross[at] = across(arrive[at])
-    home2 = across(leave2)
-    for at in third:
-        held[at] = pair(arrive[at], cross[at])
-    held3 = sum(take(held, third), [])
-    held3[0] = after(held3[0], kept1, leave2)
-    kept3, sent3 = expert(late, planes, held3, weights)
-    back1 = partner(sent1, 1)
-    leave1, stay1 = fold(kept1, back1, len(first))
-    home1 = across(leave1)
-    back3 = partner(sent3, 1)
-    leave3, stay3 = fold(kept3, back3, len(third))
-    home3 = across(leave3)
-    answer2 = (stay2 + home2.astype(jnp.float32)).astype(jnp.bfloat16)
-    for index, at in enumerate(second):
-        returned[at] = along(answer2[index * tall : (index + 1) * tall], at)
-    answer1 = (stay1 + home1.astype(jnp.float32)).astype(jnp.bfloat16)
-    for index, at in enumerate(first):
-        returned[at] = along(answer1[index * tall : (index + 1) * tall], at)
-    answer3 = (stay3 + home3.astype(jnp.float32)).astype(jnp.bfloat16)
-    answer3 = after(answer3, *take(returned, second))
-    for index, at in enumerate(third):
-        returned[at] = along(answer3[index * tall : (index + 1) * tall], at)
+    places = {
+        "own": range(1),
+        "near": range(1, half),
+        "mid": range(half, late),
+        "far": range(late, planes),
+    }
+    for group in GROUPS:
+        places[group] = [at for member in group.split("+") for at in places[member]]
+    results = {}
+
+    def result(step):
+        if step not in results:
+            results[step] = build(*step.split())
+        return results[step]
+
+    def build(kind, name):
+        if kind == "pack":
+            return [packed[at] for at in places[name]]
+        if kind == "z":
+            inputs = result("pack " + name)
+        elif kind == "y":
+            inputs = result(("pack " if name == "own" else "z ") + name)
+        elif kind == "c":
+            own = result(("pack " if name == "own" else "z ") + name)
+            inputs = [jnp.concatenate(both, axis=0) for both in zip(own, result("y " + name))]
+        elif kind == "expert":
+            inputs = []
+            for member in name.split("+"):
+                own = result(("pack " if member == "own" else "z ") + member)
+                both = [jnp.concatenate(two, axis=0) for two in zip(own, result("y " + member))]
+                for two in zip(both, result("c " + member)):
+                    inputs += two
+        elif kind == "rc":
+            inputs = result("expert " + name)[1:]
+        elif kind == "sum":
+            kept, arrived = result("expert " + name)[0], result("rc " + name)[0]
+            return fold(kept, arrived, len(places[name]))
+        elif kind == "ry":
+            inputs = result("sum " + name)[:1]
+        elif kind == "answer":
+            total = result("sum " + name)[1] + result("ry " + name)[0].astype(jnp.float32)
+            total = total.astype(jnp.bfloat16)
+            return [total[at * tall : (at + 1) * tall] for at in range(len(places[name]))]
+        elif kind == "load":
+            inputs = packed[:1]
+        elif kind == "rz":
+            inputs = [a for a, at in zip(result("answer " + name), places[name]) if at]
+        earlier = [result(step)[-1] for step in ORDER.get(kind + " " + name, ())]
+        if earlier:
+            inputs = [after(inputs[0], *earlier)] + list(inputs[1:])
+        if kind == "load":
+            return load(inputs[0])
+        if kind == "expert":
+            return expert(len(places[name]), inputs, result("load all"))
+        if kind in ("y", "ry"):
+            return [partner(array, 2) for array in inputs]
+        if kind in ("c", "rc"):
+            if kind + " " + name not in SPLIT:
+                return [partner(array, 1) for array in inputs]
+            halves = [jnp.split(array, 2, axis=0) for array in inputs]
+            if kind == "c":
+                own = result(("pack " if name == "own" else "z ") + name)
+                halves = [(one, two[1]) for one, two in zip(own, halves)]
+            halves = [[partner(half, 1) for half in pair] for pair in halves]
+            return [jnp.concatenate(pair, axis=0) for pair in halves]
+        where = [at for at in places[name] if at]
+        return [partner(array, at * SHARDS) for array, at in zip(inputs, where)]
+
+    returned = {}
+    for group in GROUPS:
+        pieces = list(result("answer " + group))
+        if group != "own":
+            pieces[-len(result("rz " + group)) :] = result("rz " + group)
+        returned.update(zip(places[group], pieces))
     returned = [returned[at] for at in range(planes)]
 
     return pl.pallas_call(

time: 66.7 us -> 59.8 us (0.90)
  waiting for transfers between devices: 26.9 us -> 14.4 us
  starting transfers between devices: 22 us -> 27.4 us
    ppermute x20 -> x22, waiting for transfers between devices: 26.9 us -> 14.4 us  [partner(): lax.ppermute(array, 'expert', [(i, i ^ distance) for i in range(devices)])]
    ppermute x20 -> x22, starting transfers between devices: 22 us -> 27.4 us  [partner(): lax.ppermute(array, 'expert', [(i, i ^ distance) for i in range(devices)])]
    unnamed x14 -> x16, local copies, waits for them, and re-layouts: 2.37 us -> 2.4 us
  transfers between devices with their start and end apart: 20 -> 22, of which waited for: 9 -> 9; matrix products, arithmetic and copies ran while one was open for 1% -> 2% of each run, Pallas kernels for 17% -> 19%
where the time goes in v5:
time: 59.8 us; the launch traced here: 59.6 us
  starting transfers between devices  27.4 us (46%)
  waiting for transfers between devices  14.4 us (24%)
  Pallas kernels  14.2 us (24%)
  local copies, waits for them, and re-layouts  2.53 us (4%)
  other arithmetic  0.73 us (1%)
    ppermute x22, starting transfers between devices, partner(): lax.ppermute(array, 'expert', [(i, i ^ distance) for i in range(devices)])  27.4 us
    ppermute x22, waiting for transfers between devices, partner(): lax.ppermute(array, 'expert', [(i, i ^ distance) for i in range(devices)])  14.4 us
    pallas_call x3, Pallas kernels, expert(): pl.pallas_call(functools.partial(expert_kernel, capacity, offsets), out_s...  7.39 us
    pallas_call x1, Pallas kernels, load(): pl.pallas_call(load_kernel, out_shape=[jax.ShapeDtypeStruct(w.shape, w.dt...  4.23 us
    unnamed x16, local copies, waits for them, and re-layouts  2.4 us
    pallas_call x1, Pallas kernels, shards(): pl.pallas_call(functools.partial(mix_kernel, capacity, planes), out_shape...  1.48 us
  transfers between devices with their start and end apart: 22, of which 9 were waited for; matrix products, arithmetic and copies ran while one was open for 2% of the time, Pallas kernels for 19%

profile of v5, /device:TPU:0, one launch (start us, length us, event | category | flops | bytes accessed | tf_op | source)
XLA Modules:
  0.0 59.6 jit_solution(898138788776674964)
XLA Ops:
  0.0 0.0 copy-start
  0.0 0.9 %copy-done = bf16[16,7168]{1,0:T(8,128)(2,1)S(1)} copy-done((bf16[16,7168]{1,0:T(8,128)(2,1)S(1)}, bf16[16,7168]{1,0:T(8,128)(2,1)}, u32[]{:S(2)}) %copy-start) | copy-done | bytes 229400
  0.9 0.7 %copy-done.1 = f32[16,56]{1,0:T(8,128)S(1)} copy-done((f32[16,56]{1,0:T(8,128)S(1)}, f32[16,56]{1,0:T(8,128)}, u32[]{:S(2)}) %copy-start.1) | copy-done | bytes 3608
  1.6 0.7 %copy-done.2 = s32[16,2]{0,1:T(2,128)S(1)} copy-done((s32[16,2]{0,1:T(2,128)S(1)}, s32[16,2]{0,1:T(2,128)}, u32[]{:S(2)}) %copy-start.2) | copy-done | bytes 152
  2.3 1.1 %shard_map.73 = (bf16[48,1792]{1,0:T(8,128)(2,1)S(1)}, bf16[48,1792]{1,0:T(8,128)(2,1)S(1)}, bf16[48,1792]{1,0:T(8,128)(2,1)S(1)}, bf16[48,1792]{1,0:T(8,128)(2,1)S(1)}) custom-call(bf16[16,7168]{1,0:T(8,128)(2,1)S(1)} %copy-done, f32[16,56]{1,0:T(8,128)S(1)} %copy-done.1, s32[2,16]{1,0:T(2,128)S(1)} %bitcast.2), custom_call_target="tpu_custom_call" | custom-call | tf_op jit(solution)/shard_map/pallas_call | solution.py:223
  3.5 4.1 %collective-permute-start.4 = (bf16[48,1792]{1,0:T(8,128)(2,1)S(1)}, bf16[48,1792]{1,0:T(8,128)(2,1)S(1)}, u32[]{:S(2)}, u32[]{:S(2)}) collective-permute-start(bf16[48,1792]{1,0:T(8,128)(2,1)S(1)} %get-tuple-element.31), channel_id=1, source_target_pairs={{0,8},{1,9},{2,10},{3,11},{4,12},{5,13},{6,14},{7,15},{8,0},{9,1},... | collective-permute-start | bytes 516104 | tf_op jit(solution)/shard_map/ppermute | solution.py:220
  7.6 1.5 %collective-permute-start = (bf16[48,1792]{1,0:T(8,128)(2,1)S(1)}, bf16[48,1792]{1,0:T(8,128)(2,1)S(1)}, u32[]{:S(2)}, u32[]{:S(2)}) collective-permute-start(bf16[48,1792]{1,0:T(8,128)(2,1)S(1)} %get-tuple-element.29.unused), channel_id=1, source_target_pairs={{0,2},{1,3},{2,0},{3,1},{4,6},{5,7},{6,4},{7,5},{8,10},{9,11},{10,... | collective-permute-start | bytes 516104 | tf_op jit(solution)/shard_map/ppermute | solution.py:220
  9.1 1.6 %collective-permute-start.1 = (bf16[48,1792]{1,0:T(8,128)(2,1)S(1)}, bf16[48,1792]{1,0:T(8,128)(2,1)S(1)}, u32[]{:S(2)}, u32[]{:S(2)}) collective-permute-start(bf16[48,1792]{1,0:T(8,128)(2,1)S(1)} %get-tuple-element.30), channel_id=1, source_target_pairs={{0,4},{1,5},{2,6},{3,7},{4,0},{5,1},{6,2},{7,3},{8,12},{9,13},{10,... | collective-permute-start | bytes 516104 | tf_op jit(solution)/shard_map/ppermute | solution.py:220
  10.7 4.2 %shard_map.74 = (bf16[1,7168,256]{2,1,0:T(8,128)(2,1)S(1)}, bf16[1,7168,256]{2,1,0:T(8,128)(2,1)S(1)}, bf16[1,256,7168]{2,1,0:T(8,128)(2,1)S(1)}) custom-call(bf16[1,7168,256]{2,1,0:T(8,128)(2,1)} %gate_hbm.1, bf16[1,7168,256]{2,1,0:T(8,128)(2,1)} %up_hbm.1, bf16[1,256,7168]{2,1,0:T(8,128)(2,1)} %down_hbm.1, bf16[48,1792]{1,0:T(8,128)(2,1)S(1)} %get-tuple-element.29.unused), custom_call_target="tpu_custom_call" | custom-call | tf_op jit(solution)/shard_map/pallas_call | solution.py:256
  14.9 0.0 collective-permute-done
  14.9 0.3 collective-permute-start.15
  15.2 0.5 collective-permute-done.4
  15.7 1.6 %collective-permute-start.5 = (bf16[48,1792]{1,0:T(8,128)(2,1)S(1)}, bf16[48,1792]{1,0:T(8,128)(2,1)S(1)}, u32[]{:S(2)}, u32[]{:S(2)}) collective-permute-start(bf16[48,1792]{1,0:T(8,128)(2,1)S(1)} %collective-permute-done.4), channel_id=1, source_target_pairs={{0,2},{1,3},{2,0},{3,1},{4,6},{5,7},{6,4},{7,5},{8,10},{9,11},{10,... | collective-permute-start | bytes 516104 | tf_op jit(solution)/shard_map/ppermute | solution.py:220
  17.3 0.0 collective-permute-start.11
  17.3 0.0 collective-permute-done.1
  17.3 0.5 collective-permute-start.3
  17.9 0.3 collective-permute-start.2
  18.2 3.8 %collective-permute-done.5 = bf16[48,1792]{1,0:T(8,128)(2,1)S(1)} collective-permute-done((bf16[48,1792]{1,0:T(8,128)(2,1)S(1)}, bf16[48,1792]{1,0:T(8,128)(2,1)S(1)}, u32[]{:S(2)}, u32[]{:S(2)}) %collective-permute-start.5) | collective-permute-done | bytes 172064 | tf_op jit(solution)/shard_map/ppermute | solution.py:220
  22.0 0.1 collective-permute-start.12
  22.1 0.2 collective-permute-done.15
  22.2 2.4 %collective-permute-start.16 = (bf16[48,1792]{1,0:T(8,128)(2,1)S(1)}, bf16[48,1792]{1,0:T(8,128)(2,1)S(1)}, u32[]{:S(2)}, u32[]{:S(2)}) collective-permute-start(bf16[48,1792]{1,0:T(8,128)(2,1)S(1)} %collective-permute-done.15), channel_id=1, source_target_pairs={{0,2},{1,3},{2,0},{3,1},{4,6},{5,7},{6,4},{7,5},{8,10},{9,11},{10,... | collective-permute-start | bytes 516104 | tf_op jit(solution)/shard_map/ppermute | solution.py:220
  24.6 0.2 collective-permute-done.3
  24.9 0.1 collective-permute-start.6
  25.0 0.0 collective-permute-done.11
  25.0 0.0 collective-permute-done.2
  25.1 0.0 collective-permute-done.12
  25.1 2.3 %shard_map.76 = (bf16[96,1792]{1,0:T(8,128)(2,1)S(1)}, bf16[96,1792]{1,0:T(8,128)(2,1)S(1)}) custom-call(bf16[96,1792]{1,0:T(8,128)(2,1)S(1)} %constant_dynamic-update-slice_fusion.6.refs_0_, bf16[96,1792]{1,0:T(8,128)(2,1)S(1)} %constant_dynamic-update-slice_fusion.8.refs_1_, bf16[1,7168,256]{2,1,0:T(8,128)(2,1)S(1)} %get-tuple-element.35.refs_4_.refs_2_, ...), custom_call_target="tpu_custom_call" | custom-call | flops 528482304 | tf_op jit(solution)/shard_map/pallas_call | solution.py:241
  27.4 0.6 collective-permute-start.13
  27.9 1.7 %collective-permute-done.16 = bf16[48,1792]{1,0:T(8,128)(2,1)S(1)} collective-permute-done((bf16[48,1792]{1,0:T(8,128)(2,1)S(1)}, bf16[48,1792]{1,0:T(8,128)(2,1)S(1)}, u32[]{:S(2)}, u32[]{:S(2)}) %collective-permute-start.16) | collective-permute-done | bytes 172064 | tf_op jit(solution)/shard_map/ppermute | solution.py:220
  29.6 0.1 collective-permute-start.17
  29.8 0.0 collective-permute-done.6
  29.8 0.6 collective-permute-start.7
  30.3 0.0 collective-permute-done.13
  30.4 1.8 %collective-permute-start.14 = (bf16[48,1792]{1,0:T(8,128)(2,1)S(1)}, bf16[48,1792]{1,0:T(8,128)(2,1)S(1)}, u32[]{:S(2)}, u32[]{:S(2)}) collective-permute-start(bf16[48,1792]{1,0:T(8,128)(2,1)S(1)} %fusion.6), channel_id=1, source_target_pairs={{0,2},{1,3},{2,0},{3,1},{4,6},{5,7},{6,4},{7,5},{8,10},{9,11},{10,... | collective-permute-start | bytes 516104 | tf_op jit(solution)/shard_map/ppermute | solution.py:220
  32.3 0.0 collective-permute-done.17.refs_1_
  32.3 2.3 %shard_map.77 = (bf16[96,1792]{1,0:T(8,128)(2,1)S(1)}, bf16[96,1792]{1,0:T(8,128)(2,1)S(1)}) custom-call(bf16[96,1792]{1,0:T(8,128)(2,1)S(1)} %constant_dynamic-update-slice_fusion.10.refs_0_, bf16[96,1792]{1,0:T(8,128)(2,1)S(1)} %collective-permute-done.17.refs_1_, bf16[1,7168,256]{2,1,0:T(8,128)(2,1)S(1)} %get-tuple-element.35.refs_4_.refs_2_, ...), custom_call_target="tpu_custom_call" | custom-call | flops 528482304 | tf_op jit(solution)/shard_map/pallas_call | solution.py:241
  34.6 0.1 collective-permute-start.18
  34.7 0.0 collective-permute-done.7.refs_1_
  34.7 2.8 %shard_map.75 = (bf16[192,1792]{1,0:T(8,128)(2,1)S(1)}, bf16[192,1792]{1,0:T(8,128)(2,1)S(1)}) custom-call(bf16[96,1792]{1,0:T(8,128)(2,1)S(1)} %constant_dynamic-update-slice_fusion.refs_0_, bf16[96,1792]{1,0:T(8,128)(2,1)S(1)} %collective-permute-done.7.refs_1_, bf16[96,1792]{1,0:T(8,128)(2,1)S(1)} %constant_dynamic-update-slice_fusion.2.refs_2_, ...), custom_call_target="tpu_custom_call" | custom-call | flops 1056964608 | tf_op jit(solution)/shard_map/pallas_call | solution.py:241
  37.5 0.6 collective-permute-start.8
  38.1 0.1 convert_element_type.45
  38.2 0.0 collective-permute-done.14
  38.2 0.1 fusion.8
  38.2 0.0 collective-permute-done.18
  38.3 0.1 fusion.3
  38.4 0.0 copy-start.4
  38.4 0.9 %collective-permute-start.20 = (bf16[48,1792]{1,0:T(8,128)(2,1)S(1)}, bf16[48,1792]{1,0:T(8,128)(2,1)S(1)}, u32[]{:S(2)}, u32[]{:S(2)}) collective-permute-start(bf16[48,1792]{1,0:T(8,128)(2,1)S(1)} %fusion.3), channel_id=1, source_target_pairs={{0,2},{1,3},{2,0},{3,1},{4,6},{5,7},{6,4},{7,5},{8,10},{9,11},{10,... | collective-permute-start | bytes 516104 | tf_op jit(solution)/shard_map/ppermute | solution.py:220
  39.3 2.1 %collective-permute-start.19 = (bf16[48,1792]{1,0:T(8,128)(2,1)S(1)}, bf16[48,1792]{1,0:T(8,128)(2,1)S(1)}, u32[]{:S(2)}, u32[]{:S(2)}) collective-permute-start(bf16[48,1792]{1,0:T(8,128)(2,1)S(1)} %fusion.8), channel_id=1, source_target_pairs={{0,8},{1,9},{2,10},{3,11},{4,12},{5,13},{6,14},{7,15},{8,0},{9,1},... | collective-permute-start | bytes 516104 | tf_op jit(solution)/shard_map/ppermute | solution.py:220
  41.4 0.0 collective-permute-done.8
  41.4 0.1 convert_element_type.46
  41.5 0.1 fusion
  41.5 1.3 %collective-permute-start.9 = (bf16[96,1792]{1,0:T(8,128)(2,1)S(1)}, bf16[96,1792]{1,0:T(8,128)(2,1)S(1)}, u32[]{:S(2)}, u32[]{:S(2)}) collective-permute-start(bf16[96,1792]{1,0:T(8,128)(2,1)S(1)} %fusion), channel_id=1, source_target_pairs={{0,2},{1,3},{2,0},{3,1},{4,6},{5,7},{6,4},{7,5},{8,10},{9,11},{10,... | collective-permute-start | bytes 1032200 | tf_op jit(solution)/shard_map/ppermute | solution.py:220
  42.8 2.9 %collective-permute-done.20 = bf16[48,1792]{1,0:T(8,128)(2,1)S(1)} collective-permute-done((bf16[48,1792]{1,0:T(8,128)(2,1)S(1)}, bf16[48,1792]{1,0:T(8,128)(2,1)S(1)}, u32[]{:S(2)}, u32[]{:S(2)}) %collective-permute-start.20) | collective-permute-done | bytes 172064 | tf_op jit(solution)/shard_map/ppermute | solution.py:220
  45.7 0.1 fusion.5
  45.7 4.8 %collective-permute-start.21 = (bf16[48,1792]{1,0:T(8,128)(2,1)S(1)}, bf16[48,1792]{1,0:T(8,128)(2,1)S(1)}, u32[]{:S(2)}, u32[]{:S(2)}) collective-permute-start(bf16[48,1792]{1,0:T(8,128)(2,1)S(1)} %fusion.5), channel_id=1, source_target_pairs={{0,12},{1,13},{2,14},{3,15},{4,8},{5,9},{6,10},{7,11},{8,4},{9,5},... | collective-permute-start | bytes 516104 | tf_op jit(solution)/shard_map/ppermute | solution.py:220
  50.6 1.6 %collective-permute-done.9 = bf16[96,1792]{1,0:T(8,128)(2,1)S(1)} collective-permute-done((bf16[96,1792]{1,0:T(8,128)(2,1)S(1)}, bf16[96,1792]{1,0:T(8,128)(2,1)S(1)}, u32[]{:S(2)}, u32[]{:S(2)}) %collective-permute-start.9) | collective-permute-done | bytes 344096 | tf_op jit(solution)/shard_map/ppermute | solution.py:220
  52.1 0.1 fusion.2
  52.2 2.3 %collective-permute-start.10 = (bf16[48,1792]{1,0:T(8,128)(2,1)S(1)}, bf16[48,1792]{1,0:T(8,128)(2,1)S(1)}, u32[]{:S(2)}, u32[]{:S(2)}) collective-permute-start(bf16[48,1792]{1,0:T(8,128)(2,1)S(1)} %get-tuple-element.53), channel_id=1, source_target_pairs={{0,4},{1,5},{2,6},{3,7},{4,0},{5,1},{6,2},{7,3},{8,12},{9,13},{10,... | collective-permute-start | bytes 516104 | tf_op jit(solution)/shard_map/ppermute | solution.py:220
  54.6 0.3 collective-permute-done.19.refs_2_
  54.8 0.0 collective-permute-done.21.refs_3_
  54.8 3.3 %collective-permute-done.10.refs_1_ = bf16[48,1792]{1,0:T(8,128)(2,1)S(1)} collective-permute-done((bf16[48,1792]{1,0:T(8,128)(2,1)S(1)}, bf16[48,1792]{1,0:T(8,128)(2,1)S(1)}, u32[]{:S(2)}, u32[]{:S(2)}) %collective-permute-start.10) | collective-permute-done | bytes 172064 | tf_op jit(solution)/shard_map/ppermute | solution.py:220
  58.1 0.0 copy-done.3
  58.1 0.0 copy-done.4
  58.1 1.5 %shard_map.78 = bf16[16,7168]{1,0:T(8,128)(2,1)} custom-call(s32[2,16]{1,0:T(2,128)S(1)} %bitcast.3, s32[2,16]{1,0:T(2,128)S(1)} %bitcast.4, bf16[48,1792]{1,0:T(8,128)(2,1)S(1)} %get-tuple-element.54.refs_0_, bf16[48,1792]{1,0:T(8,128)(2,1)S(1)} %collective-permute-done.10.refs_1_, bf16[48,1792]{1,0:T(8,128)(2,1)S(1)} %collective-permute-done.19.refs_2_, ...), custom_call_target="tpu_custom_call" | custom-call | tf_op jit(solution)/shard_map/pallas_call | solution.py:348
  (23 shorter events, 0.4 us)
Async XLA Ops:
  0.0 0.9 %copy-start = (bf16[16,7168]{1,0:T(8,128)(2,1)S(1)}, bf16[16,7168]{1,0:T(8,128)(2,1)}, u32[]{:S(2)}) copy-start(bf16[16,7168]{1,0:T(8,128)(2,1)} %tok_hbm.1) | copy-start | bytes 688132
  0.9 0.7 %copy-start.1 = (f32[16,56]{1,0:T(8,128)S(1)}, f32[16,56]{1,0:T(8,128)}, u32[]{:S(2)}) copy-start(f32[16,56]{1,0:T(8,128)} %scale_hbm.1) | copy-start | bytes 10756
  1.6 0.7 %copy-start.2 = (s32[16,2]{0,1:T(2,128)S(1)}, s32[16,2]{0,1:T(2,128)}, u32[]{:S(2)}) copy-start(s32[16,2]{0,1:T(2,128)} %param.9) | copy-start | bytes 388
  3.5 12.3 %collective-permute-start.4 = (bf16[48,1792]{1,0:T(8,128)(2,1)S(1)}, bf16[48,1792]{1,0:T(8,128)(2,1)S(1)}, u32[]{:S(2)}, u32[]{:S(2)}) collective-permute-start(bf16[48,1792]{1,0:T(8,128)(2,1)S(1)} %get-tuple-element.31), channel_id=1, source_target_pairs={{0,8},{1,9},{2,10},{3,11},{4,12},{5,13},{6,14},{7,15},{8,0},{9,1},... | collective-permute-start | bytes 516104 | tf_op jit(solution)/shard_map/ppermute | solution.py:220
  7.6 7.4 %collective-permute-start = (bf16[48,1792]{1,0:T(8,128)(2,1)S(1)}, bf16[48,1792]{1,0:T(8,128)(2,1)S(1)}, u32[]{:S(2)}, u32[]{:S(2)}) collective-permute-start(bf16[48,1792]{1,0:T(8,128)(2,1)S(1)} %get-tuple-element.29.unused), channel_id=1, source_target_pairs={{0,2},{1,3},{2,0},{3,1},{4,6},{5,7},{6,4},{7,5},{8,10},{9,11},{10,... | collective-permute-start | bytes 516104 | tf_op jit(solution)/shard_map/ppermute | solution.py:220
  9.1 8.2 %collective-permute-start.1 = (bf16[48,1792]{1,0:T(8,128)(2,1)S(1)}, bf16[48,1792]{1,0:T(8,128)(2,1)S(1)}, u32[]{:S(2)}, u32[]{:S(2)}) collective-permute-start(bf16[48,1792]{1,0:T(8,128)(2,1)S(1)} %get-tuple-element.30), channel_id=1, source_target_pairs={{0,4},{1,5},{2,6},{3,7},{4,0},{5,1},{6,2},{7,3},{8,12},{9,13},{10,... | collective-permute-start | bytes 516104 | tf_op jit(solution)/shard_map/ppermute | solution.py:220
  14.9 7.3 %collective-permute-start.15 = (bf16[48,1792]{1,0:T(8,128)(2,1)S(1)}, bf16[48,1792]{1,0:T(8,128)(2,1)S(1)}, u32[]{:S(2)}, u32[]{:S(2)}) collective-permute-start(bf16[48,1792]{1,0:T(8,128)(2,1)S(1)} %get-tuple-element.45), channel_id=1, source_target_pairs={{0,12},{1,13},{2,14},{3,15},{4,8},{5,9},{6,10},{7,11},{8,4},{9,5},... | collective-permute-start | bytes 516104 | tf_op jit(solution)/shard_map/ppermute | solution.py:220
  15.7 6.2 %collective-permute-start.5 = (bf16[48,1792]{1,0:T(8,128)(2,1)S(1)}, bf16[48,1792]{1,0:T(8,128)(2,1)S(1)}, u32[]{:S(2)}, u32[]{:S(2)}) collective-permute-start(bf16[48,1792]{1,0:T(8,128)(2,1)S(1)} %collective-permute-done.4), channel_id=1, source_target_pairs={{0,2},{1,3},{2,0},{3,1},{4,6},{5,7},{6,4},{7,5},{8,10},{9,11},{10,... | collective-permute-start | bytes 516104 | tf_op jit(solution)/shard_map/ppermute | solution.py:220
  17.3 7.7 %collective-permute-start.11 = (bf16[48,1792]{1,0:T(8,128)(2,1)S(1)}, bf16[48,1792]{1,0:T(8,128)(2,1)S(1)}, u32[]{:S(2)}, u32[]{:S(2)}) collective-permute-start(bf16[48,1792]{1,0:T(8,128)(2,1)S(1)} %collective-permute-done.4), channel_id=1, source_target_pairs={{0,1},{1,0},{2,3},{3,2},{4,5},{5,4},{6,7},{7,6},{8,9},{9,8},{10,11... | collective-permute-start | bytes 516104 | tf_op jit(solution)/shard_map/ppermute | solution.py:220
  17.3 7.5 %collective-permute-start.3 = (bf16[48,1792]{1,0:T(8,128)(2,1)S(1)}, bf16[48,1792]{1,0:T(8,128)(2,1)S(1)}, u32[]{:S(2)}, u32[]{:S(2)}) collective-permute-start(bf16[48,1792]{1,0:T(8,128)(2,1)S(1)} %collective-permute-done.1), channel_id=1, source_target_pairs={{0,2},{1,3},{2,0},{3,1},{4,6},{5,7},{6,4},{7,5},{8,10},{9,11},{10,... | collective-permute-start | bytes 516104 | tf_op jit(solution)/shard_map/ppermute | solution.py:220
  17.9 7.2 %collective-permute-start.2 = (bf16[48,1792]{1,0:T(8,128)(2,1)S(1)}, bf16[48,1792]{1,0:T(8,128)(2,1)S(1)}, u32[]{:S(2)}, u32[]{:S(2)}) collective-permute-start(bf16[48,1792]{1,0:T(8,128)(2,1)S(1)} %collective-permute-done.1), channel_id=1, source_target_pairs={{0,1},{1,0},{2,3},{3,2},{4,5},{5,4},{6,7},{7,6},{8,9},{9,8},{10,11... | collective-permute-start | bytes 516104 | tf_op jit(solution)/shard_map/ppermute | solution.py:220
  22.0 3.1 %collective-permute-start.12 = (bf16[48,1792]{1,0:T(8,128)(2,1)S(1)}, bf16[48,1792]{1,0:T(8,128)(2,1)S(1)}, u32[]{:S(2)}, u32[]{:S(2)}) collective-permute-start(bf16[48,1792]{1,0:T(8,128)(2,1)S(1)} %split.7), channel_id=1, source_target_pairs={{0,1},{1,0},{2,3},{3,2},{4,5},{5,4},{6,7},{7,6},{8,9},{9,8},{10,11... | collective-permute-start | bytes 516104 | tf_op jit(solution)/shard_map/ppermute | solution.py:220
  22.2 7.4 %collective-permute-start.16 = (bf16[48,1792]{1,0:T(8,128)(2,1)S(1)}, bf16[48,1792]{1,0:T(8,128)(2,1)S(1)}, u32[]{:S(2)}, u32[]{:S(2)}) collective-permute-start(bf16[48,1792]{1,0:T(8,128)(2,1)S(1)} %collective-permute-done.15), channel_id=1, source_target_pairs={{0,2},{1,3},{2,0},{3,1},{4,6},{5,7},{6,4},{7,5},{8,10},{9,11},{10,... | collective-permute-start | bytes 516104 | tf_op jit(solution)/shard_map/ppermute | solution.py:220
  24.9 4.9 %collective-permute-start.6 = (bf16[48,1792]{1,0:T(8,128)(2,1)S(1)}, bf16[48,1792]{1,0:T(8,128)(2,1)S(1)}, u32[]{:S(2)}, u32[]{:S(2)}) collective-permute-start(bf16[48,1792]{1,0:T(8,128)(2,1)S(1)} %split.6), channel_id=1, source_target_pairs={{0,1},{1,0},{2,3},{3,2},{4,5},{5,4},{6,7},{7,6},{8,9},{9,8},{10,11... | collective-permute-start | bytes 516104 | tf_op jit(solution)/shard_map/ppermute | solution.py:220
  27.4 3.0 %collective-permute-start.13 = (bf16[96,1792]{1,0:T(8,128)(2,1)S(1)}, bf16[96,1792]{1,0:T(8,128)(2,1)S(1)}, u32[]{:S(2)}, u32[]{:S(2)}) collective-permute-start(bf16[96,1792]{1,0:T(8,128)(2,1)S(1)} %get-tuple-element.43), channel_id=1, source_target_pairs={{0,1},{1,0},{2,3},{3,2},{4,5},{5,4},{6,7},{7,6},{8,9},{9,8},{10,11... | collective-permute-start | bytes 1032200 | tf_op jit(solution)/shard_map/ppermute | solution.py:220
  29.6 2.6 %collective-permute-start.17 = (bf16[96,1792]{1,0:T(8,128)(2,1)S(1)}, bf16[96,1792]{1,0:T(8,128)(2,1)S(1)}, u32[]{:S(2)}, u32[]{:S(2)}) collective-permute-start(bf16[96,1792]{1,0:T(8,128)(2,1)S(1)} %constant_dynamic-update-slice_fusion.10.refs_0_), channel_id=1, source_target_pairs={{0,1},{1,0},{2,3},{3,2},{4,5},{5,4},{6,7},{7,6},{8,9},{9,8},{10,11... | collective-permute-start | bytes 1032200 | tf_op jit(solution)/shard_map/ppermute | solution.py:220
  29.8 4.9 %collective-permute-start.7 = (bf16[96,1792]{1,0:T(8,128)(2,1)S(1)}, bf16[96,1792]{1,0:T(8,128)(2,1)S(1)}, u32[]{:S(2)}, u32[]{:S(2)}) collective-permute-start(bf16[96,1792]{1,0:T(8,128)(2,1)S(1)} %constant_dynamic-update-slice_fusion.refs_0_), channel_id=1, source_target_pairs={{0,1},{1,0},{2,3},{3,2},{4,5},{5,4},{6,7},{7,6},{8,9},{9,8},{10,11... | collective-permute-start | bytes 1032200 | tf_op jit(solution)/shard_map/ppermute | solution.py:220
  30.4 7.7 %collective-permute-start.14 = (bf16[48,1792]{1,0:T(8,128)(2,1)S(1)}, bf16[48,1792]{1,0:T(8,128)(2,1)S(1)}, u32[]{:S(2)}, u32[]{:S(2)}) collective-permute-start(bf16[48,1792]{1,0:T(8,128)(2,1)S(1)} %fusion.6), channel_id=1, source_target_pairs={{0,2},{1,3},{2,0},{3,1},{4,6},{5,7},{6,4},{7,5},{8,10},{9,11},{10,... | collective-permute-start | bytes 516104 | tf_op jit(solution)/shard_map/ppermute | solution.py:220
  34.6 3.7 %collective-permute-start.18 = (bf16[96,1792]{1,0:T(8,128)(2,1)S(1)}, bf16[96,1792]{1,0:T(8,128)(2,1)S(1)}, u32[]{:S(2)}, u32[]{:S(2)}) collective-permute-start(bf16[96,1792]{1,0:T(8,128)(2,1)S(1)} %get-tuple-element.49), channel_id=1, source_target_pairs={{0,1},{1,0},{2,3},{3,2},{4,5},{5,4},{6,7},{7,6},{8,9},{9,8},{10,11... | collective-permute-start | bytes 1032200 | tf_op jit(solution)/shard_map/ppermute | solution.py:220
  37.5 3.8 %collective-permute-start.8 = (bf16[192,1792]{1,0:T(8,128)(2,1)S(1)}, bf16[192,1792]{1,0:T(8,128)(2,1)S(1)}, u32[]{:S(2)}, u32[]{:S(2)}) collective-permute-start(bf16[192,1792]{1,0:T(8,128)(2,1)S(1)} %get-tuple-element.38), channel_id=1, source_target_pairs={{0,1},{1,0},{2,3},{3,2},{4,5},{5,4},{6,7},{7,6},{8,9},{9,8},{10,11... | collective-permute-start | bytes 2064392 | tf_op jit(solution)/shard_map/ppermute | solution.py:220
  38.4 19.8 %copy-start.3 = (s32[16,2]{0,1:T(2,128)S(1)}, s32[16,2]{0,1:T(2,128)}, u32[]{:S(2)}) copy-start(s32[16,2]{0,1:T(2,128)} %param.9) | copy-start | bytes 388
  38.4 19.8 %copy-start.4 = (s32[16,2]{0,1:T(2,128)S(1)}, s32[16,2]{0,1:T(2,128)}, u32[]{:S(2)}) copy-start(s32[16,2]{0,1:T(2,128)} %param.10) | copy-start | bytes 388
  38.4 7.3 %collective-permute-start.20 = (bf16[48,1792]{1,0:T(8,128)(2,1)S(1)}, bf16[48,1792]{1,0:T(8,128)(2,1)S(1)}, u32[]{:S(2)}, u32[]{:S(2)}) collective-permute-start(bf16[48,1792]{1,0:T(8,128)(2,1)S(1)} %fusion.3), channel_id=1, source_target_pairs={{0,2},{1,3},{2,0},{3,1},{4,6},{5,7},{6,4},{7,5},{8,10},{9,11},{10,... | collective-permute-start | bytes 516104 | tf_op jit(solution)/shard_map/ppermute | solution.py:220
  39.3 15.5 %collective-permute-start.19 = (bf16[48,1792]{1,0:T(8,128)(2,1)S(1)}, bf16[48,1792]{1,0:T(8,128)(2,1)S(1)}, u32[]{:S(2)}, u32[]{:S(2)}) collective-permute-start(bf16[48,1792]{1,0:T(8,128)(2,1)S(1)} %fusion.8), channel_id=1, source_target_pairs={{0,8},{1,9},{2,10},{3,11},{4,12},{5,13},{6,14},{7,15},{8,0},{9,1},... | collective-permute-start | bytes 516104 | tf_op jit(solution)/shard_map/ppermute | solution.py:220
  41.5 10.6 %collective-permute-start.9 = (bf16[96,1792]{1,0:T(8,128)(2,1)S(1)}, bf16[96,1792]{1,0:T(8,128)(2,1)S(1)}, u32[]{:S(2)}, u32[]{:S(2)}) collective-permute-start(bf16[96,1792]{1,0:T(8,128)(2,1)S(1)} %fusion), channel_id=1, source_target_pairs={{0,2},{1,3},{2,0},{3,1},{4,6},{5,7},{6,4},{7,5},{8,10},{9,11},{10,... | collective-permute-start | bytes 1032200 | tf_op jit(solution)/shard_map/ppermute | solution.py:220
  45.7 9.1 %collective-permute-start.21 = (bf16[48,1792]{1,0:T(8,128)(2,1)S(1)}, bf16[48,1792]{1,0:T(8,128)(2,1)S(1)}, u32[]{:S(2)}, u32[]{:S(2)}) collective-permute-start(bf16[48,1792]{1,0:T(8,128)(2,1)S(1)} %fusion.5), channel_id=1, source_target_pairs={{0,12},{1,13},{2,14},{3,15},{4,8},{5,9},{6,10},{7,11},{8,4},{9,5},... | collective-permute-start | bytes 516104 | tf_op jit(solution)/shard_map/ppermute | solution.py:220
  52.2 5.9 %collective-permute-start.10 = (bf16[48,1792]{1,0:T(8,128)(2,1)S(1)}, bf16[48,1792]{1,0:T(8,128)(2,1)S(1)}, u32[]{:S(2)}, u32[]{:S(2)}) collective-permute-start(bf16[48,1792]{1,0:T(8,128)(2,1)S(1)} %get-tuple-element.53), channel_id=1, source_target_pairs={{0,4},{1,5},{2,6},{3,7},{4,0},{5,1},{6,2},{7,3},{8,12},{9,13},{10,... | collective-permute-start | bytes 516104 | tf_op jit(solution)/shard_map/ppermute | solution.py:220

commit v6 on v5

--- a/solution.py
+++ b/solution.py
@@ -9,23 +9,26 @@
 
 SHARDS = 4
 QUARTERS = 4
-GROUPS = ("own+near", "mid", "far")
-SPLIT = ("c mid", "c near",)
+GROUPS = ("own", "near", "mid", "far")
+SPLIT = ()
 ORDER = {
-    "z far": ("y own",),
-    "expert far": ("rc mid",),
-    "rz far": ("z mid",),
-    "c own": ("c near",),
-    "c mid": ("y mid",),
-    "rz mid": ("rc far", "c mid", "z near",),
-    "c far": ("z near",),
-    "ry own+near": ("y near",),
-    "y far": ("z near",),
-    "expert mid": ("c mid",),
-    "c near": ("y mid", "load all",),
+    "z mid": ("z near",),
+    "y far": ("z far",),
+    "y mid": ("z far",),
+    "expert far": ("z near",),
+    "rc far": ("load all",),
+    "expert near": ("c mid",),
+    "c mid": ("rc far",),
+    "rc near": ("z far",),
+    "ry near": ("c far", "y near",),
+    "rc mid": ("expert near",),
+    "c own": ("rc near", "z mid",),
+    "rz far": ("c near", "rc far", "ry far", "expert mid",),
+    "ry mid": ("load all",),
+    "rz near": ("rc own", "y far",),
+    "rc own": ("c mid",),
 }
 VMEM_BYTES = 16 * 1024 * 1024
-PACK_VMEM_BYTES = 48 * 1024 * 1024
 LOAD_VMEM_BYTES = 40 * 1024 * 1024
 
 
@@ -41,38 +44,18 @@
     return jnp.dot(left, right, preferred_element_type=jnp.float32)
 
 
-def pack_kernel(capacity, planes, tok_hbm, scale_hbm, route_ref, *rest):
-    outs = rest[:planes]
-    quarters_ref, tok_ref, scale_ref, tok_sem, scale_sem = rest[planes:]
-    tok_copy = pltpu.make_async_copy(tok_hbm, tok_ref, tok_sem)
-    scale_copy = pltpu.make_async_copy(scale_hbm, scale_ref, scale_sem)
-    tok_copy.start()
-    scale_copy.start()
+def spread(table_ref, pick, plane, rows, shape, axis):
+    place = lax.broadcasted_iota(jnp.int32, shape, axis) % rows
+    out = jnp.zeros(shape, jnp.int32)
+    for row in range(rows):
+        out = jnp.where(place == row, table_ref[pick, row] ^ plane, out)
+    return out
+
+
+def pack_kernel(capacity, planes, route_ref, tok_ref, scale_ref, *rest):
+    outs, quarters_ref = rest[:planes], rest[planes]
     rows, features = tok_ref.shape
-    width = features // QUARTERS
-    plane = lax.axis_index("expert") // SHARDS
-    offsets = (route_ref[...] ^ plane).astype(jnp.float32).astype(jnp.bfloat16)
-    columns = QUARTERS * rows
-    picks = offsets.shape[0]
-    copies = zero_one(
-        lax.broadcasted_iota(jnp.int32, (rows, columns), 1) % rows
-        == lax.broadcasted_iota(jnp.int32, (rows, columns), 0)
-    )
-    turned = exact_dot(offsets, copies)
-    numbers = lax.broadcasted_iota(jnp.int32, (planes, columns), 0).astype(jnp.float32)
-    named = jnp.zeros((planes, columns), jnp.float32)
-    for pick in range(picks):
-        named = named + jnp.where(turned[pick : pick + 1, :] == numbers, 1.0, 0.0)
-    first = lax.broadcasted_iota(jnp.int32, (columns, columns), 0)
-    second = lax.broadcasted_iota(jnp.int32, (columns, columns), 1)
-    before = zero_one((first // rows == second // rows) & (first < second))
-    position = exact_dot(named.astype(jnp.bfloat16), before)
-    slot_row = lax.broadcasted_iota(jnp.int32, (QUARTERS * capacity, columns), 0)
-    slot_col = lax.broadcasted_iota(jnp.int32, (QUARTERS * capacity, columns), 1)
-    same_quarter = slot_row // capacity == slot_col // rows
-    slot = (slot_row % capacity).astype(jnp.float32)
-    tok_copy.wait()
-    scale_copy.wait()
+    picks, width = route_ref.shape[0], features // QUARTERS
     for block in range(features // 128):
         quarter, at = divmod(block * 128, width)
         codes = tok_ref[:, block * 128 : (block + 1) * 128].astype(jnp.float32)
@@ -80,14 +63,33 @@
         quarters_ref[quarter * rows : (quarter + 1) * rows, at : at + 128] = (
             codes * factors
         ).astype(jnp.bfloat16)
-    values = quarters_ref[...]
-    for offset in range(planes):
-        pick_out = zero_one(
+    plane = lax.axis_index("expert") // SHARDS
+    columns = QUARTERS * rows
+    numbers = lax.broadcasted_iota(jnp.int32, (planes, columns), 0)
+    named = jnp.zeros((planes, columns), jnp.float32)
+    for pick in range(picks):
+        turned = spread(route_ref, pick, plane, rows, (1, columns), 1)
+        named = named + jnp.where(turned == numbers, 1.0, 0.0)
+    first = lax.broadcasted_iota(jnp.int32, (columns, columns), 0)
+    second = lax.broadcasted_iota(jnp.int32, (columns, columns), 1)
+    before = zero_one((first // rows == second // rows) & (first < second))
+    position = exact_dot(named.astype(jnp.bfloat16), before)
+    tall = QUARTERS * capacity
+    slot_row = lax.broadcasted_iota(jnp.int32, (tall, columns), 0)
+    slot_col = lax.broadcasted_iota(jnp.int32, (tall, columns), 1)
+    same_quarter = slot_row // capacity == slot_col // rows
+    slot = (slot_row % capacity).astype(jnp.float32)
+    pick_out = [
+        zero_one(
             same_quarter
             & (named[offset : offset + 1, :] > 0.5)
             & (position[offset : offset + 1, :] == slot)
         )
-        outs[offset][...] = exact_dot(pick_out, values).astype(jnp.bfloat16)
+        for offset in range(planes)
+    ]
+    moved = exact_dot(jnp.concatenate(pick_out, axis=0), quarters_ref[...])
+    for offset in range(planes):
+        outs[offset][...] = moved[offset * tall : (offset + 1) * tall, :].astype(jnp.bfloat16)
 
 
 def order_matrix(capacity, turned):
@@ -152,33 +154,20 @@
             out_ref[at : at + tall, :] = answer[member * tall : (member + 1) * tall, :]
 
 
-def mix_kernel(capacity, planes, route_ref, code_ref, *refs):
-    returned, out_ref = refs[:planes], refs[planes]
-    picks, rows = route_ref.shape
-    width = out_ref.shape[1] // QUARTERS
+def plan_kernel(capacity, planes, rows, route_ref, code_ref, unused, plan_ref):
+    picks = route_ref.shape[0]
     tall = QUARTERS * rows
     plane = lax.axis_index("expert") // SHARDS
-    copies = zero_one(
-        lax.broadcasted_iota(jnp.int32, (tall, rows), 0) % rows
-        == lax.broadcasted_iota(jnp.int32, (tall, rows), 1)
-    )
-
-    def turned(numbers):
-        numbers = numbers.astype(jnp.float32).astype(jnp.bfloat16)
-        return lax.dot_general(
-            copies, numbers, (((1,), (1,)), ((), ())), preferred_element_type=jnp.float32
-        )
-
-    offsets = turned(route_ref[...] ^ plane)
-    codes = code_ref[...]
-    weights = (turned(codes // 256) * 256.0 + turned(codes % 256)) / 65536.0
-    numbers = lax.broadcasted_iota(jnp.int32, (tall, planes), 1).astype(jnp.float32)
+    numbers = lax.broadcasted_iota(jnp.int32, (tall, planes), 1)
     named = jnp.zeros((tall, planes), jnp.float32)
-    factors = jnp.zeros((tall, planes), jnp.float32)
+    coarse = jnp.zeros((tall, planes), jnp.float32)
+    fine = jnp.zeros((tall, planes), jnp.float32)
     for pick in range(picks):
-        here = offsets[:, pick : pick + 1] == numbers
+        here = spread(route_ref, pick, plane, rows, (tall, 1), 0) == numbers
+        codes = spread(code_ref, pick, 0, rows, (tall, 1), 0)
         named = named + jnp.where(here, 1.0, 0.0)
-        factors = factors + jnp.where(here, weights[:, pick : pick + 1], 0.0)
+        coarse = coarse + jnp.where(here, (codes // 256).astype(jnp.float32) / 256.0, 0.0)
+        fine = fine + jnp.where(here, (codes % 256).astype(jnp.float32) / 65536.0, 0.0)
     first = lax.broadcasted_iota(jnp.int32, (tall, tall), 0)
     second = lax.broadcasted_iota(jnp.int32, (tall, tall), 1)
     before = zero_one((first // rows == second // rows) & (second < first))
@@ -187,15 +176,26 @@
     slot_col = lax.broadcasted_iota(jnp.int32, (tall, QUARTERS * capacity), 1)
     same_quarter = slot_row // rows == slot_col // capacity
     slot = (slot_col % capacity).astype(jnp.float32)
-    total = jnp.zeros((tall, width), jnp.float32)
     for offset in range(planes):
-        take = zero_one(
-            same_quarter
-            & (named[:, offset : offset + 1] > 0.5)
-            & (position[:, offset : offset + 1] == slot)
-        )
-        total = total + factors[:, offset : offset + 1] * exact_dot(take, returned[offset][...])
-    total = total.astype(jnp.bfloat16)
+        column = slice(offset, offset + 1)
+        take = same_quarter & (named[:, column] > 0.5) & (position[:, column] == slot)
+        for half, factor in enumerate((coarse, fine)):
+            plan_ref[offset, half * tall : (half + 1) * tall, :] = jnp.where(
+                take, factor[:, column], 0.0
+            ).astype(jnp.bfloat16)
+
+
+def mix_kernel(planes, plan_ref, *refs):
+    returned, out_ref = refs[:planes], refs[planes]
+    rows, features = out_ref.shape
+    width, tall = features // QUARTERS, QUARTERS * rows
+    total = jnp.zeros((2 * tall, width), jnp.float32)
+    for at in range(0, planes, 4):
+        some = range(at, min(at + 4, planes))
+        plan = jnp.concatenate([plan_ref[offset] for offset in some], axis=1)
+        answers = jnp.concatenate([returned[offset][...] for offset in some], axis=0)
+        total = total + exact_dot(plan, answers)
+    total = (total[:tall] + total[tall:]).astype(jnp.bfloat16)
     for quarter in range(QUARTERS):
         out_ref[:, quarter * width : (quarter + 1) * width] = total[
             quarter * rows : (quarter + 1) * rows, :
@@ -213,27 +213,28 @@
     vmem = pl.BlockSpec(memory_space=pltpu.VMEM)
     hbm = pl.BlockSpec(memory_space=pl.ANY)
     params = pltpu.CompilerParams(vmem_limit_bytes=VMEM_BYTES)
-    pack_params = pltpu.CompilerParams(vmem_limit_bytes=PACK_VMEM_BYTES)
     load_params = pltpu.CompilerParams(vmem_limit_bytes=LOAD_VMEM_BYTES)
 
     def partner(array, distance):
         return lax.ppermute(array, "expert", [(i, i ^ distance) for i in range(devices)])
 
     block = jax.ShapeDtypeStruct((tall, width), jnp.bfloat16)
+    smem = pl.BlockSpec(memory_space=pltpu.SMEM)
     packed = pl.pallas_call(
         functools.partial(pack_kernel, capacity, planes),
         out_shape=[block] * planes,
-        in_specs=[hbm] * 2 + [vmem],
+        in_specs=[smem, vmem, vmem],
         out_specs=[vmem] * planes,
-        scratch_shapes=[
-            pltpu.VMEM((QUARTERS * tok_rows, width), jnp.bfloat16),
-            pltpu.VMEM(tokens.shape, tokens.dtype),
-            pltpu.VMEM(scales.shape, scales.dtype),
-            pltpu.SemaphoreType.DMA,
-            pltpu.SemaphoreType.DMA,
-        ],
-        compiler_params=pack_params,
-    )(tokens, scales, routes.T)
+        scratch_shapes=[pltpu.VMEM((QUARTERS * tok_rows, width), jnp.bfloat16)],
+        compiler_params=params,
+    )(routes.T, tokens, scales)
+    plan = pl.pallas_call(
+        functools.partial(plan_kernel, capacity, planes, tok_rows),
+        out_shape=jax.ShapeDtypeStruct((planes, 2 * QUARTERS * tok_rows, tall), jnp.bfloat16),
+        in_specs=[smem, smem, hbm],
+        out_specs=vmem,
+        compiler_params=params,
+    )(routes.T, gate_codes.T, packed[0])
 
     def expert(offsets, held, weights):
         rows = offsets * SHARDS * capacity
@@ -346,12 +347,12 @@
     returned = [returned[at] for at in range(planes)]
 
     return pl.pallas_call(
-        functools.partial(mix_kernel, capacity, planes),
+        functools.partial(mix_kernel, planes),
         out_shape=jax.ShapeDtypeStruct((tok_rows, features), jnp.bfloat16),
-        in_specs=[vmem] * (planes + 2),
+        in_specs=[vmem] * (planes + 1),
         out_specs=vmem,
         compiler_params=params,
-    )(routes.T, gate_codes.T, *returned)
+    )(plan, *returned)
 
 
 def solution(mesh):

time: 59.8 us -> 62.1 us (1.038)
  starting transfers between devices: 27.4 us -> 20.8 us
  waiting for transfers between devices: 14.4 us -> 20.6 us
  Pallas kernels: 14.2 us -> 16.3 us
    ppermute x22, starting transfers between devices: 27.4 us -> 20.8 us  [partner(): lax.ppermute(array, 'expert', [(i, i ^ distance) for i in range(devices)])]
    ppermute x22, waiting for transfers between devices: 14.4 us -> 20.6 us  [partner(): lax.ppermute(array, 'expert', [(i, i ^ distance) for i in range(devices)])]
    pallas_call x3 -> x4, Pallas kernels: 7.39 us -> 9.16 us  [expert(): pl.pallas_call(functools.partial(expert_kernel, capacity, offsets), out_s...]
    unnamed x16 -> x12, local copies, waits for them, and re-layouts: 2.4 us -> 3.04 us
    pallas_call x1 -> x2, Pallas kernels: 1.48 us -> 1.87 us  [the longest x1 1.01 us: shards(): pl.pallas_call(functools.partial(mix_kernel, planes), out_shape=jax.Shape...]
  transfers between devices with their start and end apart: 22 -> 22, of which waited for: 9 -> 12; matrix products, arithmetic and copies ran while one was open for 2% -> 1% of each run, Pallas kernels for 19% -> 23%
where the time goes in v6:
time: 62.1 us; the launch traced here: 61.9 us
  starting transfers between devices  20.8 us (33%)
  waiting for transfers between devices  20.6 us (33%)
  Pallas kernels  16.3 us (26%)
  local copies, waits for them, and re-layouts  3.09 us (5%)
  other arithmetic  0.72 us (1%)
    ppermute x22, starting transfers between devices, partner(): lax.ppermute(array, 'expert', [(i, i ^ distance) for i in range(devices)])  20.8 us
    ppermute x22, waiting for transfers between devices, partner(): lax.ppermute(array, 'expert', [(i, i ^ distance) for i in range(devices)])  20.6 us
    pallas_call x4, Pallas kernels, expert(): pl.pallas_call(functools.partial(expert_kernel, capacity, offsets), out_s...  9.16 us
    pallas_call x1, Pallas kernels, load(): pl.pallas_call(load_kernel, out_shape=[jax.ShapeDtypeStruct(w.shape, w.dt...  4.23 us
    unnamed x12, local copies, waits for them, and re-layouts  3.04 us
  transfers between devices with their start and end apart: 22, of which 12 were waited for; matrix products, arithmetic and copies ran while one was open for 1% of the time, Pallas kernels for 23%

profile of v6, /device:TPU:0, one launch (start us, length us, event | category | flops | bytes accessed | tf_op | source)
XLA Modules:
  0.0 61.9 jit_solution(8670183240033273994)
XLA Ops:
  0.0 0.0 copy-start
  0.0 0.9 %copy-done = bf16[16,7168]{1,0:T(8,128)(2,1)S(1)} copy-done((bf16[16,7168]{1,0:T(8,128)(2,1)S(1)}, bf16[16,7168]{1,0:T(8,128)(2,1)}, u32[]{:S(2)}) %copy-start) | copy-done | bytes 229400
  0.9 0.0 copy-start.1
  0.9 0.7 %copy-done.1 = f32[16,56]{1,0:T(8,128)S(1)} copy-done((f32[16,56]{1,0:T(8,128)S(1)}, f32[16,56]{1,0:T(8,128)}, u32[]{:S(2)}) %copy-start.1) | copy-done | bytes 3608
  1.6 0.0 copy-start.2
  1.6 0.7 %copy-done.2 = s32[16,2]{0,1:T(2,128)S(1)} copy-done((s32[16,2]{0,1:T(2,128)S(1)}, s32[16,2]{0,1:T(2,128)}, u32[]{:S(2)}) %copy-start.2) | copy-done | bytes 152
  2.3 1.1 %shard_map.73 = (bf16[48,1792]{1,0:T(8,128)(2,1)S(1)}, bf16[48,1792]{1,0:T(8,128)(2,1)S(1)}, bf16[48,1792]{1,0:T(8,128)(2,1)S(1)}, bf16[48,1792]{1,0:T(8,128)(2,1)S(1)}) custom-call(s32[2,16]{1,0:T(2,128)S(1)} %bitcast.2, bf16[16,7168]{1,0:T(8,128)(2,1)S(1)} %copy-done, f32[16,56]{1,0:T(8,128)S(1)} %copy-done.1), custom_call_target="tpu_custom_call" | custom-call | tf_op jit(solution)/shard_map/pallas_call | solution.py:223
  3.4 5.1 %collective-permute-start.4 = (bf16[48,1792]{1,0:T(8,128)(2,1)S(1)}, bf16[48,1792]{1,0:T(8,128)(2,1)S(1)}, u32[]{:S(2)}, u32[]{:S(2)}) collective-permute-start(bf16[48,1792]{1,0:T(8,128)(2,1)S(1)} %get-tuple-element.39), channel_id=1, source_target_pairs={{0,12},{1,13},{2,14},{3,15},{4,8},{5,9},{6,10},{7,11},{8,4},{9,5},... | collective-permute-start | bytes 516104 | tf_op jit(solution)/shard_map/ppermute | solution.py:219
  8.5 0.0 collective-permute-start.1
  8.5 1.5 %collective-permute-start = (bf16[48,1792]{1,0:T(8,128)(2,1)S(1)}, bf16[48,1792]{1,0:T(8,128)(2,1)S(1)}, u32[]{:S(2)}, u32[]{:S(2)}) collective-permute-start(bf16[48,1792]{1,0:T(8,128)(2,1)S(1)} %get-tuple-element.35.unused), channel_id=1, source_target_pairs={{0,2},{1,3},{2,0},{3,1},{4,6},{5,7},{6,4},{7,5},{8,10},{9,11},{10,... | collective-permute-start | bytes 516104 | tf_op jit(solution)/shard_map/ppermute | solution.py:219
  10.0 0.0 copy-start.3
  10.0 0.7 %copy-done.3 = s32[16,2]{0,1:T(2,128)S(1)} copy-done((s32[16,2]{0,1:T(2,128)S(1)}, s32[16,2]{0,1:T(2,128)}, u32[]{:S(2)}) %copy-start.3) | copy-done | bytes 152
  10.7 0.9 %shard_map.74.plan_ref = bf16[4,128,48]{2,1,0:T(8,128)(2,1)S(1)} custom-call(s32[2,16]{1,0:T(2,128)S(1)} %bitcast.3, s32[2,16]{1,0:T(2,128)S(1)} %bitcast.4, bf16[48,1792]{1,0:T(8,128)(2,1)S(1)} %get-tuple-element.35.unused), custom_call_target="tpu_custom_call" | custom-call | tf_op jit(solution)/shard_map/pallas_call | solution.py:231
  11.6 4.2 %shard_map.75 = (bf16[1,7168,256]{2,1,0:T(8,128)(2,1)S(1)}, bf16[1,7168,256]{2,1,0:T(8,128)(2,1)S(1)}, bf16[1,256,7168]{2,1,0:T(8,128)(2,1)S(1)}) custom-call(bf16[1,7168,256]{2,1,0:T(8,128)(2,1)} %gate_hbm.1, bf16[1,7168,256]{2,1,0:T(8,128)(2,1)} %up_hbm.1, bf16[1,256,7168]{2,1,0:T(8,128)(2,1)} %down_hbm.1, bf16[48,1792]{1,0:T(8,128)(2,1)S(1)} %get-tuple-element.35.unused), custom_call_target="tpu_custom_call" | custom-call | tf_op jit(solution)/shard_map/pallas_call | solution.py:257
  15.8 0.0 collective-permute-done.4
  15.8 0.6 collective-permute-start.6
  16.4 0.2 collective-permute-done.1
  16.6 2.2 %collective-permute-start.3 = (bf16[48,1792]{1,0:T(8,128)(2,1)S(1)}, bf16[48,1792]{1,0:T(8,128)(2,1)S(1)}, u32[]{:S(2)}, u32[]{:S(2)}) collective-permute-start(bf16[48,1792]{1,0:T(8,128)(2,1)S(1)} %get-tuple-element.38), channel_id=1, source_target_pairs={{0,8},{1,9},{2,10},{3,11},{4,12},{5,13},{6,14},{7,15},{8,0},{9,1},... | collective-permute-start | bytes 516104 | tf_op jit(solution)/shard_map/ppermute | solution.py:219
  18.8 0.5 collective-permute-start.2
  19.3 3.9 %collective-permute-done.6 = bf16[48,1792]{1,0:T(8,128)(2,1)S(1)} collective-permute-done((bf16[48,1792]{1,0:T(8,128)(2,1)S(1)}, bf16[48,1792]{1,0:T(8,128)(2,1)S(1)}, u32[]{:S(2)}, u32[]{:S(2)}) %collective-permute-start.6) | collective-permute-done | bytes 172064 | tf_op jit(solution)/shard_map/ppermute | solution.py:219
  23.2 0.1 collective-permute-start.7
  23.3 4.2 %collective-permute-done.3 = bf16[48,1792]{1,0:T(8,128)(2,1)S(1)} collective-permute-done((bf16[48,1792]{1,0:T(8,128)(2,1)S(1)}, bf16[48,1792]{1,0:T(8,128)(2,1)S(1)}, u32[]{:S(2)}, u32[]{:S(2)}) %collective-permute-start.3) | collective-permute-done | bytes 172064 | tf_op jit(solution)/shard_map/ppermute | solution.py:219
  27.5 1.5 %collective-permute-start.5 = (bf16[48,1792]{1,0:T(8,128)(2,1)S(1)}, bf16[48,1792]{1,0:T(8,128)(2,1)S(1)}, u32[]{:S(2)}, u32[]{:S(2)}) collective-permute-start(bf16[48,1792]{1,0:T(8,128)(2,1)S(1)} %collective-permute-done.3), channel_id=1, source_target_pairs={{0,2},{1,3},{2,0},{3,1},{4,6},{5,7},{6,4},{7,5},{8,10},{9,11},{10,... | collective-permute-start | bytes 516104 | tf_op jit(solution)/shard_map/ppermute | solution.py:219
  29.1 0.0 collective-permute-done.2
  29.1 0.1 collective-permute-start.10
  29.2 0.0 collective-permute-done.7.refs_1_
  29.2 2.3 %shard_map.76 = (bf16[96,1792]{1,0:T(8,128)(2,1)S(1)}, bf16[96,1792]{1,0:T(8,128)(2,1)S(1)}) custom-call(bf16[96,1792]{1,0:T(8,128)(2,1)S(1)} %constant_dynamic-update-slice_fusion.6.refs_0_, bf16[96,1792]{1,0:T(8,128)(2,1)S(1)} %collective-permute-done.7.refs_1_, bf16[1,7168,256]{2,1,0:T(8,128)(2,1)S(1)} %get-tuple-element.43.refs_2_, ...), custom_call_target="tpu_custom_call" | custom-call | flops 528482304 | tf_op jit(solution)/shard_map/pallas_call | solution.py:242
  31.5 0.6 collective-permute-start.8
  32.0 1.7 %collective-permute-done.5 = bf16[48,1792]{1,0:T(8,128)(2,1)S(1)} collective-permute-done((bf16[48,1792]{1,0:T(8,128)(2,1)S(1)}, bf16[48,1792]{1,0:T(8,128)(2,1)S(1)}, u32[]{:S(2)}, u32[]{:S(2)}) %collective-permute-start.5) | collective-permute-done | bytes 172064 | tf_op jit(solution)/shard_map/ppermute | solution.py:219
  33.8 0.0 collective-permute-done.8
  33.8 0.1 collective-permute-start.9
  34.0 1.6 %collective-permute-start.20 = (bf16[48,1792]{1,0:T(8,128)(2,1)S(1)}, bf16[48,1792]{1,0:T(8,128)(2,1)S(1)}, u32[]{:S(2)}, u32[]{:S(2)}) collective-permute-start(bf16[48,1792]{1,0:T(8,128)(2,1)S(1)} %fusion), channel_id=1, source_target_pairs={{0,2},{1,3},{2,0},{3,1},{4,6},{5,7},{6,4},{7,5},{8,10},{9,11},{10,... | collective-permute-start | bytes 516104 | tf_op jit(solution)/shard_map/ppermute | solution.py:219
  35.6 0.0 collective-permute-done
  35.6 0.0 collective-permute-done.9.refs_1_
  35.6 2.3 %shard_map.79 = (bf16[96,1792]{1,0:T(8,128)(2,1)S(1)}, bf16[96,1792]{1,0:T(8,128)(2,1)S(1)}) custom-call(bf16[96,1792]{1,0:T(8,128)(2,1)S(1)} %constant_dynamic-update-slice_fusion.4.refs_0_, bf16[96,1792]{1,0:T(8,128)(2,1)S(1)} %collective-permute-done.9.refs_1_, bf16[1,7168,256]{2,1,0:T(8,128)(2,1)S(1)} %get-tuple-element.43.refs_2_, ...), custom_call_target="tpu_custom_call" | custom-call | flops 528482304 | tf_op jit(solution)/shard_map/pallas_call | solution.py:242
  37.9 0.0 collective-permute-done.10.refs_1_
  37.9 2.3 %shard_map.77 = (bf16[96,1792]{1,0:T(8,128)(2,1)S(1)}, bf16[96,1792]{1,0:T(8,128)(2,1)S(1)}) custom-call(bf16[96,1792]{1,0:T(8,128)(2,1)S(1)} %constant_dynamic-update-slice_fusion.2.refs_0_, bf16[96,1792]{1,0:T(8,128)(2,1)S(1)} %collective-permute-done.10.refs_1_, bf16[1,7168,256]{2,1,0:T(8,128)(2,1)S(1)} %get-tuple-element.43.refs_2_, ...), custom_call_target="tpu_custom_call" | custom-call | flops 528482304 | tf_op jit(solution)/shard_map/pallas_call | solution.py:242
  40.2 0.3 collective-permute-start.17
  40.5 0.3 collective-permute-done.20
  40.8 0.1 fusion.2
  40.9 0.1 collective-permute-start.21
  41.0 0.1 collective-permute-start.11
  41.1 0.8 %collective-permute-done.17 = bf16[96,1792]{1,0:T(8,128)(2,1)S(1)} collective-permute-done((bf16[96,1792]{1,0:T(8,128)(2,1)S(1)}, bf16[96,1792]{1,0:T(8,128)(2,1)S(1)}, u32[]{:S(2)}, u32[]{:S(2)}) %collective-permute-start.17) | collective-permute-done | bytes 344096 | tf_op jit(solution)/shard_map/ppermute | solution.py:219
  42.0 1.5 %collective-permute-start.18 = (bf16[48,1792]{1,0:T(8,128)(2,1)S(1)}, bf16[48,1792]{1,0:T(8,128)(2,1)S(1)}, u32[]{:S(2)}, u32[]{:S(2)}) collective-permute-start(bf16[48,1792]{1,0:T(8,128)(2,1)S(1)} %fusion.3), channel_id=1, source_target_pairs={{0,2},{1,3},{2,0},{3,1},{4,6},{5,7},{6,4},{7,5},{8,10},{9,11},{10,... | collective-permute-start | bytes 516104 | tf_op jit(solution)/shard_map/ppermute | solution.py:219
  43.5 0.0 collective-permute-done.11
  43.5 0.0 collective-permute-start.12
  43.6 0.9 %collective-permute-start.15 = (bf16[48,1792]{1,0:T(8,128)(2,1)S(1)}, bf16[48,1792]{1,0:T(8,128)(2,1)S(1)}, u32[]{:S(2)}, u32[]{:S(2)}) collective-permute-start(bf16[48,1792]{1,0:T(8,128)(2,1)S(1)} %fusion.6), channel_id=1, source_target_pairs={{0,2},{1,3},{2,0},{3,1},{4,6},{5,7},{6,4},{7,5},{8,10},{9,11},{10,... | collective-permute-start | bytes 516104 | tf_op jit(solution)/shard_map/ppermute | solution.py:219
  44.6 0.6 collective-permute-done.12.refs_1_
  45.2 2.3 %shard_map.78 = (bf16[96,1792]{1,0:T(8,128)(2,1)S(1)}, bf16[96,1792]{1,0:T(8,128)(2,1)S(1)}) custom-call(bf16[96,1792]{1,0:T(8,128)(2,1)S(1)} %constant_dynamic-update-slice_fusion.refs_0_, bf16[96,1792]{1,0:T(8,128)(2,1)S(1)} %collective-permute-done.12.refs_1_, bf16[1,7168,256]{2,1,0:T(8,128)(2,1)S(1)} %get-tuple-element.43.refs_2_, ...), custom_call_target="tpu_custom_call" | custom-call | flops 528482304 | tf_op jit(solution)/shard_map/pallas_call | solution.py:242
  47.5 0.2 collective-permute-start.13
  47.7 1.6 %collective-permute-done.18 = bf16[48,1792]{1,0:T(8,128)(2,1)S(1)} collective-permute-done((bf16[48,1792]{1,0:T(8,128)(2,1)S(1)}, bf16[48,1792]{1,0:T(8,128)(2,1)S(1)}, u32[]{:S(2)}, u32[]{:S(2)}) %collective-permute-start.18) | collective-permute-done | bytes 172064 | tf_op jit(solution)/shard_map/ppermute | solution.py:219
  49.3 0.1 fusion.5
  49.3 0.1 collective-permute-start.19
  49.5 0.0 collective-permute-done.13
  49.6 1.5 %collective-permute-start.14 = (bf16[48,1792]{1,0:T(8,128)(2,1)S(1)}, bf16[48,1792]{1,0:T(8,128)(2,1)S(1)}, u32[]{:S(2)}, u32[]{:S(2)}) collective-permute-start(bf16[48,1792]{1,0:T(8,128)(2,1)S(1)} %fusion.9), channel_id=1, source_target_pairs={{0,2},{1,3},{2,0},{3,1},{4,6},{5,7},{6,4},{7,5},{8,10},{9,11},{10,... | collective-permute-start | bytes 516104 | tf_op jit(solution)/shard_map/ppermute | solution.py:219
  51.1 1.3 %collective-permute-done.15 = bf16[48,1792]{1,0:T(8,128)(2,1)S(1)} collective-permute-done((bf16[48,1792]{1,0:T(8,128)(2,1)S(1)}, bf16[48,1792]{1,0:T(8,128)(2,1)S(1)}, u32[]{:S(2)}, u32[]{:S(2)}) %collective-permute-start.15) | collective-permute-done | bytes 172064 | tf_op jit(solution)/shard_map/ppermute | solution.py:219
  52.4 2.4 %collective-permute-start.16 = (bf16[48,1792]{1,0:T(8,128)(2,1)S(1)}, bf16[48,1792]{1,0:T(8,128)(2,1)S(1)}, u32[]{:S(2)}, u32[]{:S(2)}) collective-permute-start(bf16[48,1792]{1,0:T(8,128)(2,1)S(1)} %fusion.8), channel_id=1, source_target_pairs={{0,4},{1,5},{2,6},{3,7},{4,0},{5,1},{6,2},{7,3},{8,12},{9,13},{10,... | collective-permute-start | bytes 516104 | tf_op jit(solution)/shard_map/ppermute | solution.py:219
  54.8 1.1 %collective-permute-done.14 = bf16[48,1792]{1,0:T(8,128)(2,1)S(1)} collective-permute-done((bf16[48,1792]{1,0:T(8,128)(2,1)S(1)}, bf16[48,1792]{1,0:T(8,128)(2,1)S(1)}, u32[]{:S(2)}, u32[]{:S(2)}) %collective-permute-start.14) | collective-permute-done | bytes 172064 | tf_op jit(solution)/shard_map/ppermute | solution.py:219
  55.9 0.1 fusion.11.refs_0_
  56.0 0.0 collective-permute-done.21.refs_3_
  56.0 3.1 %collective-permute-done.19.refs_2_ = bf16[48,1792]{1,0:T(8,128)(2,1)S(1)} collective-permute-done((bf16[48,1792]{1,0:T(8,128)(2,1)S(1)}, bf16[48,1792]{1,0:T(8,128)(2,1)S(1)}, u32[]{:S(2)}, u32[]{:S(2)}) %collective-permute-start.19) | collective-permute-done | bytes 172064 | tf_op jit(solution)/shard_map/ppermute | solution.py:219
  59.1 1.7 %collective-permute-done.16.refs_1_ = bf16[48,1792]{1,0:T(8,128)(2,1)S(1)} collective-permute-done((bf16[48,1792]{1,0:T(8,128)(2,1)S(1)}, bf16[48,1792]{1,0:T(8,128)(2,1)S(1)}, u32[]{:S(2)}, u32[]{:S(2)}) %collective-permute-start.16) | collective-permute-done | bytes 172064 | tf_op jit(solution)/shard_map/ppermute | solution.py:219
  60.9 1.0 %shard_map.80 = bf16[16,7168]{1,0:T(8,128)(2,1)} custom-call(bf16[4,128,48]{2,1,0:T(8,128)(2,1)S(1)} %shard_map.74.plan_ref, bf16[48,1792]{1,0:T(8,128)(2,1)S(1)} %fusion.11.refs_0_, bf16[48,1792]{1,0:T(8,128)(2,1)S(1)} %collective-permute-done.16.refs_1_, bf16[48,1792]{1,0:T(8,128)(2,1)S(1)} %collective-permute-done.19.refs_2_, ...), custom_call_target="tpu_custom_call" | custom-call | tf_op jit(solution)/shard_map/pallas_call | solution.py:349
  (21 shorter events, 0.7 us)
Async XLA Ops:
  0.0 0.9 %copy-start = (bf16[16,7168]{1,0:T(8,128)(2,1)S(1)}, bf16[16,7168]{1,0:T(8,128)(2,1)}, u32[]{:S(2)}) copy-start(bf16[16,7168]{1,0:T(8,128)(2,1)} %tok_ref.1) | copy-start | bytes 688132
  0.9 0.7 %copy-start.1 = (f32[16,56]{1,0:T(8,128)S(1)}, f32[16,56]{1,0:T(8,128)}, u32[]{:S(2)}) copy-start(f32[16,56]{1,0:T(8,128)} %scale_ref.1) | copy-start | bytes 10756
  1.6 0.7 %copy-start.2 = (s32[16,2]{0,1:T(2,128)S(1)}, s32[16,2]{0,1:T(2,128)}, u32[]{:S(2)}) copy-start(s32[16,2]{0,1:T(2,128)} %param.9) | copy-start | bytes 388
  3.4 12.5 %collective-permute-start.4 = (bf16[48,1792]{1,0:T(8,128)(2,1)S(1)}, bf16[48,1792]{1,0:T(8,128)(2,1)S(1)}, u32[]{:S(2)}, u32[]{:S(2)}) collective-permute-start(bf16[48,1792]{1,0:T(8,128)(2,1)S(1)} %get-tuple-element.39), channel_id=1, source_target_pairs={{0,12},{1,13},{2,14},{3,15},{4,8},{5,9},{6,10},{7,11},{8,4},{9,5},... | collective-permute-start | bytes 516104 | tf_op jit(solution)/shard_map/ppermute | solution.py:219
  8.5 8.2 %collective-permute-start.1 = (bf16[48,1792]{1,0:T(8,128)(2,1)S(1)}, bf16[48,1792]{1,0:T(8,128)(2,1)S(1)}, u32[]{:S(2)}, u32[]{:S(2)}) collective-permute-start(bf16[48,1792]{1,0:T(8,128)(2,1)S(1)} %get-tuple-element.36), channel_id=1, source_target_pairs={{0,4},{1,5},{2,6},{3,7},{4,0},{5,1},{6,2},{7,3},{8,12},{9,13},{10,... | collective-permute-start | bytes 516104 | tf_op jit(solution)/shard_map/ppermute | solution.py:219
  8.5 27.1 %collective-permute-start = (bf16[48,1792]{1,0:T(8,128)(2,1)S(1)}, bf16[48,1792]{1,0:T(8,128)(2,1)S(1)}, u32[]{:S(2)}, u32[]{:S(2)}) collective-permute-start(bf16[48,1792]{1,0:T(8,128)(2,1)S(1)} %get-tuple-element.35.unused), channel_id=1, source_target_pairs={{0,2},{1,3},{2,0},{3,1},{4,6},{5,7},{6,4},{7,5},{8,10},{9,11},{10,... | collective-permute-start | bytes 516104 | tf_op jit(solution)/shard_map/ppermute | solution.py:219
  10.0 0.7 %copy-start.3 = (s32[16,2]{0,1:T(2,128)S(1)}, s32[16,2]{0,1:T(2,128)}, u32[]{:S(2)}) copy-start(s32[16,2]{0,1:T(2,128)} %param.10) | copy-start | bytes 388
  15.8 7.4 %collective-permute-start.6 = (bf16[48,1792]{1,0:T(8,128)(2,1)S(1)}, bf16[48,1792]{1,0:T(8,128)(2,1)S(1)}, u32[]{:S(2)}, u32[]{:S(2)}) collective-permute-start(bf16[48,1792]{1,0:T(8,128)(2,1)S(1)} %collective-permute-done.4), channel_id=1, source_target_pairs={{0,2},{1,3},{2,0},{3,1},{4,6},{5,7},{6,4},{7,5},{8,10},{9,11},{10,... | collective-permute-start | bytes 516104 | tf_op jit(solution)/shard_map/ppermute | solution.py:219
  16.6 10.9 %collective-permute-start.3 = (bf16[48,1792]{1,0:T(8,128)(2,1)S(1)}, bf16[48,1792]{1,0:T(8,128)(2,1)S(1)}, u32[]{:S(2)}, u32[]{:S(2)}) collective-permute-start(bf16[48,1792]{1,0:T(8,128)(2,1)S(1)} %get-tuple-element.38), channel_id=1, source_target_pairs={{0,8},{1,9},{2,10},{3,11},{4,12},{5,13},{6,14},{7,15},{8,0},{9,1},... | collective-permute-start | bytes 516104 | tf_op jit(solution)/shard_map/ppermute | solution.py:219
  18.8 10.3 %collective-permute-start.2 = (bf16[48,1792]{1,0:T(8,128)(2,1)S(1)}, bf16[48,1792]{1,0:T(8,128)(2,1)S(1)}, u32[]{:S(2)}, u32[]{:S(2)}) collective-permute-start(bf16[48,1792]{1,0:T(8,128)(2,1)S(1)} %collective-permute-done.1), channel_id=1, source_target_pairs={{0,2},{1,3},{2,0},{3,1},{4,6},{5,7},{6,4},{7,5},{8,10},{9,11},{10,... | collective-permute-start | bytes 516104 | tf_op jit(solution)/shard_map/ppermute | solution.py:219
  23.2 5.9 %collective-permute-start.7 = (bf16[96,1792]{1,0:T(8,128)(2,1)S(1)}, bf16[96,1792]{1,0:T(8,128)(2,1)S(1)}, u32[]{:S(2)}, u32[]{:S(2)}) collective-permute-start(bf16[96,1792]{1,0:T(8,128)(2,1)S(1)} %constant_dynamic-update-slice_fusion.6.refs_0_), channel_id=1, source_target_pairs={{0,1},{1,0},{2,3},{3,2},{4,5},{5,4},{6,7},{7,6},{8,9},{9,8},{10,11... | collective-permute-start | bytes 1032200 | tf_op jit(solution)/shard_map/ppermute | solution.py:219
  27.5 6.2 %collective-permute-start.5 = (bf16[48,1792]{1,0:T(8,128)(2,1)S(1)}, bf16[48,1792]{1,0:T(8,128)(2,1)S(1)}, u32[]{:S(2)}, u32[]{:S(2)}) collective-permute-start(bf16[48,1792]{1,0:T(8,128)(2,1)S(1)} %collective-permute-done.3), channel_id=1, source_target_pairs={{0,2},{1,3},{2,0},{3,1},{4,6},{5,7},{6,4},{7,5},{8,10},{9,11},{10,... | collective-permute-start | bytes 516104 | tf_op jit(solution)/shard_map/ppermute | solution.py:219
  29.1 8.8 %collective-permute-start.10 = (bf16[96,1792]{1,0:T(8,128)(2,1)S(1)}, bf16[96,1792]{1,0:T(8,128)(2,1)S(1)}, u32[]{:S(2)}, u32[]{:S(2)}) collective-permute-start(bf16[96,1792]{1,0:T(8,128)(2,1)S(1)} %constant_dynamic-update-slice_fusion.2.refs_0_), channel_id=1, source_target_pairs={{0,1},{1,0},{2,3},{3,2},{4,5},{5,4},{6,7},{7,6},{8,9},{9,8},{10,11... | collective-permute-start | bytes 1032200 | tf_op jit(solution)/shard_map/ppermute | solution.py:219
  31.5 2.3 %collective-permute-start.8 = (bf16[96,1792]{1,0:T(8,128)(2,1)S(1)}, bf16[96,1792]{1,0:T(8,128)(2,1)S(1)}, u32[]{:S(2)}, u32[]{:S(2)}) collective-permute-start(bf16[96,1792]{1,0:T(8,128)(2,1)S(1)} %get-tuple-element.47), channel_id=1, source_target_pairs={{0,1},{1,0},{2,3},{3,2},{4,5},{5,4},{6,7},{7,6},{8,9},{9,8},{10,11... | collective-permute-start | bytes 1032200 | tf_op jit(solution)/shard_map/ppermute | solution.py:219
  33.8 1.8 %collective-permute-start.9 = (bf16[96,1792]{1,0:T(8,128)(2,1)S(1)}, bf16[96,1792]{1,0:T(8,128)(2,1)S(1)}, u32[]{:S(2)}, u32[]{:S(2)}) collective-permute-start(bf16[96,1792]{1,0:T(8,128)(2,1)S(1)} %constant_dynamic-update-slice_fusion.4.refs_0_), channel_id=1, source_target_pairs={{0,1},{1,0},{2,3},{3,2},{4,5},{5,4},{6,7},{7,6},{8,9},{9,8},{10,11... | collective-permute-start | bytes 1032200 | tf_op jit(solution)/shard_map/ppermute | solution.py:219
  34.0 6.8 %collective-permute-start.20 = (bf16[48,1792]{1,0:T(8,128)(2,1)S(1)}, bf16[48,1792]{1,0:T(8,128)(2,1)S(1)}, u32[]{:S(2)}, u32[]{:S(2)}) collective-permute-start(bf16[48,1792]{1,0:T(8,128)(2,1)S(1)} %fusion), channel_id=1, source_target_pairs={{0,2},{1,3},{2,0},{3,1},{4,6},{5,7},{6,4},{7,5},{8,10},{9,11},{10,... | collective-permute-start | bytes 516104 | tf_op jit(solution)/shard_map/ppermute | solution.py:219
  40.2 1.7 %collective-permute-start.17 = (bf16[96,1792]{1,0:T(8,128)(2,1)S(1)}, bf16[96,1792]{1,0:T(8,128)(2,1)S(1)}, u32[]{:S(2)}, u32[]{:S(2)}) collective-permute-start(bf16[96,1792]{1,0:T(8,128)(2,1)S(1)} %get-tuple-element.61), channel_id=1, source_target_pairs={{0,1},{1,0},{2,3},{3,2},{4,5},{5,4},{6,7},{7,6},{8,9},{9,8},{10,11... | collective-permute-start | bytes 1032200 | tf_op jit(solution)/shard_map/ppermute | solution.py:219
  40.9 15.1 %collective-permute-start.21 = (bf16[48,1792]{1,0:T(8,128)(2,1)S(1)}, bf16[48,1792]{1,0:T(8,128)(2,1)S(1)}, u32[]{:S(2)}, u32[]{:S(2)}) collective-permute-start(bf16[48,1792]{1,0:T(8,128)(2,1)S(1)} %fusion.2), channel_id=1, source_target_pairs={{0,12},{1,13},{2,14},{3,15},{4,8},{5,9},{6,10},{7,11},{8,4},{9,5},... | collective-permute-start | bytes 516104 | tf_op jit(solution)/shard_map/ppermute | solution.py:219
  41.0 2.5 %collective-permute-start.11 = (bf16[96,1792]{1,0:T(8,128)(2,1)S(1)}, bf16[96,1792]{1,0:T(8,128)(2,1)S(1)}, u32[]{:S(2)}, u32[]{:S(2)}) collective-permute-start(bf16[96,1792]{1,0:T(8,128)(2,1)S(1)} %get-tuple-element.51), channel_id=1, source_target_pairs={{0,1},{1,0},{2,3},{3,2},{4,5},{5,4},{6,7},{7,6},{8,9},{9,8},{10,11... | collective-permute-start | bytes 1032200 | tf_op jit(solution)/shard_map/ppermute | solution.py:219
  42.0 7.3 %collective-permute-start.18 = (bf16[48,1792]{1,0:T(8,128)(2,1)S(1)}, bf16[48,1792]{1,0:T(8,128)(2,1)S(1)}, u32[]{:S(2)}, u32[]{:S(2)}) collective-permute-start(bf16[48,1792]{1,0:T(8,128)(2,1)S(1)} %fusion.3), channel_id=1, source_target_pairs={{0,2},{1,3},{2,0},{3,1},{4,6},{5,7},{6,4},{7,5},{8,10},{9,11},{10,... | collective-permute-start | bytes 516104 | tf_op jit(solution)/shard_map/ppermute | solution.py:219
  43.5 1.7 %collective-permute-start.12 = (bf16[96,1792]{1,0:T(8,128)(2,1)S(1)}, bf16[96,1792]{1,0:T(8,128)(2,1)S(1)}, u32[]{:S(2)}, u32[]{:S(2)}) collective-permute-start(bf16[96,1792]{1,0:T(8,128)(2,1)S(1)} %constant_dynamic-update-slice_fusion.refs_0_), channel_id=1, source_target_pairs={{0,1},{1,0},{2,3},{3,2},{4,5},{5,4},{6,7},{7,6},{8,9},{9,8},{10,11... | collective-permute-start | bytes 1032200 | tf_op jit(solution)/shard_map/ppermute | solution.py:219
  43.6 8.7 %collective-permute-start.15 = (bf16[48,1792]{1,0:T(8,128)(2,1)S(1)}, bf16[48,1792]{1,0:T(8,128)(2,1)S(1)}, u32[]{:S(2)}, u32[]{:S(2)}) collective-permute-start(bf16[48,1792]{1,0:T(8,128)(2,1)S(1)} %fusion.6), channel_id=1, source_target_pairs={{0,2},{1,3},{2,0},{3,1},{4,6},{5,7},{6,4},{7,5},{8,10},{9,11},{10,... | collective-permute-start | bytes 516104 | tf_op jit(solution)/shard_map/ppermute | solution.py:219
  47.5 2.0 %collective-permute-start.13 = (bf16[96,1792]{1,0:T(8,128)(2,1)S(1)}, bf16[96,1792]{1,0:T(8,128)(2,1)S(1)}, u32[]{:S(2)}, u32[]{:S(2)}) collective-permute-start(bf16[96,1792]{1,0:T(8,128)(2,1)S(1)} %get-tuple-element.55), channel_id=1, source_target_pairs={{0,1},{1,0},{2,3},{3,2},{4,5},{5,4},{6,7},{7,6},{8,9},{9,8},{10,11... | collective-permute-start | bytes 1032200 | tf_op jit(solution)/shard_map/ppermute | solution.py:219
  49.3 9.8 %collective-permute-start.19 = (bf16[48,1792]{1,0:T(8,128)(2,1)S(1)}, bf16[48,1792]{1,0:T(8,128)(2,1)S(1)}, u32[]{:S(2)}, u32[]{:S(2)}) collective-permute-start(bf16[48,1792]{1,0:T(8,128)(2,1)S(1)} %fusion.5), channel_id=1, source_target_pairs={{0,8},{1,9},{2,10},{3,11},{4,12},{5,13},{6,14},{7,15},{8,0},{9,1},... | collective-permute-start | bytes 516104 | tf_op jit(solution)/shard_map/ppermute | solution.py:219
  49.6 6.3 %collective-permute-start.14 = (bf16[48,1792]{1,0:T(8,128)(2,1)S(1)}, bf16[48,1792]{1,0:T(8,128)(2,1)S(1)}, u32[]{:S(2)}, u32[]{:S(2)}) collective-permute-start(bf16[48,1792]{1,0:T(8,128)(2,1)S(1)} %fusion.9), channel_id=1, source_target_pairs={{0,2},{1,3},{2,0},{3,1},{4,6},{5,7},{6,4},{7,5},{8,10},{9,11},{10,... | collective-permute-start | bytes 516104 | tf_op jit(solution)/shard_map/ppermute | solution.py:219
  52.4 8.5 %collective-permute-start.16 = (bf16[48,1792]{1,0:T(8,128)(2,1)S(1)}, bf16[48,1792]{1,0:T(8,128)(2,1)S(1)}, u32[]{:S(2)}, u32[]{:S(2)}) collective-permute-start(bf16[48,1792]{1,0:T(8,128)(2,1)S(1)} %fusion.8), channel_id=1, source_target_pairs={{0,4},{1,5},{2,6},{3,7},{4,0},{5,1},{6,2},{7,3},{8,12},{9,13},{10,... | collective-permute-start | bytes 516104 | tf_op jit(solution)/shard_map/ppermute | solution.py:219

commit v7 on v6

--- a/solution.py
+++ b/solution.py
@@ -9,24 +9,17 @@
 
 SHARDS = 4
 QUARTERS = 4
-GROUPS = ("own", "near", "mid", "far")
-SPLIT = ()
+GROUPS = ("own+near", "mid", "far")
+SPLIT = ("c mid", "c near", "rc mid",)
 ORDER = {
-    "z mid": ("z near",),
-    "y far": ("z far",),
-    "y mid": ("z far",),
-    "expert far": ("z near",),
-    "rc far": ("load all",),
-    "expert near": ("c mid",),
-    "c mid": ("rc far",),
-    "rc near": ("z far",),
-    "ry near": ("c far", "y near",),
-    "rc mid": ("expert near",),
-    "c own": ("rc near", "z mid",),
-    "rz far": ("c near", "rc far", "ry far", "expert mid",),
-    "ry mid": ("load all",),
-    "rz near": ("rc own", "y far",),
-    "rc own": ("c mid",),
+    "z far": ("y own",),
+    "expert own+near": ("y own",),
+    "expert far": ("rc mid",),
+    "c own": ("c near",),
+    "rz mid": ("rc far", "z near",),
+    "c far": ("z near", "expert mid",),
+    "ry own+near": ("y near",),
+    "y far": ("z near",),
 }
 VMEM_BYTES = 16 * 1024 * 1024
 LOAD_VMEM_BYTES = 40 * 1024 * 1024
@@ -52,17 +45,19 @@
     return out
 
 
-def pack_kernel(capacity, planes, route_ref, tok_ref, scale_ref, *rest):
-    outs, quarters_ref = rest[:planes], rest[planes]
+def pack_kernel(capacity, planes, route_hbm, tok_hbm, scale_hbm, *rest):
+    outs = rest[:planes]
+    quarters_ref, tok_ref, scale_ref, route_ref, sems = rest[planes:]
+    sources, targets = (route_hbm, scale_hbm, tok_hbm), (route_ref, scale_ref, tok_ref)
+    copies = [
+        pltpu.make_async_copy(source, target, sems.at[index])
+        for index, (source, target) in enumerate(zip(sources, targets))
+    ]
+    for copy in copies:
+        copy.start()
     rows, features = tok_ref.shape
     picks, width = route_ref.shape[0], features // QUARTERS
-    for block in range(features // 128):
-        quarter, at = divmod(block * 128, width)
-        codes = tok_ref[:, block * 128 : (block + 1) * 128].astype(jnp.float32)
-        factors = scale_ref[:, block : block + 1]
-        quarters_ref[quarter * rows : (quarter + 1) * rows, at : at + 128] = (
-            codes * factors
-        ).astype(jnp.bfloat16)
+    copies[0].wait()
     plane = lax.axis_index("expert") // SHARDS
     columns = QUARTERS * rows
     numbers = lax.broadcasted_iota(jnp.int32, (planes, columns), 0)
@@ -87,6 +82,15 @@
         )
         for offset in range(planes)
     ]
+    copies[1].wait()
+    copies[2].wait()
+    for block in range(features // 128):
+        quarter, at = divmod(block * 128, width)
+        codes = tok_ref[:, block * 128 : (block + 1) * 128].astype(jnp.float32)
+        factors = scale_ref[:, block : block + 1]
+        quarters_ref[quarter * rows : (quarter + 1) * rows, at : at + 128] = (
+            codes * factors
+        ).astype(jnp.bfloat16)
     moved = exact_dot(jnp.concatenate(pick_out, axis=0), quarters_ref[...])
     for offset in range(planes):
         outs[offset][...] = moved[offset * tall : (offset + 1) * tall, :].astype(jnp.bfloat16)
@@ -154,7 +158,16 @@
             out_ref[at : at + tall, :] = answer[member * tall : (member + 1) * tall, :]
 
 
-def plan_kernel(capacity, planes, rows, route_ref, code_ref, unused, plan_ref):
+def plan_kernel(capacity, planes, rows, route_hbm, code_hbm, unused, plan_ref, *scratch):
+    route_ref, code_ref, sems = scratch
+    copies = [
+        pltpu.make_async_copy(route_hbm, route_ref, sems.at[0]),
+        pltpu.make_async_copy(code_hbm, code_ref, sems.at[1]),
+    ]
+    for copy in copies:
+        copy.start()
+    for copy in copies:
+        copy.wait()
     picks = route_ref.shape[0]
     tall = QUARTERS * rows
     plane = lax.axis_index("expert") // SHARDS
@@ -215,26 +228,36 @@
     params = pltpu.CompilerParams(vmem_limit_bytes=VMEM_BYTES)
     load_params = pltpu.CompilerParams(vmem_limit_bytes=LOAD_VMEM_BYTES)
 
+    def in_hbm(array):
+        return pltpu.with_memory_space_constraint(array, pltpu.HBM)
+
     def partner(array, distance):
         return lax.ppermute(array, "expert", [(i, i ^ distance) for i in range(devices)])
 
     block = jax.ShapeDtypeStruct((tall, width), jnp.bfloat16)
-    smem = pl.BlockSpec(memory_space=pltpu.SMEM)
     packed = pl.pallas_call(
         functools.partial(pack_kernel, capacity, planes),
         out_shape=[block] * planes,
-        in_specs=[smem, vmem, vmem],
+        in_specs=[hbm] * 3,
         out_specs=[vmem] * planes,
-        scratch_shapes=[pltpu.VMEM((QUARTERS * tok_rows, width), jnp.bfloat16)],
+        scratch_shapes=[
+            pltpu.VMEM((QUARTERS * tok_rows, width), jnp.bfloat16),
+            pltpu.VMEM(tokens.shape, tokens.dtype),
+            pltpu.VMEM(scales.shape, scales.dtype),
+            pltpu.SMEM(routes.T.shape, routes.dtype),
+            pltpu.SemaphoreType.DMA((3,)),
+        ],
         compiler_params=params,
-    )(routes.T, tokens, scales)
+    )(in_hbm(routes.T), in_hbm(tokens), in_hbm(scales))
     plan = pl.pallas_call(
         functools.partial(plan_kernel, capacity, planes, tok_rows),
         out_shape=jax.ShapeDtypeStruct((planes, 2 * QUARTERS * tok_rows, tall), jnp.bfloat16),
-        in_specs=[smem, smem, hbm],
+        in_specs=[hbm] * 3,
         out_specs=vmem,
+        scratch_shapes=[pltpu.SMEM(routes.T.shape, routes.dtype)] * 2
+        + [pltpu.SemaphoreType.DMA((2,))],
         compiler_params=params,
-    )(routes.T, gate_codes.T, packed[0])
+    )(in_hbm(routes.T), in_hbm(gate_codes.T), packed[0])
 
     def expert(offsets, held, weights):
         rows = offsets * SHARDS * capacity
@@ -261,7 +284,7 @@
             out_specs=[vmem] * 3,
             scratch_shapes=[pltpu.SemaphoreType.DMA((3,))],
             compiler_params=load_params,
-        )(w_gate, w_up, w_down, gate)
+        )(in_hbm(w_gate), in_hbm(w_up), in_hbm(w_down), gate)
 
     def fold(kept, arrived, offsets):
         middle = offsets * tall

time: 62.1 us -> 57.8 us (0.931)
  waiting for transfers between devices: 20.6 us -> 15.8 us
  starting transfers between devices: 20.8 us -> 25.4 us
  local copies, waits for them, and re-layouts: 3.09 us -> 0.15 us
  Pallas kernels: 16.3 us -> 15.1 us
    ppermute x22 -> x23, waiting for transfers between devices: 20.6 us -> 15.8 us  [partner(): lax.ppermute(array, 'expert', [(i, i ^ distance) for i in range(devices)])]
    ppermute x22 -> x23, starting transfers between devices: 20.8 us -> 25.4 us  [partner(): lax.ppermute(array, 'expert', [(i, i ^ distance) for i in range(devices)])]
    unnamed x12 -> x4, local copies, waits for them, and re-layouts: 3.04 us -> 0.05 us
    pallas_call x4 -> x3, Pallas kernels: 9.16 us -> 7.39 us  [expert(): pl.pallas_call(functools.partial(expert_kernel, capacity, offsets), out_s...]
  transfers between devices with their start and end apart: 22 -> 23, of which waited for: 12 -> 8; matrix products, arithmetic and copies ran while one was open for 1% -> 2% of each run, Pallas kernels for 23% -> 22%
where the time goes in v7:
time: 57.8 us; the launch traced here: 57.6 us
  starting transfers between devices  25.4 us (44%)
  waiting for transfers between devices  15.8 us (27%)
  Pallas kernels  15.1 us (26%)
  other arithmetic  0.83 us (1%)
    ppermute x23, starting transfers between devices, partner(): lax.ppermute(array, 'expert', [(i, i ^ distance) for i in range(devices)])  25.4 us
    ppermute x23, waiting for transfers between devices, partner(): lax.ppermute(array, 'expert', [(i, i ^ distance) for i in range(devices)])  15.8 us
    pallas_call x3, Pallas kernels, expert(): pl.pallas_call(functools.partial(expert_kernel, capacity, offsets), out_s...  7.39 us
    pallas_call x1, Pallas kernels, load(): pl.pallas_call(load_kernel, out_shape=[jax.ShapeDtypeStruct(w.shape, w.dt...  4.23 us
    pallas_call x1, Pallas kernels, shards(): pl.pallas_call(functools.partial(pack_kernel, capacity, planes), out_shap...  1.48 us
  transfers between devices with their start and end apart: 23, of which 8 were waited for; matrix products, arithmetic and copies ran while one was open for 2% of the time, Pallas kernels for 22%

profile of v7, /device:TPU:0, one launch (start us, length us, event | category | flops | bytes accessed | tf_op | source)
XLA Modules:
  0.0 57.6 jit_solution(2678248985098954650)
XLA Ops:
  0.0 1.5 %shard_map.73 = (bf16[48,1792]{1,0:T(8,128)(2,1)S(1)}, bf16[48,1792]{1,0:T(8,128)(2,1)S(1)}, bf16[48,1792]{1,0:T(8,128)(2,1)S(1)}, bf16[48,1792]{1,0:T(8,128)(2,1)S(1)}) custom-call(s32[2,16]{1,0:T(2,128)} %bitcast.2, bf16[16,7168]{1,0:T(8,128)(2,1)} %tok_hbm.1, f32[16,56]{1,0:T(8,128)} %scale_hbm.1), custom_call_target="tpu_custom_call" | custom-call | tf_op jit(solution)/shard_map/pallas_call | solution.py:238
  1.5 4.1 %collective-permute-start.9 = (bf16[48,1792]{1,0:T(8,128)(2,1)S(1)}, bf16[48,1792]{1,0:T(8,128)(2,1)S(1)}, u32[]{:S(2)}, u32[]{:S(2)}) collective-permute-start(bf16[48,1792]{1,0:T(8,128)(2,1)S(1)} %get-tuple-element.36), channel_id=1, source_target_pairs={{0,8},{1,9},{2,10},{3,11},{4,12},{5,13},{6,14},{7,15},{8,0},{9,1},... | collective-permute-start | bytes 516104 | tf_op jit(solution)/shard_map/ppermute | solution.py:235
  5.6 1.5 %collective-permute-start = (bf16[48,1792]{1,0:T(8,128)(2,1)S(1)}, bf16[48,1792]{1,0:T(8,128)(2,1)S(1)}, u32[]{:S(2)}, u32[]{:S(2)}) collective-permute-start(bf16[48,1792]{1,0:T(8,128)(2,1)S(1)} %get-tuple-element.26.unused), channel_id=1, source_target_pairs={{0,2},{1,3},{2,0},{3,1},{4,6},{5,7},{6,4},{7,5},{8,10},{9,11},{10,... | collective-permute-start | bytes 516104 | tf_op jit(solution)/shard_map/ppermute | solution.py:235
  7.1 1.6 %collective-permute-start.1 = (bf16[48,1792]{1,0:T(8,128)(2,1)S(1)}, bf16[48,1792]{1,0:T(8,128)(2,1)S(1)}, u32[]{:S(2)}, u32[]{:S(2)}) collective-permute-start(bf16[48,1792]{1,0:T(8,128)(2,1)S(1)} %get-tuple-element.28), channel_id=1, source_target_pairs={{0,4},{1,5},{2,6},{3,7},{4,0},{5,1},{6,2},{7,3},{8,12},{9,13},{10,... | collective-permute-start | bytes 516104 | tf_op jit(solution)/shard_map/ppermute | solution.py:235
  8.7 4.2 %shard_map.75 = (bf16[1,7168,256]{2,1,0:T(8,128)(2,1)S(1)}, bf16[1,7168,256]{2,1,0:T(8,128)(2,1)S(1)}, bf16[1,256,7168]{2,1,0:T(8,128)(2,1)S(1)}) custom-call(bf16[1,7168,256]{2,1,0:T(8,128)(2,1)} %gate_hbm.1, bf16[1,7168,256]{2,1,0:T(8,128)(2,1)} %up_hbm.1, bf16[1,256,7168]{2,1,0:T(8,128)(2,1)} %down_hbm.1, bf16[48,1792]{1,0:T(8,128)(2,1)S(1)} %get-tuple-element.26.unused), custom_call_target="tpu_custom_call" | custom-call | tf_op jit(solution)/shard_map/pallas_call | solution.py:280
  12.9 0.0 collective-permute-done
  13.0 0.3 collective-permute-start.16
  13.2 0.5 collective-permute-done.9
  13.8 1.6 %collective-permute-start.10 = (bf16[48,1792]{1,0:T(8,128)(2,1)S(1)}, bf16[48,1792]{1,0:T(8,128)(2,1)S(1)}, u32[]{:S(2)}, u32[]{:S(2)}) collective-permute-start(bf16[48,1792]{1,0:T(8,128)(2,1)S(1)} %collective-permute-done.9), channel_id=1, source_target_pairs={{0,2},{1,3},{2,0},{3,1},{4,6},{5,7},{6,4},{7,5},{8,10},{9,11},{10,... | collective-permute-start | bytes 516104 | tf_op jit(solution)/shard_map/ppermute | solution.py:235
  15.3 0.1 collective-permute-start.11
  15.4 0.0 collective-permute-done.1
  15.4 0.5 collective-permute-start.3
  16.0 0.2 collective-permute-start.2
  16.1 4.2 %collective-permute-done.16 = bf16[48,1792]{1,0:T(8,128)(2,1)S(1)} collective-permute-done((bf16[48,1792]{1,0:T(8,128)(2,1)S(1)}, bf16[48,1792]{1,0:T(8,128)(2,1)S(1)}, u32[]{:S(2)}, u32[]{:S(2)}) %collective-permute-start.16) | collective-permute-done | bytes 172064 | tf_op jit(solution)/shard_map/ppermute | solution.py:235
  20.3 0.5 collective-permute-start.17
  20.8 0.0 collective-permute-done.10
  20.8 0.0 collective-permute-start.12
  20.8 2.9 %collective-permute-done.3 = bf16[48,1792]{1,0:T(8,128)(2,1)S(1)} collective-permute-done((bf16[48,1792]{1,0:T(8,128)(2,1)S(1)}, bf16[48,1792]{1,0:T(8,128)(2,1)S(1)}, u32[]{:S(2)}, u32[]{:S(2)}) %collective-permute-start.3) | collective-permute-done | bytes 172064 | tf_op jit(solution)/shard_map/ppermute | solution.py:235
  23.7 0.0 collective-permute-start.4
  23.7 0.0 collective-permute-done.2
  23.7 0.0 collective-permute-done.11
  23.7 0.0 collective-permute-done.12
  23.8 2.3 %shard_map.77 = (bf16[96,1792]{1,0:T(8,128)(2,1)S(1)}, bf16[96,1792]{1,0:T(8,128)(2,1)S(1)}) custom-call(bf16[96,1792]{1,0:T(8,128)(2,1)S(1)} %pad_maximum_fusion.1.refs_0_, bf16[96,1792]{1,0:T(8,128)(2,1)S(1)} %pad_maximum_fusion.2.refs_1_, bf16[1,7168,256]{2,1,0:T(8,128)(2,1)S(1)} %get-tuple-element.30.refs_4_.refs_2_, ...), custom_call_target="tpu_custom_call" | custom-call | flops 528482304 | tf_op jit(solution)/shard_map/pallas_call | solution.py:265
  26.1 0.6 collective-permute-start.13
  26.7 0.1 collective-permute-start.14
  26.8 0.0 collective-permute-done.17
  26.8 0.5 collective-permute-start.18
  27.3 0.0 collective-permute-done.4
  27.4 0.1 collective-permute-start.5
  27.5 0.2 collective-permute-done.13
  27.7 0.4 collective-permute-done.14
  28.2 2.5 %collective-permute-start.15 = (bf16[48,1792]{1,0:T(8,128)(2,1)S(1)}, bf16[48,1792]{1,0:T(8,128)(2,1)S(1)}, u32[]{:S(2)}, u32[]{:S(2)}) collective-permute-start(bf16[48,1792]{1,0:T(8,128)(2,1)S(1)} %fusion.6), channel_id=1, source_target_pairs={{0,2},{1,3},{2,0},{3,1},{4,6},{5,7},{6,4},{7,5},{8,10},{9,11},{10,... | collective-permute-start | bytes 516104 | tf_op jit(solution)/shard_map/ppermute | solution.py:235
  30.8 0.0 collective-permute-done.18.refs_1_
  30.8 2.3 %shard_map.78 = (bf16[96,1792]{1,0:T(8,128)(2,1)S(1)}, bf16[96,1792]{1,0:T(8,128)(2,1)S(1)}) custom-call(bf16[96,1792]{1,0:T(8,128)(2,1)S(1)} %constant_dynamic-update-slice_fusion.6.refs_0_, bf16[96,1792]{1,0:T(8,128)(2,1)S(1)} %collective-permute-done.18.refs_1_, bf16[1,7168,256]{2,1,0:T(8,128)(2,1)S(1)} %get-tuple-element.30.refs_4_.refs_2_, ...), custom_call_target="tpu_custom_call" | custom-call | flops 528482304 | tf_op jit(solution)/shard_map/pallas_call | solution.py:265
  33.1 0.1 collective-permute-start.19
  33.2 0.0 collective-permute-done.5.refs_1_
  33.2 2.8 %shard_map.76 = (bf16[192,1792]{1,0:T(8,128)(2,1)S(1)}, bf16[192,1792]{1,0:T(8,128)(2,1)S(1)}) custom-call(bf16[96,1792]{1,0:T(8,128)(2,1)S(1)} %constant_dynamic-update-slice_fusion.refs_0_, bf16[96,1792]{1,0:T(8,128)(2,1)S(1)} %collective-permute-done.5.refs_1_, bf16[96,1792]{1,0:T(8,128)(2,1)S(1)} %pad_maximum_fusion.refs_2_, ...), custom_call_target="tpu_custom_call" | custom-call | flops 1056964608 | tf_op jit(solution)/shard_map/pallas_call | solution.py:265
  36.0 0.6 collective-permute-start.6
  36.5 0.0 collective-permute-done.15
  36.5 0.1 fusion.8
  36.7 0.1 convert_element_type.45
  36.8 0.0 collective-permute-done.19
  36.9 0.8 %collective-permute-start.21 = (bf16[48,1792]{1,0:T(8,128)(2,1)S(1)}, bf16[48,1792]{1,0:T(8,128)(2,1)S(1)}, u32[]{:S(2)}, u32[]{:S(2)}) collective-permute-start(bf16[48,1792]{1,0:T(8,128)(2,1)S(1)} %fusion.3), channel_id=1, source_target_pairs={{0,2},{1,3},{2,0},{3,1},{4,6},{5,7},{6,4},{7,5},{8,10},{9,11},{10,... | collective-permute-start | bytes 516104 | tf_op jit(solution)/shard_map/ppermute | solution.py:235
  37.7 1.7 %collective-permute-start.20 = (bf16[48,1792]{1,0:T(8,128)(2,1)S(1)}, bf16[48,1792]{1,0:T(8,128)(2,1)S(1)}, u32[]{:S(2)}, u32[]{:S(2)}) collective-permute-start(bf16[48,1792]{1,0:T(8,128)(2,1)S(1)} %fusion.8), channel_id=1, source_target_pairs={{0,8},{1,9},{2,10},{3,11},{4,12},{5,13},{6,14},{7,15},{8,0},{9,1},... | collective-permute-start | bytes 516104 | tf_op jit(solution)/shard_map/ppermute | solution.py:235
  39.4 0.0 collective-permute-done.6
  39.4 0.1 convert_element_type.46
  39.5 0.1 fusion
  39.5 1.3 %collective-permute-start.7 = (bf16[96,1792]{1,0:T(8,128)(2,1)S(1)}, bf16[96,1792]{1,0:T(8,128)(2,1)S(1)}, u32[]{:S(2)}, u32[]{:S(2)}) collective-permute-start(bf16[96,1792]{1,0:T(8,128)(2,1)S(1)} %fusion), channel_id=1, source_target_pairs={{0,2},{1,3},{2,0},{3,1},{4,6},{5,7},{6,4},{7,5},{8,10},{9,11},{10,... | collective-permute-start | bytes 1032200 | tf_op jit(solution)/shard_map/ppermute | solution.py:235
  40.9 3.3 %collective-permute-done.21 = bf16[48,1792]{1,0:T(8,128)(2,1)S(1)} collective-permute-done((bf16[48,1792]{1,0:T(8,128)(2,1)S(1)}, bf16[48,1792]{1,0:T(8,128)(2,1)S(1)}, u32[]{:S(2)}, u32[]{:S(2)}) %collective-permute-start.21) | collective-permute-done | bytes 172064 | tf_op jit(solution)/shard_map/ppermute | solution.py:235
  44.2 4.8 %collective-permute-start.22 = (bf16[48,1792]{1,0:T(8,128)(2,1)S(1)}, bf16[48,1792]{1,0:T(8,128)(2,1)S(1)}, u32[]{:S(2)}, u32[]{:S(2)}) collective-permute-start(bf16[48,1792]{1,0:T(8,128)(2,1)S(1)} %fusion.5), channel_id=1, source_target_pairs={{0,12},{1,13},{2,14},{3,15},{4,8},{5,9},{6,10},{7,11},{8,4},{9,5},... | collective-permute-start | bytes 516104 | tf_op jit(solution)/shard_map/ppermute | solution.py:235
  49.0 1.6 %collective-permute-done.7 = bf16[96,1792]{1,0:T(8,128)(2,1)S(1)} collective-permute-done((bf16[96,1792]{1,0:T(8,128)(2,1)S(1)}, bf16[96,1792]{1,0:T(8,128)(2,1)S(1)}, u32[]{:S(2)}, u32[]{:S(2)}) %collective-permute-start.7) | collective-permute-done | bytes 344096 | tf_op jit(solution)/shard_map/ppermute | solution.py:235
  50.6 0.1 fusion.2
  50.8 2.0 %collective-permute-start.8 = (bf16[48,1792]{1,0:T(8,128)(2,1)S(1)}, bf16[48,1792]{1,0:T(8,128)(2,1)S(1)}, u32[]{:S(2)}, u32[]{:S(2)}) collective-permute-start(bf16[48,1792]{1,0:T(8,128)(2,1)S(1)} %get-tuple-element.49), channel_id=1, source_target_pairs={{0,4},{1,5},{2,6},{3,7},{4,0},{5,1},{6,2},{7,3},{8,12},{9,13},{10,... | collective-permute-start | bytes 516104 | tf_op jit(solution)/shard_map/ppermute | solution.py:235
  52.8 1.0 %shard_map.74.plan_ref = bf16[4,128,48]{2,1,0:T(8,128)(2,1)S(1)} custom-call(s32[2,16]{1,0:T(2,128)} %bitcast.3, s32[2,16]{1,0:T(2,128)} %bitcast.4, bf16[48,1792]{1,0:T(8,128)(2,1)S(1)} %get-tuple-element.26.unused), custom_call_target="tpu_custom_call" | custom-call | tf_op jit(solution)/shard_map/pallas_call | solution.py:252
  53.8 0.0 collective-permute-done.20.refs_2_
  53.8 0.0 collective-permute-done.22.refs_3_
  53.8 2.8 %collective-permute-done.8.refs_1_ = bf16[48,1792]{1,0:T(8,128)(2,1)S(1)} collective-permute-done((bf16[48,1792]{1,0:T(8,128)(2,1)S(1)}, bf16[48,1792]{1,0:T(8,128)(2,1)S(1)}, u32[]{:S(2)}, u32[]{:S(2)}) %collective-permute-start.8) | collective-permute-done | bytes 172064 | tf_op jit(solution)/shard_map/ppermute | solution.py:235
  56.6 1.0 %shard_map.79 = bf16[16,7168]{1,0:T(8,128)(2,1)} custom-call(bf16[4,128,48]{2,1,0:T(8,128)(2,1)S(1)} %shard_map.74.plan_ref, bf16[48,1792]{1,0:T(8,128)(2,1)S(1)} %get-tuple-element.50.refs_0_, bf16[48,1792]{1,0:T(8,128)(2,1)S(1)} %collective-permute-done.8.refs_1_, bf16[48,1792]{1,0:T(8,128)(2,1)S(1)} %collective-permute-done.20.refs_2_, ...), custom_call_target="tpu_custom_call" | custom-call | tf_op jit(solution)/shard_map/pallas_call | solution.py:372
  (20 shorter events, 0.5 us)
Async XLA Ops:
  1.5 12.3 %collective-permute-start.9 = (bf16[48,1792]{1,0:T(8,128)(2,1)S(1)}, bf16[48,1792]{1,0:T(8,128)(2,1)S(1)}, u32[]{:S(2)}, u32[]{:S(2)}) collective-permute-start(bf16[48,1792]{1,0:T(8,128)(2,1)S(1)} %get-tuple-element.36), channel_id=1, source_target_pairs={{0,8},{1,9},{2,10},{3,11},{4,12},{5,13},{6,14},{7,15},{8,0},{9,1},... | collective-permute-start | bytes 516104 | tf_op jit(solution)/shard_map/ppermute | solution.py:235
  5.6 7.4 %collective-permute-start = (bf16[48,1792]{1,0:T(8,128)(2,1)S(1)}, bf16[48,1792]{1,0:T(8,128)(2,1)S(1)}, u32[]{:S(2)}, u32[]{:S(2)}) collective-permute-start(bf16[48,1792]{1,0:T(8,128)(2,1)S(1)} %get-tuple-element.26.unused), channel_id=1, source_target_pairs={{0,2},{1,3},{2,0},{3,1},{4,6},{5,7},{6,4},{7,5},{8,10},{9,11},{10,... | collective-permute-start | bytes 516104 | tf_op jit(solution)/shard_map/ppermute | solution.py:235
  7.1 8.3 %collective-permute-start.1 = (bf16[48,1792]{1,0:T(8,128)(2,1)S(1)}, bf16[48,1792]{1,0:T(8,128)(2,1)S(1)}, u32[]{:S(2)}, u32[]{:S(2)}) collective-permute-start(bf16[48,1792]{1,0:T(8,128)(2,1)S(1)} %get-tuple-element.28), channel_id=1, source_target_pairs={{0,4},{1,5},{2,6},{3,7},{4,0},{5,1},{6,2},{7,3},{8,12},{9,13},{10,... | collective-permute-start | bytes 516104 | tf_op jit(solution)/shard_map/ppermute | solution.py:235
  13.0 7.3 %collective-permute-start.16 = (bf16[48,1792]{1,0:T(8,128)(2,1)S(1)}, bf16[48,1792]{1,0:T(8,128)(2,1)S(1)}, u32[]{:S(2)}, u32[]{:S(2)}) collective-permute-start(bf16[48,1792]{1,0:T(8,128)(2,1)S(1)} %get-tuple-element.40), channel_id=1, source_target_pairs={{0,12},{1,13},{2,14},{3,15},{4,8},{5,9},{6,10},{7,11},{8,4},{9,5},... | collective-permute-start | bytes 516104 | tf_op jit(solution)/shard_map/ppermute | solution.py:235
  13.8 7.0 %collective-permute-start.10 = (bf16[48,1792]{1,0:T(8,128)(2,1)S(1)}, bf16[48,1792]{1,0:T(8,128)(2,1)S(1)}, u32[]{:S(2)}, u32[]{:S(2)}) collective-permute-start(bf16[48,1792]{1,0:T(8,128)(2,1)S(1)} %collective-permute-done.9), channel_id=1, source_target_pairs={{0,2},{1,3},{2,0},{3,1},{4,6},{5,7},{6,4},{7,5},{8,10},{9,11},{10,... | collective-permute-start | bytes 516104 | tf_op jit(solution)/shard_map/ppermute | solution.py:235
  15.3 8.4 %collective-permute-start.11 = (bf16[48,1792]{1,0:T(8,128)(2,1)S(1)}, bf16[48,1792]{1,0:T(8,128)(2,1)S(1)}, u32[]{:S(2)}, u32[]{:S(2)}) collective-permute-start(bf16[48,1792]{1,0:T(8,128)(2,1)S(1)} %collective-permute-done.9), channel_id=1, source_target_pairs={{0,1},{1,0},{2,3},{3,2},{4,5},{5,4},{6,7},{7,6},{8,9},{9,8},{10,11... | collective-permute-start | bytes 516104 | tf_op jit(solution)/shard_map/ppermute | solution.py:235
  15.4 8.2 %collective-permute-start.3 = (bf16[48,1792]{1,0:T(8,128)(2,1)S(1)}, bf16[48,1792]{1,0:T(8,128)(2,1)S(1)}, u32[]{:S(2)}, u32[]{:S(2)}) collective-permute-start(bf16[48,1792]{1,0:T(8,128)(2,1)S(1)} %collective-permute-done.1), channel_id=1, source_target_pairs={{0,2},{1,3},{2,0},{3,1},{4,6},{5,7},{6,4},{7,5},{8,10},{9,11},{10,... | collective-permute-start | bytes 516104 | tf_op jit(solution)/shard_map/ppermute | solution.py:235
  16.0 7.7 %collective-permute-start.2 = (bf16[48,1792]{1,0:T(8,128)(2,1)S(1)}, bf16[48,1792]{1,0:T(8,128)(2,1)S(1)}, u32[]{:S(2)}, u32[]{:S(2)}) collective-permute-start(bf16[48,1792]{1,0:T(8,128)(2,1)S(1)} %collective-permute-done.1), channel_id=1, source_target_pairs={{0,1},{1,0},{2,3},{3,2},{4,5},{5,4},{6,7},{7,6},{8,9},{9,8},{10,11... | collective-permute-start | bytes 516104 | tf_op jit(solution)/shard_map/ppermute | solution.py:235
  20.3 6.5 %collective-permute-start.17 = (bf16[48,1792]{1,0:T(8,128)(2,1)S(1)}, bf16[48,1792]{1,0:T(8,128)(2,1)S(1)}, u32[]{:S(2)}, u32[]{:S(2)}) collective-permute-start(bf16[48,1792]{1,0:T(8,128)(2,1)S(1)} %collective-permute-done.16), channel_id=1, source_target_pairs={{0,2},{1,3},{2,0},{3,1},{4,6},{5,7},{6,4},{7,5},{8,10},{9,11},{10,... | collective-permute-start | bytes 516104 | tf_op jit(solution)/shard_map/ppermute | solution.py:235
  20.8 3.0 %collective-permute-start.12 = (bf16[48,1792]{1,0:T(8,128)(2,1)S(1)}, bf16[48,1792]{1,0:T(8,128)(2,1)S(1)}, u32[]{:S(2)}, u32[]{:S(2)}) collective-permute-start(bf16[48,1792]{1,0:T(8,128)(2,1)S(1)} %collective-permute-done.10), channel_id=1, source_target_pairs={{0,1},{1,0},{2,3},{3,2},{4,5},{5,4},{6,7},{7,6},{8,9},{9,8},{10,11... | collective-permute-start | bytes 516104 | tf_op jit(solution)/shard_map/ppermute | solution.py:235
  23.7 3.6 %collective-permute-start.4 = (bf16[48,1792]{1,0:T(8,128)(2,1)S(1)}, bf16[48,1792]{1,0:T(8,128)(2,1)S(1)}, u32[]{:S(2)}, u32[]{:S(2)}) collective-permute-start(bf16[48,1792]{1,0:T(8,128)(2,1)S(1)} %collective-permute-done.3), channel_id=1, source_target_pairs={{0,1},{1,0},{2,3},{3,2},{4,5},{5,4},{6,7},{7,6},{8,9},{9,8},{10,11... | collective-permute-start | bytes 516104 | tf_op jit(solution)/shard_map/ppermute | solution.py:235
  26.1 1.6 %collective-permute-start.13 = (bf16[48,1792]{1,0:T(8,128)(2,1)S(1)}, bf16[48,1792]{1,0:T(8,128)(2,1)S(1)}, u32[]{:S(2)}, u32[]{:S(2)}) collective-permute-start(bf16[48,1792]{1,0:T(8,128)(2,1)S(1)} %get-tuple-element.48), channel_id=1, source_target_pairs={{0,1},{1,0},{2,3},{3,2},{4,5},{5,4},{6,7},{7,6},{8,9},{9,8},{10,11... | collective-permute-start | bytes 516104 | tf_op jit(solution)/shard_map/ppermute | solution.py:235
  26.7 1.4 %collective-permute-start.14 = (bf16[48,1792]{1,0:T(8,128)(2,1)S(1)}, bf16[48,1792]{1,0:T(8,128)(2,1)S(1)}, u32[]{:S(2)}, u32[]{:S(2)}) collective-permute-start(bf16[48,1792]{1,0:T(8,128)(2,1)S(1)} %get-tuple-element.47), channel_id=1, source_target_pairs={{0,1},{1,0},{2,3},{3,2},{4,5},{5,4},{6,7},{7,6},{8,9},{9,8},{10,11... | collective-permute-start | bytes 516104 | tf_op jit(solution)/shard_map/ppermute | solution.py:235
  26.8 4.0 %collective-permute-start.18 = (bf16[96,1792]{1,0:T(8,128)(2,1)S(1)}, bf16[96,1792]{1,0:T(8,128)(2,1)S(1)}, u32[]{:S(2)}, u32[]{:S(2)}) collective-permute-start(bf16[96,1792]{1,0:T(8,128)(2,1)S(1)} %constant_dynamic-update-slice_fusion.6.refs_0_), channel_id=1, source_target_pairs={{0,1},{1,0},{2,3},{3,2},{4,5},{5,4},{6,7},{7,6},{8,9},{9,8},{10,11... | collective-permute-start | bytes 1032200 | tf_op jit(solution)/shard_map/ppermute | solution.py:235
  27.4 5.8 %collective-permute-start.5 = (bf16[96,1792]{1,0:T(8,128)(2,1)S(1)}, bf16[96,1792]{1,0:T(8,128)(2,1)S(1)}, u32[]{:S(2)}, u32[]{:S(2)}) collective-permute-start(bf16[96,1792]{1,0:T(8,128)(2,1)S(1)} %constant_dynamic-update-slice_fusion.refs_0_), channel_id=1, source_target_pairs={{0,1},{1,0},{2,3},{3,2},{4,5},{5,4},{6,7},{7,6},{8,9},{9,8},{10,11... | collective-permute-start | bytes 1032200 | tf_op jit(solution)/shard_map/ppermute | solution.py:235
  28.2 8.3 %collective-permute-start.15 = (bf16[48,1792]{1,0:T(8,128)(2,1)S(1)}, bf16[48,1792]{1,0:T(8,128)(2,1)S(1)}, u32[]{:S(2)}, u32[]{:S(2)}) collective-permute-start(bf16[48,1792]{1,0:T(8,128)(2,1)S(1)} %fusion.6), channel_id=1, source_target_pairs={{0,2},{1,3},{2,0},{3,1},{4,6},{5,7},{6,4},{7,5},{8,10},{9,11},{10,... | collective-permute-start | bytes 516104 | tf_op jit(solution)/shard_map/ppermute | solution.py:235
  33.1 3.7 %collective-permute-start.19 = (bf16[96,1792]{1,0:T(8,128)(2,1)S(1)}, bf16[96,1792]{1,0:T(8,128)(2,1)S(1)}, u32[]{:S(2)}, u32[]{:S(2)}) collective-permute-start(bf16[96,1792]{1,0:T(8,128)(2,1)S(1)} %get-tuple-element.44), channel_id=1, source_target_pairs={{0,1},{1,0},{2,3},{3,2},{4,5},{5,4},{6,7},{7,6},{8,9},{9,8},{10,11... | collective-permute-start | bytes 1032200 | tf_op jit(solution)/shard_map/ppermute | solution.py:235
  36.0 3.4 %collective-permute-start.6 = (bf16[192,1792]{1,0:T(8,128)(2,1)S(1)}, bf16[192,1792]{1,0:T(8,128)(2,1)S(1)}, u32[]{:S(2)}, u32[]{:S(2)}) collective-permute-start(bf16[192,1792]{1,0:T(8,128)(2,1)S(1)} %get-tuple-element.34), channel_id=1, source_target_pairs={{0,1},{1,0},{2,3},{3,2},{4,5},{5,4},{6,7},{7,6},{8,9},{9,8},{10,11... | collective-permute-start | bytes 2064392 | tf_op jit(solution)/shard_map/ppermute | solution.py:235
  36.9 7.3 %collective-permute-start.21 = (bf16[48,1792]{1,0:T(8,128)(2,1)S(1)}, bf16[48,1792]{1,0:T(8,128)(2,1)S(1)}, u32[]{:S(2)}, u32[]{:S(2)}) collective-permute-start(bf16[48,1792]{1,0:T(8,128)(2,1)S(1)} %fusion.3), channel_id=1, source_target_pairs={{0,2},{1,3},{2,0},{3,1},{4,6},{5,7},{6,4},{7,5},{8,10},{9,11},{10,... | collective-permute-start | bytes 516104 | tf_op jit(solution)/shard_map/ppermute | solution.py:235
  37.7 16.1 %collective-permute-start.20 = (bf16[48,1792]{1,0:T(8,128)(2,1)S(1)}, bf16[48,1792]{1,0:T(8,128)(2,1)S(1)}, u32[]{:S(2)}, u32[]{:S(2)}) collective-permute-start(bf16[48,1792]{1,0:T(8,128)(2,1)S(1)} %fusion.8), channel_id=1, source_target_pairs={{0,8},{1,9},{2,10},{3,11},{4,12},{5,13},{6,14},{7,15},{8,0},{9,1},... | collective-permute-start | bytes 516104 | tf_op jit(solution)/shard_map/ppermute | solution.py:235
  39.5 11.1 %collective-permute-start.7 = (bf16[96,1792]{1,0:T(8,128)(2,1)S(1)}, bf16[96,1792]{1,0:T(8,128)(2,1)S(1)}, u32[]{:S(2)}, u32[]{:S(2)}) collective-permute-start(bf16[96,1792]{1,0:T(8,128)(2,1)S(1)} %fusion), channel_id=1, source_target_pairs={{0,2},{1,3},{2,0},{3,1},{4,6},{5,7},{6,4},{7,5},{8,10},{9,11},{10,... | collective-permute-start | bytes 1032200 | tf_op jit(solution)/shard_map/ppermute | solution.py:235
  44.2 9.6 %collective-permute-start.22 = (bf16[48,1792]{1,0:T(8,128)(2,1)S(1)}, bf16[48,1792]{1,0:T(8,128)(2,1)S(1)}, u32[]{:S(2)}, u32[]{:S(2)}) collective-permute-start(bf16[48,1792]{1,0:T(8,128)(2,1)S(1)} %fusion.5), channel_id=1, source_target_pairs={{0,12},{1,13},{2,14},{3,15},{4,8},{5,9},{6,10},{7,11},{8,4},{9,5},... | collective-permute-start | bytes 516104 | tf_op jit(solution)/shard_map/ppermute | solution.py:235
  50.8 5.8 %collective-permute-start.8 = (bf16[48,1792]{1,0:T(8,128)(2,1)S(1)}, bf16[48,1792]{1,0:T(8,128)(2,1)S(1)}, u32[]{:S(2)}, u32[]{:S(2)}) collective-permute-start(bf16[48,1792]{1,0:T(8,128)(2,1)S(1)} %get-tuple-element.49), channel_id=1, source_target_pairs={{0,4},{1,5},{2,6},{3,7},{4,0},{5,1},{6,2},{7,3},{8,12},{9,13},{10,... | collective-permute-start | bytes 516104 | tf_op jit(solution)/shard_map/ppermute | solution.py:235

commit v8 on v7

--- a/solution.py
+++ b/solution.py
@@ -10,14 +10,18 @@
 SHARDS = 4
 QUARTERS = 4
 GROUPS = ("own+near", "mid", "far")
+FIRST = "mid"
 SPLIT = ("c mid", "c near", "rc mid",)
+DIRECT = ()
 ORDER = {
     "z far": ("y own",),
     "expert own+near": ("y own",),
-    "expert far": ("rc mid",),
+    "expert far": ("rc mid", "c own",),
+    "rz far": ("load all",),
     "c own": ("c near",),
-    "rz mid": ("rc far", "z near",),
-    "c far": ("z near", "expert mid",),
+    "rc far": ("y far",),
+    "rz mid": ("rc far",),
+    "c far": ("z near",),
     "ry own+near": ("y near",),
     "y far": ("z near",),
 }
@@ -104,12 +108,10 @@
     return zero_one(col == (block * QUARTERS + quarter) * capacity + slot)
 
 
-def load_kernel(gate_hbm, up_hbm, down_hbm, unused, gate_ref, up_ref, down_ref, sems):
+def load_kernel(gate_hbm, up_hbm, unused, gate_ref, up_ref, sems):
     copies = [
-        pltpu.make_async_copy(source, target, sems.at[index])
-        for index, (source, target) in enumerate(
-            ((gate_hbm, gate_ref), (up_hbm, up_ref), (down_hbm, down_ref))
-        )
+        pltpu.make_async_copy(gate_hbm, gate_ref, sems.at[0]),
+        pltpu.make_async_copy(up_hbm, up_ref, sems.at[1]),
     ]
     for copy in copies:
         copy.start()
@@ -117,10 +119,16 @@
         copy.wait()
 
 
-def expert_kernel(capacity, offsets, *refs):
+def expert_kernel(capacity, offsets, first, *refs):
     count = 2 * offsets
     blocks = refs[:count]
-    gate_ref, up_ref, down_ref, kept_ref, sent_ref, rows_ref, part_ref = refs[count:]
+    if first:
+        gate_ref, up_ref, down_hbm, kept_ref, sent_ref, down_ref, *scratch = refs[count:]
+        rows_ref, part_ref, sem = scratch
+        down_copy = pltpu.make_async_copy(down_hbm, down_ref, sem)
+        down_copy.start()
+    else:
+        gate_ref, up_ref, down_ref, kept_ref, sent_ref, rows_ref, part_ref = refs[count:]
     group, tall = SHARDS * capacity, QUARTERS * capacity
     width = blocks[0].shape[1]
     spans = [slice(quarter * width, (quarter + 1) * width) for quarter in range(QUARTERS)]
@@ -140,6 +148,8 @@
         gate = gate + exact_dot(rows_ref[quarter], gate_ref[0, span, :])
         upward = upward + exact_dot(rows_ref[quarter], up_ref[0, span, :])
     hidden = (gate / (1.0 + jnp.exp(-gate)) * upward).astype(jnp.bfloat16)
+    if first:
+        down_copy.wait()
     for quarter, span in enumerate(spans):
         part_ref[quarter] = exact_dot(hidden, down_ref[0, :, span]).astype(jnp.bfloat16)
     back = order_matrix(capacity, True)
@@ -259,32 +269,39 @@
         compiler_params=params,
     )(in_hbm(routes.T), in_hbm(gate_codes.T), packed[0])
 
+    held_down = []
+
     def expert(offsets, held, weights):
         rows = offsets * SHARDS * capacity
+        first = not held_down
         half = jax.ShapeDtypeStruct((2 * offsets * tall, width), jnp.bfloat16)
-        return pl.pallas_call(
-            functools.partial(expert_kernel, capacity, offsets),
-            out_shape=[half] * 2,
-            in_specs=[vmem] * (offsets * 2 + 3),
-            out_specs=[vmem] * 2,
-            scratch_shapes=[pltpu.VMEM((QUARTERS, rows, width), jnp.bfloat16)] * 2,
-            compiler_params=params,
+        whole = jax.ShapeDtypeStruct(w_down.shape, w_down.dtype)
+        kept, sent, *down = pl.pallas_call(
+            functools.partial(expert_kernel, capacity, offsets, first),
+            out_shape=[half] * 2 + [whole] * first,
+            in_specs=[vmem] * (offsets * 2 + 2) + [hbm if first else vmem],
+            out_specs=[vmem] * (2 + first),
+            scratch_shapes=[pltpu.VMEM((QUARTERS, rows, width), jnp.bfloat16)] * 2
+            + [pltpu.SemaphoreType.DMA] * first,
+            compiler_params=load_params if first else params,
             cost_estimate=pl.CostEstimate(
                 flops=6 * rows * features * w_gate.shape[2],
                 bytes_accessed=0,
                 transcendentals=0,
             ),
-        )(*held, *weights)
+        )(*held, *weights, *(held_down or [in_hbm(w_down)]))
+        held_down.extend(down)
+        return kept, sent
 
     def load(gate):
         return pl.pallas_call(
             load_kernel,
-            out_shape=[jax.ShapeDtypeStruct(w.shape, w.dtype) for w in (w_gate, w_up, w_down)],
-            in_specs=[hbm] * 4,
-            out_specs=[vmem] * 3,
-            scratch_shapes=[pltpu.SemaphoreType.DMA((3,))],
+            out_shape=[jax.ShapeDtypeStruct(w.shape, w.dtype) for w in (w_gate, w_up)],
+            in_specs=[hbm] * 3,
+            out_specs=[vmem] * 2,
+            scratch_shapes=[pltpu.SemaphoreType.DMA((2,))],
             compiler_params=load_params,
-        )(in_hbm(w_gate), in_hbm(w_up), in_hbm(w_down), gate)
+        )(in_hbm(w_gate), in_hbm(w_up), gate)
 
     def fold(kept, arrived, offsets):
         middle = offsets * tall
@@ -314,7 +331,7 @@
         if kind == "z":
             inputs = result("pack " + name)
         elif kind == "y":
-            inputs = result(("pack " if name == "own" else "z ") + name)
+            inputs = result(("pack " if name == "own" or name in DIRECT else "z ") + name)
         elif kind == "c":
             own = result(("pack " if name == "own" else "z ") + name)
             inputs = [jnp.concatenate(both, axis=0) for both in zip(own, result("y " + name))]
@@ -346,7 +363,11 @@
         if kind == "load":
             return load(inputs[0])
         if kind == "expert":
+            if name != FIRST:
+                result("expert " + FIRST)
             return expert(len(places[name]), inputs, result("load all"))
+        if kind == "y" and name in DIRECT:
+            return [partner(array, at * SHARDS + 2) for array, at in zip(inputs, places[name])]
         if kind in ("y", "ry"):
             return [partner(array, 2) for array in inputs]
         if kind in ("c", "rc"):

time: 57.8 us -> 58.8 us (1.017)
  starting transfers between devices: 25.4 us -> 26.3 us
    pallas_call x1, Pallas kernels: 4.23 us -> 3.17 us  [load(): pl.pallas_call(load_kernel, out_shape=[jax.ShapeDtypeStruct(w.shape, w.dt...]
    ppermute x23, starting transfers between devices: 25.4 us -> 26.3 us  [partner(): lax.ppermute(array, 'expert', [(i, i ^ distance) for i in range(devices)])]
    pallas_call x3, Pallas kernels: 7.39 us -> 8.18 us  [expert(): pl.pallas_call(functools.partial(expert_kernel, capacity, offsets, first)...]
  transfers between devices with their start and end apart: 23 -> 23, of which waited for: 8 -> 8; matrix products, arithmetic and copies ran while one was open for 2% -> 2% of each run, Pallas kernels for 22% -> 21%
where the time goes in v8:
time: 58.8 us; the launch traced here: 58.6 us
  starting transfers between devices  26.3 us (45%)
  waiting for transfers between devices  16.2 us (28%)
  Pallas kernels  14.9 us (25%)
  other arithmetic  0.78 us (1%)
    ppermute x23, starting transfers between devices, partner(): lax.ppermute(array, 'expert', [(i, i ^ distance) for i in range(devices)])  26.3 us
    ppermute x23, waiting for transfers between devices, partner(): lax.ppermute(array, 'expert', [(i, i ^ distance) for i in range(devices)])  16.2 us
    pallas_call x3, Pallas kernels, expert(): pl.pallas_call(functools.partial(expert_kernel, capacity, offsets, first)...  8.18 us
    pallas_call x1, Pallas kernels, load(): pl.pallas_call(load_kernel, out_shape=[jax.ShapeDtypeStruct(w.shape, w.dt...  3.17 us
    pallas_call x1, Pallas kernels, shards(): pl.pallas_call(functools.partial(pack_kernel, capacity, planes), out_shap...  1.48 us
  transfers between devices with their start and end apart: 23, of which 8 were waited for; matrix products, arithmetic and copies ran while one was open for 2% of the time, Pallas kernels for 21%

profile of v8, /device:TPU:0, one launch (start us, length us, event | category | flops | bytes accessed | tf_op | source)
XLA Modules:
  0.0 58.6 jit_solution(14752866720807611747)
XLA Ops:
  0.0 1.5 %shard_map.73 = (bf16[48,1792]{1,0:T(8,128)(2,1)S(1)}, bf16[48,1792]{1,0:T(8,128)(2,1)S(1)}, bf16[48,1792]{1,0:T(8,128)(2,1)S(1)}, bf16[48,1792]{1,0:T(8,128)(2,1)S(1)}) custom-call(s32[2,16]{1,0:T(2,128)} %bitcast.2, bf16[16,7168]{1,0:T(8,128)(2,1)} %tok_hbm.1, f32[16,56]{1,0:T(8,128)} %scale_hbm.1), custom_call_target="tpu_custom_call" | custom-call | tf_op jit(solution)/shard_map/pallas_call | solution.py:248
  1.5 4.1 %collective-permute-start.6 = (bf16[48,1792]{1,0:T(8,128)(2,1)S(1)}, bf16[48,1792]{1,0:T(8,128)(2,1)S(1)}, u32[]{:S(2)}, u32[]{:S(2)}) collective-permute-start(bf16[48,1792]{1,0:T(8,128)(2,1)S(1)} %get-tuple-element.34), channel_id=1, source_target_pairs={{0,8},{1,9},{2,10},{3,11},{4,12},{5,13},{6,14},{7,15},{8,0},{9,1},... | collective-permute-start | bytes 516104 | tf_op jit(solution)/shard_map/ppermute | solution.py:245
  5.6 1.5 %collective-permute-start = (bf16[48,1792]{1,0:T(8,128)(2,1)S(1)}, bf16[48,1792]{1,0:T(8,128)(2,1)S(1)}, u32[]{:S(2)}, u32[]{:S(2)}) collective-permute-start(bf16[48,1792]{1,0:T(8,128)(2,1)S(1)} %get-tuple-element.28.unused), channel_id=1, source_target_pairs={{0,2},{1,3},{2,0},{3,1},{4,6},{5,7},{6,4},{7,5},{8,10},{9,11},{10,... | collective-permute-start | bytes 516104 | tf_op jit(solution)/shard_map/ppermute | solution.py:245
  7.1 1.6 %collective-permute-start.1 = (bf16[48,1792]{1,0:T(8,128)(2,1)S(1)}, bf16[48,1792]{1,0:T(8,128)(2,1)S(1)}, u32[]{:S(2)}, u32[]{:S(2)}) collective-permute-start(bf16[48,1792]{1,0:T(8,128)(2,1)S(1)} %get-tuple-element.30), channel_id=1, source_target_pairs={{0,4},{1,5},{2,6},{3,7},{4,0},{5,1},{6,2},{7,3},{8,12},{9,13},{10,... | collective-permute-start | bytes 516104 | tf_op jit(solution)/shard_map/ppermute | solution.py:245
  8.7 3.2 %shard_map.75 = (bf16[1,7168,256]{2,1,0:T(8,128)(2,1)S(1)}, bf16[1,7168,256]{2,1,0:T(8,128)(2,1)S(1)}) custom-call(bf16[1,7168,256]{2,1,0:T(8,128)(2,1)} %gate_hbm.1, bf16[1,7168,256]{2,1,0:T(8,128)(2,1)} %up_hbm.1, bf16[48,1792]{1,0:T(8,128)(2,1)S(1)} %get-tuple-element.28.unused), custom_call_target="tpu_custom_call" | custom-call | tf_op jit(solution)/shard_map/pallas_call | solution.py:297
  11.9 0.0 collective-permute-done
  11.9 0.9 %collective-permute-start.16 = (bf16[48,1792]{1,0:T(8,128)(2,1)S(1)}, bf16[48,1792]{1,0:T(8,128)(2,1)S(1)}, u32[]{:S(2)}, u32[]{:S(2)}) collective-permute-start(bf16[48,1792]{1,0:T(8,128)(2,1)S(1)} %get-tuple-element.42), channel_id=1, source_target_pairs={{0,12},{1,13},{2,14},{3,15},{4,8},{5,9},{6,10},{7,11},{8,4},{9,5},... | collective-permute-start | bytes 516104 | tf_op jit(solution)/shard_map/ppermute | solution.py:245
  12.8 1.0 %collective-permute-done.6 = bf16[48,1792]{1,0:T(8,128)(2,1)S(1)} collective-permute-done((bf16[48,1792]{1,0:T(8,128)(2,1)S(1)}, bf16[48,1792]{1,0:T(8,128)(2,1)S(1)}, u32[]{:S(2)}, u32[]{:S(2)}) %collective-permute-start.6) | collective-permute-done | bytes 172064 | tf_op jit(solution)/shard_map/ppermute | solution.py:245
  13.8 1.6 %collective-permute-start.7 = (bf16[48,1792]{1,0:T(8,128)(2,1)S(1)}, bf16[48,1792]{1,0:T(8,128)(2,1)S(1)}, u32[]{:S(2)}, u32[]{:S(2)}) collective-permute-start(bf16[48,1792]{1,0:T(8,128)(2,1)S(1)} %collective-permute-done.6), channel_id=1, source_target_pairs={{0,2},{1,3},{2,0},{3,1},{4,6},{5,7},{6,4},{7,5},{8,10},{9,11},{10,... | collective-permute-start | bytes 516104 | tf_op jit(solution)/shard_map/ppermute | solution.py:245
  15.3 0.1 collective-permute-start.8
  15.4 0.0 collective-permute-done.1
  15.4 0.5 collective-permute-start.3
  16.0 0.2 collective-permute-start.2
  16.1 3.1 %collective-permute-done.16 = bf16[48,1792]{1,0:T(8,128)(2,1)S(1)} collective-permute-done((bf16[48,1792]{1,0:T(8,128)(2,1)S(1)}, bf16[48,1792]{1,0:T(8,128)(2,1)S(1)}, u32[]{:S(2)}, u32[]{:S(2)}) %collective-permute-start.16) | collective-permute-done | bytes 172064 | tf_op jit(solution)/shard_map/ppermute | solution.py:245
  19.2 1.0 %collective-permute-start.17 = (bf16[48,1792]{1,0:T(8,128)(2,1)S(1)}, bf16[48,1792]{1,0:T(8,128)(2,1)S(1)}, u32[]{:S(2)}, u32[]{:S(2)}) collective-permute-start(bf16[48,1792]{1,0:T(8,128)(2,1)S(1)} %collective-permute-done.16), channel_id=1, source_target_pairs={{0,2},{1,3},{2,0},{3,1},{4,6},{5,7},{6,4},{7,5},{8,10},{9,11},{10,... | collective-permute-start | bytes 516104 | tf_op jit(solution)/shard_map/ppermute | solution.py:245
  20.2 0.0 collective-permute-done.7
  20.2 0.0 collective-permute-start.9
  20.2 3.4 %collective-permute-done.3 = bf16[48,1792]{1,0:T(8,128)(2,1)S(1)} collective-permute-done((bf16[48,1792]{1,0:T(8,128)(2,1)S(1)}, bf16[48,1792]{1,0:T(8,128)(2,1)S(1)}, u32[]{:S(2)}, u32[]{:S(2)}) %collective-permute-start.3) | collective-permute-done | bytes 172064 | tf_op jit(solution)/shard_map/ppermute | solution.py:245
  23.7 0.0 collective-permute-start.4
  23.7 0.0 collective-permute-done.2
  23.7 0.0 collective-permute-done.8
  23.7 0.0 collective-permute-done.9
  23.8 3.1 %shard_map.76 = (bf16[96,1792]{1,0:T(8,128)(2,1)S(1)}, bf16[96,1792]{1,0:T(8,128)(2,1)S(1)}, bf16[1,256,7168]{2,1,0:T(8,128)(2,1)S(1)}) custom-call(bf16[96,1792]{1,0:T(8,128)(2,1)S(1)} %pad_maximum_fusion.1.refs_0_, bf16[96,1792]{1,0:T(8,128)(2,1)S(1)} %pad_maximum_fusion.2.refs_1_, bf16[1,7168,256]{2,1,0:T(8,128)(2,1)S(1)} %get-tuple-element.32.refs_2_.refs_4_, ...), custom_call_target="tpu_custom_call" | custom-call | flops 528482304 | tf_op jit(solution)/shard_map/pallas_call | solution.py:279
  26.9 0.6 collective-permute-start.13
  27.5 0.1 collective-permute-start.14
  27.5 0.0 collective-permute-done.4
  27.6 0.5 collective-permute-start.5
  28.1 0.0 collective-permute-done.17
  28.1 0.1 collective-permute-start.18
  28.3 0.2 collective-permute-done.13
  28.5 0.4 collective-permute-done.14
  29.0 2.5 %collective-permute-start.15 = (bf16[48,1792]{1,0:T(8,128)(2,1)S(1)}, bf16[48,1792]{1,0:T(8,128)(2,1)S(1)}, u32[]{:S(2)}, u32[]{:S(2)}) collective-permute-start(bf16[48,1792]{1,0:T(8,128)(2,1)S(1)} %fusion.6), channel_id=1, source_target_pairs={{0,2},{1,3},{2,0},{3,1},{4,6},{5,7},{6,4},{7,5},{8,10},{9,11},{10,... | collective-permute-start | bytes 516104 | tf_op jit(solution)/shard_map/ppermute | solution.py:245
  31.6 0.0 collective-permute-done.5.refs_1_
  31.6 0.0 collective-permute-done.18.refs_1_
  31.6 2.3 %shard_map.78 = (bf16[96,1792]{1,0:T(8,128)(2,1)S(1)}, bf16[96,1792]{1,0:T(8,128)(2,1)S(1)}) custom-call(bf16[96,1792]{1,0:T(8,128)(2,1)S(1)} %constant_dynamic-update-slice_fusion.6.refs_0_, bf16[96,1792]{1,0:T(8,128)(2,1)S(1)} %collective-permute-done.18.refs_1_, bf16[1,7168,256]{2,1,0:T(8,128)(2,1)S(1)} %get-tuple-element.32.refs_2_.refs_4_, ...), custom_call_target="tpu_custom_call" | custom-call | flops 528482304 | tf_op jit(solution)/shard_map/pallas_call | solution.py:279
  33.9 0.1 collective-permute-start.19
  34.0 2.8 %shard_map.77 = (bf16[192,1792]{1,0:T(8,128)(2,1)S(1)}, bf16[192,1792]{1,0:T(8,128)(2,1)S(1)}) custom-call(bf16[96,1792]{1,0:T(8,128)(2,1)S(1)} %constant_dynamic-update-slice_fusion.refs_0_, bf16[96,1792]{1,0:T(8,128)(2,1)S(1)} %collective-permute-done.5.refs_1_, bf16[96,1792]{1,0:T(8,128)(2,1)S(1)} %pad_maximum_fusion.refs_2_, ...), custom_call_target="tpu_custom_call" | custom-call | flops 1056964608 | tf_op jit(solution)/shard_map/pallas_call | solution.py:279
  36.8 0.6 collective-permute-start.10
  37.3 0.0 collective-permute-done.15
  37.4 0.1 convert_element_type.45
  37.5 0.0 collective-permute-done.19
  37.7 0.8 %collective-permute-start.21 = (bf16[48,1792]{1,0:T(8,128)(2,1)S(1)}, bf16[48,1792]{1,0:T(8,128)(2,1)S(1)}, u32[]{:S(2)}, u32[]{:S(2)}) collective-permute-start(bf16[48,1792]{1,0:T(8,128)(2,1)S(1)} %fusion.3), channel_id=1, source_target_pairs={{0,2},{1,3},{2,0},{3,1},{4,6},{5,7},{6,4},{7,5},{8,10},{9,11},{10,... | collective-permute-start | bytes 516104 | tf_op jit(solution)/shard_map/ppermute | solution.py:245
  38.5 1.4 %collective-permute-start.20 = (bf16[48,1792]{1,0:T(8,128)(2,1)S(1)}, bf16[48,1792]{1,0:T(8,128)(2,1)S(1)}, u32[]{:S(2)}, u32[]{:S(2)}) collective-permute-start(bf16[48,1792]{1,0:T(8,128)(2,1)S(1)} %fusion.8), channel_id=1, source_target_pairs={{0,8},{1,9},{2,10},{3,11},{4,12},{5,13},{6,14},{7,15},{8,0},{9,1},... | collective-permute-start | bytes 516104 | tf_op jit(solution)/shard_map/ppermute | solution.py:245
  39.8 0.0 collective-permute-done.10
  39.8 0.1 convert_element_type.46
  39.9 0.1 fusion
  40.0 0.9 %collective-permute-start.11 = (bf16[96,1792]{1,0:T(8,128)(2,1)S(1)}, bf16[96,1792]{1,0:T(8,128)(2,1)S(1)}, u32[]{:S(2)}, u32[]{:S(2)}) collective-permute-start(bf16[96,1792]{1,0:T(8,128)(2,1)S(1)} %fusion), channel_id=1, source_target_pairs={{0,2},{1,3},{2,0},{3,1},{4,6},{5,7},{6,4},{7,5},{8,10},{9,11},{10,... | collective-permute-start | bytes 1032200 | tf_op jit(solution)/shard_map/ppermute | solution.py:245
  40.9 4.0 %collective-permute-done.21 = bf16[48,1792]{1,0:T(8,128)(2,1)S(1)} collective-permute-done((bf16[48,1792]{1,0:T(8,128)(2,1)S(1)}, bf16[48,1792]{1,0:T(8,128)(2,1)S(1)}, u32[]{:S(2)}, u32[]{:S(2)}) %collective-permute-start.21) | collective-permute-done | bytes 172064 | tf_op jit(solution)/shard_map/ppermute | solution.py:245
  45.0 0.1 fusion.5
  45.0 4.8 %collective-permute-start.22 = (bf16[48,1792]{1,0:T(8,128)(2,1)S(1)}, bf16[48,1792]{1,0:T(8,128)(2,1)S(1)}, u32[]{:S(2)}, u32[]{:S(2)}) collective-permute-start(bf16[48,1792]{1,0:T(8,128)(2,1)S(1)} %fusion.5), channel_id=1, source_target_pairs={{0,12},{1,13},{2,14},{3,15},{4,8},{5,9},{6,10},{7,11},{8,4},{9,5},... | collective-permute-start | bytes 516104 | tf_op jit(solution)/shard_map/ppermute | solution.py:245
  49.8 1.6 %collective-permute-done.11 = bf16[96,1792]{1,0:T(8,128)(2,1)S(1)} collective-permute-done((bf16[96,1792]{1,0:T(8,128)(2,1)S(1)}, bf16[96,1792]{1,0:T(8,128)(2,1)S(1)}, u32[]{:S(2)}, u32[]{:S(2)}) %collective-permute-start.11) | collective-permute-done | bytes 344096 | tf_op jit(solution)/shard_map/ppermute | solution.py:245
  51.4 0.1 fusion.2
  51.5 2.5 %collective-permute-start.12 = (bf16[48,1792]{1,0:T(8,128)(2,1)S(1)}, bf16[48,1792]{1,0:T(8,128)(2,1)S(1)}, u32[]{:S(2)}, u32[]{:S(2)}) collective-permute-start(bf16[48,1792]{1,0:T(8,128)(2,1)S(1)} %get-tuple-element.53), channel_id=1, source_target_pairs={{0,4},{1,5},{2,6},{3,7},{4,0},{5,1},{6,2},{7,3},{8,12},{9,13},{10,... | collective-permute-start | bytes 516104 | tf_op jit(solution)/shard_map/ppermute | solution.py:245
  54.0 1.0 %shard_map.74.plan_ref = bf16[4,128,48]{2,1,0:T(8,128)(2,1)S(1)} custom-call(s32[2,16]{1,0:T(2,128)} %bitcast.3, s32[2,16]{1,0:T(2,128)} %bitcast.4, bf16[48,1792]{1,0:T(8,128)(2,1)S(1)} %get-tuple-element.28.unused), custom_call_target="tpu_custom_call" | custom-call | tf_op jit(solution)/shard_map/pallas_call | solution.py:262
  55.0 0.0 collective-permute-done.20.refs_2_
  55.0 0.0 collective-permute-done.22.refs_3_
  55.1 2.5 %collective-permute-done.12.refs_1_ = bf16[48,1792]{1,0:T(8,128)(2,1)S(1)} collective-permute-done((bf16[48,1792]{1,0:T(8,128)(2,1)S(1)}, bf16[48,1792]{1,0:T(8,128)(2,1)S(1)}, u32[]{:S(2)}, u32[]{:S(2)}) %collective-permute-start.12) | collective-permute-done | bytes 172064 | tf_op jit(solution)/shard_map/ppermute | solution.py:245
  57.6 1.0 %shard_map.79 = bf16[16,7168]{1,0:T(8,128)(2,1)} custom-call(bf16[4,128,48]{2,1,0:T(8,128)(2,1)S(1)} %shard_map.74.plan_ref, bf16[48,1792]{1,0:T(8,128)(2,1)S(1)} %get-tuple-element.54.refs_0_, bf16[48,1792]{1,0:T(8,128)(2,1)S(1)} %collective-permute-done.12.refs_1_, bf16[48,1792]{1,0:T(8,128)(2,1)S(1)} %collective-permute-done.20.refs_2_, ...), custom_call_target="tpu_custom_call" | custom-call | tf_op jit(solution)/shard_map/pallas_call | solution.py:393
  (20 shorter events, 0.5 us)
Async XLA Ops:
  1.5 12.3 %collective-permute-start.6 = (bf16[48,1792]{1,0:T(8,128)(2,1)S(1)}, bf16[48,1792]{1,0:T(8,128)(2,1)S(1)}, u32[]{:S(2)}, u32[]{:S(2)}) collective-permute-start(bf16[48,1792]{1,0:T(8,128)(2,1)S(1)} %get-tuple-element.34), channel_id=1, source_target_pairs={{0,8},{1,9},{2,10},{3,11},{4,12},{5,13},{6,14},{7,15},{8,0},{9,1},... | collective-permute-start | bytes 516104 | tf_op jit(solution)/shard_map/ppermute | solution.py:245
  5.6 6.3 %collective-permute-start = (bf16[48,1792]{1,0:T(8,128)(2,1)S(1)}, bf16[48,1792]{1,0:T(8,128)(2,1)S(1)}, u32[]{:S(2)}, u32[]{:S(2)}) collective-permute-start(bf16[48,1792]{1,0:T(8,128)(2,1)S(1)} %get-tuple-element.28.unused), channel_id=1, source_target_pairs={{0,2},{1,3},{2,0},{3,1},{4,6},{5,7},{6,4},{7,5},{8,10},{9,11},{10,... | collective-permute-start | bytes 516104 | tf_op jit(solution)/shard_map/ppermute | solution.py:245
  7.1 8.3 %collective-permute-start.1 = (bf16[48,1792]{1,0:T(8,128)(2,1)S(1)}, bf16[48,1792]{1,0:T(8,128)(2,1)S(1)}, u32[]{:S(2)}, u32[]{:S(2)}) collective-permute-start(bf16[48,1792]{1,0:T(8,128)(2,1)S(1)} %get-tuple-element.30), channel_id=1, source_target_pairs={{0,4},{1,5},{2,6},{3,7},{4,0},{5,1},{6,2},{7,3},{8,12},{9,13},{10,... | collective-permute-start | bytes 516104 | tf_op jit(solution)/shard_map/ppermute | solution.py:245
  11.9 7.3 %collective-permute-start.16 = (bf16[48,1792]{1,0:T(8,128)(2,1)S(1)}, bf16[48,1792]{1,0:T(8,128)(2,1)S(1)}, u32[]{:S(2)}, u32[]{:S(2)}) collective-permute-start(bf16[48,1792]{1,0:T(8,128)(2,1)S(1)} %get-tuple-element.42), channel_id=1, source_target_pairs={{0,12},{1,13},{2,14},{3,15},{4,8},{5,9},{6,10},{7,11},{8,4},{9,5},... | collective-permute-start | bytes 516104 | tf_op jit(solution)/shard_map/ppermute | solution.py:245
  13.8 6.4 %collective-permute-start.7 = (bf16[48,1792]{1,0:T(8,128)(2,1)S(1)}, bf16[48,1792]{1,0:T(8,128)(2,1)S(1)}, u32[]{:S(2)}, u32[]{:S(2)}) collective-permute-start(bf16[48,1792]{1,0:T(8,128)(2,1)S(1)} %collective-permute-done.6), channel_id=1, source_target_pairs={{0,2},{1,3},{2,0},{3,1},{4,6},{5,7},{6,4},{7,5},{8,10},{9,11},{10,... | collective-permute-start | bytes 516104 | tf_op jit(solution)/shard_map/ppermute | solution.py:245
  15.3 8.4 %collective-permute-start.8 = (bf16[48,1792]{1,0:T(8,128)(2,1)S(1)}, bf16[48,1792]{1,0:T(8,128)(2,1)S(1)}, u32[]{:S(2)}, u32[]{:S(2)}) collective-permute-start(bf16[48,1792]{1,0:T(8,128)(2,1)S(1)} %collective-permute-done.6), channel_id=1, source_target_pairs={{0,1},{1,0},{2,3},{3,2},{4,5},{5,4},{6,7},{7,6},{8,9},{9,8},{10,11... | collective-permute-start | bytes 516104 | tf_op jit(solution)/shard_map/ppermute | solution.py:245
  15.4 8.2 %collective-permute-start.3 = (bf16[48,1792]{1,0:T(8,128)(2,1)S(1)}, bf16[48,1792]{1,0:T(8,128)(2,1)S(1)}, u32[]{:S(2)}, u32[]{:S(2)}) collective-permute-start(bf16[48,1792]{1,0:T(8,128)(2,1)S(1)} %collective-permute-done.1), channel_id=1, source_target_pairs={{0,2},{1,3},{2,0},{3,1},{4,6},{5,7},{6,4},{7,5},{8,10},{9,11},{10,... | collective-permute-start | bytes 516104 | tf_op jit(solution)/shard_map/ppermute | solution.py:245
  16.0 7.7 %collective-permute-start.2 = (bf16[48,1792]{1,0:T(8,128)(2,1)S(1)}, bf16[48,1792]{1,0:T(8,128)(2,1)S(1)}, u32[]{:S(2)}, u32[]{:S(2)}) collective-permute-start(bf16[48,1792]{1,0:T(8,128)(2,1)S(1)} %collective-permute-done.1), channel_id=1, source_target_pairs={{0,1},{1,0},{2,3},{3,2},{4,5},{5,4},{6,7},{7,6},{8,9},{9,8},{10,11... | collective-permute-start | bytes 516104 | tf_op jit(solution)/shard_map/ppermute | solution.py:245
  19.2 8.8 %collective-permute-start.17 = (bf16[48,1792]{1,0:T(8,128)(2,1)S(1)}, bf16[48,1792]{1,0:T(8,128)(2,1)S(1)}, u32[]{:S(2)}, u32[]{:S(2)}) collective-permute-start(bf16[48,1792]{1,0:T(8,128)(2,1)S(1)} %collective-permute-done.16), channel_id=1, source_target_pairs={{0,2},{1,3},{2,0},{3,1},{4,6},{5,7},{6,4},{7,5},{8,10},{9,11},{10,... | collective-permute-start | bytes 516104 | tf_op jit(solution)/shard_map/ppermute | solution.py:245
  20.2 3.5 %collective-permute-start.9 = (bf16[48,1792]{1,0:T(8,128)(2,1)S(1)}, bf16[48,1792]{1,0:T(8,128)(2,1)S(1)}, u32[]{:S(2)}, u32[]{:S(2)}) collective-permute-start(bf16[48,1792]{1,0:T(8,128)(2,1)S(1)} %collective-permute-done.7), channel_id=1, source_target_pairs={{0,1},{1,0},{2,3},{3,2},{4,5},{5,4},{6,7},{7,6},{8,9},{9,8},{10,11... | collective-permute-start | bytes 516104 | tf_op jit(solution)/shard_map/ppermute | solution.py:245
  23.7 3.9 %collective-permute-start.4 = (bf16[48,1792]{1,0:T(8,128)(2,1)S(1)}, bf16[48,1792]{1,0:T(8,128)(2,1)S(1)}, u32[]{:S(2)}, u32[]{:S(2)}) collective-permute-start(bf16[48,1792]{1,0:T(8,128)(2,1)S(1)} %collective-permute-done.3), channel_id=1, source_target_pairs={{0,1},{1,0},{2,3},{3,2},{4,5},{5,4},{6,7},{7,6},{8,9},{9,8},{10,11... | collective-permute-start | bytes 516104 | tf_op jit(solution)/shard_map/ppermute | solution.py:245
  26.9 1.6 %collective-permute-start.13 = (bf16[48,1792]{1,0:T(8,128)(2,1)S(1)}, bf16[48,1792]{1,0:T(8,128)(2,1)S(1)}, u32[]{:S(2)}, u32[]{:S(2)}) collective-permute-start(bf16[48,1792]{1,0:T(8,128)(2,1)S(1)} %get-tuple-element.52), channel_id=1, source_target_pairs={{0,1},{1,0},{2,3},{3,2},{4,5},{5,4},{6,7},{7,6},{8,9},{9,8},{10,11... | collective-permute-start | bytes 516104 | tf_op jit(solution)/shard_map/ppermute | solution.py:245
  27.5 1.4 %collective-permute-start.14 = (bf16[48,1792]{1,0:T(8,128)(2,1)S(1)}, bf16[48,1792]{1,0:T(8,128)(2,1)S(1)}, u32[]{:S(2)}, u32[]{:S(2)}) collective-permute-start(bf16[48,1792]{1,0:T(8,128)(2,1)S(1)} %get-tuple-element.51), channel_id=1, source_target_pairs={{0,1},{1,0},{2,3},{3,2},{4,5},{5,4},{6,7},{7,6},{8,9},{9,8},{10,11... | collective-permute-start | bytes 516104 | tf_op jit(solution)/shard_map/ppermute | solution.py:245
  27.6 4.0 %collective-permute-start.5 = (bf16[96,1792]{1,0:T(8,128)(2,1)S(1)}, bf16[96,1792]{1,0:T(8,128)(2,1)S(1)}, u32[]{:S(2)}, u32[]{:S(2)}) collective-permute-start(bf16[96,1792]{1,0:T(8,128)(2,1)S(1)} %constant_dynamic-update-slice_fusion.refs_0_), channel_id=1, source_target_pairs={{0,1},{1,0},{2,3},{3,2},{4,5},{5,4},{6,7},{7,6},{8,9},{9,8},{10,11... | collective-permute-start | bytes 1032200 | tf_op jit(solution)/shard_map/ppermute | solution.py:245
  28.1 3.5 %collective-permute-start.18 = (bf16[96,1792]{1,0:T(8,128)(2,1)S(1)}, bf16[96,1792]{1,0:T(8,128)(2,1)S(1)}, u32[]{:S(2)}, u32[]{:S(2)}) collective-permute-start(bf16[96,1792]{1,0:T(8,128)(2,1)S(1)} %constant_dynamic-update-slice_fusion.6.refs_0_), channel_id=1, source_target_pairs={{0,1},{1,0},{2,3},{3,2},{4,5},{5,4},{6,7},{7,6},{8,9},{9,8},{10,11... | collective-permute-start | bytes 1032200 | tf_op jit(solution)/shard_map/ppermute | solution.py:245
  29.0 8.4 %collective-permute-start.15 = (bf16[48,1792]{1,0:T(8,128)(2,1)S(1)}, bf16[48,1792]{1,0:T(8,128)(2,1)S(1)}, u32[]{:S(2)}, u32[]{:S(2)}) collective-permute-start(bf16[48,1792]{1,0:T(8,128)(2,1)S(1)} %fusion.6), channel_id=1, source_target_pairs={{0,2},{1,3},{2,0},{3,1},{4,6},{5,7},{6,4},{7,5},{8,10},{9,11},{10,... | collective-permute-start | bytes 516104 | tf_op jit(solution)/shard_map/ppermute | solution.py:245
  33.9 3.7 %collective-permute-start.19 = (bf16[96,1792]{1,0:T(8,128)(2,1)S(1)}, bf16[96,1792]{1,0:T(8,128)(2,1)S(1)}, u32[]{:S(2)}, u32[]{:S(2)}) collective-permute-start(bf16[96,1792]{1,0:T(8,128)(2,1)S(1)} %get-tuple-element.47), channel_id=1, source_target_pairs={{0,1},{1,0},{2,3},{3,2},{4,5},{5,4},{6,7},{7,6},{8,9},{9,8},{10,11... | collective-permute-start | bytes 1032200 | tf_op jit(solution)/shard_map/ppermute | solution.py:245
  36.8 3.1 %collective-permute-start.10 = (bf16[192,1792]{1,0:T(8,128)(2,1)S(1)}, bf16[192,1792]{1,0:T(8,128)(2,1)S(1)}, u32[]{:S(2)}, u32[]{:S(2)}) collective-permute-start(bf16[192,1792]{1,0:T(8,128)(2,1)S(1)} %get-tuple-element.37), channel_id=1, source_target_pairs={{0,1},{1,0},{2,3},{3,2},{4,5},{5,4},{6,7},{7,6},{8,9},{9,8},{10,11... | collective-permute-start | bytes 2064392 | tf_op jit(solution)/shard_map/ppermute | solution.py:245
  37.7 7.3 %collective-permute-start.21 = (bf16[48,1792]{1,0:T(8,128)(2,1)S(1)}, bf16[48,1792]{1,0:T(8,128)(2,1)S(1)}, u32[]{:S(2)}, u32[]{:S(2)}) collective-permute-start(bf16[48,1792]{1,0:T(8,128)(2,1)S(1)} %fusion.3), channel_id=1, source_target_pairs={{0,2},{1,3},{2,0},{3,1},{4,6},{5,7},{6,4},{7,5},{8,10},{9,11},{10,... | collective-permute-start | bytes 516104 | tf_op jit(solution)/shard_map/ppermute | solution.py:245
  38.5 16.6 %collective-permute-start.20 = (bf16[48,1792]{1,0:T(8,128)(2,1)S(1)}, bf16[48,1792]{1,0:T(8,128)(2,1)S(1)}, u32[]{:S(2)}, u32[]{:S(2)}) collective-permute-start(bf16[48,1792]{1,0:T(8,128)(2,1)S(1)} %fusion.8), channel_id=1, source_target_pairs={{0,8},{1,9},{2,10},{3,11},{4,12},{5,13},{6,14},{7,15},{8,0},{9,1},... | collective-permute-start | bytes 516104 | tf_op jit(solution)/shard_map/ppermute | solution.py:245
  40.0 11.4 %collective-permute-start.11 = (bf16[96,1792]{1,0:T(8,128)(2,1)S(1)}, bf16[96,1792]{1,0:T(8,128)(2,1)S(1)}, u32[]{:S(2)}, u32[]{:S(2)}) collective-permute-start(bf16[96,1792]{1,0:T(8,128)(2,1)S(1)} %fusion), channel_id=1, source_target_pairs={{0,2},{1,3},{2,0},{3,1},{4,6},{5,7},{6,4},{7,5},{8,10},{9,11},{10,... | collective-permute-start | bytes 1032200 | tf_op jit(solution)/shard_map/ppermute | solution.py:245
  45.0 10.0 %collective-permute-start.22 = (bf16[48,1792]{1,0:T(8,128)(2,1)S(1)}, bf16[48,1792]{1,0:T(8,128)(2,1)S(1)}, u32[]{:S(2)}, u32[]{:S(2)}) collective-permute-start(bf16[48,1792]{1,0:T(8,128)(2,1)S(1)} %fusion.5), channel_id=1, source_target_pairs={{0,12},{1,13},{2,14},{3,15},{4,8},{5,9},{6,10},{7,11},{8,4},{9,5},... | collective-permute-start | bytes 516104 | tf_op jit(solution)/shard_map/ppermute | solution.py:245
  51.5 6.0 %collective-permute-start.12 = (bf16[48,1792]{1,0:T(8,128)(2,1)S(1)}, bf16[48,1792]{1,0:T(8,128)(2,1)S(1)}, u32[]{:S(2)}, u32[]{:S(2)}) collective-permute-start(bf16[48,1792]{1,0:T(8,128)(2,1)S(1)} %get-tuple-element.53), channel_id=1, source_target_pairs={{0,4},{1,5},{2,6},{3,7},{4,0},{5,1},{6,2},{7,3},{8,12},{9,13},{10,... | collective-permute-start | bytes 516104 | tf_op jit(solution)/shard_map/ppermute | solution.py:245

commit v9 on v7

--- a/solution.py
+++ b/solution.py
@@ -11,13 +11,16 @@
 QUARTERS = 4
 GROUPS = ("own+near", "mid", "far")
 SPLIT = ("c mid", "c near", "rc mid",)
+DIRECT = ()
 ORDER = {
     "z far": ("y own",),
     "expert own+near": ("y own",),
-    "expert far": ("rc mid",),
+    "expert far": ("rc mid", "c own",),
+    "rz far": ("load all",),
     "c own": ("c near",),
-    "rz mid": ("rc far", "z near",),
-    "c far": ("z near", "expert mid",),
+    "rc far": ("y far",),
+    "rz mid": ("rc far",),
+    "c far": ("z near",),
     "ry own+near": ("y near",),
     "y far": ("z near",),
 }
@@ -104,12 +107,12 @@
     return zero_one(col == (block * QUARTERS + quarter) * capacity + slot)
 
 
-def load_kernel(gate_hbm, up_hbm, down_hbm, unused, gate_ref, up_ref, down_ref, sems):
+def load_kernel(gate_hbm, up_hbm, down_hbm, unused, both_ref, down_ref, sems):
+    hidden = gate_hbm.shape[2]
     copies = [
-        pltpu.make_async_copy(source, target, sems.at[index])
-        for index, (source, target) in enumerate(
-            ((gate_hbm, gate_ref), (up_hbm, up_ref), (down_hbm, down_ref))
-        )
+        pltpu.make_async_copy(gate_hbm.at[0], both_ref.at[:, pl.ds(0, hidden)], sems.at[0]),
+        pltpu.make_async_copy(up_hbm.at[0], both_ref.at[:, pl.ds(hidden, hidden)], sems.at[1]),
+        pltpu.make_async_copy(down_hbm, down_ref, sems.at[2]),
     ]
     for copy in copies:
         copy.start()
@@ -120,7 +123,7 @@
 def expert_kernel(capacity, offsets, *refs):
     count = 2 * offsets
     blocks = refs[:count]
-    gate_ref, up_ref, down_ref, kept_ref, sent_ref, rows_ref, part_ref = refs[count:]
+    both_ref, down_ref, kept_ref, sent_ref, rows_ref, part_ref = refs[count:]
     group, tall = SHARDS * capacity, QUARTERS * capacity
     width = blocks[0].shape[1]
     spans = [slice(quarter * width, (quarter + 1) * width) for quarter in range(QUARTERS)]
@@ -134,11 +137,10 @@
             rows_ref[quarter, offset * group : (offset + 1) * group, :] = sorted_rows[
                 quarter * group : (quarter + 1) * group, :
             ]
-    gate = jnp.zeros((offsets * group, gate_ref.shape[2]), jnp.float32)
-    upward = jnp.zeros((offsets * group, gate_ref.shape[2]), jnp.float32)
+    both = jnp.zeros((offsets * group, both_ref.shape[1]), jnp.float32)
     for quarter, span in enumerate(spans):
-        gate = gate + exact_dot(rows_ref[quarter], gate_ref[0, span, :])
-        upward = upward + exact_dot(rows_ref[quarter], up_ref[0, span, :])
+        both = both + exact_dot(rows_ref[quarter], both_ref[span, :])
+    gate, upward = jnp.split(both, 2, axis=1)
     hidden = (gate / (1.0 + jnp.exp(-gate)) * upward).astype(jnp.bfloat16)
     for quarter, span in enumerate(spans):
         part_ref[quarter] = exact_dot(hidden, down_ref[0, :, span]).astype(jnp.bfloat16)
@@ -265,7 +267,7 @@
         return pl.pallas_call(
             functools.partial(expert_kernel, capacity, offsets),
             out_shape=[half] * 2,
-            in_specs=[vmem] * (offsets * 2 + 3),
+            in_specs=[vmem] * (offsets * 2 + 2),
             out_specs=[vmem] * 2,
             scratch_shapes=[pltpu.VMEM((QUARTERS, rows, width), jnp.bfloat16)] * 2,
             compiler_params=params,
@@ -279,9 +281,12 @@
     def load(gate):
         return pl.pallas_call(
             load_kernel,
-            out_shape=[jax.ShapeDtypeStruct(w.shape, w.dtype) for w in (w_gate, w_up, w_down)],
+            out_shape=[
+                jax.ShapeDtypeStruct((features, 2 * w_gate.shape[2]), w_gate.dtype),
+                jax.ShapeDtypeStruct(w_down.shape, w_down.dtype),
+            ],
             in_specs=[hbm] * 4,
-            out_specs=[vmem] * 3,
+            out_specs=[vmem] * 2,
             scratch_shapes=[pltpu.SemaphoreType.DMA((3,))],
             compiler_params=load_params,
         )(in_hbm(w_gate), in_hbm(w_up), in_hbm(w_down), gate)
@@ -314,7 +319,7 @@
         if kind == "z":
             inputs = result("pack " + name)
         elif kind == "y":
-            inputs = result(("pack " if name == "own" else "z ") + name)
+            inputs = result(("pack " if name == "own" or name in DIRECT else "z ") + name)
         elif kind == "c":
             own = result(("pack " if name == "own" else "z ") + name)
             inputs = [jnp.concatenate(both, axis=0) for both in zip(own, result("y " + name))]
@@ -347,6 +352,8 @@
             return load(inputs[0])
         if kind == "expert":
             return expert(len(places[name]), inputs, result("load all"))
+        if kind == "y" and name in DIRECT:
+            return [partner(array, at * SHARDS + 2) for array, at in zip(inputs, places[name])]
         if kind in ("y", "ry"):
             return [partner(array, 2) for array in inputs]
         if kind in ("c", "rc"):

time: 57.8 us -> 58 us (level)
  no operation moved by 1% of the time
where the time goes in v9:
time: 58 us; the launch traced here: 57.8 us
  starting transfers between devices  25.3 us (44%)
  waiting for transfers between devices  16.1 us (28%)
  Pallas kernels  15.1 us (26%)
  other arithmetic  0.83 us (1%)
    ppermute x23, starting transfers between devices, partner(): lax.ppermute(array, 'expert', [(i, i ^ distance) for i in range(devices)])  25.3 us
    ppermute x23, waiting for transfers between devices, partner(): lax.ppermute(array, 'expert', [(i, i ^ distance) for i in range(devices)])  16.1 us
    pallas_call x3, Pallas kernels, expert(): pl.pallas_call(functools.partial(expert_kernel, capacity, offsets), out_s...  7.37 us
    pallas_call x1, Pallas kernels, load(): pl.pallas_call(load_kernel, out_shape=[jax.ShapeDtypeStruct((features, 2...  4.23 us
    pallas_call x1, Pallas kernels, shards(): pl.pallas_call(functools.partial(pack_kernel, capacity, planes), out_shap...  1.48 us
  transfers between devices with their start and end apart: 23, of which 8 were waited for; matrix products, arithmetic and copies ran while one was open for 2% of the time, Pallas kernels for 22%

profile of v9, /device:TPU:0, one launch (start us, length us, event | category | flops | bytes accessed | tf_op | source)
XLA Modules:
  0.0 57.8 jit_solution(4414934696166146779)
XLA Ops:
  0.0 1.5 %shard_map.73 = (bf16[48,1792]{1,0:T(8,128)(2,1)S(1)}, bf16[48,1792]{1,0:T(8,128)(2,1)S(1)}, bf16[48,1792]{1,0:T(8,128)(2,1)S(1)}, bf16[48,1792]{1,0:T(8,128)(2,1)S(1)}) custom-call(s32[2,16]{1,0:T(2,128)} %bitcast.2, bf16[16,7168]{1,0:T(8,128)(2,1)} %tok_hbm.1, f32[16,56]{1,0:T(8,128)} %scale_hbm.1), custom_call_target="tpu_custom_call" | custom-call | tf_op jit(solution)/shard_map/pallas_call | solution.py:240
  1.5 4.1 %collective-permute-start.9 = (bf16[48,1792]{1,0:T(8,128)(2,1)S(1)}, bf16[48,1792]{1,0:T(8,128)(2,1)S(1)}, u32[]{:S(2)}, u32[]{:S(2)}) collective-permute-start(bf16[48,1792]{1,0:T(8,128)(2,1)S(1)} %get-tuple-element.36), channel_id=1, source_target_pairs={{0,8},{1,9},{2,10},{3,11},{4,12},{5,13},{6,14},{7,15},{8,0},{9,1},... | collective-permute-start | bytes 516104 | tf_op jit(solution)/shard_map/ppermute | solution.py:237
  5.6 1.5 %collective-permute-start = (bf16[48,1792]{1,0:T(8,128)(2,1)S(1)}, bf16[48,1792]{1,0:T(8,128)(2,1)S(1)}, u32[]{:S(2)}, u32[]{:S(2)}) collective-permute-start(bf16[48,1792]{1,0:T(8,128)(2,1)S(1)} %get-tuple-element.27.unused), channel_id=1, source_target_pairs={{0,2},{1,3},{2,0},{3,1},{4,6},{5,7},{6,4},{7,5},{8,10},{9,11},{10,... | collective-permute-start | bytes 516104 | tf_op jit(solution)/shard_map/ppermute | solution.py:237
  7.1 1.6 %collective-permute-start.1 = (bf16[48,1792]{1,0:T(8,128)(2,1)S(1)}, bf16[48,1792]{1,0:T(8,128)(2,1)S(1)}, u32[]{:S(2)}, u32[]{:S(2)}) collective-permute-start(bf16[48,1792]{1,0:T(8,128)(2,1)S(1)} %get-tuple-element.29), channel_id=1, source_target_pairs={{0,4},{1,5},{2,6},{3,7},{4,0},{5,1},{6,2},{7,3},{8,12},{9,13},{10,... | collective-permute-start | bytes 516104 | tf_op jit(solution)/shard_map/ppermute | solution.py:237
  8.7 4.2 %shard_map.75 = (bf16[7168,512]{1,0:T(8,128)(2,1)S(1)}, bf16[1,256,7168]{2,1,0:T(8,128)(2,1)S(1)}) custom-call(bf16[1,7168,256]{2,1,0:T(8,128)(2,1)} %gate_hbm.1, bf16[1,7168,256]{2,1,0:T(8,128)(2,1)} %up_hbm.1, bf16[1,256,7168]{2,1,0:T(8,128)(2,1)} %down_hbm.1, bf16[48,1792]{1,0:T(8,128)(2,1)S(1)} %get-tuple-element.27.unused), custom_call_target="tpu_custom_call" | custom-call | tf_op jit(solution)/shard_map/pallas_call | solution.py:282
  12.9 0.0 collective-permute-done
  13.0 0.3 collective-permute-start.16
  13.2 0.5 collective-permute-done.9
  13.8 1.6 %collective-permute-start.10 = (bf16[48,1792]{1,0:T(8,128)(2,1)S(1)}, bf16[48,1792]{1,0:T(8,128)(2,1)S(1)}, u32[]{:S(2)}, u32[]{:S(2)}) collective-permute-start(bf16[48,1792]{1,0:T(8,128)(2,1)S(1)} %collective-permute-done.9), channel_id=1, source_target_pairs={{0,2},{1,3},{2,0},{3,1},{4,6},{5,7},{6,4},{7,5},{8,10},{9,11},{10,... | collective-permute-start | bytes 516104 | tf_op jit(solution)/shard_map/ppermute | solution.py:237
  15.3 0.1 collective-permute-start.11
  15.4 0.0 collective-permute-done.1
  15.4 0.5 collective-permute-start.3
  16.0 0.2 collective-permute-start.2
  16.1 4.2 %collective-permute-done.16 = bf16[48,1792]{1,0:T(8,128)(2,1)S(1)} collective-permute-done((bf16[48,1792]{1,0:T(8,128)(2,1)S(1)}, bf16[48,1792]{1,0:T(8,128)(2,1)S(1)}, u32[]{:S(2)}, u32[]{:S(2)}) %collective-permute-start.16) | collective-permute-done | bytes 172064 | tf_op jit(solution)/shard_map/ppermute | solution.py:237
  20.3 0.5 collective-permute-start.17
  20.8 0.0 collective-permute-done.10
  20.8 0.0 collective-permute-start.12
  20.8 2.9 %collective-permute-done.3 = bf16[48,1792]{1,0:T(8,128)(2,1)S(1)} collective-permute-done((bf16[48,1792]{1,0:T(8,128)(2,1)S(1)}, bf16[48,1792]{1,0:T(8,128)(2,1)S(1)}, u32[]{:S(2)}, u32[]{:S(2)}) %collective-permute-start.3) | collective-permute-done | bytes 172064 | tf_op jit(solution)/shard_map/ppermute | solution.py:237
  23.7 0.0 collective-permute-start.4
  23.7 0.0 collective-permute-done.2
  23.7 0.0 collective-permute-done.11
  23.7 0.0 collective-permute-done.12
  23.8 2.3 %shard_map.77 = (bf16[96,1792]{1,0:T(8,128)(2,1)S(1)}, bf16[96,1792]{1,0:T(8,128)(2,1)S(1)}) custom-call(bf16[96,1792]{1,0:T(8,128)(2,1)S(1)} %pad_maximum_fusion.1.refs_0_, bf16[96,1792]{1,0:T(8,128)(2,1)S(1)} %pad_maximum_fusion.2.refs_1_, bf16[7168,512]{1,0:T(8,128)(2,1)S(1)} %get-tuple-element.31.refs_4_.refs_2_, ...), custom_call_target="tpu_custom_call" | custom-call | flops 528482304 | tf_op jit(solution)/shard_map/pallas_call | solution.py:267
  26.1 0.6 collective-permute-start.13
  26.7 0.1 collective-permute-start.14
  26.8 0.0 collective-permute-done.4
  26.8 0.5 collective-permute-start.5
  27.3 0.0 collective-permute-done.17
  27.3 0.1 collective-permute-start.18
  27.5 0.2 collective-permute-done.13
  27.7 0.4 collective-permute-done.14
  28.2 2.6 %collective-permute-start.15 = (bf16[48,1792]{1,0:T(8,128)(2,1)S(1)}, bf16[48,1792]{1,0:T(8,128)(2,1)S(1)}, u32[]{:S(2)}, u32[]{:S(2)}) collective-permute-start(bf16[48,1792]{1,0:T(8,128)(2,1)S(1)} %fusion.6), channel_id=1, source_target_pairs={{0,2},{1,3},{2,0},{3,1},{4,6},{5,7},{6,4},{7,5},{8,10},{9,11},{10,... | collective-permute-start | bytes 516104 | tf_op jit(solution)/shard_map/ppermute | solution.py:237
  30.8 0.0 collective-permute-done.5.refs_1_
  30.8 0.0 collective-permute-done.18.refs_1_
  30.8 2.3 %shard_map.78 = (bf16[96,1792]{1,0:T(8,128)(2,1)S(1)}, bf16[96,1792]{1,0:T(8,128)(2,1)S(1)}) custom-call(bf16[96,1792]{1,0:T(8,128)(2,1)S(1)} %constant_dynamic-update-slice_fusion.6.refs_0_, bf16[96,1792]{1,0:T(8,128)(2,1)S(1)} %collective-permute-done.18.refs_1_, bf16[7168,512]{1,0:T(8,128)(2,1)S(1)} %get-tuple-element.31.refs_4_.refs_2_, ...), custom_call_target="tpu_custom_call" | custom-call | flops 528482304 | tf_op jit(solution)/shard_map/pallas_call | solution.py:267
  33.1 0.1 collective-permute-start.19
  33.2 2.8 %shard_map.76 = (bf16[192,1792]{1,0:T(8,128)(2,1)S(1)}, bf16[192,1792]{1,0:T(8,128)(2,1)S(1)}) custom-call(bf16[96,1792]{1,0:T(8,128)(2,1)S(1)} %constant_dynamic-update-slice_fusion.refs_0_, bf16[96,1792]{1,0:T(8,128)(2,1)S(1)} %collective-permute-done.5.refs_1_, bf16[96,1792]{1,0:T(8,128)(2,1)S(1)} %pad_maximum_fusion.refs_2_, ...), custom_call_target="tpu_custom_call" | custom-call | flops 1056964608 | tf_op jit(solution)/shard_map/pallas_call | solution.py:267
  36.0 0.6 collective-permute-start.6
  36.5 0.0 collective-permute-done.15
  36.5 0.1 fusion.8
  36.6 0.1 convert_element_type.45
  36.7 0.0 collective-permute-done.19
  36.9 0.8 %collective-permute-start.21 = (bf16[48,1792]{1,0:T(8,128)(2,1)S(1)}, bf16[48,1792]{1,0:T(8,128)(2,1)S(1)}, u32[]{:S(2)}, u32[]{:S(2)}) collective-permute-start(bf16[48,1792]{1,0:T(8,128)(2,1)S(1)} %fusion.3), channel_id=1, source_target_pairs={{0,2},{1,3},{2,0},{3,1},{4,6},{5,7},{6,4},{7,5},{8,10},{9,11},{10,... | collective-permute-start | bytes 516104 | tf_op jit(solution)/shard_map/ppermute | solution.py:237
  37.7 1.7 %collective-permute-start.20 = (bf16[48,1792]{1,0:T(8,128)(2,1)S(1)}, bf16[48,1792]{1,0:T(8,128)(2,1)S(1)}, u32[]{:S(2)}, u32[]{:S(2)}) collective-permute-start(bf16[48,1792]{1,0:T(8,128)(2,1)S(1)} %fusion.8), channel_id=1, source_target_pairs={{0,8},{1,9},{2,10},{3,11},{4,12},{5,13},{6,14},{7,15},{8,0},{9,1},... | collective-permute-start | bytes 516104 | tf_op jit(solution)/shard_map/ppermute | solution.py:237
  39.3 0.0 collective-permute-done.6
  39.3 0.1 convert_element_type.46
  39.4 0.1 fusion
  39.5 0.8 %collective-permute-start.7 = (bf16[96,1792]{1,0:T(8,128)(2,1)S(1)}, bf16[96,1792]{1,0:T(8,128)(2,1)S(1)}, u32[]{:S(2)}, u32[]{:S(2)}) collective-permute-start(bf16[96,1792]{1,0:T(8,128)(2,1)S(1)} %fusion), channel_id=1, source_target_pairs={{0,2},{1,3},{2,0},{3,1},{4,6},{5,7},{6,4},{7,5},{8,10},{9,11},{10,... | collective-permute-start | bytes 1032200 | tf_op jit(solution)/shard_map/ppermute | solution.py:237
  40.3 3.9 %collective-permute-done.21 = bf16[48,1792]{1,0:T(8,128)(2,1)S(1)} collective-permute-done((bf16[48,1792]{1,0:T(8,128)(2,1)S(1)}, bf16[48,1792]{1,0:T(8,128)(2,1)S(1)}, u32[]{:S(2)}, u32[]{:S(2)}) %collective-permute-start.21) | collective-permute-done | bytes 172064 | tf_op jit(solution)/shard_map/ppermute | solution.py:237
  44.2 4.8 %collective-permute-start.22 = (bf16[48,1792]{1,0:T(8,128)(2,1)S(1)}, bf16[48,1792]{1,0:T(8,128)(2,1)S(1)}, u32[]{:S(2)}, u32[]{:S(2)}) collective-permute-start(bf16[48,1792]{1,0:T(8,128)(2,1)S(1)} %fusion.5), channel_id=1, source_target_pairs={{0,12},{1,13},{2,14},{3,15},{4,8},{5,9},{6,10},{7,11},{8,4},{9,5},... | collective-permute-start | bytes 516104 | tf_op jit(solution)/shard_map/ppermute | solution.py:237
  49.0 1.6 %collective-permute-done.7 = bf16[96,1792]{1,0:T(8,128)(2,1)S(1)} collective-permute-done((bf16[96,1792]{1,0:T(8,128)(2,1)S(1)}, bf16[96,1792]{1,0:T(8,128)(2,1)S(1)}, u32[]{:S(2)}, u32[]{:S(2)}) %collective-permute-start.7) | collective-permute-done | bytes 344096 | tf_op jit(solution)/shard_map/ppermute | solution.py:237
  50.6 0.1 fusion.2
  50.8 2.5 %collective-permute-start.8 = (bf16[48,1792]{1,0:T(8,128)(2,1)S(1)}, bf16[48,1792]{1,0:T(8,128)(2,1)S(1)}, u32[]{:S(2)}, u32[]{:S(2)}) collective-permute-start(bf16[48,1792]{1,0:T(8,128)(2,1)S(1)} %get-tuple-element.51), channel_id=1, source_target_pairs={{0,4},{1,5},{2,6},{3,7},{4,0},{5,1},{6,2},{7,3},{8,12},{9,13},{10,... | collective-permute-start | bytes 516104 | tf_op jit(solution)/shard_map/ppermute | solution.py:237
  53.2 1.0 %shard_map.74.plan_ref = bf16[4,128,48]{2,1,0:T(8,128)(2,1)S(1)} custom-call(s32[2,16]{1,0:T(2,128)} %bitcast.3, s32[2,16]{1,0:T(2,128)} %bitcast.4, bf16[48,1792]{1,0:T(8,128)(2,1)S(1)} %get-tuple-element.27.unused), custom_call_target="tpu_custom_call" | custom-call | tf_op jit(solution)/shard_map/pallas_call | solution.py:254
  54.3 0.0 collective-permute-done.20.refs_2_
  54.3 0.0 collective-permute-done.22.refs_3_
  54.3 2.5 %collective-permute-done.8.refs_1_ = bf16[48,1792]{1,0:T(8,128)(2,1)S(1)} collective-permute-done((bf16[48,1792]{1,0:T(8,128)(2,1)S(1)}, bf16[48,1792]{1,0:T(8,128)(2,1)S(1)}, u32[]{:S(2)}, u32[]{:S(2)}) %collective-permute-start.8) | collective-permute-done | bytes 172064 | tf_op jit(solution)/shard_map/ppermute | solution.py:237
  56.8 1.0 %shard_map.79 = bf16[16,7168]{1,0:T(8,128)(2,1)} custom-call(bf16[4,128,48]{2,1,0:T(8,128)(2,1)S(1)} %shard_map.74.plan_ref, bf16[48,1792]{1,0:T(8,128)(2,1)S(1)} %get-tuple-element.52.refs_0_, bf16[48,1792]{1,0:T(8,128)(2,1)S(1)} %collective-permute-done.8.refs_1_, bf16[48,1792]{1,0:T(8,128)(2,1)S(1)} %collective-permute-done.20.refs_2_, ...), custom_call_target="tpu_custom_call" | custom-call | tf_op jit(solution)/shard_map/pallas_call | solution.py:379
  (20 shorter events, 0.5 us)
Async XLA Ops:
  1.5 12.3 %collective-permute-start.9 = (bf16[48,1792]{1,0:T(8,128)(2,1)S(1)}, bf16[48,1792]{1,0:T(8,128)(2,1)S(1)}, u32[]{:S(2)}, u32[]{:S(2)}) collective-permute-start(bf16[48,1792]{1,0:T(8,128)(2,1)S(1)} %get-tuple-element.36), channel_id=1, source_target_pairs={{0,8},{1,9},{2,10},{3,11},{4,12},{5,13},{6,14},{7,15},{8,0},{9,1},... | collective-permute-start | bytes 516104 | tf_op jit(solution)/shard_map/ppermute | solution.py:237
  5.6 7.4 %collective-permute-start = (bf16[48,1792]{1,0:T(8,128)(2,1)S(1)}, bf16[48,1792]{1,0:T(8,128)(2,1)S(1)}, u32[]{:S(2)}, u32[]{:S(2)}) collective-permute-start(bf16[48,1792]{1,0:T(8,128)(2,1)S(1)} %get-tuple-element.27.unused), channel_id=1, source_target_pairs={{0,2},{1,3},{2,0},{3,1},{4,6},{5,7},{6,4},{7,5},{8,10},{9,11},{10,... | collective-permute-start | bytes 516104 | tf_op jit(solution)/shard_map/ppermute | solution.py:237
  7.1 8.3 %collective-permute-start.1 = (bf16[48,1792]{1,0:T(8,128)(2,1)S(1)}, bf16[48,1792]{1,0:T(8,128)(2,1)S(1)}, u32[]{:S(2)}, u32[]{:S(2)}) collective-permute-start(bf16[48,1792]{1,0:T(8,128)(2,1)S(1)} %get-tuple-element.29), channel_id=1, source_target_pairs={{0,4},{1,5},{2,6},{3,7},{4,0},{5,1},{6,2},{7,3},{8,12},{9,13},{10,... | collective-permute-start | bytes 516104 | tf_op jit(solution)/shard_map/ppermute | solution.py:237
  13.0 7.3 %collective-permute-start.16 = (bf16[48,1792]{1,0:T(8,128)(2,1)S(1)}, bf16[48,1792]{1,0:T(8,128)(2,1)S(1)}, u32[]{:S(2)}, u32[]{:S(2)}) collective-permute-start(bf16[48,1792]{1,0:T(8,128)(2,1)S(1)} %get-tuple-element.40), channel_id=1, source_target_pairs={{0,12},{1,13},{2,14},{3,15},{4,8},{5,9},{6,10},{7,11},{8,4},{9,5},... | collective-permute-start | bytes 516104 | tf_op jit(solution)/shard_map/ppermute | solution.py:237
  13.8 7.0 %collective-permute-start.10 = (bf16[48,1792]{1,0:T(8,128)(2,1)S(1)}, bf16[48,1792]{1,0:T(8,128)(2,1)S(1)}, u32[]{:S(2)}, u32[]{:S(2)}) collective-permute-start(bf16[48,1792]{1,0:T(8,128)(2,1)S(1)} %collective-permute-done.9), channel_id=1, source_target_pairs={{0,2},{1,3},{2,0},{3,1},{4,6},{5,7},{6,4},{7,5},{8,10},{9,11},{10,... | collective-permute-start | bytes 516104 | tf_op jit(solution)/shard_map/ppermute | solution.py:237
  15.3 8.4 %collective-permute-start.11 = (bf16[48,1792]{1,0:T(8,128)(2,1)S(1)}, bf16[48,1792]{1,0:T(8,128)(2,1)S(1)}, u32[]{:S(2)}, u32[]{:S(2)}) collective-permute-start(bf16[48,1792]{1,0:T(8,128)(2,1)S(1)} %collective-permute-done.9), channel_id=1, source_target_pairs={{0,1},{1,0},{2,3},{3,2},{4,5},{5,4},{6,7},{7,6},{8,9},{9,8},{10,11... | collective-permute-start | bytes 516104 | tf_op jit(solution)/shard_map/ppermute | solution.py:237
  15.4 8.2 %collective-permute-start.3 = (bf16[48,1792]{1,0:T(8,128)(2,1)S(1)}, bf16[48,1792]{1,0:T(8,128)(2,1)S(1)}, u32[]{:S(2)}, u32[]{:S(2)}) collective-permute-start(bf16[48,1792]{1,0:T(8,128)(2,1)S(1)} %collective-permute-done.1), channel_id=1, source_target_pairs={{0,2},{1,3},{2,0},{3,1},{4,6},{5,7},{6,4},{7,5},{8,10},{9,11},{10,... | collective-permute-start | bytes 516104 | tf_op jit(solution)/shard_map/ppermute | solution.py:237
  16.0 7.7 %collective-permute-start.2 = (bf16[48,1792]{1,0:T(8,128)(2,1)S(1)}, bf16[48,1792]{1,0:T(8,128)(2,1)S(1)}, u32[]{:S(2)}, u32[]{:S(2)}) collective-permute-start(bf16[48,1792]{1,0:T(8,128)(2,1)S(1)} %collective-permute-done.1), channel_id=1, source_target_pairs={{0,1},{1,0},{2,3},{3,2},{4,5},{5,4},{6,7},{7,6},{8,9},{9,8},{10,11... | collective-permute-start | bytes 516104 | tf_op jit(solution)/shard_map/ppermute | solution.py:237
  20.3 7.0 %collective-permute-start.17 = (bf16[48,1792]{1,0:T(8,128)(2,1)S(1)}, bf16[48,1792]{1,0:T(8,128)(2,1)S(1)}, u32[]{:S(2)}, u32[]{:S(2)}) collective-permute-start(bf16[48,1792]{1,0:T(8,128)(2,1)S(1)} %collective-permute-done.16), channel_id=1, source_target_pairs={{0,2},{1,3},{2,0},{3,1},{4,6},{5,7},{6,4},{7,5},{8,10},{9,11},{10,... | collective-permute-start | bytes 516104 | tf_op jit(solution)/shard_map/ppermute | solution.py:237
  20.8 3.0 %collective-permute-start.12 = (bf16[48,1792]{1,0:T(8,128)(2,1)S(1)}, bf16[48,1792]{1,0:T(8,128)(2,1)S(1)}, u32[]{:S(2)}, u32[]{:S(2)}) collective-permute-start(bf16[48,1792]{1,0:T(8,128)(2,1)S(1)} %collective-permute-done.10), channel_id=1, source_target_pairs={{0,1},{1,0},{2,3},{3,2},{4,5},{5,4},{6,7},{7,6},{8,9},{9,8},{10,11... | collective-permute-start | bytes 516104 | tf_op jit(solution)/shard_map/ppermute | solution.py:237
  23.7 3.1 %collective-permute-start.4 = (bf16[48,1792]{1,0:T(8,128)(2,1)S(1)}, bf16[48,1792]{1,0:T(8,128)(2,1)S(1)}, u32[]{:S(2)}, u32[]{:S(2)}) collective-permute-start(bf16[48,1792]{1,0:T(8,128)(2,1)S(1)} %collective-permute-done.3), channel_id=1, source_target_pairs={{0,1},{1,0},{2,3},{3,2},{4,5},{5,4},{6,7},{7,6},{8,9},{9,8},{10,11... | collective-permute-start | bytes 516104 | tf_op jit(solution)/shard_map/ppermute | solution.py:237
  26.1 1.6 %collective-permute-start.13 = (bf16[48,1792]{1,0:T(8,128)(2,1)S(1)}, bf16[48,1792]{1,0:T(8,128)(2,1)S(1)}, u32[]{:S(2)}, u32[]{:S(2)}) collective-permute-start(bf16[48,1792]{1,0:T(8,128)(2,1)S(1)} %get-tuple-element.50), channel_id=1, source_target_pairs={{0,1},{1,0},{2,3},{3,2},{4,5},{5,4},{6,7},{7,6},{8,9},{9,8},{10,11... | collective-permute-start | bytes 516104 | tf_op jit(solution)/shard_map/ppermute | solution.py:237
  26.7 1.4 %collective-permute-start.14 = (bf16[48,1792]{1,0:T(8,128)(2,1)S(1)}, bf16[48,1792]{1,0:T(8,128)(2,1)S(1)}, u32[]{:S(2)}, u32[]{:S(2)}) collective-permute-start(bf16[48,1792]{1,0:T(8,128)(2,1)S(1)} %get-tuple-element.49), channel_id=1, source_target_pairs={{0,1},{1,0},{2,3},{3,2},{4,5},{5,4},{6,7},{7,6},{8,9},{9,8},{10,11... | collective-permute-start | bytes 516104 | tf_op jit(solution)/shard_map/ppermute | solution.py:237
  26.8 4.0 %collective-permute-start.5 = (bf16[96,1792]{1,0:T(8,128)(2,1)S(1)}, bf16[96,1792]{1,0:T(8,128)(2,1)S(1)}, u32[]{:S(2)}, u32[]{:S(2)}) collective-permute-start(bf16[96,1792]{1,0:T(8,128)(2,1)S(1)} %constant_dynamic-update-slice_fusion.refs_0_), channel_id=1, source_target_pairs={{0,1},{1,0},{2,3},{3,2},{4,5},{5,4},{6,7},{7,6},{8,9},{9,8},{10,11... | collective-permute-start | bytes 1032200 | tf_op jit(solution)/shard_map/ppermute | solution.py:237
  27.3 3.5 %collective-permute-start.18 = (bf16[96,1792]{1,0:T(8,128)(2,1)S(1)}, bf16[96,1792]{1,0:T(8,128)(2,1)S(1)}, u32[]{:S(2)}, u32[]{:S(2)}) collective-permute-start(bf16[96,1792]{1,0:T(8,128)(2,1)S(1)} %constant_dynamic-update-slice_fusion.6.refs_0_), channel_id=1, source_target_pairs={{0,1},{1,0},{2,3},{3,2},{4,5},{5,4},{6,7},{7,6},{8,9},{9,8},{10,11... | collective-permute-start | bytes 1032200 | tf_op jit(solution)/shard_map/ppermute | solution.py:237
  28.2 8.3 %collective-permute-start.15 = (bf16[48,1792]{1,0:T(8,128)(2,1)S(1)}, bf16[48,1792]{1,0:T(8,128)(2,1)S(1)}, u32[]{:S(2)}, u32[]{:S(2)}) collective-permute-start(bf16[48,1792]{1,0:T(8,128)(2,1)S(1)} %fusion.6), channel_id=1, source_target_pairs={{0,2},{1,3},{2,0},{3,1},{4,6},{5,7},{6,4},{7,5},{8,10},{9,11},{10,... | collective-permute-start | bytes 516104 | tf_op jit(solution)/shard_map/ppermute | solution.py:237
  33.1 3.7 %collective-permute-start.19 = (bf16[96,1792]{1,0:T(8,128)(2,1)S(1)}, bf16[96,1792]{1,0:T(8,128)(2,1)S(1)}, u32[]{:S(2)}, u32[]{:S(2)}) collective-permute-start(bf16[96,1792]{1,0:T(8,128)(2,1)S(1)} %get-tuple-element.45), channel_id=1, source_target_pairs={{0,1},{1,0},{2,3},{3,2},{4,5},{5,4},{6,7},{7,6},{8,9},{9,8},{10,11... | collective-permute-start | bytes 1032200 | tf_op jit(solution)/shard_map/ppermute | solution.py:237
  36.0 3.4 %collective-permute-start.6 = (bf16[192,1792]{1,0:T(8,128)(2,1)S(1)}, bf16[192,1792]{1,0:T(8,128)(2,1)S(1)}, u32[]{:S(2)}, u32[]{:S(2)}) collective-permute-start(bf16[192,1792]{1,0:T(8,128)(2,1)S(1)} %get-tuple-element.34), channel_id=1, source_target_pairs={{0,1},{1,0},{2,3},{3,2},{4,5},{5,4},{6,7},{7,6},{8,9},{9,8},{10,11... | collective-permute-start | bytes 2064392 | tf_op jit(solution)/shard_map/ppermute | solution.py:237
  36.9 7.3 %collective-permute-start.21 = (bf16[48,1792]{1,0:T(8,128)(2,1)S(1)}, bf16[48,1792]{1,0:T(8,128)(2,1)S(1)}, u32[]{:S(2)}, u32[]{:S(2)}) collective-permute-start(bf16[48,1792]{1,0:T(8,128)(2,1)S(1)} %fusion.3), channel_id=1, source_target_pairs={{0,2},{1,3},{2,0},{3,1},{4,6},{5,7},{6,4},{7,5},{8,10},{9,11},{10,... | collective-permute-start | bytes 516104 | tf_op jit(solution)/shard_map/ppermute | solution.py:237
  37.7 16.6 %collective-permute-start.20 = (bf16[48,1792]{1,0:T(8,128)(2,1)S(1)}, bf16[48,1792]{1,0:T(8,128)(2,1)S(1)}, u32[]{:S(2)}, u32[]{:S(2)}) collective-permute-start(bf16[48,1792]{1,0:T(8,128)(2,1)S(1)} %fusion.8), channel_id=1, source_target_pairs={{0,8},{1,9},{2,10},{3,11},{4,12},{5,13},{6,14},{7,15},{8,0},{9,1},... | collective-permute-start | bytes 516104 | tf_op jit(solution)/shard_map/ppermute | solution.py:237
  39.5 11.1 %collective-permute-start.7 = (bf16[96,1792]{1,0:T(8,128)(2,1)S(1)}, bf16[96,1792]{1,0:T(8,128)(2,1)S(1)}, u32[]{:S(2)}, u32[]{:S(2)}) collective-permute-start(bf16[96,1792]{1,0:T(8,128)(2,1)S(1)} %fusion), channel_id=1, source_target_pairs={{0,2},{1,3},{2,0},{3,1},{4,6},{5,7},{6,4},{7,5},{8,10},{9,11},{10,... | collective-permute-start | bytes 1032200 | tf_op jit(solution)/shard_map/ppermute | solution.py:237
  44.2 10.1 %collective-permute-start.22 = (bf16[48,1792]{1,0:T(8,128)(2,1)S(1)}, bf16[48,1792]{1,0:T(8,128)(2,1)S(1)}, u32[]{:S(2)}, u32[]{:S(2)}) collective-permute-start(bf16[48,1792]{1,0:T(8,128)(2,1)S(1)} %fusion.5), channel_id=1, source_target_pairs={{0,12},{1,13},{2,14},{3,15},{4,8},{5,9},{6,10},{7,11},{8,4},{9,5},... | collective-permute-start | bytes 516104 | tf_op jit(solution)/shard_map/ppermute | solution.py:237
  50.8 6.0 %collective-permute-start.8 = (bf16[48,1792]{1,0:T(8,128)(2,1)S(1)}, bf16[48,1792]{1,0:T(8,128)(2,1)S(1)}, u32[]{:S(2)}, u32[]{:S(2)}) collective-permute-start(bf16[48,1792]{1,0:T(8,128)(2,1)S(1)} %get-tuple-element.51), channel_id=1, source_target_pairs={{0,4},{1,5},{2,6},{3,7},{4,0},{5,1},{6,2},{7,3},{8,12},{9,13},{10,... | collective-permute-start | bytes 516104 | tf_op jit(solution)/shard_map/ppermute | solution.py:237

commit v10 on v7

--- a/solution.py
+++ b/solution.py
@@ -10,16 +10,17 @@
 SHARDS = 4
 QUARTERS = 4
 GROUPS = ("own+near", "mid", "far")
-SPLIT = ("c mid", "c near", "rc mid",)
+SPLIT = ("c mid", "c near",)
+DIRECT = ()
 ORDER = {
     "z far": ("y own",),
-    "expert own+near": ("y own",),
+    "expert own+near": ("c far",),
     "expert far": ("rc mid",),
-    "c own": ("c near",),
-    "rz mid": ("rc far", "z near",),
-    "c far": ("z near", "expert mid",),
-    "ry own+near": ("y near",),
+    "rz far": ("c far",),
+    "rz mid": ("rc far",),
+    "c far": ("z near",),
     "y far": ("z near",),
+    "ry mid": ("y near",),
 }
 VMEM_BYTES = 16 * 1024 * 1024
 LOAD_VMEM_BYTES = 40 * 1024 * 1024
@@ -314,7 +315,7 @@
         if kind == "z":
             inputs = result("pack " + name)
         elif kind == "y":
-            inputs = result(("pack " if name == "own" else "z ") + name)
+            inputs = result(("pack " if name == "own" or name in DIRECT else "z ") + name)
         elif kind == "c":
             own = result(("pack " if name == "own" else "z ") + name)
             inputs = [jnp.concatenate(both, axis=0) for both in zip(own, result("y " + name))]
@@ -347,6 +348,8 @@
             return load(inputs[0])
         if kind == "expert":
             return expert(len(places[name]), inputs, result("load all"))
+        if kind == "y" and name in DIRECT:
+            return [partner(array, at * SHARDS + 2) for array, at in zip(inputs, places[name])]
         if kind in ("y", "ry"):
             return [partner(array, 2) for array in inputs]
         if kind in ("c", "rc"):

time: 57.8 us -> 58.4 us (1.010)
  starting transfers between devices: 25.4 us -> 29.3 us
  waiting for transfers between devices: 15.8 us -> 12.7 us
    ppermute x23 -> x22, starting transfers between devices: 25.4 us -> 29.3 us  [partner(): lax.ppermute(array, 'expert', [(i, i ^ distance) for i in range(devices)])]
    ppermute x23 -> x22, waiting for transfers between devices: 15.8 us -> 12.7 us  [partner(): lax.ppermute(array, 'expert', [(i, i ^ distance) for i in range(devices)])]
  transfers between devices with their start and end apart: 23 -> 22, of which waited for: 8 -> 9; matrix products, arithmetic and copies ran while one was open for 2% -> 2% of each run, Pallas kernels for 22% -> 22%
where the time goes in v10:
time: 58.4 us; the launch traced here: 58.3 us
  starting transfers between devices  29.3 us (50%)
  Pallas kernels  15.1 us (26%)
  waiting for transfers between devices  12.7 us (22%)
  other arithmetic  0.86 us (1%)
    ppermute x22, starting transfers between devices, partner(): lax.ppermute(array, 'expert', [(i, i ^ distance) for i in range(devices)])  29.3 us
    ppermute x22, waiting for transfers between devices, partner(): lax.ppermute(array, 'expert', [(i, i ^ distance) for i in range(devices)])  12.7 us
    pallas_call x3, Pallas kernels, expert(): pl.pallas_call(functools.partial(expert_kernel, capacity, offsets), out_s...  7.39 us
    pallas_call x1, Pallas kernels, load(): pl.pallas_call(load_kernel, out_shape=[jax.ShapeDtypeStruct(w.shape, w.dt...  4.23 us
    pallas_call x1, Pallas kernels, shards(): pl.pallas_call(functools.partial(pack_kernel, capacity, planes), out_shap...  1.48 us
  transfers between devices with their start and end apart: 22, of which 9 were waited for; matrix products, arithmetic and copies ran while one was open for 2% of the time, Pallas kernels for 22%

profile of v10, /device:TPU:0, one launch (start us, length us, event | category | flops | bytes accessed | tf_op | source)
XLA Modules:
  0.0 58.3 jit_solution(2932746749988353750)
XLA Ops:
  0.0 1.5 %shard_map.73 = (bf16[48,1792]{1,0:T(8,128)(2,1)S(1)}, bf16[48,1792]{1,0:T(8,128)(2,1)S(1)}, bf16[48,1792]{1,0:T(8,128)(2,1)S(1)}, bf16[48,1792]{1,0:T(8,128)(2,1)S(1)}) custom-call(s32[2,16]{1,0:T(2,128)} %bitcast.2, bf16[16,7168]{1,0:T(8,128)(2,1)} %tok_hbm.1, f32[16,56]{1,0:T(8,128)} %scale_hbm.1), custom_call_target="tpu_custom_call" | custom-call | tf_op jit(solution)/shard_map/pallas_call | solution.py:239
  1.5 4.1 %collective-permute-start.12 = (bf16[48,1792]{1,0:T(8,128)(2,1)S(1)}, bf16[48,1792]{1,0:T(8,128)(2,1)S(1)}, u32[]{:S(2)}, u32[]{:S(2)}) collective-permute-start(bf16[48,1792]{1,0:T(8,128)(2,1)S(1)} %get-tuple-element.38), channel_id=1, source_target_pairs={{0,8},{1,9},{2,10},{3,11},{4,12},{5,13},{6,14},{7,15},{8,0},{9,1},... | collective-permute-start | bytes 516104 | tf_op jit(solution)/shard_map/ppermute | solution.py:236
  5.6 1.5 %collective-permute-start = (bf16[48,1792]{1,0:T(8,128)(2,1)S(1)}, bf16[48,1792]{1,0:T(8,128)(2,1)S(1)}, u32[]{:S(2)}, u32[]{:S(2)}) collective-permute-start(bf16[48,1792]{1,0:T(8,128)(2,1)S(1)} %get-tuple-element.26.unused), channel_id=1, source_target_pairs={{0,2},{1,3},{2,0},{3,1},{4,6},{5,7},{6,4},{7,5},{8,10},{9,11},{10,... | collective-permute-start | bytes 516104 | tf_op jit(solution)/shard_map/ppermute | solution.py:236
  7.1 1.6 %collective-permute-start.2 = (bf16[48,1792]{1,0:T(8,128)(2,1)S(1)}, bf16[48,1792]{1,0:T(8,128)(2,1)S(1)}, u32[]{:S(2)}, u32[]{:S(2)}) collective-permute-start(bf16[48,1792]{1,0:T(8,128)(2,1)S(1)} %get-tuple-element.29), channel_id=1, source_target_pairs={{0,4},{1,5},{2,6},{3,7},{4,0},{5,1},{6,2},{7,3},{8,12},{9,13},{10,... | collective-permute-start | bytes 516104 | tf_op jit(solution)/shard_map/ppermute | solution.py:236
  8.7 4.2 %shard_map.75 = (bf16[1,7168,256]{2,1,0:T(8,128)(2,1)S(1)}, bf16[1,7168,256]{2,1,0:T(8,128)(2,1)S(1)}, bf16[1,256,7168]{2,1,0:T(8,128)(2,1)S(1)}) custom-call(bf16[1,7168,256]{2,1,0:T(8,128)(2,1)} %gate_hbm.1, bf16[1,7168,256]{2,1,0:T(8,128)(2,1)} %up_hbm.1, bf16[1,256,7168]{2,1,0:T(8,128)(2,1)} %down_hbm.1, bf16[48,1792]{1,0:T(8,128)(2,1)S(1)} %get-tuple-element.26.unused), custom_call_target="tpu_custom_call" | custom-call | tf_op jit(solution)/shard_map/pallas_call | solution.py:281
  12.9 0.0 collective-permute-done
  13.0 0.3 collective-permute-start.1
  13.2 0.5 collective-permute-done.12
  13.8 1.6 %collective-permute-start.13 = (bf16[48,1792]{1,0:T(8,128)(2,1)S(1)}, bf16[48,1792]{1,0:T(8,128)(2,1)S(1)}, u32[]{:S(2)}, u32[]{:S(2)}) collective-permute-start(bf16[48,1792]{1,0:T(8,128)(2,1)S(1)} %collective-permute-done.12), channel_id=1, source_target_pairs={{0,2},{1,3},{2,0},{3,1},{4,6},{5,7},{6,4},{7,5},{8,10},{9,11},{10,... | collective-permute-start | bytes 516104 | tf_op jit(solution)/shard_map/ppermute | solution.py:236
  15.3 0.1 collective-permute-start.5
  15.4 0.5 collective-permute-start.14
  15.9 0.0 collective-permute-done.2
  15.9 0.5 collective-permute-start.6
  16.4 3.9 %collective-permute-done.1 = bf16[48,1792]{1,0:T(8,128)(2,1)S(1)} collective-permute-done((bf16[48,1792]{1,0:T(8,128)(2,1)S(1)}, bf16[48,1792]{1,0:T(8,128)(2,1)S(1)}, u32[]{:S(2)}, u32[]{:S(2)}) %collective-permute-start.1) | collective-permute-done | bytes 172064 | tf_op jit(solution)/shard_map/ppermute | solution.py:236
  20.3 0.0 collective-permute-start.7
  20.3 0.0 collective-permute-done.13
  20.3 2.1 %collective-permute-start.3 = (bf16[48,1792]{1,0:T(8,128)(2,1)S(1)}, bf16[48,1792]{1,0:T(8,128)(2,1)S(1)}, u32[]{:S(2)}, u32[]{:S(2)}) collective-permute-start(bf16[48,1792]{1,0:T(8,128)(2,1)S(1)} %collective-permute-done.1), channel_id=1, source_target_pairs={{0,2},{1,3},{2,0},{3,1},{4,6},{5,7},{6,4},{7,5},{8,10},{9,11},{10,... | collective-permute-start | bytes 516104 | tf_op jit(solution)/shard_map/ppermute | solution.py:236
  22.4 0.5 collective-permute-done.6
  22.9 0.0 collective-permute-start.15
  22.9 0.0 collective-permute-done.14
  22.9 0.6 collective-permute-start.8
  23.5 0.8 %collective-permute-done.15 = bf16[48,1792]{1,0:T(8,128)(2,1)S(1)} collective-permute-done((bf16[48,1792]{1,0:T(8,128)(2,1)S(1)}, bf16[48,1792]{1,0:T(8,128)(2,1)S(1)}, u32[]{:S(2)}, u32[]{:S(2)}) %collective-permute-start.15) | collective-permute-done | bytes 172064 | tf_op jit(solution)/shard_map/ppermute | solution.py:236
  24.3 2.3 %shard_map.77 = (bf16[96,1792]{1,0:T(8,128)(2,1)S(1)}, bf16[96,1792]{1,0:T(8,128)(2,1)S(1)}) custom-call(bf16[96,1792]{1,0:T(8,128)(2,1)S(1)} %pad_maximum_fusion.2.refs_0_, bf16[96,1792]{1,0:T(8,128)(2,1)S(1)} %pad_maximum_fusion.3.refs_1_, bf16[1,7168,256]{2,1,0:T(8,128)(2,1)S(1)} %get-tuple-element.33.refs_4_.refs_2_, ...), custom_call_target="tpu_custom_call" | custom-call | flops 528482304 | tf_op jit(solution)/shard_map/pallas_call | solution.py:266
  26.6 0.2 collective-permute-start.16
  26.9 0.2 collective-permute-done.3
  27.1 0.2 collective-permute-start.4
  27.4 1.0 %collective-permute-done.16 = bf16[96,1792]{1,0:T(8,128)(2,1)S(1)} collective-permute-done((bf16[96,1792]{1,0:T(8,128)(2,1)S(1)}, bf16[96,1792]{1,0:T(8,128)(2,1)S(1)}, u32[]{:S(2)}, u32[]{:S(2)}) %collective-permute-start.16) | collective-permute-done | bytes 344096 | tf_op jit(solution)/shard_map/ppermute | solution.py:236
  28.4 2.1 %collective-permute-start.17 = (bf16[48,1792]{1,0:T(8,128)(2,1)S(1)}, bf16[48,1792]{1,0:T(8,128)(2,1)S(1)}, u32[]{:S(2)}, u32[]{:S(2)}) collective-permute-start(bf16[48,1792]{1,0:T(8,128)(2,1)S(1)} %fusion.6), channel_id=1, source_target_pairs={{0,2},{1,3},{2,0},{3,1},{4,6},{5,7},{6,4},{7,5},{8,10},{9,11},{10,... | collective-permute-start | bytes 516104 | tf_op jit(solution)/shard_map/ppermute | solution.py:236
  30.5 0.0 collective-permute-done.7
  30.5 0.0 collective-permute-done.8
  30.5 0.0 collective-permute-done.4.refs_1_
  30.5 2.3 %shard_map.78 = (bf16[96,1792]{1,0:T(8,128)(2,1)S(1)}, bf16[96,1792]{1,0:T(8,128)(2,1)S(1)}) custom-call(bf16[96,1792]{1,0:T(8,128)(2,1)S(1)} %constant_dynamic-update-slice_fusion.2.refs_0_, bf16[96,1792]{1,0:T(8,128)(2,1)S(1)} %collective-permute-done.4.refs_1_, bf16[1,7168,256]{2,1,0:T(8,128)(2,1)S(1)} %get-tuple-element.33.refs_4_.refs_2_, ...), custom_call_target="tpu_custom_call" | custom-call | flops 528482304 | tf_op jit(solution)/shard_map/pallas_call | solution.py:266
  32.8 0.1 collective-permute-start.18
  33.0 0.0 collective-permute-done.5.refs_1_
  33.0 2.8 %shard_map.76 = (bf16[192,1792]{1,0:T(8,128)(2,1)S(1)}, bf16[192,1792]{1,0:T(8,128)(2,1)S(1)}) custom-call(bf16[96,1792]{1,0:T(8,128)(2,1)S(1)} %constant_dynamic-update-slice_fusion.refs_0_, bf16[96,1792]{1,0:T(8,128)(2,1)S(1)} %collective-permute-done.5.refs_1_, bf16[96,1792]{1,0:T(8,128)(2,1)S(1)} %pad_maximum_fusion.refs_2_, ...), custom_call_target="tpu_custom_call" | custom-call | flops 1056964608 | tf_op jit(solution)/shard_map/pallas_call | solution.py:266
  35.8 0.6 collective-permute-start.9
  36.4 0.1 convert_element_type.45
  36.4 0.0 collective-permute-done.17
  36.5 0.1 fusion.8
  36.5 0.0 collective-permute-done.18
  36.6 0.5 collective-permute-start.20
  37.1 2.7 %collective-permute-start.19 = (bf16[48,1792]{1,0:T(8,128)(2,1)S(1)}, bf16[48,1792]{1,0:T(8,128)(2,1)S(1)}, u32[]{:S(2)}, u32[]{:S(2)}) collective-permute-start(bf16[48,1792]{1,0:T(8,128)(2,1)S(1)} %fusion.8), channel_id=1, source_target_pairs={{0,8},{1,9},{2,10},{3,11},{4,12},{5,13},{6,14},{7,15},{8,0},{9,1},... | collective-permute-start | bytes 516104 | tf_op jit(solution)/shard_map/ppermute | solution.py:236
  39.9 0.0 collective-permute-done.9
  39.9 0.1 convert_element_type.46
  40.0 0.1 fusion
  40.0 0.7 %collective-permute-start.10 = (bf16[96,1792]{1,0:T(8,128)(2,1)S(1)}, bf16[96,1792]{1,0:T(8,128)(2,1)S(1)}, u32[]{:S(2)}, u32[]{:S(2)}) collective-permute-start(bf16[96,1792]{1,0:T(8,128)(2,1)S(1)} %fusion), channel_id=1, source_target_pairs={{0,2},{1,3},{2,0},{3,1},{4,6},{5,7},{6,4},{7,5},{8,10},{9,11},{10,... | collective-permute-start | bytes 1032200 | tf_op jit(solution)/shard_map/ppermute | solution.py:236
  40.8 2.9 %collective-permute-done.20 = bf16[48,1792]{1,0:T(8,128)(2,1)S(1)} collective-permute-done((bf16[48,1792]{1,0:T(8,128)(2,1)S(1)}, bf16[48,1792]{1,0:T(8,128)(2,1)S(1)}, u32[]{:S(2)}, u32[]{:S(2)}) %collective-permute-start.20) | collective-permute-done | bytes 172064 | tf_op jit(solution)/shard_map/ppermute | solution.py:236
  43.7 6.4 %collective-permute-start.21 = (bf16[48,1792]{1,0:T(8,128)(2,1)S(1)}, bf16[48,1792]{1,0:T(8,128)(2,1)S(1)}, u32[]{:S(2)}, u32[]{:S(2)}) collective-permute-start(bf16[48,1792]{1,0:T(8,128)(2,1)S(1)} %fusion.5), channel_id=1, source_target_pairs={{0,12},{1,13},{2,14},{3,15},{4,8},{5,9},{6,10},{7,11},{8,4},{9,5},... | collective-permute-start | bytes 516104 | tf_op jit(solution)/shard_map/ppermute | solution.py:236
  50.1 0.3 collective-permute-done.10
  50.4 0.1 fusion.2
  50.5 3.1 %collective-permute-start.11 = (bf16[48,1792]{1,0:T(8,128)(2,1)S(1)}, bf16[48,1792]{1,0:T(8,128)(2,1)S(1)}, u32[]{:S(2)}, u32[]{:S(2)}) collective-permute-start(bf16[48,1792]{1,0:T(8,128)(2,1)S(1)} %get-tuple-element.47), channel_id=1, source_target_pairs={{0,4},{1,5},{2,6},{3,7},{4,0},{5,1},{6,2},{7,3},{8,12},{9,13},{10,... | collective-permute-start | bytes 516104 | tf_op jit(solution)/shard_map/ppermute | solution.py:236
  53.6 1.0 %shard_map.74.plan_ref = bf16[4,128,48]{2,1,0:T(8,128)(2,1)S(1)} custom-call(s32[2,16]{1,0:T(2,128)} %bitcast.3, s32[2,16]{1,0:T(2,128)} %bitcast.4, bf16[48,1792]{1,0:T(8,128)(2,1)S(1)} %get-tuple-element.26.unused), custom_call_target="tpu_custom_call" | custom-call | tf_op jit(solution)/shard_map/pallas_call | solution.py:253
  54.6 0.0 collective-permute-done.19.refs_2_
  54.6 0.0 collective-permute-done.21.refs_3_
  54.7 2.6 %collective-permute-done.11.refs_1_ = bf16[48,1792]{1,0:T(8,128)(2,1)S(1)} collective-permute-done((bf16[48,1792]{1,0:T(8,128)(2,1)S(1)}, bf16[48,1792]{1,0:T(8,128)(2,1)S(1)}, u32[]{:S(2)}, u32[]{:S(2)}) %collective-permute-start.11) | collective-permute-done | bytes 172064 | tf_op jit(solution)/shard_map/ppermute | solution.py:236
  57.2 1.0 %shard_map.79 = bf16[16,7168]{1,0:T(8,128)(2,1)} custom-call(bf16[4,128,48]{2,1,0:T(8,128)(2,1)S(1)} %shard_map.74.plan_ref, bf16[48,1792]{1,0:T(8,128)(2,1)S(1)} %get-tuple-element.48.refs_0_, bf16[48,1792]{1,0:T(8,128)(2,1)S(1)} %collective-permute-done.11.refs_1_, bf16[48,1792]{1,0:T(8,128)(2,1)S(1)} %collective-permute-done.19.refs_2_, ...), custom_call_target="tpu_custom_call" | custom-call | tf_op jit(solution)/shard_map/pallas_call | solution.py:375
  (16 shorter events, 0.5 us)
Async XLA Ops:
  1.5 12.3 %collective-permute-start.12 = (bf16[48,1792]{1,0:T(8,128)(2,1)S(1)}, bf16[48,1792]{1,0:T(8,128)(2,1)S(1)}, u32[]{:S(2)}, u32[]{:S(2)}) collective-permute-start(bf16[48,1792]{1,0:T(8,128)(2,1)S(1)} %get-tuple-element.38), channel_id=1, source_target_pairs={{0,8},{1,9},{2,10},{3,11},{4,12},{5,13},{6,14},{7,15},{8,0},{9,1},... | collective-permute-start | bytes 516104 | tf_op jit(solution)/shard_map/ppermute | solution.py:236
  5.6 7.4 %collective-permute-start = (bf16[48,1792]{1,0:T(8,128)(2,1)S(1)}, bf16[48,1792]{1,0:T(8,128)(2,1)S(1)}, u32[]{:S(2)}, u32[]{:S(2)}) collective-permute-start(bf16[48,1792]{1,0:T(8,128)(2,1)S(1)} %get-tuple-element.26.unused), channel_id=1, source_target_pairs={{0,2},{1,3},{2,0},{3,1},{4,6},{5,7},{6,4},{7,5},{8,10},{9,11},{10,... | collective-permute-start | bytes 516104 | tf_op jit(solution)/shard_map/ppermute | solution.py:236
  7.1 8.8 %collective-permute-start.2 = (bf16[48,1792]{1,0:T(8,128)(2,1)S(1)}, bf16[48,1792]{1,0:T(8,128)(2,1)S(1)}, u32[]{:S(2)}, u32[]{:S(2)}) collective-permute-start(bf16[48,1792]{1,0:T(8,128)(2,1)S(1)} %get-tuple-element.29), channel_id=1, source_target_pairs={{0,4},{1,5},{2,6},{3,7},{4,0},{5,1},{6,2},{7,3},{8,12},{9,13},{10,... | collective-permute-start | bytes 516104 | tf_op jit(solution)/shard_map/ppermute | solution.py:236
  13.0 7.3 %collective-permute-start.1 = (bf16[48,1792]{1,0:T(8,128)(2,1)S(1)}, bf16[48,1792]{1,0:T(8,128)(2,1)S(1)}, u32[]{:S(2)}, u32[]{:S(2)}) collective-permute-start(bf16[48,1792]{1,0:T(8,128)(2,1)S(1)} %get-tuple-element.28), channel_id=1, source_target_pairs={{0,12},{1,13},{2,14},{3,15},{4,8},{5,9},{6,10},{7,11},{8,4},{9,5},... | collective-permute-start | bytes 516104 | tf_op jit(solution)/shard_map/ppermute | solution.py:236
  13.8 6.5 %collective-permute-start.13 = (bf16[48,1792]{1,0:T(8,128)(2,1)S(1)}, bf16[48,1792]{1,0:T(8,128)(2,1)S(1)}, u32[]{:S(2)}, u32[]{:S(2)}) collective-permute-start(bf16[48,1792]{1,0:T(8,128)(2,1)S(1)} %collective-permute-done.12), channel_id=1, source_target_pairs={{0,2},{1,3},{2,0},{3,1},{4,6},{5,7},{6,4},{7,5},{8,10},{9,11},{10,... | collective-permute-start | bytes 516104 | tf_op jit(solution)/shard_map/ppermute | solution.py:236
  15.3 17.6 %collective-permute-start.5 = (bf16[96,1792]{1,0:T(8,128)(2,1)S(1)}, bf16[96,1792]{1,0:T(8,128)(2,1)S(1)}, u32[]{:S(2)}, u32[]{:S(2)}) collective-permute-start(bf16[96,1792]{1,0:T(8,128)(2,1)S(1)} %constant_dynamic-update-slice_fusion.refs_0_), channel_id=1, source_target_pairs={{0,1},{1,0},{2,3},{3,2},{4,5},{5,4},{6,7},{7,6},{8,9},{9,8},{10,11... | collective-permute-start | bytes 1032200 | tf_op jit(solution)/shard_map/ppermute | solution.py:236
  15.4 7.5 %collective-permute-start.14 = (bf16[48,1792]{1,0:T(8,128)(2,1)S(1)}, bf16[48,1792]{1,0:T(8,128)(2,1)S(1)}, u32[]{:S(2)}, u32[]{:S(2)}) collective-permute-start(bf16[48,1792]{1,0:T(8,128)(2,1)S(1)} %collective-permute-done.12), channel_id=1, source_target_pairs={{0,1},{1,0},{2,3},{3,2},{4,5},{5,4},{6,7},{7,6},{8,9},{9,8},{10,11... | collective-permute-start | bytes 516104 | tf_op jit(solution)/shard_map/ppermute | solution.py:236
  15.9 7.0 %collective-permute-start.6 = (bf16[48,1792]{1,0:T(8,128)(2,1)S(1)}, bf16[48,1792]{1,0:T(8,128)(2,1)S(1)}, u32[]{:S(2)}, u32[]{:S(2)}) collective-permute-start(bf16[48,1792]{1,0:T(8,128)(2,1)S(1)} %collective-permute-done.2), channel_id=1, source_target_pairs={{0,2},{1,3},{2,0},{3,1},{4,6},{5,7},{6,4},{7,5},{8,10},{9,11},{10,... | collective-permute-start | bytes 516104 | tf_op jit(solution)/shard_map/ppermute | solution.py:236
  20.3 10.2 %collective-permute-start.7 = (bf16[48,1792]{1,0:T(8,128)(2,1)S(1)}, bf16[48,1792]{1,0:T(8,128)(2,1)S(1)}, u32[]{:S(2)}, u32[]{:S(2)}) collective-permute-start(bf16[48,1792]{1,0:T(8,128)(2,1)S(1)} %collective-permute-done.2), channel_id=1, source_target_pairs={{0,1},{1,0},{2,3},{3,2},{4,5},{5,4},{6,7},{7,6},{8,9},{9,8},{10,11... | collective-permute-start | bytes 516104 | tf_op jit(solution)/shard_map/ppermute | solution.py:236
  20.3 6.8 %collective-permute-start.3 = (bf16[48,1792]{1,0:T(8,128)(2,1)S(1)}, bf16[48,1792]{1,0:T(8,128)(2,1)S(1)}, u32[]{:S(2)}, u32[]{:S(2)}) collective-permute-start(bf16[48,1792]{1,0:T(8,128)(2,1)S(1)} %collective-permute-done.1), channel_id=1, source_target_pairs={{0,2},{1,3},{2,0},{3,1},{4,6},{5,7},{6,4},{7,5},{8,10},{9,11},{10,... | collective-permute-start | bytes 516104 | tf_op jit(solution)/shard_map/ppermute | solution.py:236
  22.9 1.4 %collective-permute-start.15 = (bf16[48,1792]{1,0:T(8,128)(2,1)S(1)}, bf16[48,1792]{1,0:T(8,128)(2,1)S(1)}, u32[]{:S(2)}, u32[]{:S(2)}) collective-permute-start(bf16[48,1792]{1,0:T(8,128)(2,1)S(1)} %collective-permute-done.13), channel_id=1, source_target_pairs={{0,1},{1,0},{2,3},{3,2},{4,5},{5,4},{6,7},{7,6},{8,9},{9,8},{10,11... | collective-permute-start | bytes 516104 | tf_op jit(solution)/shard_map/ppermute | solution.py:236
  22.9 7.6 %collective-permute-start.8 = (bf16[48,1792]{1,0:T(8,128)(2,1)S(1)}, bf16[48,1792]{1,0:T(8,128)(2,1)S(1)}, u32[]{:S(2)}, u32[]{:S(2)}) collective-permute-start(bf16[48,1792]{1,0:T(8,128)(2,1)S(1)} %collective-permute-done.6), channel_id=1, source_target_pairs={{0,1},{1,0},{2,3},{3,2},{4,5},{5,4},{6,7},{7,6},{8,9},{9,8},{10,11... | collective-permute-start | bytes 516104 | tf_op jit(solution)/shard_map/ppermute | solution.py:236
  26.6 1.7 %collective-permute-start.16 = (bf16[96,1792]{1,0:T(8,128)(2,1)S(1)}, bf16[96,1792]{1,0:T(8,128)(2,1)S(1)}, u32[]{:S(2)}, u32[]{:S(2)}) collective-permute-start(bf16[96,1792]{1,0:T(8,128)(2,1)S(1)} %get-tuple-element.40), channel_id=1, source_target_pairs={{0,1},{1,0},{2,3},{3,2},{4,5},{5,4},{6,7},{7,6},{8,9},{9,8},{10,11... | collective-permute-start | bytes 1032200 | tf_op jit(solution)/shard_map/ppermute | solution.py:236
  27.1 3.4 %collective-permute-start.4 = (bf16[96,1792]{1,0:T(8,128)(2,1)S(1)}, bf16[96,1792]{1,0:T(8,128)(2,1)S(1)}, u32[]{:S(2)}, u32[]{:S(2)}) collective-permute-start(bf16[96,1792]{1,0:T(8,128)(2,1)S(1)} %constant_dynamic-update-slice_fusion.2.refs_0_), channel_id=1, source_target_pairs={{0,1},{1,0},{2,3},{3,2},{4,5},{5,4},{6,7},{7,6},{8,9},{9,8},{10,11... | collective-permute-start | bytes 1032200 | tf_op jit(solution)/shard_map/ppermute | solution.py:236
  28.4 8.0 %collective-permute-start.17 = (bf16[48,1792]{1,0:T(8,128)(2,1)S(1)}, bf16[48,1792]{1,0:T(8,128)(2,1)S(1)}, u32[]{:S(2)}, u32[]{:S(2)}) collective-permute-start(bf16[48,1792]{1,0:T(8,128)(2,1)S(1)} %fusion.6), channel_id=1, source_target_pairs={{0,2},{1,3},{2,0},{3,1},{4,6},{5,7},{6,4},{7,5},{8,10},{9,11},{10,... | collective-permute-start | bytes 516104 | tf_op jit(solution)/shard_map/ppermute | solution.py:236
  32.8 3.7 %collective-permute-start.18 = (bf16[96,1792]{1,0:T(8,128)(2,1)S(1)}, bf16[96,1792]{1,0:T(8,128)(2,1)S(1)}, u32[]{:S(2)}, u32[]{:S(2)}) collective-permute-start(bf16[96,1792]{1,0:T(8,128)(2,1)S(1)} %get-tuple-element.43), channel_id=1, source_target_pairs={{0,1},{1,0},{2,3},{3,2},{4,5},{5,4},{6,7},{7,6},{8,9},{9,8},{10,11... | collective-permute-start | bytes 1032200 | tf_op jit(solution)/shard_map/ppermute | solution.py:236
  35.8 4.1 %collective-permute-start.9 = (bf16[192,1792]{1,0:T(8,128)(2,1)S(1)}, bf16[192,1792]{1,0:T(8,128)(2,1)S(1)}, u32[]{:S(2)}, u32[]{:S(2)}) collective-permute-start(bf16[192,1792]{1,0:T(8,128)(2,1)S(1)} %get-tuple-element.37), channel_id=1, source_target_pairs={{0,1},{1,0},{2,3},{3,2},{4,5},{5,4},{6,7},{7,6},{8,9},{9,8},{10,11... | collective-permute-start | bytes 2064392 | tf_op jit(solution)/shard_map/ppermute | solution.py:236
  36.6 7.0 %collective-permute-start.20 = (bf16[48,1792]{1,0:T(8,128)(2,1)S(1)}, bf16[48,1792]{1,0:T(8,128)(2,1)S(1)}, u32[]{:S(2)}, u32[]{:S(2)}) collective-permute-start(bf16[48,1792]{1,0:T(8,128)(2,1)S(1)} %fusion.3), channel_id=1, source_target_pairs={{0,2},{1,3},{2,0},{3,1},{4,6},{5,7},{6,4},{7,5},{8,10},{9,11},{10,... | collective-permute-start | bytes 516104 | tf_op jit(solution)/shard_map/ppermute | solution.py:236
  37.1 17.5 %collective-permute-start.19 = (bf16[48,1792]{1,0:T(8,128)(2,1)S(1)}, bf16[48,1792]{1,0:T(8,128)(2,1)S(1)}, u32[]{:S(2)}, u32[]{:S(2)}) collective-permute-start(bf16[48,1792]{1,0:T(8,128)(2,1)S(1)} %fusion.8), channel_id=1, source_target_pairs={{0,8},{1,9},{2,10},{3,11},{4,12},{5,13},{6,14},{7,15},{8,0},{9,1},... | collective-permute-start | bytes 516104 | tf_op jit(solution)/shard_map/ppermute | solution.py:236
  40.0 10.3 %collective-permute-start.10 = (bf16[96,1792]{1,0:T(8,128)(2,1)S(1)}, bf16[96,1792]{1,0:T(8,128)(2,1)S(1)}, u32[]{:S(2)}, u32[]{:S(2)}) collective-permute-start(bf16[96,1792]{1,0:T(8,128)(2,1)S(1)} %fusion), channel_id=1, source_target_pairs={{0,2},{1,3},{2,0},{3,1},{4,6},{5,7},{6,4},{7,5},{8,10},{9,11},{10,... | collective-permute-start | bytes 1032200 | tf_op jit(solution)/shard_map/ppermute | solution.py:236
  43.7 10.9 %collective-permute-start.21 = (bf16[48,1792]{1,0:T(8,128)(2,1)S(1)}, bf16[48,1792]{1,0:T(8,128)(2,1)S(1)}, u32[]{:S(2)}, u32[]{:S(2)}) collective-permute-start(bf16[48,1792]{1,0:T(8,128)(2,1)S(1)} %fusion.5), channel_id=1, source_target_pairs={{0,12},{1,13},{2,14},{3,15},{4,8},{5,9},{6,10},{7,11},{8,4},{9,5},... | collective-permute-start | bytes 516104 | tf_op jit(solution)/shard_map/ppermute | solution.py:236
  50.5 6.7 %collective-permute-start.11 = (bf16[48,1792]{1,0:T(8,128)(2,1)S(1)}, bf16[48,1792]{1,0:T(8,128)(2,1)S(1)}, u32[]{:S(2)}, u32[]{:S(2)}) collective-permute-start(bf16[48,1792]{1,0:T(8,128)(2,1)S(1)} %get-tuple-element.47), channel_id=1, source_target_pairs={{0,4},{1,5},{2,6},{3,7},{4,0},{5,1},{6,2},{7,3},{8,12},{9,13},{10,... | collective-permute-start | bytes 516104 | tf_op jit(solution)/shard_map/ppermute | solution.py:236

commit v11 on v7

--- a/solution.py
+++ b/solution.py
@@ -11,6 +11,7 @@
 QUARTERS = 4
 GROUPS = ("own+near", "mid", "far")
 SPLIT = ("c mid", "c near", "rc mid",)
+DIRECT = ()
 ORDER = {
     "z far": ("y own",),
     "expert own+near": ("y own",),
@@ -96,10 +97,10 @@
         outs[offset][...] = moved[offset * tall : (offset + 1) * tall, :].astype(jnp.bfloat16)
 
 
-def order_matrix(capacity, turned):
+def order_matrix(capacity):
     size = SHARDS * QUARTERS * capacity
-    row = lax.broadcasted_iota(jnp.int32, (size, size), 1 if turned else 0)
-    col = lax.broadcasted_iota(jnp.int32, (size, size), 0 if turned else 1)
+    row = lax.broadcasted_iota(jnp.int32, (size, size), 1)
+    col = lax.broadcasted_iota(jnp.int32, (size, size), 0)
     quarter, block, slot = row // (SHARDS * capacity), (row // capacity) % SHARDS, row % capacity
     return zero_one(col == (block * QUARTERS + quarter) * capacity + slot)
 
@@ -124,25 +125,26 @@
     group, tall = SHARDS * capacity, QUARTERS * capacity
     width = blocks[0].shape[1]
     spans = [slice(quarter * width, (quarter + 1) * width) for quarter in range(QUARTERS)]
-    order = order_matrix(capacity, False)
-    for offset in range(offsets):
-        held = jnp.concatenate(
-            [blocks[2 * offset][...], blocks[2 * offset + 1][...]], axis=0
-        )
-        sorted_rows = exact_dot(order, held).astype(jnp.bfloat16)
-        for quarter in range(QUARTERS):
-            rows_ref[quarter, offset * group : (offset + 1) * group, :] = sorted_rows[
-                quarter * group : (quarter + 1) * group, :
+    for index, block in enumerate(blocks):
+        rows_ref[index * 2 * tall : (index + 1) * 2 * tall, :] = block[...]
+
+    def project(weight_ref):
+        total = jnp.zeros((offsets * group, weight_ref.shape[2]), jnp.float32)
+        for quarter, span in enumerate(spans):
+            every = exact_dot(rows_ref[...], weight_ref[0, span, :])
+            starts = [
+                member * tall + quarter * capacity for member in range(offsets * SHARDS)
             ]
-    gate = jnp.zeros((offsets * group, gate_ref.shape[2]), jnp.float32)
-    upward = jnp.zeros((offsets * group, gate_ref.shape[2]), jnp.float32)
-    for quarter, span in enumerate(spans):
-        gate = gate + exact_dot(rows_ref[quarter], gate_ref[0, span, :])
-        upward = upward + exact_dot(rows_ref[quarter], up_ref[0, span, :])
+            total = total + jnp.concatenate(
+                [every[start : start + capacity, :] for start in starts], axis=0
+            )
+        return total
+
+    gate, upward = project(gate_ref), project(up_ref)
     hidden = (gate / (1.0 + jnp.exp(-gate)) * upward).astype(jnp.bfloat16)
     for quarter, span in enumerate(spans):
         part_ref[quarter] = exact_dot(hidden, down_ref[0, :, span]).astype(jnp.bfloat16)
-    back = order_matrix(capacity, True)
+    back = order_matrix(capacity)
     for offset in range(offsets):
         held = jnp.concatenate(
             [
@@ -267,7 +269,10 @@
             out_shape=[half] * 2,
             in_specs=[vmem] * (offsets * 2 + 3),
             out_specs=[vmem] * 2,
-            scratch_shapes=[pltpu.VMEM((QUARTERS, rows, width), jnp.bfloat16)] * 2,
+            scratch_shapes=[
+                pltpu.VMEM((QUARTERS * rows, width), jnp.bfloat16),
+                pltpu.VMEM((QUARTERS, rows, width), jnp.bfloat16),
+            ],
             compiler_params=params,
             cost_estimate=pl.CostEstimate(
                 flops=6 * rows * features * w_gate.shape[2],
@@ -314,7 +319,7 @@
         if kind == "z":
             inputs = result("pack " + name)
         elif kind == "y":
-            inputs = result(("pack " if name == "own" else "z ") + name)
+            inputs = result(("pack " if name == "own" or name in DIRECT else "z ") + name)
         elif kind == "c":
             own = result(("pack " if name == "own" else "z ") + name)
             inputs = [jnp.concatenate(both, axis=0) for both in zip(own, result("y " + name))]
@@ -347,6 +352,8 @@
             return load(inputs[0])
         if kind == "expert":
             return expert(len(places[name]), inputs, result("load all"))
+        if kind == "y" and name in DIRECT:
+            return [partner(array, at * SHARDS + 2) for array, at in zip(inputs, places[name])]
         if kind in ("y", "ry"):
             return [partner(array, 2) for array in inputs]
         if kind in ("c", "rc"):

time: 57.8 us -> 59.3 us (1.026)
  Pallas kernels: 15.1 us -> 16.9 us
    pallas_call x3, Pallas kernels: 7.39 us -> 9.15 us  [expert(): pl.pallas_call(functools.partial(expert_kernel, capacity, offsets), out_s...]
  transfers between devices with their start and end apart: 23 -> 23, of which waited for: 8 -> 8; matrix products, arithmetic and copies ran while one was open for 2% -> 2% of each run, Pallas kernels for 22% -> 24%
where the time goes in v11:
time: 59.3 us; the launch traced here: 59.1 us
  starting transfers between devices  25.2 us (42%)
  Pallas kernels  16.9 us (28%)
  waiting for transfers between devices  15.7 us (26%)
  other arithmetic  0.83 us (1%)
    ppermute x23, starting transfers between devices, partner(): lax.ppermute(array, 'expert', [(i, i ^ distance) for i in range(devices)])  25.2 us
    ppermute x23, waiting for transfers between devices, partner(): lax.ppermute(array, 'expert', [(i, i ^ distance) for i in range(devices)])  15.7 us
    pallas_call x3, Pallas kernels, expert(): pl.pallas_call(functools.partial(expert_kernel, capacity, offsets), out_s...  9.15 us
    pallas_call x1, Pallas kernels, load(): pl.pallas_call(load_kernel, out_shape=[jax.ShapeDtypeStruct(w.shape, w.dt...  4.23 us
    pallas_call x1, Pallas kernels, shards(): pl.pallas_call(functools.partial(pack_kernel, capacity, planes), out_shap...  1.48 us
  transfers between devices with their start and end apart: 23, of which 8 were waited for; matrix products, arithmetic and copies ran while one was open for 2% of the time, Pallas kernels for 24%

profile of v11, /device:TPU:0, one launch (start us, length us, event | category | flops | bytes accessed | tf_op | source)
XLA Modules:
  0.0 59.1 jit_solution(5657927084207769266)
XLA Ops:
  0.0 1.5 %shard_map.73 = (bf16[48,1792]{1,0:T(8,128)(2,1)S(1)}, bf16[48,1792]{1,0:T(8,128)(2,1)S(1)}, bf16[48,1792]{1,0:T(8,128)(2,1)S(1)}, bf16[48,1792]{1,0:T(8,128)(2,1)S(1)}) custom-call(s32[2,16]{1,0:T(2,128)} %bitcast.2, bf16[16,7168]{1,0:T(8,128)(2,1)} %tok_hbm.1, f32[16,56]{1,0:T(8,128)} %scale_hbm.1), custom_call_target="tpu_custom_call" | custom-call | tf_op jit(solution)/shard_map/pallas_call | solution.py:240
  1.5 4.1 %collective-permute-start.9 = (bf16[48,1792]{1,0:T(8,128)(2,1)S(1)}, bf16[48,1792]{1,0:T(8,128)(2,1)S(1)}, u32[]{:S(2)}, u32[]{:S(2)}) collective-permute-start(bf16[48,1792]{1,0:T(8,128)(2,1)S(1)} %get-tuple-element.36), channel_id=1, source_target_pairs={{0,8},{1,9},{2,10},{3,11},{4,12},{5,13},{6,14},{7,15},{8,0},{9,1},... | collective-permute-start | bytes 516104 | tf_op jit(solution)/shard_map/ppermute | solution.py:237
  5.6 1.5 %collective-permute-start = (bf16[48,1792]{1,0:T(8,128)(2,1)S(1)}, bf16[48,1792]{1,0:T(8,128)(2,1)S(1)}, u32[]{:S(2)}, u32[]{:S(2)}) collective-permute-start(bf16[48,1792]{1,0:T(8,128)(2,1)S(1)} %get-tuple-element.26.unused), channel_id=1, source_target_pairs={{0,2},{1,3},{2,0},{3,1},{4,6},{5,7},{6,4},{7,5},{8,10},{9,11},{10,... | collective-permute-start | bytes 516104 | tf_op jit(solution)/shard_map/ppermute | solution.py:237
  7.1 1.6 %collective-permute-start.1 = (bf16[48,1792]{1,0:T(8,128)(2,1)S(1)}, bf16[48,1792]{1,0:T(8,128)(2,1)S(1)}, u32[]{:S(2)}, u32[]{:S(2)}) collective-permute-start(bf16[48,1792]{1,0:T(8,128)(2,1)S(1)} %get-tuple-element.28), channel_id=1, source_target_pairs={{0,4},{1,5},{2,6},{3,7},{4,0},{5,1},{6,2},{7,3},{8,12},{9,13},{10,... | collective-permute-start | bytes 516104 | tf_op jit(solution)/shard_map/ppermute | solution.py:237
  8.7 4.2 %shard_map.75 = (bf16[1,7168,256]{2,1,0:T(8,128)(2,1)S(1)}, bf16[1,7168,256]{2,1,0:T(8,128)(2,1)S(1)}, bf16[1,256,7168]{2,1,0:T(8,128)(2,1)S(1)}) custom-call(bf16[1,7168,256]{2,1,0:T(8,128)(2,1)} %gate_hbm.1, bf16[1,7168,256]{2,1,0:T(8,128)(2,1)} %up_hbm.1, bf16[1,256,7168]{2,1,0:T(8,128)(2,1)} %down_hbm.1, bf16[48,1792]{1,0:T(8,128)(2,1)S(1)} %get-tuple-element.26.unused), custom_call_target="tpu_custom_call" | custom-call | tf_op jit(solution)/shard_map/pallas_call | solution.py:285
  12.9 0.0 collective-permute-done
  13.0 0.3 collective-permute-start.16
  13.2 0.5 collective-permute-done.9
  13.8 1.6 %collective-permute-start.10 = (bf16[48,1792]{1,0:T(8,128)(2,1)S(1)}, bf16[48,1792]{1,0:T(8,128)(2,1)S(1)}, u32[]{:S(2)}, u32[]{:S(2)}) collective-permute-start(bf16[48,1792]{1,0:T(8,128)(2,1)S(1)} %collective-permute-done.9), channel_id=1, source_target_pairs={{0,2},{1,3},{2,0},{3,1},{4,6},{5,7},{6,4},{7,5},{8,10},{9,11},{10,... | collective-permute-start | bytes 516104 | tf_op jit(solution)/shard_map/ppermute | solution.py:237
  15.3 0.1 collective-permute-start.11
  15.4 0.0 collective-permute-done.1
  15.4 0.5 collective-permute-start.3
  16.0 0.2 collective-permute-start.2
  16.1 4.2 %collective-permute-done.16 = bf16[48,1792]{1,0:T(8,128)(2,1)S(1)} collective-permute-done((bf16[48,1792]{1,0:T(8,128)(2,1)S(1)}, bf16[48,1792]{1,0:T(8,128)(2,1)S(1)}, u32[]{:S(2)}, u32[]{:S(2)}) %collective-permute-start.16) | collective-permute-done | bytes 172064 | tf_op jit(solution)/shard_map/ppermute | solution.py:237
  20.3 0.5 collective-permute-start.17
  20.8 0.0 collective-permute-done.10
  20.8 0.0 collective-permute-start.12
  20.8 2.9 %collective-permute-done.3 = bf16[48,1792]{1,0:T(8,128)(2,1)S(1)} collective-permute-done((bf16[48,1792]{1,0:T(8,128)(2,1)S(1)}, bf16[48,1792]{1,0:T(8,128)(2,1)S(1)}, u32[]{:S(2)}, u32[]{:S(2)}) %collective-permute-start.3) | collective-permute-done | bytes 172064 | tf_op jit(solution)/shard_map/ppermute | solution.py:237
  23.7 0.0 collective-permute-start.4
  23.7 0.0 collective-permute-done.2
  23.7 0.0 collective-permute-done.11
  23.7 0.0 collective-permute-done.12
  23.8 2.5 %shard_map.77 = (bf16[96,1792]{1,0:T(8,128)(2,1)S(1)}, bf16[96,1792]{1,0:T(8,128)(2,1)S(1)}) custom-call(bf16[96,1792]{1,0:T(8,128)(2,1)S(1)} %pad_maximum_fusion.1.refs_0_, bf16[96,1792]{1,0:T(8,128)(2,1)S(1)} %pad_maximum_fusion.2.refs_1_, bf16[1,7168,256]{2,1,0:T(8,128)(2,1)S(1)} %get-tuple-element.30.refs_4_.refs_2_, ...), custom_call_target="tpu_custom_call" | custom-call | flops 528482304 | tf_op jit(solution)/shard_map/pallas_call | solution.py:267
  26.4 0.6 collective-permute-start.13
  26.9 0.1 collective-permute-start.14
  27.0 0.0 collective-permute-done.17
  27.0 0.5 collective-permute-start.18
  27.6 0.0 collective-permute-done.4
  27.6 0.1 collective-permute-start.5
  27.8 0.2 collective-permute-done.13
  28.0 0.4 collective-permute-done.14
  28.5 2.5 %collective-permute-start.15 = (bf16[48,1792]{1,0:T(8,128)(2,1)S(1)}, bf16[48,1792]{1,0:T(8,128)(2,1)S(1)}, u32[]{:S(2)}, u32[]{:S(2)}) collective-permute-start(bf16[48,1792]{1,0:T(8,128)(2,1)S(1)} %fusion.6), channel_id=1, source_target_pairs={{0,2},{1,3},{2,0},{3,1},{4,6},{5,7},{6,4},{7,5},{8,10},{9,11},{10,... | collective-permute-start | bytes 516104 | tf_op jit(solution)/shard_map/ppermute | solution.py:237
  31.0 0.0 collective-permute-done.18.refs_1_
  31.0 2.5 %shard_map.78 = (bf16[96,1792]{1,0:T(8,128)(2,1)S(1)}, bf16[96,1792]{1,0:T(8,128)(2,1)S(1)}) custom-call(bf16[96,1792]{1,0:T(8,128)(2,1)S(1)} %constant_dynamic-update-slice_fusion.6.refs_0_, bf16[96,1792]{1,0:T(8,128)(2,1)S(1)} %collective-permute-done.18.refs_1_, bf16[1,7168,256]{2,1,0:T(8,128)(2,1)S(1)} %get-tuple-element.30.refs_4_.refs_2_, ...), custom_call_target="tpu_custom_call" | custom-call | flops 528482304 | tf_op jit(solution)/shard_map/pallas_call | solution.py:267
  33.6 0.1 collective-permute-start.19
  33.6 0.0 collective-permute-done.5.refs_1_
  33.7 4.1 %shard_map.76 = (bf16[192,1792]{1,0:T(8,128)(2,1)S(1)}, bf16[192,1792]{1,0:T(8,128)(2,1)S(1)}) custom-call(bf16[96,1792]{1,0:T(8,128)(2,1)S(1)} %constant_dynamic-update-slice_fusion.refs_0_, bf16[96,1792]{1,0:T(8,128)(2,1)S(1)} %collective-permute-done.5.refs_1_, bf16[96,1792]{1,0:T(8,128)(2,1)S(1)} %pad_maximum_fusion.refs_2_, ...), custom_call_target="tpu_custom_call" | custom-call | flops 1056964608 | tf_op jit(solution)/shard_map/pallas_call | solution.py:267
  37.8 0.6 collective-permute-start.6
  38.3 0.0 collective-permute-done.15
  38.3 0.1 fusion.8
  38.4 0.1 convert_element_type.45
  38.5 0.0 collective-permute-done.19
  38.6 0.3 collective-permute-start.21
  39.0 1.9 %collective-permute-start.20 = (bf16[48,1792]{1,0:T(8,128)(2,1)S(1)}, bf16[48,1792]{1,0:T(8,128)(2,1)S(1)}, u32[]{:S(2)}, u32[]{:S(2)}) collective-permute-start(bf16[48,1792]{1,0:T(8,128)(2,1)S(1)} %fusion.8), channel_id=1, source_target_pairs={{0,8},{1,9},{2,10},{3,11},{4,12},{5,13},{6,14},{7,15},{8,0},{9,1},... | collective-permute-start | bytes 516104 | tf_op jit(solution)/shard_map/ppermute | solution.py:237
  40.9 0.0 collective-permute-done.6
  40.9 0.1 convert_element_type.46
  41.0 0.1 fusion
  41.1 1.4 %collective-permute-start.7 = (bf16[96,1792]{1,0:T(8,128)(2,1)S(1)}, bf16[96,1792]{1,0:T(8,128)(2,1)S(1)}, u32[]{:S(2)}, u32[]{:S(2)}) collective-permute-start(bf16[96,1792]{1,0:T(8,128)(2,1)S(1)} %fusion), channel_id=1, source_target_pairs={{0,2},{1,3},{2,0},{3,1},{4,6},{5,7},{6,4},{7,5},{8,10},{9,11},{10,... | collective-permute-start | bytes 1032200 | tf_op jit(solution)/shard_map/ppermute | solution.py:237
  42.4 3.5 %collective-permute-done.21 = bf16[48,1792]{1,0:T(8,128)(2,1)S(1)} collective-permute-done((bf16[48,1792]{1,0:T(8,128)(2,1)S(1)}, bf16[48,1792]{1,0:T(8,128)(2,1)S(1)}, u32[]{:S(2)}, u32[]{:S(2)}) %collective-permute-start.21) | collective-permute-done | bytes 172064 | tf_op jit(solution)/shard_map/ppermute | solution.py:237
  46.0 4.8 %collective-permute-start.22 = (bf16[48,1792]{1,0:T(8,128)(2,1)S(1)}, bf16[48,1792]{1,0:T(8,128)(2,1)S(1)}, u32[]{:S(2)}, u32[]{:S(2)}) collective-permute-start(bf16[48,1792]{1,0:T(8,128)(2,1)S(1)} %fusion.5), channel_id=1, source_target_pairs={{0,12},{1,13},{2,14},{3,15},{4,8},{5,9},{6,10},{7,11},{8,4},{9,5},... | collective-permute-start | bytes 516104 | tf_op jit(solution)/shard_map/ppermute | solution.py:237
  50.8 1.6 %collective-permute-done.7 = bf16[96,1792]{1,0:T(8,128)(2,1)S(1)} collective-permute-done((bf16[96,1792]{1,0:T(8,128)(2,1)S(1)}, bf16[96,1792]{1,0:T(8,128)(2,1)S(1)}, u32[]{:S(2)}, u32[]{:S(2)}) %collective-permute-start.7) | collective-permute-done | bytes 344096 | tf_op jit(solution)/shard_map/ppermute | solution.py:237
  52.4 0.1 fusion.2
  52.5 2.0 %collective-permute-start.8 = (bf16[48,1792]{1,0:T(8,128)(2,1)S(1)}, bf16[48,1792]{1,0:T(8,128)(2,1)S(1)}, u32[]{:S(2)}, u32[]{:S(2)}) collective-permute-start(bf16[48,1792]{1,0:T(8,128)(2,1)S(1)} %get-tuple-element.49), channel_id=1, source_target_pairs={{0,4},{1,5},{2,6},{3,7},{4,0},{5,1},{6,2},{7,3},{8,12},{9,13},{10,... | collective-permute-start | bytes 516104 | tf_op jit(solution)/shard_map/ppermute | solution.py:237
  54.5 1.0 %shard_map.74.plan_ref = bf16[4,128,48]{2,1,0:T(8,128)(2,1)S(1)} custom-call(s32[2,16]{1,0:T(2,128)} %bitcast.3, s32[2,16]{1,0:T(2,128)} %bitcast.4, bf16[48,1792]{1,0:T(8,128)(2,1)S(1)} %get-tuple-element.26.unused), custom_call_target="tpu_custom_call" | custom-call | tf_op jit(solution)/shard_map/pallas_call | solution.py:254
  55.6 0.0 collective-permute-done.20.refs_2_
  55.6 0.0 collective-permute-done.22.refs_3_
  55.6 2.5 %collective-permute-done.8.refs_1_ = bf16[48,1792]{1,0:T(8,128)(2,1)S(1)} collective-permute-done((bf16[48,1792]{1,0:T(8,128)(2,1)S(1)}, bf16[48,1792]{1,0:T(8,128)(2,1)S(1)}, u32[]{:S(2)}, u32[]{:S(2)}) %collective-permute-start.8) | collective-permute-done | bytes 172064 | tf_op jit(solution)/shard_map/ppermute | solution.py:237
  58.1 1.0 %shard_map.79 = bf16[16,7168]{1,0:T(8,128)(2,1)} custom-call(bf16[4,128,48]{2,1,0:T(8,128)(2,1)S(1)} %shard_map.74.plan_ref, bf16[48,1792]{1,0:T(8,128)(2,1)S(1)} %get-tuple-element.50.refs_0_, bf16[48,1792]{1,0:T(8,128)(2,1)S(1)} %collective-permute-done.8.refs_1_, bf16[48,1792]{1,0:T(8,128)(2,1)S(1)} %collective-permute-done.20.refs_2_, ...), custom_call_target="tpu_custom_call" | custom-call | tf_op jit(solution)/shard_map/pallas_call | solution.py:379
  (20 shorter events, 0.5 us)
Async XLA Ops:
  1.5 12.3 %collective-permute-start.9 = (bf16[48,1792]{1,0:T(8,128)(2,1)S(1)}, bf16[48,1792]{1,0:T(8,128)(2,1)S(1)}, u32[]{:S(2)}, u32[]{:S(2)}) collective-permute-start(bf16[48,1792]{1,0:T(8,128)(2,1)S(1)} %get-tuple-element.36), channel_id=1, source_target_pairs={{0,8},{1,9},{2,10},{3,11},{4,12},{5,13},{6,14},{7,15},{8,0},{9,1},... | collective-permute-start | bytes 516104 | tf_op jit(solution)/shard_map/ppermute | solution.py:237
  5.6 7.4 %collective-permute-start = (bf16[48,1792]{1,0:T(8,128)(2,1)S(1)}, bf16[48,1792]{1,0:T(8,128)(2,1)S(1)}, u32[]{:S(2)}, u32[]{:S(2)}) collective-permute-start(bf16[48,1792]{1,0:T(8,128)(2,1)S(1)} %get-tuple-element.26.unused), channel_id=1, source_target_pairs={{0,2},{1,3},{2,0},{3,1},{4,6},{5,7},{6,4},{7,5},{8,10},{9,11},{10,... | collective-permute-start | bytes 516104 | tf_op jit(solution)/shard_map/ppermute | solution.py:237
  7.1 8.3 %collective-permute-start.1 = (bf16[48,1792]{1,0:T(8,128)(2,1)S(1)}, bf16[48,1792]{1,0:T(8,128)(2,1)S(1)}, u32[]{:S(2)}, u32[]{:S(2)}) collective-permute-start(bf16[48,1792]{1,0:T(8,128)(2,1)S(1)} %get-tuple-element.28), channel_id=1, source_target_pairs={{0,4},{1,5},{2,6},{3,7},{4,0},{5,1},{6,2},{7,3},{8,12},{9,13},{10,... | collective-permute-start | bytes 516104 | tf_op jit(solution)/shard_map/ppermute | solution.py:237
  13.0 7.3 %collective-permute-start.16 = (bf16[48,1792]{1,0:T(8,128)(2,1)S(1)}, bf16[48,1792]{1,0:T(8,128)(2,1)S(1)}, u32[]{:S(2)}, u32[]{:S(2)}) collective-permute-start(bf16[48,1792]{1,0:T(8,128)(2,1)S(1)} %get-tuple-element.40), channel_id=1, source_target_pairs={{0,12},{1,13},{2,14},{3,15},{4,8},{5,9},{6,10},{7,11},{8,4},{9,5},... | collective-permute-start | bytes 516104 | tf_op jit(solution)/shard_map/ppermute | solution.py:237
  13.8 7.0 %collective-permute-start.10 = (bf16[48,1792]{1,0:T(8,128)(2,1)S(1)}, bf16[48,1792]{1,0:T(8,128)(2,1)S(1)}, u32[]{:S(2)}, u32[]{:S(2)}) collective-permute-start(bf16[48,1792]{1,0:T(8,128)(2,1)S(1)} %collective-permute-done.9), channel_id=1, source_target_pairs={{0,2},{1,3},{2,0},{3,1},{4,6},{5,7},{6,4},{7,5},{8,10},{9,11},{10,... | collective-permute-start | bytes 516104 | tf_op jit(solution)/shard_map/ppermute | solution.py:237
  15.3 8.4 %collective-permute-start.11 = (bf16[48,1792]{1,0:T(8,128)(2,1)S(1)}, bf16[48,1792]{1,0:T(8,128)(2,1)S(1)}, u32[]{:S(2)}, u32[]{:S(2)}) collective-permute-start(bf16[48,1792]{1,0:T(8,128)(2,1)S(1)} %collective-permute-done.9), channel_id=1, source_target_pairs={{0,1},{1,0},{2,3},{3,2},{4,5},{5,4},{6,7},{7,6},{8,9},{9,8},{10,11... | collective-permute-start | bytes 516104 | tf_op jit(solution)/shard_map/ppermute | solution.py:237
  15.4 8.2 %collective-permute-start.3 = (bf16[48,1792]{1,0:T(8,128)(2,1)S(1)}, bf16[48,1792]{1,0:T(8,128)(2,1)S(1)}, u32[]{:S(2)}, u32[]{:S(2)}) collective-permute-start(bf16[48,1792]{1,0:T(8,128)(2,1)S(1)} %collective-permute-done.1), channel_id=1, source_target_pairs={{0,2},{1,3},{2,0},{3,1},{4,6},{5,7},{6,4},{7,5},{8,10},{9,11},{10,... | collective-permute-start | bytes 516104 | tf_op jit(solution)/shard_map/ppermute | solution.py:237
  16.0 7.7 %collective-permute-start.2 = (bf16[48,1792]{1,0:T(8,128)(2,1)S(1)}, bf16[48,1792]{1,0:T(8,128)(2,1)S(1)}, u32[]{:S(2)}, u32[]{:S(2)}) collective-permute-start(bf16[48,1792]{1,0:T(8,128)(2,1)S(1)} %collective-permute-done.1), channel_id=1, source_target_pairs={{0,1},{1,0},{2,3},{3,2},{4,5},{5,4},{6,7},{7,6},{8,9},{9,8},{10,11... | collective-permute-start | bytes 516104 | tf_op jit(solution)/shard_map/ppermute | solution.py:237
  20.3 6.7 %collective-permute-start.17 = (bf16[48,1792]{1,0:T(8,128)(2,1)S(1)}, bf16[48,1792]{1,0:T(8,128)(2,1)S(1)}, u32[]{:S(2)}, u32[]{:S(2)}) collective-permute-start(bf16[48,1792]{1,0:T(8,128)(2,1)S(1)} %collective-permute-done.16), channel_id=1, source_target_pairs={{0,2},{1,3},{2,0},{3,1},{4,6},{5,7},{6,4},{7,5},{8,10},{9,11},{10,... | collective-permute-start | bytes 516104 | tf_op jit(solution)/shard_map/ppermute | solution.py:237
  20.8 3.0 %collective-permute-start.12 = (bf16[48,1792]{1,0:T(8,128)(2,1)S(1)}, bf16[48,1792]{1,0:T(8,128)(2,1)S(1)}, u32[]{:S(2)}, u32[]{:S(2)}) collective-permute-start(bf16[48,1792]{1,0:T(8,128)(2,1)S(1)} %collective-permute-done.10), channel_id=1, source_target_pairs={{0,1},{1,0},{2,3},{3,2},{4,5},{5,4},{6,7},{7,6},{8,9},{9,8},{10,11... | collective-permute-start | bytes 516104 | tf_op jit(solution)/shard_map/ppermute | solution.py:237
  23.7 3.9 %collective-permute-start.4 = (bf16[48,1792]{1,0:T(8,128)(2,1)S(1)}, bf16[48,1792]{1,0:T(8,128)(2,1)S(1)}, u32[]{:S(2)}, u32[]{:S(2)}) collective-permute-start(bf16[48,1792]{1,0:T(8,128)(2,1)S(1)} %collective-permute-done.3), channel_id=1, source_target_pairs={{0,1},{1,0},{2,3},{3,2},{4,5},{5,4},{6,7},{7,6},{8,9},{9,8},{10,11... | collective-permute-start | bytes 516104 | tf_op jit(solution)/shard_map/ppermute | solution.py:237
  26.4 1.6 %collective-permute-start.13 = (bf16[48,1792]{1,0:T(8,128)(2,1)S(1)}, bf16[48,1792]{1,0:T(8,128)(2,1)S(1)}, u32[]{:S(2)}, u32[]{:S(2)}) collective-permute-start(bf16[48,1792]{1,0:T(8,128)(2,1)S(1)} %get-tuple-element.48), channel_id=1, source_target_pairs={{0,1},{1,0},{2,3},{3,2},{4,5},{5,4},{6,7},{7,6},{8,9},{9,8},{10,11... | collective-permute-start | bytes 516104 | tf_op jit(solution)/shard_map/ppermute | solution.py:237
  26.9 1.4 %collective-permute-start.14 = (bf16[48,1792]{1,0:T(8,128)(2,1)S(1)}, bf16[48,1792]{1,0:T(8,128)(2,1)S(1)}, u32[]{:S(2)}, u32[]{:S(2)}) collective-permute-start(bf16[48,1792]{1,0:T(8,128)(2,1)S(1)} %get-tuple-element.47), channel_id=1, source_target_pairs={{0,1},{1,0},{2,3},{3,2},{4,5},{5,4},{6,7},{7,6},{8,9},{9,8},{10,11... | collective-permute-start | bytes 516104 | tf_op jit(solution)/shard_map/ppermute | solution.py:237
  27.0 4.0 %collective-permute-start.18 = (bf16[96,1792]{1,0:T(8,128)(2,1)S(1)}, bf16[96,1792]{1,0:T(8,128)(2,1)S(1)}, u32[]{:S(2)}, u32[]{:S(2)}) collective-permute-start(bf16[96,1792]{1,0:T(8,128)(2,1)S(1)} %constant_dynamic-update-slice_fusion.6.refs_0_), channel_id=1, source_target_pairs={{0,1},{1,0},{2,3},{3,2},{4,5},{5,4},{6,7},{7,6},{8,9},{9,8},{10,11... | collective-permute-start | bytes 1032200 | tf_op jit(solution)/shard_map/ppermute | solution.py:237
  27.6 6.0 %collective-permute-start.5 = (bf16[96,1792]{1,0:T(8,128)(2,1)S(1)}, bf16[96,1792]{1,0:T(8,128)(2,1)S(1)}, u32[]{:S(2)}, u32[]{:S(2)}) collective-permute-start(bf16[96,1792]{1,0:T(8,128)(2,1)S(1)} %constant_dynamic-update-slice_fusion.refs_0_), channel_id=1, source_target_pairs={{0,1},{1,0},{2,3},{3,2},{4,5},{5,4},{6,7},{7,6},{8,9},{9,8},{10,11... | collective-permute-start | bytes 1032200 | tf_op jit(solution)/shard_map/ppermute | solution.py:237
  28.5 9.9 %collective-permute-start.15 = (bf16[48,1792]{1,0:T(8,128)(2,1)S(1)}, bf16[48,1792]{1,0:T(8,128)(2,1)S(1)}, u32[]{:S(2)}, u32[]{:S(2)}) collective-permute-start(bf16[48,1792]{1,0:T(8,128)(2,1)S(1)} %fusion.6), channel_id=1, source_target_pairs={{0,2},{1,3},{2,0},{3,1},{4,6},{5,7},{6,4},{7,5},{8,10},{9,11},{10,... | collective-permute-start | bytes 516104 | tf_op jit(solution)/shard_map/ppermute | solution.py:237
  33.6 5.0 %collective-permute-start.19 = (bf16[96,1792]{1,0:T(8,128)(2,1)S(1)}, bf16[96,1792]{1,0:T(8,128)(2,1)S(1)}, u32[]{:S(2)}, u32[]{:S(2)}) collective-permute-start(bf16[96,1792]{1,0:T(8,128)(2,1)S(1)} %get-tuple-element.44), channel_id=1, source_target_pairs={{0,1},{1,0},{2,3},{3,2},{4,5},{5,4},{6,7},{7,6},{8,9},{9,8},{10,11... | collective-permute-start | bytes 1032200 | tf_op jit(solution)/shard_map/ppermute | solution.py:237
  37.8 3.1 %collective-permute-start.6 = (bf16[192,1792]{1,0:T(8,128)(2,1)S(1)}, bf16[192,1792]{1,0:T(8,128)(2,1)S(1)}, u32[]{:S(2)}, u32[]{:S(2)}) collective-permute-start(bf16[192,1792]{1,0:T(8,128)(2,1)S(1)} %get-tuple-element.34), channel_id=1, source_target_pairs={{0,1},{1,0},{2,3},{3,2},{4,5},{5,4},{6,7},{7,6},{8,9},{9,8},{10,11... | collective-permute-start | bytes 2064392 | tf_op jit(solution)/shard_map/ppermute | solution.py:237
  38.6 7.3 %collective-permute-start.21 = (bf16[48,1792]{1,0:T(8,128)(2,1)S(1)}, bf16[48,1792]{1,0:T(8,128)(2,1)S(1)}, u32[]{:S(2)}, u32[]{:S(2)}) collective-permute-start(bf16[48,1792]{1,0:T(8,128)(2,1)S(1)} %fusion.3), channel_id=1, source_target_pairs={{0,2},{1,3},{2,0},{3,1},{4,6},{5,7},{6,4},{7,5},{8,10},{9,11},{10,... | collective-permute-start | bytes 516104 | tf_op jit(solution)/shard_map/ppermute | solution.py:237
  39.0 16.6 %collective-permute-start.20 = (bf16[48,1792]{1,0:T(8,128)(2,1)S(1)}, bf16[48,1792]{1,0:T(8,128)(2,1)S(1)}, u32[]{:S(2)}, u32[]{:S(2)}) collective-permute-start(bf16[48,1792]{1,0:T(8,128)(2,1)S(1)} %fusion.8), channel_id=1, source_target_pairs={{0,8},{1,9},{2,10},{3,11},{4,12},{5,13},{6,14},{7,15},{8,0},{9,1},... | collective-permute-start | bytes 516104 | tf_op jit(solution)/shard_map/ppermute | solution.py:237
  41.1 11.3 %collective-permute-start.7 = (bf16[96,1792]{1,0:T(8,128)(2,1)S(1)}, bf16[96,1792]{1,0:T(8,128)(2,1)S(1)}, u32[]{:S(2)}, u32[]{:S(2)}) collective-permute-start(bf16[96,1792]{1,0:T(8,128)(2,1)S(1)} %fusion), channel_id=1, source_target_pairs={{0,2},{1,3},{2,0},{3,1},{4,6},{5,7},{6,4},{7,5},{8,10},{9,11},{10,... | collective-permute-start | bytes 1032200 | tf_op jit(solution)/shard_map/ppermute | solution.py:237
  46.0 9.6 %collective-permute-start.22 = (bf16[48,1792]{1,0:T(8,128)(2,1)S(1)}, bf16[48,1792]{1,0:T(8,128)(2,1)S(1)}, u32[]{:S(2)}, u32[]{:S(2)}) collective-permute-start(bf16[48,1792]{1,0:T(8,128)(2,1)S(1)} %fusion.5), channel_id=1, source_target_pairs={{0,12},{1,13},{2,14},{3,15},{4,8},{5,9},{6,10},{7,11},{8,4},{9,5},... | collective-permute-start | bytes 516104 | tf_op jit(solution)/shard_map/ppermute | solution.py:237
  52.5 5.6 %collective-permute-start.8 = (bf16[48,1792]{1,0:T(8,128)(2,1)S(1)}, bf16[48,1792]{1,0:T(8,128)(2,1)S(1)}, u32[]{:S(2)}, u32[]{:S(2)}) collective-permute-start(bf16[48,1792]{1,0:T(8,128)(2,1)S(1)} %get-tuple-element.49), channel_id=1, source_target_pairs={{0,4},{1,5},{2,6},{3,7},{4,0},{5,1},{6,2},{7,3},{8,12},{9,13},{10,... | collective-permute-start | bytes 516104 | tf_op jit(solution)/shard_map/ppermute | solution.py:237

commit v12 on v10

--- a/solution.py
+++ b/solution.py
@@ -9,18 +9,25 @@
 
 SHARDS = 4
 QUARTERS = 4
-GROUPS = ("own+near", "mid", "far")
-SPLIT = ("c mid", "c near",)
+GROUPS = ("own", "near", "mid", "far")
+SPLIT = ("c mid",)
 DIRECT = ()
 ORDER = {
-    "z far": ("y own",),
-    "expert own+near": ("c far",),
-    "expert far": ("rc mid",),
-    "rz far": ("c far",),
-    "rz mid": ("rc far",),
-    "c far": ("z near",),
-    "y far": ("z near",),
-    "ry mid": ("y near",),
+    "z mid": ("z near",),
+    "y far": ("z far",),
+    "expert far": ("z near",),
+    "rc far": ("load all",),
+    "expert near": ("c mid",),
+    "c mid": ("rc far",),
+    "rc near": ("z far",),
+    "expert mid": ("expert near",),
+    "ry near": ("c far", "y near", "z far",),
+    "rc mid": ("expert near", "z mid",),
+    "c own": ("rc near", "z mid", "rc mid",),
+    "rz far": ("rc far", "ry far", "expert mid",),
+    "ry mid": ("load all",),
+    "rz near": ("rc own", "y far", "y own",),
+    "rc own": ("c mid",),
 }
 VMEM_BYTES = 16 * 1024 * 1024
 LOAD_VMEM_BYTES = 40 * 1024 * 1024
@@ -58,7 +65,8 @@
         copy.start()
     rows, features = tok_ref.shape
     picks, width = route_ref.shape[0], features // QUARTERS
-    copies[0].wait()
+    for copy in copies:
+        copy.wait()
     plane = lax.axis_index("expert") // SHARDS
     columns = QUARTERS * rows
     numbers = lax.broadcasted_iota(jnp.int32, (planes, columns), 0)
@@ -83,8 +91,6 @@
         )
         for offset in range(planes)
     ]
-    copies[1].wait()
-    copies[2].wait()
     for block in range(features // 128):
         quarter, at = divmod(block * 128, width)
         codes = tok_ref[:, block * 128 : (block + 1) * 128].astype(jnp.float32)

time: 58.4 us -> 60.1 us (1.029)
  starting transfers between devices: 29.3 us -> 20.5 us
  waiting for transfers between devices: 12.7 us -> 21.3 us
  Pallas kernels: 15.1 us -> 16.9 us
    ppermute x22 -> x23, starting transfers between devices: 29.3 us -> 20.5 us  [partner(): lax.ppermute(array, 'expert', [(i, i ^ distance) for i in range(devices)])]
    ppermute x22 -> x23, waiting for transfers between devices: 12.7 us -> 21.3 us  [partner(): lax.ppermute(array, 'expert', [(i, i ^ distance) for i in range(devices)])]
    pallas_call x3 -> x4, Pallas kernels: 7.39 us -> 9.15 us  [expert(): pl.pallas_call(functools.partial(expert_kernel, capacity, offsets), out_s...]
  transfers between devices with their start and end apart: 22 -> 23, of which waited for: 9 -> 13; matrix products, arithmetic and copies ran while one was open for 2% -> 1% of each run, Pallas kernels for 22% -> 24%
where the time goes in v12:
time: 60.1 us; the launch traced here: 59.9 us
  waiting for transfers between devices  21.3 us (35%)
  starting transfers between devices  20.5 us (34%)
  Pallas kernels  16.9 us (28%)
  other arithmetic  0.76 us (1%)
    ppermute x23, waiting for transfers between devices, partner(): lax.ppermute(array, 'expert', [(i, i ^ distance) for i in range(devices)])  21.3 us
    ppermute x23, starting transfers between devices, partner(): lax.ppermute(array, 'expert', [(i, i ^ distance) for i in range(devices)])  20.5 us
    pallas_call x4, Pallas kernels, expert(): pl.pallas_call(functools.partial(expert_kernel, capacity, offsets), out_s...  9.15 us
    pallas_call x1, Pallas kernels, load(): pl.pallas_call(load_kernel, out_shape=[jax.ShapeDtypeStruct(w.shape, w.dt...  4.23 us
    pallas_call x1, Pallas kernels, shards(): pl.pallas_call(functools.partial(pack_kernel, capacity, planes), out_shap...  1.48 us
  transfers between devices with their start and end apart: 23, of which 13 were waited for; matrix products, arithmetic and copies ran while one was open for 1% of the time, Pallas kernels for 24%

profile of v12, /device:TPU:0, one launch (start us, length us, event | category | flops | bytes accessed | tf_op | source)
XLA Modules:
  0.0 59.9 jit_solution(13861484144576234283)
XLA Ops:
  0.0 1.5 %shard_map.73 = (bf16[48,1792]{1,0:T(8,128)(2,1)S(1)}, bf16[48,1792]{1,0:T(8,128)(2,1)S(1)}, bf16[48,1792]{1,0:T(8,128)(2,1)S(1)}, bf16[48,1792]{1,0:T(8,128)(2,1)S(1)}) custom-call(s32[2,16]{1,0:T(2,128)} %bitcast.2, bf16[16,7168]{1,0:T(8,128)(2,1)} %tok_hbm.1, f32[16,56]{1,0:T(8,128)} %scale_hbm.1), custom_call_target="tpu_custom_call" | custom-call | tf_op jit(solution)/shard_map/pallas_call | solution.py:245
  1.5 5.1 %collective-permute-start.6 = (bf16[48,1792]{1,0:T(8,128)(2,1)S(1)}, bf16[48,1792]{1,0:T(8,128)(2,1)S(1)}, u32[]{:S(2)}, u32[]{:S(2)}) collective-permute-start(bf16[48,1792]{1,0:T(8,128)(2,1)S(1)} %get-tuple-element.39), channel_id=1, source_target_pairs={{0,12},{1,13},{2,14},{3,15},{4,8},{5,9},{6,10},{7,11},{8,4},{9,5},... | collective-permute-start | bytes 516104 | tf_op jit(solution)/shard_map/ppermute | solution.py:242
  6.6 0.0 collective-permute-start.1
  6.6 1.5 %collective-permute-start = (bf16[48,1792]{1,0:T(8,128)(2,1)S(1)}, bf16[48,1792]{1,0:T(8,128)(2,1)S(1)}, u32[]{:S(2)}, u32[]{:S(2)}) collective-permute-start(bf16[48,1792]{1,0:T(8,128)(2,1)S(1)} %get-tuple-element.35.unused), channel_id=1, source_target_pairs={{0,2},{1,3},{2,0},{3,1},{4,6},{5,7},{6,4},{7,5},{8,10},{9,11},{10,... | collective-permute-start | bytes 516104 | tf_op jit(solution)/shard_map/ppermute | solution.py:242
  8.1 1.0 %shard_map.74.plan_ref = bf16[4,128,48]{2,1,0:T(8,128)(2,1)S(1)} custom-call(s32[2,16]{1,0:T(2,128)} %bitcast.3, s32[2,16]{1,0:T(2,128)} %bitcast.4, bf16[48,1792]{1,0:T(8,128)(2,1)S(1)} %get-tuple-element.35.unused), custom_call_target="tpu_custom_call" | custom-call | tf_op jit(solution)/shard_map/pallas_call | solution.py:259
  9.2 4.2 %shard_map.75 = (bf16[1,7168,256]{2,1,0:T(8,128)(2,1)S(1)}, bf16[1,7168,256]{2,1,0:T(8,128)(2,1)S(1)}, bf16[1,256,7168]{2,1,0:T(8,128)(2,1)S(1)}) custom-call(bf16[1,7168,256]{2,1,0:T(8,128)(2,1)} %gate_hbm.1, bf16[1,7168,256]{2,1,0:T(8,128)(2,1)} %up_hbm.1, bf16[1,256,7168]{2,1,0:T(8,128)(2,1)} %down_hbm.1, bf16[48,1792]{1,0:T(8,128)(2,1)S(1)} %get-tuple-element.35.unused), custom_call_target="tpu_custom_call" | custom-call | tf_op jit(solution)/shard_map/pallas_call | solution.py:287
  13.4 0.0 collective-permute-done.6
  13.4 0.6 collective-permute-start.7
  14.0 0.8 %collective-permute-done.1 = bf16[48,1792]{1,0:T(8,128)(2,1)S(1)} collective-permute-done((bf16[48,1792]{1,0:T(8,128)(2,1)S(1)}, bf16[48,1792]{1,0:T(8,128)(2,1)S(1)}, u32[]{:S(2)}, u32[]{:S(2)}) %collective-permute-start.1) | collective-permute-done | bytes 172064 | tf_op jit(solution)/shard_map/ppermute | solution.py:242
  14.8 2.2 %collective-permute-start.3 = (bf16[48,1792]{1,0:T(8,128)(2,1)S(1)}, bf16[48,1792]{1,0:T(8,128)(2,1)S(1)}, u32[]{:S(2)}, u32[]{:S(2)}) collective-permute-start(bf16[48,1792]{1,0:T(8,128)(2,1)S(1)} %get-tuple-element.38), channel_id=1, source_target_pairs={{0,8},{1,9},{2,10},{3,11},{4,12},{5,13},{6,14},{7,15},{8,0},{9,1},... | collective-permute-start | bytes 516104 | tf_op jit(solution)/shard_map/ppermute | solution.py:242
  16.9 0.6 collective-permute-start.2
  17.5 0.0 collective-permute-done
  17.6 3.1 %collective-permute-done.7 = bf16[48,1792]{1,0:T(8,128)(2,1)S(1)} collective-permute-done((bf16[48,1792]{1,0:T(8,128)(2,1)S(1)}, bf16[48,1792]{1,0:T(8,128)(2,1)S(1)}, u32[]{:S(2)}, u32[]{:S(2)}) %collective-permute-start.7) | collective-permute-done | bytes 172064 | tf_op jit(solution)/shard_map/ppermute | solution.py:242
  20.7 0.1 collective-permute-start.8
  20.7 2.0 %collective-permute-done.2 = bf16[48,1792]{1,0:T(8,128)(2,1)S(1)} collective-permute-done((bf16[48,1792]{1,0:T(8,128)(2,1)S(1)}, bf16[48,1792]{1,0:T(8,128)(2,1)S(1)}, u32[]{:S(2)}, u32[]{:S(2)}) %collective-permute-start.2) | collective-permute-done | bytes 172064 | tf_op jit(solution)/shard_map/ppermute | solution.py:242
  22.8 0.1 collective-permute-start.11
  22.8 2.8 %collective-permute-done.3 = bf16[48,1792]{1,0:T(8,128)(2,1)S(1)} collective-permute-done((bf16[48,1792]{1,0:T(8,128)(2,1)S(1)}, bf16[48,1792]{1,0:T(8,128)(2,1)S(1)}, u32[]{:S(2)}, u32[]{:S(2)}) %collective-permute-start.3) | collective-permute-done | bytes 172064 | tf_op jit(solution)/shard_map/ppermute | solution.py:242
  25.7 1.5 %collective-permute-start.5 = (bf16[48,1792]{1,0:T(8,128)(2,1)S(1)}, bf16[48,1792]{1,0:T(8,128)(2,1)S(1)}, u32[]{:S(2)}, u32[]{:S(2)}) collective-permute-start(bf16[48,1792]{1,0:T(8,128)(2,1)S(1)} %collective-permute-done.3), channel_id=1, source_target_pairs={{0,2},{1,3},{2,0},{3,1},{4,6},{5,7},{6,4},{7,5},{8,10},{9,11},{10,... | collective-permute-start | bytes 516104 | tf_op jit(solution)/shard_map/ppermute | solution.py:242
  27.2 0.0 collective-permute-start.4
  27.2 0.0 collective-permute-done.8.refs_1_
  27.2 2.3 %shard_map.76 = (bf16[96,1792]{1,0:T(8,128)(2,1)S(1)}, bf16[96,1792]{1,0:T(8,128)(2,1)S(1)}) custom-call(bf16[96,1792]{1,0:T(8,128)(2,1)S(1)} %constant_dynamic-update-slice_fusion.6.refs_0_, bf16[96,1792]{1,0:T(8,128)(2,1)S(1)} %collective-permute-done.8.refs_1_, bf16[1,7168,256]{2,1,0:T(8,128)(2,1)S(1)} %get-tuple-element.42.refs_2_, ...), custom_call_target="tpu_custom_call" | custom-call | flops 528482304 | tf_op jit(solution)/shard_map/pallas_call | solution.py:272
  29.5 0.6 collective-permute-start.9
  30.1 0.0 collective-permute-done.4
  30.1 1.7 %collective-permute-done.5 = bf16[48,1792]{1,0:T(8,128)(2,1)S(1)} collective-permute-done((bf16[48,1792]{1,0:T(8,128)(2,1)S(1)}, bf16[48,1792]{1,0:T(8,128)(2,1)S(1)}, u32[]{:S(2)}, u32[]{:S(2)}) %collective-permute-start.5) | collective-permute-done | bytes 172064 | tf_op jit(solution)/shard_map/ppermute | solution.py:242
  31.9 0.0 collective-permute-done.9
  31.9 0.1 collective-permute-start.10
  32.1 1.6 %collective-permute-start.21 = (bf16[48,1792]{1,0:T(8,128)(2,1)S(1)}, bf16[48,1792]{1,0:T(8,128)(2,1)S(1)}, u32[]{:S(2)}, u32[]{:S(2)}) collective-permute-start(bf16[48,1792]{1,0:T(8,128)(2,1)S(1)} %fusion), channel_id=1, source_target_pairs={{0,2},{1,3},{2,0},{3,1},{4,6},{5,7},{6,4},{7,5},{8,10},{9,11},{10,... | collective-permute-start | bytes 516104 | tf_op jit(solution)/shard_map/ppermute | solution.py:242
  33.7 0.0 collective-permute-done.10
  33.7 0.0 collective-permute-done.11.refs_1_
  33.7 2.3 %shard_map.77 = (bf16[96,1792]{1,0:T(8,128)(2,1)S(1)}, bf16[96,1792]{1,0:T(8,128)(2,1)S(1)}) custom-call(bf16[96,1792]{1,0:T(8,128)(2,1)S(1)} %constant_dynamic-update-slice_fusion.2.refs_0_, bf16[96,1792]{1,0:T(8,128)(2,1)S(1)} %collective-permute-done.11.refs_1_, bf16[1,7168,256]{2,1,0:T(8,128)(2,1)S(1)} %get-tuple-element.42.refs_2_, ...), custom_call_target="tpu_custom_call" | custom-call | flops 528482304 | tf_op jit(solution)/shard_map/pallas_call | solution.py:272
  36.0 2.3 %shard_map.78 = (bf16[96,1792]{1,0:T(8,128)(2,1)S(1)}, bf16[96,1792]{1,0:T(8,128)(2,1)S(1)}) custom-call(bf16[96,1792]{1,0:T(8,128)(2,1)S(1)} %constant_dynamic-update-slice_fusion.4.refs_0_, bf16[96,1792]{1,0:T(8,128)(2,1)S(1)} %constant_dynamic-update-slice_fusion.8.refs_1_, bf16[1,7168,256]{2,1,0:T(8,128)(2,1)S(1)} %get-tuple-element.42.refs_2_, ...), custom_call_target="tpu_custom_call" | custom-call | flops 528482304 | tf_op jit(solution)/shard_map/pallas_call | solution.py:272
  38.3 0.3 collective-permute-start.13
  38.6 0.4 collective-permute-done.21
  39.0 0.1 fusion.2
  39.0 0.1 collective-permute-start.22
  39.1 0.1 collective-permute-start.12
  39.3 0.8 %collective-permute-done.13 = bf16[96,1792]{1,0:T(8,128)(2,1)S(1)} collective-permute-done((bf16[96,1792]{1,0:T(8,128)(2,1)S(1)}, bf16[96,1792]{1,0:T(8,128)(2,1)S(1)}, u32[]{:S(2)}, u32[]{:S(2)}) %collective-permute-start.13) | collective-permute-done | bytes 344096 | tf_op jit(solution)/shard_map/ppermute | solution.py:242
  40.1 1.3 %collective-permute-start.19 = (bf16[48,1792]{1,0:T(8,128)(2,1)S(1)}, bf16[48,1792]{1,0:T(8,128)(2,1)S(1)}, u32[]{:S(2)}, u32[]{:S(2)}) collective-permute-start(bf16[48,1792]{1,0:T(8,128)(2,1)S(1)} %fusion.3), channel_id=1, source_target_pairs={{0,2},{1,3},{2,0},{3,1},{4,6},{5,7},{6,4},{7,5},{8,10},{9,11},{10,... | collective-permute-start | bytes 516104 | tf_op jit(solution)/shard_map/ppermute | solution.py:242
  41.4 0.0 collective-permute-done.12
  41.4 0.0 collective-permute-start.14
  41.5 0.1 fusion.6
  41.5 1.2 %collective-permute-start.17 = (bf16[48,1792]{1,0:T(8,128)(2,1)S(1)}, bf16[48,1792]{1,0:T(8,128)(2,1)S(1)}, u32[]{:S(2)}, u32[]{:S(2)}) collective-permute-start(bf16[48,1792]{1,0:T(8,128)(2,1)S(1)} %fusion.6), channel_id=1, source_target_pairs={{0,2},{1,3},{2,0},{3,1},{4,6},{5,7},{6,4},{7,5},{8,10},{9,11},{10,... | collective-permute-start | bytes 516104 | tf_op jit(solution)/shard_map/ppermute | solution.py:242
  42.7 0.4 collective-permute-done.14.refs_1_
  43.1 2.3 %shard_map.79 = (bf16[96,1792]{1,0:T(8,128)(2,1)S(1)}, bf16[96,1792]{1,0:T(8,128)(2,1)S(1)}) custom-call(bf16[96,1792]{1,0:T(8,128)(2,1)S(1)} %constant_dynamic-update-slice_fusion.refs_0_, bf16[96,1792]{1,0:T(8,128)(2,1)S(1)} %collective-permute-done.14.refs_1_, bf16[1,7168,256]{2,1,0:T(8,128)(2,1)S(1)} %get-tuple-element.42.refs_2_, ...), custom_call_target="tpu_custom_call" | custom-call | flops 528482304 | tf_op jit(solution)/shard_map/pallas_call | solution.py:272
  45.4 0.2 collective-permute-start.15
  45.6 1.8 %collective-permute-done.19 = bf16[48,1792]{1,0:T(8,128)(2,1)S(1)} collective-permute-done((bf16[48,1792]{1,0:T(8,128)(2,1)S(1)}, bf16[48,1792]{1,0:T(8,128)(2,1)S(1)}, u32[]{:S(2)}, u32[]{:S(2)}) %collective-permute-start.19) | collective-permute-done | bytes 172064 | tf_op jit(solution)/shard_map/ppermute | solution.py:242
  47.4 0.1 fusion.5
  47.5 0.3 collective-permute-start.20
  47.8 0.0 collective-permute-done.15
  47.9 1.1 %collective-permute-start.16 = (bf16[48,1792]{1,0:T(8,128)(2,1)S(1)}, bf16[48,1792]{1,0:T(8,128)(2,1)S(1)}, u32[]{:S(2)}, u32[]{:S(2)}) collective-permute-start(bf16[48,1792]{1,0:T(8,128)(2,1)S(1)} %fusion.9), channel_id=1, source_target_pairs={{0,2},{1,3},{2,0},{3,1},{4,6},{5,7},{6,4},{7,5},{8,10},{9,11},{10,... | collective-permute-start | bytes 516104 | tf_op jit(solution)/shard_map/ppermute | solution.py:242
  49.0 1.7 %collective-permute-done.17 = bf16[48,1792]{1,0:T(8,128)(2,1)S(1)} collective-permute-done((bf16[48,1792]{1,0:T(8,128)(2,1)S(1)}, bf16[48,1792]{1,0:T(8,128)(2,1)S(1)}, u32[]{:S(2)}, u32[]{:S(2)}) %collective-permute-start.17) | collective-permute-done | bytes 172064 | tf_op jit(solution)/shard_map/ppermute | solution.py:242
  50.7 0.1 fusion.8
  50.8 2.2 %collective-permute-start.18 = (bf16[48,1792]{1,0:T(8,128)(2,1)S(1)}, bf16[48,1792]{1,0:T(8,128)(2,1)S(1)}, u32[]{:S(2)}, u32[]{:S(2)}) collective-permute-start(bf16[48,1792]{1,0:T(8,128)(2,1)S(1)} %fusion.8), channel_id=1, source_target_pairs={{0,4},{1,5},{2,6},{3,7},{4,0},{5,1},{6,2},{7,3},{8,12},{9,13},{10,... | collective-permute-start | bytes 516104 | tf_op jit(solution)/shard_map/ppermute | solution.py:242
  53.0 1.1 %collective-permute-done.16 = bf16[48,1792]{1,0:T(8,128)(2,1)S(1)} collective-permute-done((bf16[48,1792]{1,0:T(8,128)(2,1)S(1)}, bf16[48,1792]{1,0:T(8,128)(2,1)S(1)}, u32[]{:S(2)}, u32[]{:S(2)}) %collective-permute-start.16) | collective-permute-done | bytes 172064 | tf_op jit(solution)/shard_map/ppermute | solution.py:242
  54.1 0.1 fusion.11.refs_0_
  54.1 0.0 collective-permute-done.22.refs_3_
  54.1 3.0 %collective-permute-done.20.refs_2_ = bf16[48,1792]{1,0:T(8,128)(2,1)S(1)} collective-permute-done((bf16[48,1792]{1,0:T(8,128)(2,1)S(1)}, bf16[48,1792]{1,0:T(8,128)(2,1)S(1)}, u32[]{:S(2)}, u32[]{:S(2)}) %collective-permute-start.20) | collective-permute-done | bytes 172064 | tf_op jit(solution)/shard_map/ppermute | solution.py:242
  57.2 1.7 %collective-permute-done.18.refs_1_ = bf16[48,1792]{1,0:T(8,128)(2,1)S(1)} collective-permute-done((bf16[48,1792]{1,0:T(8,128)(2,1)S(1)}, bf16[48,1792]{1,0:T(8,128)(2,1)S(1)}, u32[]{:S(2)}, u32[]{:S(2)}) %collective-permute-start.18) | collective-permute-done | bytes 172064 | tf_op jit(solution)/shard_map/ppermute | solution.py:242
  58.9 1.0 %shard_map.80 = bf16[16,7168]{1,0:T(8,128)(2,1)} custom-call(bf16[4,128,48]{2,1,0:T(8,128)(2,1)S(1)} %shard_map.74.plan_ref, bf16[48,1792]{1,0:T(8,128)(2,1)S(1)} %fusion.11.refs_0_, bf16[48,1792]{1,0:T(8,128)(2,1)S(1)} %collective-permute-done.18.refs_1_, bf16[48,1792]{1,0:T(8,128)(2,1)S(1)} %collective-permute-done.20.refs_2_, ...), custom_call_target="tpu_custom_call" | custom-call | tf_op jit(solution)/shard_map/pallas_call | solution.py:381
  (22 shorter events, 0.6 us)
Async XLA Ops:
  1.5 11.9 %collective-permute-start.6 = (bf16[48,1792]{1,0:T(8,128)(2,1)S(1)}, bf16[48,1792]{1,0:T(8,128)(2,1)S(1)}, u32[]{:S(2)}, u32[]{:S(2)}) collective-permute-start(bf16[48,1792]{1,0:T(8,128)(2,1)S(1)} %get-tuple-element.39), channel_id=1, source_target_pairs={{0,12},{1,13},{2,14},{3,15},{4,8},{5,9},{6,10},{7,11},{8,4},{9,5},... | collective-permute-start | bytes 516104 | tf_op jit(solution)/shard_map/ppermute | solution.py:242
  6.6 8.2 %collective-permute-start.1 = (bf16[48,1792]{1,0:T(8,128)(2,1)S(1)}, bf16[48,1792]{1,0:T(8,128)(2,1)S(1)}, u32[]{:S(2)}, u32[]{:S(2)}) collective-permute-start(bf16[48,1792]{1,0:T(8,128)(2,1)S(1)} %get-tuple-element.36), channel_id=1, source_target_pairs={{0,4},{1,5},{2,6},{3,7},{4,0},{5,1},{6,2},{7,3},{8,12},{9,13},{10,... | collective-permute-start | bytes 516104 | tf_op jit(solution)/shard_map/ppermute | solution.py:242
  6.6 10.9 %collective-permute-start = (bf16[48,1792]{1,0:T(8,128)(2,1)S(1)}, bf16[48,1792]{1,0:T(8,128)(2,1)S(1)}, u32[]{:S(2)}, u32[]{:S(2)}) collective-permute-start(bf16[48,1792]{1,0:T(8,128)(2,1)S(1)} %get-tuple-element.35.unused), channel_id=1, source_target_pairs={{0,2},{1,3},{2,0},{3,1},{4,6},{5,7},{6,4},{7,5},{8,10},{9,11},{10,... | collective-permute-start | bytes 516104 | tf_op jit(solution)/shard_map/ppermute | solution.py:242
  13.4 7.2 %collective-permute-start.7 = (bf16[48,1792]{1,0:T(8,128)(2,1)S(1)}, bf16[48,1792]{1,0:T(8,128)(2,1)S(1)}, u32[]{:S(2)}, u32[]{:S(2)}) collective-permute-start(bf16[48,1792]{1,0:T(8,128)(2,1)S(1)} %collective-permute-done.6), channel_id=1, source_target_pairs={{0,2},{1,3},{2,0},{3,1},{4,6},{5,7},{6,4},{7,5},{8,10},{9,11},{10,... | collective-permute-start | bytes 516104 | tf_op jit(solution)/shard_map/ppermute | solution.py:242
  14.8 10.9 %collective-permute-start.3 = (bf16[48,1792]{1,0:T(8,128)(2,1)S(1)}, bf16[48,1792]{1,0:T(8,128)(2,1)S(1)}, u32[]{:S(2)}, u32[]{:S(2)}) collective-permute-start(bf16[48,1792]{1,0:T(8,128)(2,1)S(1)} %get-tuple-element.38), channel_id=1, source_target_pairs={{0,8},{1,9},{2,10},{3,11},{4,12},{5,13},{6,14},{7,15},{8,0},{9,1},... | collective-permute-start | bytes 516104 | tf_op jit(solution)/shard_map/ppermute | solution.py:242
  16.9 5.8 %collective-permute-start.2 = (bf16[48,1792]{1,0:T(8,128)(2,1)S(1)}, bf16[48,1792]{1,0:T(8,128)(2,1)S(1)}, u32[]{:S(2)}, u32[]{:S(2)}) collective-permute-start(bf16[48,1792]{1,0:T(8,128)(2,1)S(1)} %collective-permute-done.1), channel_id=1, source_target_pairs={{0,2},{1,3},{2,0},{3,1},{4,6},{5,7},{6,4},{7,5},{8,10},{9,11},{10,... | collective-permute-start | bytes 516104 | tf_op jit(solution)/shard_map/ppermute | solution.py:242
  20.7 6.5 %collective-permute-start.8 = (bf16[96,1792]{1,0:T(8,128)(2,1)S(1)}, bf16[96,1792]{1,0:T(8,128)(2,1)S(1)}, u32[]{:S(2)}, u32[]{:S(2)}) collective-permute-start(bf16[96,1792]{1,0:T(8,128)(2,1)S(1)} %constant_dynamic-update-slice_fusion.6.refs_0_), channel_id=1, source_target_pairs={{0,1},{1,0},{2,3},{3,2},{4,5},{5,4},{6,7},{7,6},{8,9},{9,8},{10,11... | collective-permute-start | bytes 1032200 | tf_op jit(solution)/shard_map/ppermute | solution.py:242
  22.8 11.0 %collective-permute-start.11 = (bf16[96,1792]{1,0:T(8,128)(2,1)S(1)}, bf16[96,1792]{1,0:T(8,128)(2,1)S(1)}, u32[]{:S(2)}, u32[]{:S(2)}) collective-permute-start(bf16[96,1792]{1,0:T(8,128)(2,1)S(1)} %constant_dynamic-update-slice_fusion.2.refs_0_), channel_id=1, source_target_pairs={{0,1},{1,0},{2,3},{3,2},{4,5},{5,4},{6,7},{7,6},{8,9},{9,8},{10,11... | collective-permute-start | bytes 1032200 | tf_op jit(solution)/shard_map/ppermute | solution.py:242
  25.7 6.2 %collective-permute-start.5 = (bf16[48,1792]{1,0:T(8,128)(2,1)S(1)}, bf16[48,1792]{1,0:T(8,128)(2,1)S(1)}, u32[]{:S(2)}, u32[]{:S(2)}) collective-permute-start(bf16[48,1792]{1,0:T(8,128)(2,1)S(1)} %collective-permute-done.3), channel_id=1, source_target_pairs={{0,2},{1,3},{2,0},{3,1},{4,6},{5,7},{6,4},{7,5},{8,10},{9,11},{10,... | collective-permute-start | bytes 516104 | tf_op jit(solution)/shard_map/ppermute | solution.py:242
  27.2 2.9 %collective-permute-start.4 = (bf16[48,1792]{1,0:T(8,128)(2,1)S(1)}, bf16[48,1792]{1,0:T(8,128)(2,1)S(1)}, u32[]{:S(2)}, u32[]{:S(2)}) collective-permute-start(bf16[48,1792]{1,0:T(8,128)(2,1)S(1)} %collective-permute-done.3), channel_id=1, source_target_pairs={{0,1},{1,0},{2,3},{3,2},{4,5},{5,4},{6,7},{7,6},{8,9},{9,8},{10,11... | collective-permute-start | bytes 516104 | tf_op jit(solution)/shard_map/ppermute | solution.py:242
  29.5 2.4 %collective-permute-start.9 = (bf16[96,1792]{1,0:T(8,128)(2,1)S(1)}, bf16[96,1792]{1,0:T(8,128)(2,1)S(1)}, u32[]{:S(2)}, u32[]{:S(2)}) collective-permute-start(bf16[96,1792]{1,0:T(8,128)(2,1)S(1)} %get-tuple-element.46), channel_id=1, source_target_pairs={{0,1},{1,0},{2,3},{3,2},{4,5},{5,4},{6,7},{7,6},{8,9},{9,8},{10,11... | collective-permute-start | bytes 1032200 | tf_op jit(solution)/shard_map/ppermute | solution.py:242
  31.9 1.8 %collective-permute-start.10 = (bf16[48,1792]{1,0:T(8,128)(2,1)S(1)}, bf16[48,1792]{1,0:T(8,128)(2,1)S(1)}, u32[]{:S(2)}, u32[]{:S(2)}) collective-permute-start(bf16[48,1792]{1,0:T(8,128)(2,1)S(1)} %split.3), channel_id=1, source_target_pairs={{0,1},{1,0},{2,3},{3,2},{4,5},{5,4},{6,7},{7,6},{8,9},{9,8},{10,11... | collective-permute-start | bytes 516104 | tf_op jit(solution)/shard_map/ppermute | solution.py:242
  32.1 6.8 %collective-permute-start.21 = (bf16[48,1792]{1,0:T(8,128)(2,1)S(1)}, bf16[48,1792]{1,0:T(8,128)(2,1)S(1)}, u32[]{:S(2)}, u32[]{:S(2)}) collective-permute-start(bf16[48,1792]{1,0:T(8,128)(2,1)S(1)} %fusion), channel_id=1, source_target_pairs={{0,2},{1,3},{2,0},{3,1},{4,6},{5,7},{6,4},{7,5},{8,10},{9,11},{10,... | collective-permute-start | bytes 516104 | tf_op jit(solution)/shard_map/ppermute | solution.py:242
  38.3 1.7 %collective-permute-start.13 = (bf16[96,1792]{1,0:T(8,128)(2,1)S(1)}, bf16[96,1792]{1,0:T(8,128)(2,1)S(1)}, u32[]{:S(2)}, u32[]{:S(2)}) collective-permute-start(bf16[96,1792]{1,0:T(8,128)(2,1)S(1)} %get-tuple-element.53), channel_id=1, source_target_pairs={{0,1},{1,0},{2,3},{3,2},{4,5},{5,4},{6,7},{7,6},{8,9},{9,8},{10,11... | collective-permute-start | bytes 1032200 | tf_op jit(solution)/shard_map/ppermute | solution.py:242
  39.0 15.1 %collective-permute-start.22 = (bf16[48,1792]{1,0:T(8,128)(2,1)S(1)}, bf16[48,1792]{1,0:T(8,128)(2,1)S(1)}, u32[]{:S(2)}, u32[]{:S(2)}) collective-permute-start(bf16[48,1792]{1,0:T(8,128)(2,1)S(1)} %fusion.2), channel_id=1, source_target_pairs={{0,12},{1,13},{2,14},{3,15},{4,8},{5,9},{6,10},{7,11},{8,4},{9,5},... | collective-permute-start | bytes 516104 | tf_op jit(solution)/shard_map/ppermute | solution.py:242
  39.1 2.3 %collective-permute-start.12 = (bf16[96,1792]{1,0:T(8,128)(2,1)S(1)}, bf16[96,1792]{1,0:T(8,128)(2,1)S(1)}, u32[]{:S(2)}, u32[]{:S(2)}) collective-permute-start(bf16[96,1792]{1,0:T(8,128)(2,1)S(1)} %get-tuple-element.50), channel_id=1, source_target_pairs={{0,1},{1,0},{2,3},{3,2},{4,5},{5,4},{6,7},{7,6},{8,9},{9,8},{10,11... | collective-permute-start | bytes 1032200 | tf_op jit(solution)/shard_map/ppermute | solution.py:242
  40.1 7.3 %collective-permute-start.19 = (bf16[48,1792]{1,0:T(8,128)(2,1)S(1)}, bf16[48,1792]{1,0:T(8,128)(2,1)S(1)}, u32[]{:S(2)}, u32[]{:S(2)}) collective-permute-start(bf16[48,1792]{1,0:T(8,128)(2,1)S(1)} %fusion.3), channel_id=1, source_target_pairs={{0,2},{1,3},{2,0},{3,1},{4,6},{5,7},{6,4},{7,5},{8,10},{9,11},{10,... | collective-permute-start | bytes 516104 | tf_op jit(solution)/shard_map/ppermute | solution.py:242
  41.4 1.7 %collective-permute-start.14 = (bf16[96,1792]{1,0:T(8,128)(2,1)S(1)}, bf16[96,1792]{1,0:T(8,128)(2,1)S(1)}, u32[]{:S(2)}, u32[]{:S(2)}) collective-permute-start(bf16[96,1792]{1,0:T(8,128)(2,1)S(1)} %constant_dynamic-update-slice_fusion.refs_0_), channel_id=1, source_target_pairs={{0,1},{1,0},{2,3},{3,2},{4,5},{5,4},{6,7},{7,6},{8,9},{9,8},{10,11... | collective-permute-start | bytes 1032200 | tf_op jit(solution)/shard_map/ppermute | solution.py:242
  41.5 9.2 %collective-permute-start.17 = (bf16[48,1792]{1,0:T(8,128)(2,1)S(1)}, bf16[48,1792]{1,0:T(8,128)(2,1)S(1)}, u32[]{:S(2)}, u32[]{:S(2)}) collective-permute-start(bf16[48,1792]{1,0:T(8,128)(2,1)S(1)} %fusion.6), channel_id=1, source_target_pairs={{0,2},{1,3},{2,0},{3,1},{4,6},{5,7},{6,4},{7,5},{8,10},{9,11},{10,... | collective-permute-start | bytes 516104 | tf_op jit(solution)/shard_map/ppermute | solution.py:242
  45.4 2.4 %collective-permute-start.15 = (bf16[96,1792]{1,0:T(8,128)(2,1)S(1)}, bf16[96,1792]{1,0:T(8,128)(2,1)S(1)}, u32[]{:S(2)}, u32[]{:S(2)}) collective-permute-start(bf16[96,1792]{1,0:T(8,128)(2,1)S(1)} %get-tuple-element.57), channel_id=1, source_target_pairs={{0,1},{1,0},{2,3},{3,2},{4,5},{5,4},{6,7},{7,6},{8,9},{9,8},{10,11... | collective-permute-start | bytes 1032200 | tf_op jit(solution)/shard_map/ppermute | solution.py:242
  47.5 9.7 %collective-permute-start.20 = (bf16[48,1792]{1,0:T(8,128)(2,1)S(1)}, bf16[48,1792]{1,0:T(8,128)(2,1)S(1)}, u32[]{:S(2)}, u32[]{:S(2)}) collective-permute-start(bf16[48,1792]{1,0:T(8,128)(2,1)S(1)} %fusion.5), channel_id=1, source_target_pairs={{0,8},{1,9},{2,10},{3,11},{4,12},{5,13},{6,14},{7,15},{8,0},{9,1},... | collective-permute-start | bytes 516104 | tf_op jit(solution)/shard_map/ppermute | solution.py:242
  47.9 6.2 %collective-permute-start.16 = (bf16[48,1792]{1,0:T(8,128)(2,1)S(1)}, bf16[48,1792]{1,0:T(8,128)(2,1)S(1)}, u32[]{:S(2)}, u32[]{:S(2)}) collective-permute-start(bf16[48,1792]{1,0:T(8,128)(2,1)S(1)} %fusion.9), channel_id=1, source_target_pairs={{0,2},{1,3},{2,0},{3,1},{4,6},{5,7},{6,4},{7,5},{8,10},{9,11},{10,... | collective-permute-start | bytes 516104 | tf_op jit(solution)/shard_map/ppermute | solution.py:242
  50.8 8.2 %collective-permute-start.18 = (bf16[48,1792]{1,0:T(8,128)(2,1)S(1)}, bf16[48,1792]{1,0:T(8,128)(2,1)S(1)}, u32[]{:S(2)}, u32[]{:S(2)}) collective-permute-start(bf16[48,1792]{1,0:T(8,128)(2,1)S(1)} %fusion.8), channel_id=1, source_target_pairs={{0,4},{1,5},{2,6},{3,7},{4,0},{5,1},{6,2},{7,3},{8,12},{9,13},{10,... | collective-permute-start | bytes 516104 | tf_op jit(solution)/shard_map/ppermute | solution.py:242

commit v13 on v7

--- a/solution.py
+++ b/solution.py
@@ -10,7 +10,8 @@
 SHARDS = 4
 QUARTERS = 4
 GROUPS = ("own+near", "mid", "far")
-SPLIT = ("c mid", "c near", "rc mid",)
+SPLIT = ("c mid", "c near",)
+DIRECT = ()
 ORDER = {
     "z far": ("y own",),
     "expert own+near": ("y own",),
@@ -314,7 +315,7 @@
         if kind == "z":
             inputs = result("pack " + name)
         elif kind == "y":
-            inputs = result(("pack " if name == "own" else "z ") + name)
+            inputs = result(("pack " if name == "own" or name in DIRECT else "z ") + name)
         elif kind == "c":
             own = result(("pack " if name == "own" else "z ") + name)
             inputs = [jnp.concatenate(both, axis=0) for both in zip(own, result("y " + name))]
@@ -347,6 +348,8 @@
             return load(inputs[0])
         if kind == "expert":
             return expert(len(places[name]), inputs, result("load all"))
+        if kind == "y" and name in DIRECT:
+            return [partner(array, at * SHARDS + 2) for array, at in zip(inputs, places[name])]
         if kind in ("y", "ry"):
             return [partner(array, 2) for array in inputs]
         if kind in ("c", "rc"):

time: 57.8 us -> 57.7 us (level)
    ppermute x23 -> x22, waiting for transfers between devices: 15.8 us -> 15.7 us  [partner(): lax.ppermute(array, 'expert', [(i, i ^ distance) for i in range(devices)])]
    ppermute x23 -> x22, starting transfers between devices: 25.4 us -> 25.5 us  [partner(): lax.ppermute(array, 'expert', [(i, i ^ distance) for i in range(devices)])]
  transfers between devices with their start and end apart: 23 -> 22, of which waited for: 8 -> 7; matrix products, arithmetic and copies ran while one was open for 2% -> 2% of each run, Pallas kernels for 22% -> 22%
where the time goes in v13:
time: 57.7 us; the launch traced here: 57.5 us
  starting transfers between devices  25.5 us (44%)
  waiting for transfers between devices  15.7 us (27%)
  Pallas kernels  15.1 us (26%)
  other arithmetic  0.83 us (1%)
    ppermute x22, starting transfers between devices, partner(): lax.ppermute(array, 'expert', [(i, i ^ distance) for i in range(devices)])  25.5 us
    ppermute x22, waiting for transfers between devices, partner(): lax.ppermute(array, 'expert', [(i, i ^ distance) for i in range(devices)])  15.7 us
    pallas_call x3, Pallas kernels, expert(): pl.pallas_call(functools.partial(expert_kernel, capacity, offsets), out_s...  7.39 us
    pallas_call x1, Pallas kernels, load(): pl.pallas_call(load_kernel, out_shape=[jax.ShapeDtypeStruct(w.shape, w.dt...  4.23 us
    pallas_call x1, Pallas kernels, shards(): pl.pallas_call(functools.partial(pack_kernel, capacity, planes), out_shap...  1.48 us
  transfers between devices with their start and end apart: 22, of which 7 were waited for; matrix products, arithmetic and copies ran while one was open for 2% of the time, Pallas kernels for 22%

profile of v13, /device:TPU:0, one launch (start us, length us, event | category | flops | bytes accessed | tf_op | source)
XLA Modules:
  0.0 57.5 jit_solution(16966186095356609494)
XLA Ops:
  0.0 1.5 %shard_map.73 = (bf16[48,1792]{1,0:T(8,128)(2,1)S(1)}, bf16[48,1792]{1,0:T(8,128)(2,1)S(1)}, bf16[48,1792]{1,0:T(8,128)(2,1)S(1)}, bf16[48,1792]{1,0:T(8,128)(2,1)S(1)}) custom-call(s32[2,16]{1,0:T(2,128)} %bitcast.2, bf16[16,7168]{1,0:T(8,128)(2,1)} %tok_hbm.1, f32[16,56]{1,0:T(8,128)} %scale_hbm.1), custom_call_target="tpu_custom_call" | custom-call | tf_op jit(solution)/shard_map/pallas_call | solution.py:239
  1.5 4.1 %collective-permute-start.9 = (bf16[48,1792]{1,0:T(8,128)(2,1)S(1)}, bf16[48,1792]{1,0:T(8,128)(2,1)S(1)}, u32[]{:S(2)}, u32[]{:S(2)}) collective-permute-start(bf16[48,1792]{1,0:T(8,128)(2,1)S(1)} %get-tuple-element.36), channel_id=1, source_target_pairs={{0,8},{1,9},{2,10},{3,11},{4,12},{5,13},{6,14},{7,15},{8,0},{9,1},... | collective-permute-start | bytes 516104 | tf_op jit(solution)/shard_map/ppermute | solution.py:236
  5.6 1.5 %collective-permute-start = (bf16[48,1792]{1,0:T(8,128)(2,1)S(1)}, bf16[48,1792]{1,0:T(8,128)(2,1)S(1)}, u32[]{:S(2)}, u32[]{:S(2)}) collective-permute-start(bf16[48,1792]{1,0:T(8,128)(2,1)S(1)} %get-tuple-element.26.unused), channel_id=1, source_target_pairs={{0,2},{1,3},{2,0},{3,1},{4,6},{5,7},{6,4},{7,5},{8,10},{9,11},{10,... | collective-permute-start | bytes 516104 | tf_op jit(solution)/shard_map/ppermute | solution.py:236
  7.1 1.6 %collective-permute-start.1 = (bf16[48,1792]{1,0:T(8,128)(2,1)S(1)}, bf16[48,1792]{1,0:T(8,128)(2,1)S(1)}, u32[]{:S(2)}, u32[]{:S(2)}) collective-permute-start(bf16[48,1792]{1,0:T(8,128)(2,1)S(1)} %get-tuple-element.28), channel_id=1, source_target_pairs={{0,4},{1,5},{2,6},{3,7},{4,0},{5,1},{6,2},{7,3},{8,12},{9,13},{10,... | collective-permute-start | bytes 516104 | tf_op jit(solution)/shard_map/ppermute | solution.py:236
  8.7 4.2 %shard_map.75 = (bf16[1,7168,256]{2,1,0:T(8,128)(2,1)S(1)}, bf16[1,7168,256]{2,1,0:T(8,128)(2,1)S(1)}, bf16[1,256,7168]{2,1,0:T(8,128)(2,1)S(1)}) custom-call(bf16[1,7168,256]{2,1,0:T(8,128)(2,1)} %gate_hbm.1, bf16[1,7168,256]{2,1,0:T(8,128)(2,1)} %up_hbm.1, bf16[1,256,7168]{2,1,0:T(8,128)(2,1)} %down_hbm.1, bf16[48,1792]{1,0:T(8,128)(2,1)S(1)} %get-tuple-element.26.unused), custom_call_target="tpu_custom_call" | custom-call | tf_op jit(solution)/shard_map/pallas_call | solution.py:281
  12.9 0.0 collective-permute-done
  13.0 0.3 collective-permute-start.15
  13.2 0.5 collective-permute-done.9
  13.8 1.6 %collective-permute-start.10 = (bf16[48,1792]{1,0:T(8,128)(2,1)S(1)}, bf16[48,1792]{1,0:T(8,128)(2,1)S(1)}, u32[]{:S(2)}, u32[]{:S(2)}) collective-permute-start(bf16[48,1792]{1,0:T(8,128)(2,1)S(1)} %collective-permute-done.9), channel_id=1, source_target_pairs={{0,2},{1,3},{2,0},{3,1},{4,6},{5,7},{6,4},{7,5},{8,10},{9,11},{10,... | collective-permute-start | bytes 516104 | tf_op jit(solution)/shard_map/ppermute | solution.py:236
  15.3 0.1 collective-permute-start.11
  15.4 0.0 collective-permute-done.1
  15.4 0.5 collective-permute-start.3
  16.0 0.2 collective-permute-start.2
  16.1 4.2 %collective-permute-done.15 = bf16[48,1792]{1,0:T(8,128)(2,1)S(1)} collective-permute-done((bf16[48,1792]{1,0:T(8,128)(2,1)S(1)}, bf16[48,1792]{1,0:T(8,128)(2,1)S(1)}, u32[]{:S(2)}, u32[]{:S(2)}) %collective-permute-start.15) | collective-permute-done | bytes 172064 | tf_op jit(solution)/shard_map/ppermute | solution.py:236
  20.3 0.5 collective-permute-start.16
  20.8 0.0 collective-permute-done.10
  20.8 0.0 collective-permute-start.12
  20.8 2.9 %collective-permute-done.3 = bf16[48,1792]{1,0:T(8,128)(2,1)S(1)} collective-permute-done((bf16[48,1792]{1,0:T(8,128)(2,1)S(1)}, bf16[48,1792]{1,0:T(8,128)(2,1)S(1)}, u32[]{:S(2)}, u32[]{:S(2)}) %collective-permute-start.3) | collective-permute-done | bytes 172064 | tf_op jit(solution)/shard_map/ppermute | solution.py:236
  23.7 0.0 collective-permute-start.4
  23.7 0.0 collective-permute-done.2
  23.7 0.0 collective-permute-done.11
  23.7 0.0 collective-permute-done.12
  23.8 2.3 %shard_map.77 = (bf16[96,1792]{1,0:T(8,128)(2,1)S(1)}, bf16[96,1792]{1,0:T(8,128)(2,1)S(1)}) custom-call(bf16[96,1792]{1,0:T(8,128)(2,1)S(1)} %pad_maximum_fusion.1.refs_0_, bf16[96,1792]{1,0:T(8,128)(2,1)S(1)} %pad_maximum_fusion.2.refs_1_, bf16[1,7168,256]{2,1,0:T(8,128)(2,1)S(1)} %get-tuple-element.30.refs_4_.refs_2_, ...), custom_call_target="tpu_custom_call" | custom-call | flops 528482304 | tf_op jit(solution)/shard_map/pallas_call | solution.py:266
  26.1 0.6 collective-permute-start.13
  26.7 0.0 collective-permute-done.16
  26.7 0.1 collective-permute-start.17
  26.8 0.0 collective-permute-done.4
  26.8 0.5 collective-permute-start.5
  27.4 0.5 collective-permute-done.13
  28.0 2.6 %collective-permute-start.14 = (bf16[48,1792]{1,0:T(8,128)(2,1)S(1)}, bf16[48,1792]{1,0:T(8,128)(2,1)S(1)}, u32[]{:S(2)}, u32[]{:S(2)}) collective-permute-start(bf16[48,1792]{1,0:T(8,128)(2,1)S(1)} %fusion.6), channel_id=1, source_target_pairs={{0,2},{1,3},{2,0},{3,1},{4,6},{5,7},{6,4},{7,5},{8,10},{9,11},{10,... | collective-permute-start | bytes 516104 | tf_op jit(solution)/shard_map/ppermute | solution.py:236
  30.6 0.0 collective-permute-done.17.refs_1_
  30.6 2.3 %shard_map.78 = (bf16[96,1792]{1,0:T(8,128)(2,1)S(1)}, bf16[96,1792]{1,0:T(8,128)(2,1)S(1)}) custom-call(bf16[96,1792]{1,0:T(8,128)(2,1)S(1)} %constant_dynamic-update-slice_fusion.4.refs_0_, bf16[96,1792]{1,0:T(8,128)(2,1)S(1)} %collective-permute-done.17.refs_1_, bf16[1,7168,256]{2,1,0:T(8,128)(2,1)S(1)} %get-tuple-element.30.refs_4_.refs_2_, ...), custom_call_target="tpu_custom_call" | custom-call | flops 528482304 | tf_op jit(solution)/shard_map/pallas_call | solution.py:266
  32.9 0.1 collective-permute-start.18
  33.1 0.0 collective-permute-done.5.refs_1_
  33.1 2.8 %shard_map.76 = (bf16[192,1792]{1,0:T(8,128)(2,1)S(1)}, bf16[192,1792]{1,0:T(8,128)(2,1)S(1)}) custom-call(bf16[96,1792]{1,0:T(8,128)(2,1)S(1)} %constant_dynamic-update-slice_fusion.refs_0_, bf16[96,1792]{1,0:T(8,128)(2,1)S(1)} %collective-permute-done.5.refs_1_, bf16[96,1792]{1,0:T(8,128)(2,1)S(1)} %pad_maximum_fusion.refs_2_, ...), custom_call_target="tpu_custom_call" | custom-call | flops 1056964608 | tf_op jit(solution)/shard_map/pallas_call | solution.py:266
  35.9 0.5 collective-permute-start.6
  36.4 0.1 convert_element_type.45
  36.5 0.0 collective-permute-done.14
  36.5 0.1 fusion.8
  36.6 0.0 collective-permute-done.18
  36.7 0.8 %collective-permute-start.20 = (bf16[48,1792]{1,0:T(8,128)(2,1)S(1)}, bf16[48,1792]{1,0:T(8,128)(2,1)S(1)}, u32[]{:S(2)}, u32[]{:S(2)}) collective-permute-start(bf16[48,1792]{1,0:T(8,128)(2,1)S(1)} %fusion.3), channel_id=1, source_target_pairs={{0,2},{1,3},{2,0},{3,1},{4,6},{5,7},{6,4},{7,5},{8,10},{9,11},{10,... | collective-permute-start | bytes 516104 | tf_op jit(solution)/shard_map/ppermute | solution.py:236
  37.5 1.9 %collective-permute-start.19 = (bf16[48,1792]{1,0:T(8,128)(2,1)S(1)}, bf16[48,1792]{1,0:T(8,128)(2,1)S(1)}, u32[]{:S(2)}, u32[]{:S(2)}) collective-permute-start(bf16[48,1792]{1,0:T(8,128)(2,1)S(1)} %fusion.8), channel_id=1, source_target_pairs={{0,8},{1,9},{2,10},{3,11},{4,12},{5,13},{6,14},{7,15},{8,0},{9,1},... | collective-permute-start | bytes 516104 | tf_op jit(solution)/shard_map/ppermute | solution.py:236
  39.4 0.0 collective-permute-done.6
  39.4 0.1 convert_element_type.46
  39.5 0.1 fusion
  39.5 1.3 %collective-permute-start.7 = (bf16[96,1792]{1,0:T(8,128)(2,1)S(1)}, bf16[96,1792]{1,0:T(8,128)(2,1)S(1)}, u32[]{:S(2)}, u32[]{:S(2)}) collective-permute-start(bf16[96,1792]{1,0:T(8,128)(2,1)S(1)} %fusion), channel_id=1, source_target_pairs={{0,2},{1,3},{2,0},{3,1},{4,6},{5,7},{6,4},{7,5},{8,10},{9,11},{10,... | collective-permute-start | bytes 1032200 | tf_op jit(solution)/shard_map/ppermute | solution.py:236
  40.8 3.2 %collective-permute-done.20 = bf16[48,1792]{1,0:T(8,128)(2,1)S(1)} collective-permute-done((bf16[48,1792]{1,0:T(8,128)(2,1)S(1)}, bf16[48,1792]{1,0:T(8,128)(2,1)S(1)}, u32[]{:S(2)}, u32[]{:S(2)}) %collective-permute-start.20) | collective-permute-done | bytes 172064 | tf_op jit(solution)/shard_map/ppermute | solution.py:236
  44.0 4.8 %collective-permute-start.21 = (bf16[48,1792]{1,0:T(8,128)(2,1)S(1)}, bf16[48,1792]{1,0:T(8,128)(2,1)S(1)}, u32[]{:S(2)}, u32[]{:S(2)}) collective-permute-start(bf16[48,1792]{1,0:T(8,128)(2,1)S(1)} %fusion.5), channel_id=1, source_target_pairs={{0,12},{1,13},{2,14},{3,15},{4,8},{5,9},{6,10},{7,11},{8,4},{9,5},... | collective-permute-start | bytes 516104 | tf_op jit(solution)/shard_map/ppermute | solution.py:236
  48.9 1.6 %collective-permute-done.7 = bf16[96,1792]{1,0:T(8,128)(2,1)S(1)} collective-permute-done((bf16[96,1792]{1,0:T(8,128)(2,1)S(1)}, bf16[96,1792]{1,0:T(8,128)(2,1)S(1)}, u32[]{:S(2)}, u32[]{:S(2)}) %collective-permute-start.7) | collective-permute-done | bytes 344096 | tf_op jit(solution)/shard_map/ppermute | solution.py:236
  50.5 0.1 fusion.2
  50.7 2.0 %collective-permute-start.8 = (bf16[48,1792]{1,0:T(8,128)(2,1)S(1)}, bf16[48,1792]{1,0:T(8,128)(2,1)S(1)}, u32[]{:S(2)}, u32[]{:S(2)}) collective-permute-start(bf16[48,1792]{1,0:T(8,128)(2,1)S(1)} %get-tuple-element.47), channel_id=1, source_target_pairs={{0,4},{1,5},{2,6},{3,7},{4,0},{5,1},{6,2},{7,3},{8,12},{9,13},{10,... | collective-permute-start | bytes 516104 | tf_op jit(solution)/shard_map/ppermute | solution.py:236
  52.6 1.0 %shard_map.74.plan_ref = bf16[4,128,48]{2,1,0:T(8,128)(2,1)S(1)} custom-call(s32[2,16]{1,0:T(2,128)} %bitcast.3, s32[2,16]{1,0:T(2,128)} %bitcast.4, bf16[48,1792]{1,0:T(8,128)(2,1)S(1)} %get-tuple-element.26.unused), custom_call_target="tpu_custom_call" | custom-call | tf_op jit(solution)/shard_map/pallas_call | solution.py:253
  53.7 0.0 collective-permute-done.19.refs_2_
  53.7 0.0 collective-permute-done.21.refs_3_
  53.7 2.8 %collective-permute-done.8.refs_1_ = bf16[48,1792]{1,0:T(8,128)(2,1)S(1)} collective-permute-done((bf16[48,1792]{1,0:T(8,128)(2,1)S(1)}, bf16[48,1792]{1,0:T(8,128)(2,1)S(1)}, u32[]{:S(2)}, u32[]{:S(2)}) %collective-permute-start.8) | collective-permute-done | bytes 172064 | tf_op jit(solution)/shard_map/ppermute | solution.py:236
  56.5 1.0 %shard_map.79 = bf16[16,7168]{1,0:T(8,128)(2,1)} custom-call(bf16[4,128,48]{2,1,0:T(8,128)(2,1)S(1)} %shard_map.74.plan_ref, bf16[48,1792]{1,0:T(8,128)(2,1)S(1)} %get-tuple-element.48.refs_0_, bf16[48,1792]{1,0:T(8,128)(2,1)S(1)} %collective-permute-done.8.refs_1_, bf16[48,1792]{1,0:T(8,128)(2,1)S(1)} %collective-permute-done.19.refs_2_, ...), custom_call_target="tpu_custom_call" | custom-call | tf_op jit(solution)/shard_map/pallas_call | solution.py:375
  (17 shorter events, 0.5 us)
Async XLA Ops:
  1.5 12.3 %collective-permute-start.9 = (bf16[48,1792]{1,0:T(8,128)(2,1)S(1)}, bf16[48,1792]{1,0:T(8,128)(2,1)S(1)}, u32[]{:S(2)}, u32[]{:S(2)}) collective-permute-start(bf16[48,1792]{1,0:T(8,128)(2,1)S(1)} %get-tuple-element.36), channel_id=1, source_target_pairs={{0,8},{1,9},{2,10},{3,11},{4,12},{5,13},{6,14},{7,15},{8,0},{9,1},... | collective-permute-start | bytes 516104 | tf_op jit(solution)/shard_map/ppermute | solution.py:236
  5.6 7.4 %collective-permute-start = (bf16[48,1792]{1,0:T(8,128)(2,1)S(1)}, bf16[48,1792]{1,0:T(8,128)(2,1)S(1)}, u32[]{:S(2)}, u32[]{:S(2)}) collective-permute-start(bf16[48,1792]{1,0:T(8,128)(2,1)S(1)} %get-tuple-element.26.unused), channel_id=1, source_target_pairs={{0,2},{1,3},{2,0},{3,1},{4,6},{5,7},{6,4},{7,5},{8,10},{9,11},{10,... | collective-permute-start | bytes 516104 | tf_op jit(solution)/shard_map/ppermute | solution.py:236
  7.1 8.3 %collective-permute-start.1 = (bf16[48,1792]{1,0:T(8,128)(2,1)S(1)}, bf16[48,1792]{1,0:T(8,128)(2,1)S(1)}, u32[]{:S(2)}, u32[]{:S(2)}) collective-permute-start(bf16[48,1792]{1,0:T(8,128)(2,1)S(1)} %get-tuple-element.28), channel_id=1, source_target_pairs={{0,4},{1,5},{2,6},{3,7},{4,0},{5,1},{6,2},{7,3},{8,12},{9,13},{10,... | collective-permute-start | bytes 516104 | tf_op jit(solution)/shard_map/ppermute | solution.py:236
  13.0 7.3 %collective-permute-start.15 = (bf16[48,1792]{1,0:T(8,128)(2,1)S(1)}, bf16[48,1792]{1,0:T(8,128)(2,1)S(1)}, u32[]{:S(2)}, u32[]{:S(2)}) collective-permute-start(bf16[48,1792]{1,0:T(8,128)(2,1)S(1)} %get-tuple-element.40), channel_id=1, source_target_pairs={{0,12},{1,13},{2,14},{3,15},{4,8},{5,9},{6,10},{7,11},{8,4},{9,5},... | collective-permute-start | bytes 516104 | tf_op jit(solution)/shard_map/ppermute | solution.py:236
  13.8 7.0 %collective-permute-start.10 = (bf16[48,1792]{1,0:T(8,128)(2,1)S(1)}, bf16[48,1792]{1,0:T(8,128)(2,1)S(1)}, u32[]{:S(2)}, u32[]{:S(2)}) collective-permute-start(bf16[48,1792]{1,0:T(8,128)(2,1)S(1)} %collective-permute-done.9), channel_id=1, source_target_pairs={{0,2},{1,3},{2,0},{3,1},{4,6},{5,7},{6,4},{7,5},{8,10},{9,11},{10,... | collective-permute-start | bytes 516104 | tf_op jit(solution)/shard_map/ppermute | solution.py:236
  15.3 8.4 %collective-permute-start.11 = (bf16[48,1792]{1,0:T(8,128)(2,1)S(1)}, bf16[48,1792]{1,0:T(8,128)(2,1)S(1)}, u32[]{:S(2)}, u32[]{:S(2)}) collective-permute-start(bf16[48,1792]{1,0:T(8,128)(2,1)S(1)} %collective-permute-done.9), channel_id=1, source_target_pairs={{0,1},{1,0},{2,3},{3,2},{4,5},{5,4},{6,7},{7,6},{8,9},{9,8},{10,11... | collective-permute-start | bytes 516104 | tf_op jit(solution)/shard_map/ppermute | solution.py:236
  15.4 8.2 %collective-permute-start.3 = (bf16[48,1792]{1,0:T(8,128)(2,1)S(1)}, bf16[48,1792]{1,0:T(8,128)(2,1)S(1)}, u32[]{:S(2)}, u32[]{:S(2)}) collective-permute-start(bf16[48,1792]{1,0:T(8,128)(2,1)S(1)} %collective-permute-done.1), channel_id=1, source_target_pairs={{0,2},{1,3},{2,0},{3,1},{4,6},{5,7},{6,4},{7,5},{8,10},{9,11},{10,... | collective-permute-start | bytes 516104 | tf_op jit(solution)/shard_map/ppermute | solution.py:236
  16.0 7.7 %collective-permute-start.2 = (bf16[48,1792]{1,0:T(8,128)(2,1)S(1)}, bf16[48,1792]{1,0:T(8,128)(2,1)S(1)}, u32[]{:S(2)}, u32[]{:S(2)}) collective-permute-start(bf16[48,1792]{1,0:T(8,128)(2,1)S(1)} %collective-permute-done.1), channel_id=1, source_target_pairs={{0,1},{1,0},{2,3},{3,2},{4,5},{5,4},{6,7},{7,6},{8,9},{9,8},{10,11... | collective-permute-start | bytes 516104 | tf_op jit(solution)/shard_map/ppermute | solution.py:236
  20.3 6.4 %collective-permute-start.16 = (bf16[48,1792]{1,0:T(8,128)(2,1)S(1)}, bf16[48,1792]{1,0:T(8,128)(2,1)S(1)}, u32[]{:S(2)}, u32[]{:S(2)}) collective-permute-start(bf16[48,1792]{1,0:T(8,128)(2,1)S(1)} %collective-permute-done.15), channel_id=1, source_target_pairs={{0,2},{1,3},{2,0},{3,1},{4,6},{5,7},{6,4},{7,5},{8,10},{9,11},{10,... | collective-permute-start | bytes 516104 | tf_op jit(solution)/shard_map/ppermute | solution.py:236
  20.8 3.0 %collective-permute-start.12 = (bf16[48,1792]{1,0:T(8,128)(2,1)S(1)}, bf16[48,1792]{1,0:T(8,128)(2,1)S(1)}, u32[]{:S(2)}, u32[]{:S(2)}) collective-permute-start(bf16[48,1792]{1,0:T(8,128)(2,1)S(1)} %collective-permute-done.10), channel_id=1, source_target_pairs={{0,1},{1,0},{2,3},{3,2},{4,5},{5,4},{6,7},{7,6},{8,9},{9,8},{10,11... | collective-permute-start | bytes 516104 | tf_op jit(solution)/shard_map/ppermute | solution.py:236
  23.7 3.1 %collective-permute-start.4 = (bf16[48,1792]{1,0:T(8,128)(2,1)S(1)}, bf16[48,1792]{1,0:T(8,128)(2,1)S(1)}, u32[]{:S(2)}, u32[]{:S(2)}) collective-permute-start(bf16[48,1792]{1,0:T(8,128)(2,1)S(1)} %collective-permute-done.3), channel_id=1, source_target_pairs={{0,1},{1,0},{2,3},{3,2},{4,5},{5,4},{6,7},{7,6},{8,9},{9,8},{10,11... | collective-permute-start | bytes 516104 | tf_op jit(solution)/shard_map/ppermute | solution.py:236
  26.1 1.9 %collective-permute-start.13 = (bf16[96,1792]{1,0:T(8,128)(2,1)S(1)}, bf16[96,1792]{1,0:T(8,128)(2,1)S(1)}, u32[]{:S(2)}, u32[]{:S(2)}) collective-permute-start(bf16[96,1792]{1,0:T(8,128)(2,1)S(1)} %get-tuple-element.38), channel_id=1, source_target_pairs={{0,1},{1,0},{2,3},{3,2},{4,5},{5,4},{6,7},{7,6},{8,9},{9,8},{10,11... | collective-permute-start | bytes 1032200 | tf_op jit(solution)/shard_map/ppermute | solution.py:236
  26.7 3.9 %collective-permute-start.17 = (bf16[96,1792]{1,0:T(8,128)(2,1)S(1)}, bf16[96,1792]{1,0:T(8,128)(2,1)S(1)}, u32[]{:S(2)}, u32[]{:S(2)}) collective-permute-start(bf16[96,1792]{1,0:T(8,128)(2,1)S(1)} %constant_dynamic-update-slice_fusion.4.refs_0_), channel_id=1, source_target_pairs={{0,1},{1,0},{2,3},{3,2},{4,5},{5,4},{6,7},{7,6},{8,9},{9,8},{10,11... | collective-permute-start | bytes 1032200 | tf_op jit(solution)/shard_map/ppermute | solution.py:236
  26.8 6.3 %collective-permute-start.5 = (bf16[96,1792]{1,0:T(8,128)(2,1)S(1)}, bf16[96,1792]{1,0:T(8,128)(2,1)S(1)}, u32[]{:S(2)}, u32[]{:S(2)}) collective-permute-start(bf16[96,1792]{1,0:T(8,128)(2,1)S(1)} %constant_dynamic-update-slice_fusion.refs_0_), channel_id=1, source_target_pairs={{0,1},{1,0},{2,3},{3,2},{4,5},{5,4},{6,7},{7,6},{8,9},{9,8},{10,11... | collective-permute-start | bytes 1032200 | tf_op jit(solution)/shard_map/ppermute | solution.py:236
  28.0 8.5 %collective-permute-start.14 = (bf16[48,1792]{1,0:T(8,128)(2,1)S(1)}, bf16[48,1792]{1,0:T(8,128)(2,1)S(1)}, u32[]{:S(2)}, u32[]{:S(2)}) collective-permute-start(bf16[48,1792]{1,0:T(8,128)(2,1)S(1)} %fusion.6), channel_id=1, source_target_pairs={{0,2},{1,3},{2,0},{3,1},{4,6},{5,7},{6,4},{7,5},{8,10},{9,11},{10,... | collective-permute-start | bytes 516104 | tf_op jit(solution)/shard_map/ppermute | solution.py:236
  32.9 3.7 %collective-permute-start.18 = (bf16[96,1792]{1,0:T(8,128)(2,1)S(1)}, bf16[96,1792]{1,0:T(8,128)(2,1)S(1)}, u32[]{:S(2)}, u32[]{:S(2)}) collective-permute-start(bf16[96,1792]{1,0:T(8,128)(2,1)S(1)} %get-tuple-element.44), channel_id=1, source_target_pairs={{0,1},{1,0},{2,3},{3,2},{4,5},{5,4},{6,7},{7,6},{8,9},{9,8},{10,11... | collective-permute-start | bytes 1032200 | tf_op jit(solution)/shard_map/ppermute | solution.py:236
  35.9 3.4 %collective-permute-start.6 = (bf16[192,1792]{1,0:T(8,128)(2,1)S(1)}, bf16[192,1792]{1,0:T(8,128)(2,1)S(1)}, u32[]{:S(2)}, u32[]{:S(2)}) collective-permute-start(bf16[192,1792]{1,0:T(8,128)(2,1)S(1)} %get-tuple-element.34), channel_id=1, source_target_pairs={{0,1},{1,0},{2,3},{3,2},{4,5},{5,4},{6,7},{7,6},{8,9},{9,8},{10,11... | collective-permute-start | bytes 2064392 | tf_op jit(solution)/shard_map/ppermute | solution.py:236
  36.7 7.3 %collective-permute-start.20 = (bf16[48,1792]{1,0:T(8,128)(2,1)S(1)}, bf16[48,1792]{1,0:T(8,128)(2,1)S(1)}, u32[]{:S(2)}, u32[]{:S(2)}) collective-permute-start(bf16[48,1792]{1,0:T(8,128)(2,1)S(1)} %fusion.3), channel_id=1, source_target_pairs={{0,2},{1,3},{2,0},{3,1},{4,6},{5,7},{6,4},{7,5},{8,10},{9,11},{10,... | collective-permute-start | bytes 516104 | tf_op jit(solution)/shard_map/ppermute | solution.py:236
  37.5 16.2 %collective-permute-start.19 = (bf16[48,1792]{1,0:T(8,128)(2,1)S(1)}, bf16[48,1792]{1,0:T(8,128)(2,1)S(1)}, u32[]{:S(2)}, u32[]{:S(2)}) collective-permute-start(bf16[48,1792]{1,0:T(8,128)(2,1)S(1)} %fusion.8), channel_id=1, source_target_pairs={{0,8},{1,9},{2,10},{3,11},{4,12},{5,13},{6,14},{7,15},{8,0},{9,1},... | collective-permute-start | bytes 516104 | tf_op jit(solution)/shard_map/ppermute | solution.py:236
  39.5 11.0 %collective-permute-start.7 = (bf16[96,1792]{1,0:T(8,128)(2,1)S(1)}, bf16[96,1792]{1,0:T(8,128)(2,1)S(1)}, u32[]{:S(2)}, u32[]{:S(2)}) collective-permute-start(bf16[96,1792]{1,0:T(8,128)(2,1)S(1)} %fusion), channel_id=1, source_target_pairs={{0,2},{1,3},{2,0},{3,1},{4,6},{5,7},{6,4},{7,5},{8,10},{9,11},{10,... | collective-permute-start | bytes 1032200 | tf_op jit(solution)/shard_map/ppermute | solution.py:236
  44.0 9.6 %collective-permute-start.21 = (bf16[48,1792]{1,0:T(8,128)(2,1)S(1)}, bf16[48,1792]{1,0:T(8,128)(2,1)S(1)}, u32[]{:S(2)}, u32[]{:S(2)}) collective-permute-start(bf16[48,1792]{1,0:T(8,128)(2,1)S(1)} %fusion.5), channel_id=1, source_target_pairs={{0,12},{1,13},{2,14},{3,15},{4,8},{5,9},{6,10},{7,11},{8,4},{9,5},... | collective-permute-start | bytes 516104 | tf_op jit(solution)/shard_map/ppermute | solution.py:236
  50.7 5.8 %collective-permute-start.8 = (bf16[48,1792]{1,0:T(8,128)(2,1)S(1)}, bf16[48,1792]{1,0:T(8,128)(2,1)S(1)}, u32[]{:S(2)}, u32[]{:S(2)}) collective-permute-start(bf16[48,1792]{1,0:T(8,128)(2,1)S(1)} %get-tuple-element.47), channel_id=1, source_target_pairs={{0,4},{1,5},{2,6},{3,7},{4,0},{5,1},{6,2},{7,3},{8,12},{9,13},{10,... | collective-permute-start | bytes 516104 | tf_op jit(solution)/shard_map/ppermute | solution.py:236

commit v14 on v13

--- a/solution.py
+++ b/solution.py
@@ -14,11 +14,10 @@
 DIRECT = ()
 ORDER = {
     "z far": ("y own",),
-    "expert own+near": ("y own",),
-    "expert far": ("rc mid",),
+    "expert far": ("rc mid", "c own",),
     "c own": ("c near",),
-    "rz mid": ("rc far", "z near",),
-    "c far": ("z near", "expert mid",),
+    "rz mid": ("rc far",),
+    "c far": ("z near",),
     "ry own+near": ("y near",),
     "y far": ("z near",),
 }

time: 57.7 us -> 57.9 us (level)
  no operation moved by 1% of the time
where the time goes in v14:
time: 57.9 us; the launch traced here: 57.7 us
  starting transfers between devices  25.7 us (44%)
  waiting for transfers between devices  15.7 us (27%)
  Pallas kernels  15.1 us (26%)
  other arithmetic  0.83 us (1%)
    ppermute x22, starting transfers between devices, partner(): lax.ppermute(array, 'expert', [(i, i ^ distance) for i in range(devices)])  25.7 us
    ppermute x22, waiting for transfers between devices, partner(): lax.ppermute(array, 'expert', [(i, i ^ distance) for i in range(devices)])  15.7 us
    pallas_call x3, Pallas kernels, expert(): pl.pallas_call(functools.partial(expert_kernel, capacity, offsets), out_s...  7.39 us
    pallas_call x1, Pallas kernels, load(): pl.pallas_call(load_kernel, out_shape=[jax.ShapeDtypeStruct(w.shape, w.dt...  4.23 us
    pallas_call x1, Pallas kernels, shards(): pl.pallas_call(functools.partial(pack_kernel, capacity, planes), out_shap...  1.48 us
  transfers between devices with their start and end apart: 22, of which 7 were waited for; matrix products, arithmetic and copies ran while one was open for 2% of the time, Pallas kernels for 22%

profile of v14, /device:TPU:0, one launch (start us, length us, event | category | flops | bytes accessed | tf_op | source)
XLA Modules:
  0.0 57.7 jit_solution(7646650127511518857)
XLA Ops:
  0.0 1.5 %shard_map.73 = (bf16[48,1792]{1,0:T(8,128)(2,1)S(1)}, bf16[48,1792]{1,0:T(8,128)(2,1)S(1)}, bf16[48,1792]{1,0:T(8,128)(2,1)S(1)}, bf16[48,1792]{1,0:T(8,128)(2,1)S(1)}) custom-call(s32[2,16]{1,0:T(2,128)} %bitcast.2, bf16[16,7168]{1,0:T(8,128)(2,1)} %tok_hbm.1, f32[16,56]{1,0:T(8,128)} %scale_hbm.1), custom_call_target="tpu_custom_call" | custom-call | tf_op jit(solution)/shard_map/pallas_call | solution.py:238
  1.5 4.1 %collective-permute-start.9 = (bf16[48,1792]{1,0:T(8,128)(2,1)S(1)}, bf16[48,1792]{1,0:T(8,128)(2,1)S(1)}, u32[]{:S(2)}, u32[]{:S(2)}) collective-permute-start(bf16[48,1792]{1,0:T(8,128)(2,1)S(1)} %get-tuple-element.34), channel_id=1, source_target_pairs={{0,8},{1,9},{2,10},{3,11},{4,12},{5,13},{6,14},{7,15},{8,0},{9,1},... | collective-permute-start | bytes 516104 | tf_op jit(solution)/shard_map/ppermute | solution.py:235
  5.6 1.6 %collective-permute-start.1 = (bf16[48,1792]{1,0:T(8,128)(2,1)S(1)}, bf16[48,1792]{1,0:T(8,128)(2,1)S(1)}, u32[]{:S(2)}, u32[]{:S(2)}) collective-permute-start(bf16[48,1792]{1,0:T(8,128)(2,1)S(1)} %get-tuple-element.26), channel_id=1, source_target_pairs={{0,4},{1,5},{2,6},{3,7},{4,0},{5,1},{6,2},{7,3},{8,12},{9,13},{10,... | collective-permute-start | bytes 516104 | tf_op jit(solution)/shard_map/ppermute | solution.py:235
  7.2 1.5 %collective-permute-start = (bf16[48,1792]{1,0:T(8,128)(2,1)S(1)}, bf16[48,1792]{1,0:T(8,128)(2,1)S(1)}, u32[]{:S(2)}, u32[]{:S(2)}) collective-permute-start(bf16[48,1792]{1,0:T(8,128)(2,1)S(1)} %get-tuple-element.25.unused), channel_id=1, source_target_pairs={{0,2},{1,3},{2,0},{3,1},{4,6},{5,7},{6,4},{7,5},{8,10},{9,11},{10,... | collective-permute-start | bytes 516104 | tf_op jit(solution)/shard_map/ppermute | solution.py:235
  8.7 4.2 %shard_map.75 = (bf16[1,7168,256]{2,1,0:T(8,128)(2,1)S(1)}, bf16[1,7168,256]{2,1,0:T(8,128)(2,1)S(1)}, bf16[1,256,7168]{2,1,0:T(8,128)(2,1)S(1)}) custom-call(bf16[1,7168,256]{2,1,0:T(8,128)(2,1)} %gate_hbm.1, bf16[1,7168,256]{2,1,0:T(8,128)(2,1)} %up_hbm.1, bf16[1,256,7168]{2,1,0:T(8,128)(2,1)} %down_hbm.1, bf16[48,1792]{1,0:T(8,128)(2,1)S(1)} %get-tuple-element.25.unused), custom_call_target="tpu_custom_call" | custom-call | tf_op jit(solution)/shard_map/pallas_call | solution.py:280
  12.9 0.0 collective-permute-done
  13.0 0.3 collective-permute-start.15
  13.2 0.5 collective-permute-done.9
  13.8 1.6 %collective-permute-start.10 = (bf16[48,1792]{1,0:T(8,128)(2,1)S(1)}, bf16[48,1792]{1,0:T(8,128)(2,1)S(1)}, u32[]{:S(2)}, u32[]{:S(2)}) collective-permute-start(bf16[48,1792]{1,0:T(8,128)(2,1)S(1)} %collective-permute-done.9), channel_id=1, source_target_pairs={{0,2},{1,3},{2,0},{3,1},{4,6},{5,7},{6,4},{7,5},{8,10},{9,11},{10,... | collective-permute-start | bytes 516104 | tf_op jit(solution)/shard_map/ppermute | solution.py:235
  15.4 0.0 collective-permute-start.11
  15.4 0.0 collective-permute-done.1
  15.4 0.4 collective-permute-start.3
  15.8 0.2 collective-permute-start.2
  16.0 4.2 %collective-permute-done.15 = bf16[48,1792]{1,0:T(8,128)(2,1)S(1)} collective-permute-done((bf16[48,1792]{1,0:T(8,128)(2,1)S(1)}, bf16[48,1792]{1,0:T(8,128)(2,1)S(1)}, u32[]{:S(2)}, u32[]{:S(2)}) %collective-permute-start.15) | collective-permute-done | bytes 172064 | tf_op jit(solution)/shard_map/ppermute | solution.py:235
  20.3 1.3 %collective-permute-start.16 = (bf16[48,1792]{1,0:T(8,128)(2,1)S(1)}, bf16[48,1792]{1,0:T(8,128)(2,1)S(1)}, u32[]{:S(2)}, u32[]{:S(2)}) collective-permute-start(bf16[48,1792]{1,0:T(8,128)(2,1)S(1)} %collective-permute-done.15), channel_id=1, source_target_pairs={{0,2},{1,3},{2,0},{3,1},{4,6},{5,7},{6,4},{7,5},{8,10},{9,11},{10,... | collective-permute-start | bytes 516104 | tf_op jit(solution)/shard_map/ppermute | solution.py:235
  21.6 0.0 collective-permute-done.10
  21.6 0.0 collective-permute-start.12
  21.6 2.2 %collective-permute-done.3 = bf16[48,1792]{1,0:T(8,128)(2,1)S(1)} collective-permute-done((bf16[48,1792]{1,0:T(8,128)(2,1)S(1)}, bf16[48,1792]{1,0:T(8,128)(2,1)S(1)}, u32[]{:S(2)}, u32[]{:S(2)}) %collective-permute-start.3) | collective-permute-done | bytes 172064 | tf_op jit(solution)/shard_map/ppermute | solution.py:235
  23.8 0.0 collective-permute-start.4
  23.8 0.0 collective-permute-done.2
  23.8 0.0 collective-permute-done.11
  23.9 0.0 collective-permute-done.12
  23.9 2.3 %shard_map.77 = (bf16[96,1792]{1,0:T(8,128)(2,1)S(1)}, bf16[96,1792]{1,0:T(8,128)(2,1)S(1)}) custom-call(bf16[96,1792]{1,0:T(8,128)(2,1)S(1)} %pad_maximum_fusion.1.refs_0_, bf16[96,1792]{1,0:T(8,128)(2,1)S(1)} %pad_maximum_fusion.2.refs_1_, bf16[1,7168,256]{2,1,0:T(8,128)(2,1)S(1)} %get-tuple-element.28.refs_4_.refs_2_, ...), custom_call_target="tpu_custom_call" | custom-call | flops 528482304 | tf_op jit(solution)/shard_map/pallas_call | solution.py:265
  26.2 0.6 collective-permute-start.13
  26.8 0.0 collective-permute-done.4
  26.8 0.1 collective-permute-start.5
  26.9 0.0 collective-permute-done.16
  26.9 0.5 collective-permute-start.17
  27.5 0.5 collective-permute-done.13
  28.1 2.5 %collective-permute-start.14 = (bf16[48,1792]{1,0:T(8,128)(2,1)S(1)}, bf16[48,1792]{1,0:T(8,128)(2,1)S(1)}, u32[]{:S(2)}, u32[]{:S(2)}) collective-permute-start(bf16[48,1792]{1,0:T(8,128)(2,1)S(1)} %fusion.6), channel_id=1, source_target_pairs={{0,2},{1,3},{2,0},{3,1},{4,6},{5,7},{6,4},{7,5},{8,10},{9,11},{10,... | collective-permute-start | bytes 516104 | tf_op jit(solution)/shard_map/ppermute | solution.py:235
  30.7 0.0 collective-permute-done.5.refs_1_
  30.7 0.0 collective-permute-done.17.refs_1_
  30.7 2.3 %shard_map.78 = (bf16[96,1792]{1,0:T(8,128)(2,1)S(1)}, bf16[96,1792]{1,0:T(8,128)(2,1)S(1)}) custom-call(bf16[96,1792]{1,0:T(8,128)(2,1)S(1)} %constant_dynamic-update-slice_fusion.4.refs_0_, bf16[96,1792]{1,0:T(8,128)(2,1)S(1)} %collective-permute-done.17.refs_1_, bf16[1,7168,256]{2,1,0:T(8,128)(2,1)S(1)} %get-tuple-element.28.refs_4_.refs_2_, ...), custom_call_target="tpu_custom_call" | custom-call | flops 528482304 | tf_op jit(solution)/shard_map/pallas_call | solution.py:265
  33.0 0.1 collective-permute-start.18
  33.2 2.8 %shard_map.76 = (bf16[192,1792]{1,0:T(8,128)(2,1)S(1)}, bf16[192,1792]{1,0:T(8,128)(2,1)S(1)}) custom-call(bf16[96,1792]{1,0:T(8,128)(2,1)S(1)} %constant_dynamic-update-slice_fusion.refs_0_, bf16[96,1792]{1,0:T(8,128)(2,1)S(1)} %collective-permute-done.5.refs_1_, bf16[96,1792]{1,0:T(8,128)(2,1)S(1)} %pad_maximum_fusion.refs_2_, ...), custom_call_target="tpu_custom_call" | custom-call | flops 1056964608 | tf_op jit(solution)/shard_map/pallas_call | solution.py:265
  36.0 0.5 collective-permute-start.6
  36.5 0.1 convert_element_type.45
  36.6 0.0 collective-permute-done.14
  36.6 0.1 fusion.8
  36.7 0.0 collective-permute-done.18
  36.8 0.8 %collective-permute-start.20 = (bf16[48,1792]{1,0:T(8,128)(2,1)S(1)}, bf16[48,1792]{1,0:T(8,128)(2,1)S(1)}, u32[]{:S(2)}, u32[]{:S(2)}) collective-permute-start(bf16[48,1792]{1,0:T(8,128)(2,1)S(1)} %fusion.3), channel_id=1, source_target_pairs={{0,2},{1,3},{2,0},{3,1},{4,6},{5,7},{6,4},{7,5},{8,10},{9,11},{10,... | collective-permute-start | bytes 516104 | tf_op jit(solution)/shard_map/ppermute | solution.py:235
  37.6 1.7 %collective-permute-start.19 = (bf16[48,1792]{1,0:T(8,128)(2,1)S(1)}, bf16[48,1792]{1,0:T(8,128)(2,1)S(1)}, u32[]{:S(2)}, u32[]{:S(2)}) collective-permute-start(bf16[48,1792]{1,0:T(8,128)(2,1)S(1)} %fusion.8), channel_id=1, source_target_pairs={{0,8},{1,9},{2,10},{3,11},{4,12},{5,13},{6,14},{7,15},{8,0},{9,1},... | collective-permute-start | bytes 516104 | tf_op jit(solution)/shard_map/ppermute | solution.py:235
  39.3 0.0 collective-permute-done.6
  39.3 0.1 convert_element_type.46
  39.4 0.1 fusion
  39.5 0.7 %collective-permute-start.7 = (bf16[96,1792]{1,0:T(8,128)(2,1)S(1)}, bf16[96,1792]{1,0:T(8,128)(2,1)S(1)}, u32[]{:S(2)}, u32[]{:S(2)}) collective-permute-start(bf16[96,1792]{1,0:T(8,128)(2,1)S(1)} %fusion), channel_id=1, source_target_pairs={{0,2},{1,3},{2,0},{3,1},{4,6},{5,7},{6,4},{7,5},{8,10},{9,11},{10,... | collective-permute-start | bytes 1032200 | tf_op jit(solution)/shard_map/ppermute | solution.py:235
  40.3 3.8 %collective-permute-done.20 = bf16[48,1792]{1,0:T(8,128)(2,1)S(1)} collective-permute-done((bf16[48,1792]{1,0:T(8,128)(2,1)S(1)}, bf16[48,1792]{1,0:T(8,128)(2,1)S(1)}, u32[]{:S(2)}, u32[]{:S(2)}) %collective-permute-start.20) | collective-permute-done | bytes 172064 | tf_op jit(solution)/shard_map/ppermute | solution.py:235
  44.1 4.7 %collective-permute-start.21 = (bf16[48,1792]{1,0:T(8,128)(2,1)S(1)}, bf16[48,1792]{1,0:T(8,128)(2,1)S(1)}, u32[]{:S(2)}, u32[]{:S(2)}) collective-permute-start(bf16[48,1792]{1,0:T(8,128)(2,1)S(1)} %fusion.5), channel_id=1, source_target_pairs={{0,12},{1,13},{2,14},{3,15},{4,8},{5,9},{6,10},{7,11},{8,4},{9,5},... | collective-permute-start | bytes 516104 | tf_op jit(solution)/shard_map/ppermute | solution.py:235
  48.9 1.7 %collective-permute-done.7 = bf16[96,1792]{1,0:T(8,128)(2,1)S(1)} collective-permute-done((bf16[96,1792]{1,0:T(8,128)(2,1)S(1)}, bf16[96,1792]{1,0:T(8,128)(2,1)S(1)}, u32[]{:S(2)}, u32[]{:S(2)}) %collective-permute-start.7) | collective-permute-done | bytes 344096 | tf_op jit(solution)/shard_map/ppermute | solution.py:235
  50.6 0.1 fusion.2
  50.8 2.3 %collective-permute-start.8 = (bf16[48,1792]{1,0:T(8,128)(2,1)S(1)}, bf16[48,1792]{1,0:T(8,128)(2,1)S(1)}, u32[]{:S(2)}, u32[]{:S(2)}) collective-permute-start(bf16[48,1792]{1,0:T(8,128)(2,1)S(1)} %get-tuple-element.45), channel_id=1, source_target_pairs={{0,4},{1,5},{2,6},{3,7},{4,0},{5,1},{6,2},{7,3},{8,12},{9,13},{10,... | collective-permute-start | bytes 516104 | tf_op jit(solution)/shard_map/ppermute | solution.py:235
  53.1 1.0 %shard_map.74.plan_ref = bf16[4,128,48]{2,1,0:T(8,128)(2,1)S(1)} custom-call(s32[2,16]{1,0:T(2,128)} %bitcast.3, s32[2,16]{1,0:T(2,128)} %bitcast.4, bf16[48,1792]{1,0:T(8,128)(2,1)S(1)} %get-tuple-element.25.unused), custom_call_target="tpu_custom_call" | custom-call | tf_op jit(solution)/shard_map/pallas_call | solution.py:252
  54.1 0.0 collective-permute-done.19.refs_2_
  54.1 0.0 collective-permute-done.21.refs_3_
  54.2 2.5 %collective-permute-done.8.refs_1_ = bf16[48,1792]{1,0:T(8,128)(2,1)S(1)} collective-permute-done((bf16[48,1792]{1,0:T(8,128)(2,1)S(1)}, bf16[48,1792]{1,0:T(8,128)(2,1)S(1)}, u32[]{:S(2)}, u32[]{:S(2)}) %collective-permute-start.8) | collective-permute-done | bytes 172064 | tf_op jit(solution)/shard_map/ppermute | solution.py:235
  56.7 1.0 %shard_map.79 = bf16[16,7168]{1,0:T(8,128)(2,1)} custom-call(bf16[4,128,48]{2,1,0:T(8,128)(2,1)S(1)} %shard_map.74.plan_ref, bf16[48,1792]{1,0:T(8,128)(2,1)S(1)} %get-tuple-element.46.refs_0_, bf16[48,1792]{1,0:T(8,128)(2,1)S(1)} %collective-permute-done.8.refs_1_, bf16[48,1792]{1,0:T(8,128)(2,1)S(1)} %collective-permute-done.19.refs_2_, ...), custom_call_target="tpu_custom_call" | custom-call | tf_op jit(solution)/shard_map/pallas_call | solution.py:374
  (17 shorter events, 0.5 us)
Async XLA Ops:
  1.5 12.3 %collective-permute-start.9 = (bf16[48,1792]{1,0:T(8,128)(2,1)S(1)}, bf16[48,1792]{1,0:T(8,128)(2,1)S(1)}, u32[]{:S(2)}, u32[]{:S(2)}) collective-permute-start(bf16[48,1792]{1,0:T(8,128)(2,1)S(1)} %get-tuple-element.34), channel_id=1, source_target_pairs={{0,8},{1,9},{2,10},{3,11},{4,12},{5,13},{6,14},{7,15},{8,0},{9,1},... | collective-permute-start | bytes 516104 | tf_op jit(solution)/shard_map/ppermute | solution.py:235
  5.6 9.8 %collective-permute-start.1 = (bf16[48,1792]{1,0:T(8,128)(2,1)S(1)}, bf16[48,1792]{1,0:T(8,128)(2,1)S(1)}, u32[]{:S(2)}, u32[]{:S(2)}) collective-permute-start(bf16[48,1792]{1,0:T(8,128)(2,1)S(1)} %get-tuple-element.26), channel_id=1, source_target_pairs={{0,4},{1,5},{2,6},{3,7},{4,0},{5,1},{6,2},{7,3},{8,12},{9,13},{10,... | collective-permute-start | bytes 516104 | tf_op jit(solution)/shard_map/ppermute | solution.py:235
  7.2 5.8 %collective-permute-start = (bf16[48,1792]{1,0:T(8,128)(2,1)S(1)}, bf16[48,1792]{1,0:T(8,128)(2,1)S(1)}, u32[]{:S(2)}, u32[]{:S(2)}) collective-permute-start(bf16[48,1792]{1,0:T(8,128)(2,1)S(1)} %get-tuple-element.25.unused), channel_id=1, source_target_pairs={{0,2},{1,3},{2,0},{3,1},{4,6},{5,7},{6,4},{7,5},{8,10},{9,11},{10,... | collective-permute-start | bytes 516104 | tf_op jit(solution)/shard_map/ppermute | solution.py:235
  13.0 7.3 %collective-permute-start.15 = (bf16[48,1792]{1,0:T(8,128)(2,1)S(1)}, bf16[48,1792]{1,0:T(8,128)(2,1)S(1)}, u32[]{:S(2)}, u32[]{:S(2)}) collective-permute-start(bf16[48,1792]{1,0:T(8,128)(2,1)S(1)} %get-tuple-element.38), channel_id=1, source_target_pairs={{0,12},{1,13},{2,14},{3,15},{4,8},{5,9},{6,10},{7,11},{8,4},{9,5},... | collective-permute-start | bytes 516104 | tf_op jit(solution)/shard_map/ppermute | solution.py:235
  13.8 7.8 %collective-permute-start.10 = (bf16[48,1792]{1,0:T(8,128)(2,1)S(1)}, bf16[48,1792]{1,0:T(8,128)(2,1)S(1)}, u32[]{:S(2)}, u32[]{:S(2)}) collective-permute-start(bf16[48,1792]{1,0:T(8,128)(2,1)S(1)} %collective-permute-done.9), channel_id=1, source_target_pairs={{0,2},{1,3},{2,0},{3,1},{4,6},{5,7},{6,4},{7,5},{8,10},{9,11},{10,... | collective-permute-start | bytes 516104 | tf_op jit(solution)/shard_map/ppermute | solution.py:235
  15.4 8.5 %collective-permute-start.11 = (bf16[48,1792]{1,0:T(8,128)(2,1)S(1)}, bf16[48,1792]{1,0:T(8,128)(2,1)S(1)}, u32[]{:S(2)}, u32[]{:S(2)}) collective-permute-start(bf16[48,1792]{1,0:T(8,128)(2,1)S(1)} %collective-permute-done.9), channel_id=1, source_target_pairs={{0,1},{1,0},{2,3},{3,2},{4,5},{5,4},{6,7},{7,6},{8,9},{9,8},{10,11... | collective-permute-start | bytes 516104 | tf_op jit(solution)/shard_map/ppermute | solution.py:235
  15.4 8.4 %collective-permute-start.3 = (bf16[48,1792]{1,0:T(8,128)(2,1)S(1)}, bf16[48,1792]{1,0:T(8,128)(2,1)S(1)}, u32[]{:S(2)}, u32[]{:S(2)}) collective-permute-start(bf16[48,1792]{1,0:T(8,128)(2,1)S(1)} %collective-permute-done.1), channel_id=1, source_target_pairs={{0,2},{1,3},{2,0},{3,1},{4,6},{5,7},{6,4},{7,5},{8,10},{9,11},{10,... | collective-permute-start | bytes 516104 | tf_op jit(solution)/shard_map/ppermute | solution.py:235
  15.8 8.0 %collective-permute-start.2 = (bf16[48,1792]{1,0:T(8,128)(2,1)S(1)}, bf16[48,1792]{1,0:T(8,128)(2,1)S(1)}, u32[]{:S(2)}, u32[]{:S(2)}) collective-permute-start(bf16[48,1792]{1,0:T(8,128)(2,1)S(1)} %collective-permute-done.1), channel_id=1, source_target_pairs={{0,1},{1,0},{2,3},{3,2},{4,5},{5,4},{6,7},{7,6},{8,9},{9,8},{10,11... | collective-permute-start | bytes 516104 | tf_op jit(solution)/shard_map/ppermute | solution.py:235
  20.3 6.6 %collective-permute-start.16 = (bf16[48,1792]{1,0:T(8,128)(2,1)S(1)}, bf16[48,1792]{1,0:T(8,128)(2,1)S(1)}, u32[]{:S(2)}, u32[]{:S(2)}) collective-permute-start(bf16[48,1792]{1,0:T(8,128)(2,1)S(1)} %collective-permute-done.15), channel_id=1, source_target_pairs={{0,2},{1,3},{2,0},{3,1},{4,6},{5,7},{6,4},{7,5},{8,10},{9,11},{10,... | collective-permute-start | bytes 516104 | tf_op jit(solution)/shard_map/ppermute | solution.py:235
  21.6 2.3 %collective-permute-start.12 = (bf16[48,1792]{1,0:T(8,128)(2,1)S(1)}, bf16[48,1792]{1,0:T(8,128)(2,1)S(1)}, u32[]{:S(2)}, u32[]{:S(2)}) collective-permute-start(bf16[48,1792]{1,0:T(8,128)(2,1)S(1)} %collective-permute-done.10), channel_id=1, source_target_pairs={{0,1},{1,0},{2,3},{3,2},{4,5},{5,4},{6,7},{7,6},{8,9},{9,8},{10,11... | collective-permute-start | bytes 516104 | tf_op jit(solution)/shard_map/ppermute | solution.py:235
  23.8 3.0 %collective-permute-start.4 = (bf16[48,1792]{1,0:T(8,128)(2,1)S(1)}, bf16[48,1792]{1,0:T(8,128)(2,1)S(1)}, u32[]{:S(2)}, u32[]{:S(2)}) collective-permute-start(bf16[48,1792]{1,0:T(8,128)(2,1)S(1)} %collective-permute-done.3), channel_id=1, source_target_pairs={{0,1},{1,0},{2,3},{3,2},{4,5},{5,4},{6,7},{7,6},{8,9},{9,8},{10,11... | collective-permute-start | bytes 516104 | tf_op jit(solution)/shard_map/ppermute | solution.py:235
  26.2 1.9 %collective-permute-start.13 = (bf16[96,1792]{1,0:T(8,128)(2,1)S(1)}, bf16[96,1792]{1,0:T(8,128)(2,1)S(1)}, u32[]{:S(2)}, u32[]{:S(2)}) collective-permute-start(bf16[96,1792]{1,0:T(8,128)(2,1)S(1)} %get-tuple-element.36), channel_id=1, source_target_pairs={{0,1},{1,0},{2,3},{3,2},{4,5},{5,4},{6,7},{7,6},{8,9},{9,8},{10,11... | collective-permute-start | bytes 1032200 | tf_op jit(solution)/shard_map/ppermute | solution.py:235
  26.8 3.9 %collective-permute-start.5 = (bf16[96,1792]{1,0:T(8,128)(2,1)S(1)}, bf16[96,1792]{1,0:T(8,128)(2,1)S(1)}, u32[]{:S(2)}, u32[]{:S(2)}) collective-permute-start(bf16[96,1792]{1,0:T(8,128)(2,1)S(1)} %constant_dynamic-update-slice_fusion.refs_0_), channel_id=1, source_target_pairs={{0,1},{1,0},{2,3},{3,2},{4,5},{5,4},{6,7},{7,6},{8,9},{9,8},{10,11... | collective-permute-start | bytes 1032200 | tf_op jit(solution)/shard_map/ppermute | solution.py:235
  26.9 3.8 %collective-permute-start.17 = (bf16[96,1792]{1,0:T(8,128)(2,1)S(1)}, bf16[96,1792]{1,0:T(8,128)(2,1)S(1)}, u32[]{:S(2)}, u32[]{:S(2)}) collective-permute-start(bf16[96,1792]{1,0:T(8,128)(2,1)S(1)} %constant_dynamic-update-slice_fusion.4.refs_0_), channel_id=1, source_target_pairs={{0,1},{1,0},{2,3},{3,2},{4,5},{5,4},{6,7},{7,6},{8,9},{9,8},{10,11... | collective-permute-start | bytes 1032200 | tf_op jit(solution)/shard_map/ppermute | solution.py:235
  28.1 8.5 %collective-permute-start.14 = (bf16[48,1792]{1,0:T(8,128)(2,1)S(1)}, bf16[48,1792]{1,0:T(8,128)(2,1)S(1)}, u32[]{:S(2)}, u32[]{:S(2)}) collective-permute-start(bf16[48,1792]{1,0:T(8,128)(2,1)S(1)} %fusion.6), channel_id=1, source_target_pairs={{0,2},{1,3},{2,0},{3,1},{4,6},{5,7},{6,4},{7,5},{8,10},{9,11},{10,... | collective-permute-start | bytes 516104 | tf_op jit(solution)/shard_map/ppermute | solution.py:235
  33.0 3.7 %collective-permute-start.18 = (bf16[96,1792]{1,0:T(8,128)(2,1)S(1)}, bf16[96,1792]{1,0:T(8,128)(2,1)S(1)}, u32[]{:S(2)}, u32[]{:S(2)}) collective-permute-start(bf16[96,1792]{1,0:T(8,128)(2,1)S(1)} %get-tuple-element.42), channel_id=1, source_target_pairs={{0,1},{1,0},{2,3},{3,2},{4,5},{5,4},{6,7},{7,6},{8,9},{9,8},{10,11... | collective-permute-start | bytes 1032200 | tf_op jit(solution)/shard_map/ppermute | solution.py:235
  36.0 3.3 %collective-permute-start.6 = (bf16[192,1792]{1,0:T(8,128)(2,1)S(1)}, bf16[192,1792]{1,0:T(8,128)(2,1)S(1)}, u32[]{:S(2)}, u32[]{:S(2)}) collective-permute-start(bf16[192,1792]{1,0:T(8,128)(2,1)S(1)} %get-tuple-element.32), channel_id=1, source_target_pairs={{0,1},{1,0},{2,3},{3,2},{4,5},{5,4},{6,7},{7,6},{8,9},{9,8},{10,11... | collective-permute-start | bytes 2064392 | tf_op jit(solution)/shard_map/ppermute | solution.py:235
  36.8 7.3 %collective-permute-start.20 = (bf16[48,1792]{1,0:T(8,128)(2,1)S(1)}, bf16[48,1792]{1,0:T(8,128)(2,1)S(1)}, u32[]{:S(2)}, u32[]{:S(2)}) collective-permute-start(bf16[48,1792]{1,0:T(8,128)(2,1)S(1)} %fusion.3), channel_id=1, source_target_pairs={{0,2},{1,3},{2,0},{3,1},{4,6},{5,7},{6,4},{7,5},{8,10},{9,11},{10,... | collective-permute-start | bytes 516104 | tf_op jit(solution)/shard_map/ppermute | solution.py:235
  37.6 16.5 %collective-permute-start.19 = (bf16[48,1792]{1,0:T(8,128)(2,1)S(1)}, bf16[48,1792]{1,0:T(8,128)(2,1)S(1)}, u32[]{:S(2)}, u32[]{:S(2)}) collective-permute-start(bf16[48,1792]{1,0:T(8,128)(2,1)S(1)} %fusion.8), channel_id=1, source_target_pairs={{0,8},{1,9},{2,10},{3,11},{4,12},{5,13},{6,14},{7,15},{8,0},{9,1},... | collective-permute-start | bytes 516104 | tf_op jit(solution)/shard_map/ppermute | solution.py:235
  39.5 11.1 %collective-permute-start.7 = (bf16[96,1792]{1,0:T(8,128)(2,1)S(1)}, bf16[96,1792]{1,0:T(8,128)(2,1)S(1)}, u32[]{:S(2)}, u32[]{:S(2)}) collective-permute-start(bf16[96,1792]{1,0:T(8,128)(2,1)S(1)} %fusion), channel_id=1, source_target_pairs={{0,2},{1,3},{2,0},{3,1},{4,6},{5,7},{6,4},{7,5},{8,10},{9,11},{10,... | collective-permute-start | bytes 1032200 | tf_op jit(solution)/shard_map/ppermute | solution.py:235
  44.1 10.0 %collective-permute-start.21 = (bf16[48,1792]{1,0:T(8,128)(2,1)S(1)}, bf16[48,1792]{1,0:T(8,128)(2,1)S(1)}, u32[]{:S(2)}, u32[]{:S(2)}) collective-permute-start(bf16[48,1792]{1,0:T(8,128)(2,1)S(1)} %fusion.5), channel_id=1, source_target_pairs={{0,12},{1,13},{2,14},{3,15},{4,8},{5,9},{6,10},{7,11},{8,4},{9,5},... | collective-permute-start | bytes 516104 | tf_op jit(solution)/shard_map/ppermute | solution.py:235
  50.8 5.9 %collective-permute-start.8 = (bf16[48,1792]{1,0:T(8,128)(2,1)S(1)}, bf16[48,1792]{1,0:T(8,128)(2,1)S(1)}, u32[]{:S(2)}, u32[]{:S(2)}) collective-permute-start(bf16[48,1792]{1,0:T(8,128)(2,1)S(1)} %get-tuple-element.45), channel_id=1, source_target_pairs={{0,4},{1,5},{2,6},{3,7},{4,0},{5,1},{6,2},{7,3},{8,12},{9,13},{10,... | collective-permute-start | bytes 516104 | tf_op jit(solution)/shard_map/ppermute | solution.py:235

commit v15 on v13

--- a/solution.py
+++ b/solution.py
@@ -12,6 +12,7 @@
 GROUPS = ("own+near", "mid", "far")
 SPLIT = ("c mid", "c near",)
 DIRECT = ()
+APART = ("own+near",)
 ORDER = {
     "z far": ("y own",),
     "expert own+near": ("y own",),
@@ -200,14 +201,16 @@
 
 
 def mix_kernel(planes, plan_ref, *refs):
-    returned, out_ref = refs[:planes], refs[planes]
+    stay_ref, across_ref, *others, out_ref = refs
+    own = (stay_ref[...] + across_ref[...].astype(jnp.float32)).astype(jnp.bfloat16)
     rows, features = out_ref.shape
     width, tall = features // QUARTERS, QUARTERS * rows
     total = jnp.zeros((2 * tall, width), jnp.float32)
     for at in range(0, planes, 4):
         some = range(at, min(at + 4, planes))
         plan = jnp.concatenate([plan_ref[offset] for offset in some], axis=1)
-        answers = jnp.concatenate([returned[offset][...] for offset in some], axis=0)
+        answers = [others[offset - 1][...] if offset else own for offset in some]
+        answers = jnp.concatenate(answers, axis=0)
         total = total + exact_dot(plan, answers)
     total = (total[:tall] + total[tall:]).astype(jnp.bfloat16)
     for quarter in range(QUARTERS):
@@ -332,11 +335,20 @@
             kept, arrived = result("expert " + name)[0], result("rc " + name)[0]
             return fold(kept, arrived, len(places[name]))
         elif kind == "ry":
-            inputs = result("sum " + name)[:1]
+            leaving, count = result("sum " + name)[0], len(places[name])
+            inputs = jnp.split(leaving, count, axis=0) if name in APART else [leaving]
         elif kind == "answer":
-            total = result("sum " + name)[1] + result("ry " + name)[0].astype(jnp.float32)
-            total = total.astype(jnp.bfloat16)
-            return [total[at * tall : (at + 1) * tall] for at in range(len(places[name]))]
+            stay, count = result("sum " + name)[1], len(places[name])
+            if name not in APART:
+                total = stay + result("ry " + name)[0].astype(jnp.float32)
+                return jnp.split(total.astype(jnp.bfloat16), count, axis=0)
+            pieces = list(zip(jnp.split(stay, count, axis=0), result("ry " + name)))
+            return [None] + [
+                (one + two.astype(jnp.float32)).astype(jnp.bfloat16) for one, two in pieces[1:]
+            ]
+        elif kind == "last":
+            stay = jnp.split(result("sum " + name)[1], len(places[name]), axis=0)[0]
+            return [stay, result("ry " + name)[0]]
         elif kind == "load":
             inputs = packed[:1]
         elif kind == "rz":
@@ -370,12 +382,12 @@
         if group != "own":
             pieces[-len(result("rz " + group)) :] = result("rz " + group)
         returned.update(zip(places[group], pieces))
-    returned = [returned[at] for at in range(planes)]
+    returned = result("last " + APART[0]) + [returned[at] for at in range(1, planes)]
 
     return pl.pallas_call(
         functools.partial(mix_kernel, planes),
         out_shape=jax.ShapeDtypeStruct((tok_rows, features), jnp.bfloat16),
-        in_specs=[vmem] * (planes + 1),
+        in_specs=[vmem] * (planes + 2),
         out_specs=vmem,
         compiler_params=params,
     )(plan, *returned)

time: 57.7 us -> 57.3 us (level)
    ppermute x22 -> x23, starting transfers between devices: 25.5 us -> 25.1 us  [partner(): lax.ppermute(array, 'expert', [(i, i ^ distance) for i in range(devices)])]
    ppermute x22 -> x23, waiting for transfers between devices: 15.7 us -> 15.7 us  [partner(): lax.ppermute(array, 'expert', [(i, i ^ distance) for i in range(devices)])]
  transfers between devices with their start and end apart: 22 -> 23, of which waited for: 7 -> 8; matrix products, arithmetic and copies ran while one was open for 2% -> 2% of each run, Pallas kernels for 22% -> 22%
where the time goes in v15:
time: 57.3 us; the launch traced here: 57.2 us
  starting transfers between devices  25.1 us (44%)
  waiting for transfers between devices  15.7 us (27%)
  Pallas kernels  15.1 us (26%)
  other arithmetic  0.83 us (1%)
    ppermute x23, starting transfers between devices, partner(): lax.ppermute(array, 'expert', [(i, i ^ distance) for i in range(devices)])  25.1 us
    ppermute x23, waiting for transfers between devices, partner(): lax.ppermute(array, 'expert', [(i, i ^ distance) for i in range(devices)])  15.7 us
    pallas_call x3, Pallas kernels, expert(): pl.pallas_call(functools.partial(expert_kernel, capacity, offsets), out_s...  7.39 us
    pallas_call x1, Pallas kernels, load(): pl.pallas_call(load_kernel, out_shape=[jax.ShapeDtypeStruct(w.shape, w.dt...  4.23 us
    pallas_call x1, Pallas kernels, shards(): pl.pallas_call(functools.partial(pack_kernel, capacity, planes), out_shap...  1.48 us
  transfers between devices with their start and end apart: 23, of which 8 were waited for; matrix products, arithmetic and copies ran while one was open for 2% of the time, Pallas kernels for 22%

profile of v15, /device:TPU:0, one launch (start us, length us, event | category | flops | bytes accessed | tf_op | source)
XLA Modules:
  0.0 57.2 jit_solution(5894951559263089449)
XLA Ops:
  0.0 1.5 %shard_map.73 = (bf16[48,1792]{1,0:T(8,128)(2,1)S(1)}, bf16[48,1792]{1,0:T(8,128)(2,1)S(1)}, bf16[48,1792]{1,0:T(8,128)(2,1)S(1)}, bf16[48,1792]{1,0:T(8,128)(2,1)S(1)}) custom-call(s32[2,16]{1,0:T(2,128)} %bitcast.2, bf16[16,7168]{1,0:T(8,128)(2,1)} %tok_hbm.1, f32[16,56]{1,0:T(8,128)} %scale_hbm.1), custom_call_target="tpu_custom_call" | custom-call | tf_op jit(solution)/shard_map/pallas_call | solution.py:242
  1.5 4.1 %collective-permute-start.10 = (bf16[48,1792]{1,0:T(8,128)(2,1)S(1)}, bf16[48,1792]{1,0:T(8,128)(2,1)S(1)}, u32[]{:S(2)}, u32[]{:S(2)}) collective-permute-start(bf16[48,1792]{1,0:T(8,128)(2,1)S(1)} %get-tuple-element.36), channel_id=1, source_target_pairs={{0,8},{1,9},{2,10},{3,11},{4,12},{5,13},{6,14},{7,15},{8,0},{9,1},... | collective-permute-start | bytes 516104 | tf_op jit(solution)/shard_map/ppermute | solution.py:239
  5.6 1.5 %collective-permute-start = (bf16[48,1792]{1,0:T(8,128)(2,1)S(1)}, bf16[48,1792]{1,0:T(8,128)(2,1)S(1)}, u32[]{:S(2)}, u32[]{:S(2)}) collective-permute-start(bf16[48,1792]{1,0:T(8,128)(2,1)S(1)} %get-tuple-element.26.unused), channel_id=1, source_target_pairs={{0,2},{1,3},{2,0},{3,1},{4,6},{5,7},{6,4},{7,5},{8,10},{9,11},{10,... | collective-permute-start | bytes 516104 | tf_op jit(solution)/shard_map/ppermute | solution.py:239
  7.1 1.6 %collective-permute-start.1 = (bf16[48,1792]{1,0:T(8,128)(2,1)S(1)}, bf16[48,1792]{1,0:T(8,128)(2,1)S(1)}, u32[]{:S(2)}, u32[]{:S(2)}) collective-permute-start(bf16[48,1792]{1,0:T(8,128)(2,1)S(1)} %get-tuple-element.28), channel_id=1, source_target_pairs={{0,4},{1,5},{2,6},{3,7},{4,0},{5,1},{6,2},{7,3},{8,12},{9,13},{10,... | collective-permute-start | bytes 516104 | tf_op jit(solution)/shard_map/ppermute | solution.py:239
  8.7 4.2 %shard_map.75 = (bf16[1,7168,256]{2,1,0:T(8,128)(2,1)S(1)}, bf16[1,7168,256]{2,1,0:T(8,128)(2,1)S(1)}, bf16[1,256,7168]{2,1,0:T(8,128)(2,1)S(1)}) custom-call(bf16[1,7168,256]{2,1,0:T(8,128)(2,1)} %gate_hbm.1, bf16[1,7168,256]{2,1,0:T(8,128)(2,1)} %up_hbm.1, bf16[1,256,7168]{2,1,0:T(8,128)(2,1)} %down_hbm.1, bf16[48,1792]{1,0:T(8,128)(2,1)S(1)} %get-tuple-element.26.unused), custom_call_target="tpu_custom_call" | custom-call | tf_op jit(solution)/shard_map/pallas_call | solution.py:284
  12.9 0.0 collective-permute-done
  13.0 0.3 collective-permute-start.16
  13.2 0.5 collective-permute-done.10
  13.8 1.6 %collective-permute-start.11 = (bf16[48,1792]{1,0:T(8,128)(2,1)S(1)}, bf16[48,1792]{1,0:T(8,128)(2,1)S(1)}, u32[]{:S(2)}, u32[]{:S(2)}) collective-permute-start(bf16[48,1792]{1,0:T(8,128)(2,1)S(1)} %collective-permute-done.10), channel_id=1, source_target_pairs={{0,2},{1,3},{2,0},{3,1},{4,6},{5,7},{6,4},{7,5},{8,10},{9,11},{10,... | collective-permute-start | bytes 516104 | tf_op jit(solution)/shard_map/ppermute | solution.py:239
  15.3 0.1 collective-permute-start.12
  15.4 0.0 collective-permute-done.1
  15.4 0.5 collective-permute-start.3
  16.0 0.2 collective-permute-start.2
  16.1 4.2 %collective-permute-done.16 = bf16[48,1792]{1,0:T(8,128)(2,1)S(1)} collective-permute-done((bf16[48,1792]{1,0:T(8,128)(2,1)S(1)}, bf16[48,1792]{1,0:T(8,128)(2,1)S(1)}, u32[]{:S(2)}, u32[]{:S(2)}) %collective-permute-start.16) | collective-permute-done | bytes 172064 | tf_op jit(solution)/shard_map/ppermute | solution.py:239
  20.3 0.5 collective-permute-start.17
  20.8 0.0 collective-permute-done.11
  20.8 0.0 collective-permute-start.13
  20.8 2.9 %collective-permute-done.3 = bf16[48,1792]{1,0:T(8,128)(2,1)S(1)} collective-permute-done((bf16[48,1792]{1,0:T(8,128)(2,1)S(1)}, bf16[48,1792]{1,0:T(8,128)(2,1)S(1)}, u32[]{:S(2)}, u32[]{:S(2)}) %collective-permute-start.3) | collective-permute-done | bytes 172064 | tf_op jit(solution)/shard_map/ppermute | solution.py:239
  23.7 0.0 collective-permute-start.4
  23.7 0.0 collective-permute-done.2
  23.7 0.0 collective-permute-done.12
  23.7 0.0 collective-permute-done.13
  23.8 2.3 %shard_map.77 = (bf16[96,1792]{1,0:T(8,128)(2,1)S(1)}, bf16[96,1792]{1,0:T(8,128)(2,1)S(1)}) custom-call(bf16[96,1792]{1,0:T(8,128)(2,1)S(1)} %pad_maximum_fusion.1.refs_0_, bf16[96,1792]{1,0:T(8,128)(2,1)S(1)} %pad_maximum_fusion.2.refs_1_, bf16[1,7168,256]{2,1,0:T(8,128)(2,1)S(1)} %get-tuple-element.30.refs_4_.refs_2_, ...), custom_call_target="tpu_custom_call" | custom-call | flops 528482304 | tf_op jit(solution)/shard_map/pallas_call | solution.py:269
  26.1 0.6 collective-permute-start.14
  26.7 0.0 collective-permute-done.17
  26.7 0.1 collective-permute-start.18
  26.8 0.0 collective-permute-done.4
  26.8 0.5 collective-permute-start.5
  27.4 0.5 collective-permute-done.14
  28.0 2.6 %collective-permute-start.15 = (bf16[48,1792]{1,0:T(8,128)(2,1)S(1)}, bf16[48,1792]{1,0:T(8,128)(2,1)S(1)}, u32[]{:S(2)}, u32[]{:S(2)}) collective-permute-start(bf16[48,1792]{1,0:T(8,128)(2,1)S(1)} %fusion.4), channel_id=1, source_target_pairs={{0,2},{1,3},{2,0},{3,1},{4,6},{5,7},{6,4},{7,5},{8,10},{9,11},{10,... | collective-permute-start | bytes 516104 | tf_op jit(solution)/shard_map/ppermute | solution.py:239
  30.6 0.0 collective-permute-done.18.refs_1_
  30.6 2.3 %shard_map.78 = (bf16[96,1792]{1,0:T(8,128)(2,1)S(1)}, bf16[96,1792]{1,0:T(8,128)(2,1)S(1)}) custom-call(bf16[96,1792]{1,0:T(8,128)(2,1)S(1)} %constant_dynamic-update-slice_fusion.4.refs_0_, bf16[96,1792]{1,0:T(8,128)(2,1)S(1)} %collective-permute-done.18.refs_1_, bf16[1,7168,256]{2,1,0:T(8,128)(2,1)S(1)} %get-tuple-element.30.refs_4_.refs_2_, ...), custom_call_target="tpu_custom_call" | custom-call | flops 528482304 | tf_op jit(solution)/shard_map/pallas_call | solution.py:269
  32.9 0.1 collective-permute-start.19
  33.1 0.0 collective-permute-done.5.refs_1_
  33.1 2.8 %shard_map.76 = (bf16[192,1792]{1,0:T(8,128)(2,1)S(1)}, bf16[192,1792]{1,0:T(8,128)(2,1)S(1)}) custom-call(bf16[96,1792]{1,0:T(8,128)(2,1)S(1)} %constant_dynamic-update-slice_fusion.refs_0_, bf16[96,1792]{1,0:T(8,128)(2,1)S(1)} %collective-permute-done.5.refs_1_, bf16[96,1792]{1,0:T(8,128)(2,1)S(1)} %pad_maximum_fusion.refs_2_, ...), custom_call_target="tpu_custom_call" | custom-call | flops 1056964608 | tf_op jit(solution)/shard_map/pallas_call | solution.py:269
  35.9 0.5 collective-permute-start.6
  36.4 0.1 convert_element_type.45
  36.5 0.0 collective-permute-done.15
  36.5 0.1 fusion.6
  36.6 0.0 collective-permute-done.19
  36.7 0.1 fusion.1
  36.7 0.8 %collective-permute-start.21 = (bf16[48,1792]{1,0:T(8,128)(2,1)S(1)}, bf16[48,1792]{1,0:T(8,128)(2,1)S(1)}, u32[]{:S(2)}, u32[]{:S(2)}) collective-permute-start(bf16[48,1792]{1,0:T(8,128)(2,1)S(1)} %fusion.1), channel_id=1, source_target_pairs={{0,2},{1,3},{2,0},{3,1},{4,6},{5,7},{6,4},{7,5},{8,10},{9,11},{10,... | collective-permute-start | bytes 516104 | tf_op jit(solution)/shard_map/ppermute | solution.py:239
  37.5 1.9 %collective-permute-start.20 = (bf16[48,1792]{1,0:T(8,128)(2,1)S(1)}, bf16[48,1792]{1,0:T(8,128)(2,1)S(1)}, u32[]{:S(2)}, u32[]{:S(2)}) collective-permute-start(bf16[48,1792]{1,0:T(8,128)(2,1)S(1)} %fusion.6), channel_id=1, source_target_pairs={{0,8},{1,9},{2,10},{3,11},{4,12},{5,13},{6,14},{7,15},{8,0},{9,1},... | collective-permute-start | bytes 516104 | tf_op jit(solution)/shard_map/ppermute | solution.py:239
  39.4 0.0 collective-permute-done.6
  39.4 0.1 convert_element_type.46
  39.5 0.1 fusion
  39.6 1.3 %collective-permute-start.8 = (bf16[48,1792]{1,0:T(8,128)(2,1)S(1)}, bf16[48,1792]{1,0:T(8,128)(2,1)S(1)}, u32[]{:S(2)}, u32[]{:S(2)}) collective-permute-start(bf16[48,1792]{1,0:T(8,128)(2,1)S(1)} %get-tuple-element.51), channel_id=1, source_target_pairs={{0,2},{1,3},{2,0},{3,1},{4,6},{5,7},{6,4},{7,5},{8,10},{9,11},{10,... | collective-permute-start | bytes 516104 | tf_op jit(solution)/shard_map/ppermute | solution.py:239
  40.9 3.1 %collective-permute-done.21 = bf16[48,1792]{1,0:T(8,128)(2,1)S(1)} collective-permute-done((bf16[48,1792]{1,0:T(8,128)(2,1)S(1)}, bf16[48,1792]{1,0:T(8,128)(2,1)S(1)}, u32[]{:S(2)}, u32[]{:S(2)}) %collective-permute-start.21) | collective-permute-done | bytes 172064 | tf_op jit(solution)/shard_map/ppermute | solution.py:239
  44.0 0.1 fusion.3
  44.1 4.8 %collective-permute-start.22 = (bf16[48,1792]{1,0:T(8,128)(2,1)S(1)}, bf16[48,1792]{1,0:T(8,128)(2,1)S(1)}, u32[]{:S(2)}, u32[]{:S(2)}) collective-permute-start(bf16[48,1792]{1,0:T(8,128)(2,1)S(1)} %fusion.3), channel_id=1, source_target_pairs={{0,12},{1,13},{2,14},{3,15},{4,8},{5,9},{6,10},{7,11},{8,4},{9,5},... | collective-permute-start | bytes 516104 | tf_op jit(solution)/shard_map/ppermute | solution.py:239
  48.9 0.7 %collective-permute-start.7 = (bf16[48,1792]{1,0:T(8,128)(2,1)S(1)}, bf16[48,1792]{1,0:T(8,128)(2,1)S(1)}, u32[]{:S(2)}, u32[]{:S(2)}) collective-permute-start(bf16[48,1792]{1,0:T(8,128)(2,1)S(1)} %get-tuple-element.35), channel_id=1, source_target_pairs={{0,2},{1,3},{2,0},{3,1},{4,6},{5,7},{6,4},{7,5},{8,10},{9,11},{10,... | collective-permute-start | bytes 516104 | tf_op jit(solution)/shard_map/ppermute | solution.py:239
  49.6 0.0 collective-permute-done.8
  49.7 0.9 %collective-permute-start.9 = (bf16[48,1792]{1,0:T(8,128)(2,1)S(1)}, bf16[48,1792]{1,0:T(8,128)(2,1)S(1)}, u32[]{:S(2)}, u32[]{:S(2)}) collective-permute-start(bf16[48,1792]{1,0:T(8,128)(2,1)S(1)} %get-tuple-element.49), channel_id=1, source_target_pairs={{0,4},{1,5},{2,6},{3,7},{4,0},{5,1},{6,2},{7,3},{8,12},{9,13},{10,... | collective-permute-start | bytes 516104 | tf_op jit(solution)/shard_map/ppermute | solution.py:239
  50.6 1.0 %shard_map.74.plan_ref = bf16[4,128,48]{2,1,0:T(8,128)(2,1)S(1)} custom-call(s32[2,16]{1,0:T(2,128)} %bitcast.3, s32[2,16]{1,0:T(2,128)} %bitcast.4, bf16[48,1792]{1,0:T(8,128)(2,1)S(1)} %get-tuple-element.26.unused), custom_call_target="tpu_custom_call" | custom-call | tf_op jit(solution)/shard_map/pallas_call | solution.py:256
  51.6 1.4 %collective-permute-done.20.refs_3_ = bf16[48,1792]{1,0:T(8,128)(2,1)S(1)} collective-permute-done((bf16[48,1792]{1,0:T(8,128)(2,1)S(1)}, bf16[48,1792]{1,0:T(8,128)(2,1)S(1)}, u32[]{:S(2)}, u32[]{:S(2)}) %collective-permute-start.20) | collective-permute-done | bytes 172064 | tf_op jit(solution)/shard_map/ppermute | solution.py:239
  53.0 0.0 collective-permute-done.22.refs_4_
  53.0 1.3 %collective-permute-done.7.refs_1_ = bf16[48,1792]{1,0:T(8,128)(2,1)S(1)} collective-permute-done((bf16[48,1792]{1,0:T(8,128)(2,1)S(1)}, bf16[48,1792]{1,0:T(8,128)(2,1)S(1)}, u32[]{:S(2)}, u32[]{:S(2)}) %collective-permute-start.7) | collective-permute-done | bytes 172064 | tf_op jit(solution)/shard_map/ppermute | solution.py:239
  54.3 1.9 %collective-permute-done.9.refs_2_ = bf16[48,1792]{1,0:T(8,128)(2,1)S(1)} collective-permute-done((bf16[48,1792]{1,0:T(8,128)(2,1)S(1)}, bf16[48,1792]{1,0:T(8,128)(2,1)S(1)}, u32[]{:S(2)}, u32[]{:S(2)}) %collective-permute-start.9) | collective-permute-done | bytes 172064 | tf_op jit(solution)/shard_map/ppermute | solution.py:239
  56.2 1.0 %shard_map.79 = bf16[16,7168]{1,0:T(8,128)(2,1)} custom-call(bf16[4,128,48]{2,1,0:T(8,128)(2,1)S(1)} %shard_map.74.plan_ref, f32[48,1792]{1,0:T(8,128)S(1)} %get-tuple-element.50.refs_0_, bf16[48,1792]{1,0:T(8,128)(2,1)S(1)} %collective-permute-done.7.refs_1_, bf16[48,1792]{1,0:T(8,128)(2,1)S(1)} %collective-permute-done.9.refs_2_, ...), custom_call_target="tpu_custom_call" | custom-call | tf_op jit(solution)/shard_map/pallas_call | solution.py:387
  (16 shorter events, 0.4 us)
Async XLA Ops:
  1.5 12.3 %collective-permute-start.10 = (bf16[48,1792]{1,0:T(8,128)(2,1)S(1)}, bf16[48,1792]{1,0:T(8,128)(2,1)S(1)}, u32[]{:S(2)}, u32[]{:S(2)}) collective-permute-start(bf16[48,1792]{1,0:T(8,128)(2,1)S(1)} %get-tuple-element.36), channel_id=1, source_target_pairs={{0,8},{1,9},{2,10},{3,11},{4,12},{5,13},{6,14},{7,15},{8,0},{9,1},... | collective-permute-start | bytes 516104 | tf_op jit(solution)/shard_map/ppermute | solution.py:239
  5.6 7.4 %collective-permute-start = (bf16[48,1792]{1,0:T(8,128)(2,1)S(1)}, bf16[48,1792]{1,0:T(8,128)(2,1)S(1)}, u32[]{:S(2)}, u32[]{:S(2)}) collective-permute-start(bf16[48,1792]{1,0:T(8,128)(2,1)S(1)} %get-tuple-element.26.unused), channel_id=1, source_target_pairs={{0,2},{1,3},{2,0},{3,1},{4,6},{5,7},{6,4},{7,5},{8,10},{9,11},{10,... | collective-permute-start | bytes 516104 | tf_op jit(solution)/shard_map/ppermute | solution.py:239
  7.1 8.3 %collective-permute-start.1 = (bf16[48,1792]{1,0:T(8,128)(2,1)S(1)}, bf16[48,1792]{1,0:T(8,128)(2,1)S(1)}, u32[]{:S(2)}, u32[]{:S(2)}) collective-permute-start(bf16[48,1792]{1,0:T(8,128)(2,1)S(1)} %get-tuple-element.28), channel_id=1, source_target_pairs={{0,4},{1,5},{2,6},{3,7},{4,0},{5,1},{6,2},{7,3},{8,12},{9,13},{10,... | collective-permute-start | bytes 516104 | tf_op jit(solution)/shard_map/ppermute | solution.py:239
  13.0 7.3 %collective-permute-start.16 = (bf16[48,1792]{1,0:T(8,128)(2,1)S(1)}, bf16[48,1792]{1,0:T(8,128)(2,1)S(1)}, u32[]{:S(2)}, u32[]{:S(2)}) collective-permute-start(bf16[48,1792]{1,0:T(8,128)(2,1)S(1)} %get-tuple-element.40), channel_id=1, source_target_pairs={{0,12},{1,13},{2,14},{3,15},{4,8},{5,9},{6,10},{7,11},{8,4},{9,5},... | collective-permute-start | bytes 516104 | tf_op jit(solution)/shard_map/ppermute | solution.py:239
  13.8 7.0 %collective-permute-start.11 = (bf16[48,1792]{1,0:T(8,128)(2,1)S(1)}, bf16[48,1792]{1,0:T(8,128)(2,1)S(1)}, u32[]{:S(2)}, u32[]{:S(2)}) collective-permute-start(bf16[48,1792]{1,0:T(8,128)(2,1)S(1)} %collective-permute-done.10), channel_id=1, source_target_pairs={{0,2},{1,3},{2,0},{3,1},{4,6},{5,7},{6,4},{7,5},{8,10},{9,11},{10,... | collective-permute-start | bytes 516104 | tf_op jit(solution)/shard_map/ppermute | solution.py:239
  15.3 8.4 %collective-permute-start.12 = (bf16[48,1792]{1,0:T(8,128)(2,1)S(1)}, bf16[48,1792]{1,0:T(8,128)(2,1)S(1)}, u32[]{:S(2)}, u32[]{:S(2)}) collective-permute-start(bf16[48,1792]{1,0:T(8,128)(2,1)S(1)} %collective-permute-done.10), channel_id=1, source_target_pairs={{0,1},{1,0},{2,3},{3,2},{4,5},{5,4},{6,7},{7,6},{8,9},{9,8},{10,11... | collective-permute-start | bytes 516104 | tf_op jit(solution)/shard_map/ppermute | solution.py:239
  15.4 8.2 %collective-permute-start.3 = (bf16[48,1792]{1,0:T(8,128)(2,1)S(1)}, bf16[48,1792]{1,0:T(8,128)(2,1)S(1)}, u32[]{:S(2)}, u32[]{:S(2)}) collective-permute-start(bf16[48,1792]{1,0:T(8,128)(2,1)S(1)} %collective-permute-done.1), channel_id=1, source_target_pairs={{0,2},{1,3},{2,0},{3,1},{4,6},{5,7},{6,4},{7,5},{8,10},{9,11},{10,... | collective-permute-start | bytes 516104 | tf_op jit(solution)/shard_map/ppermute | solution.py:239
  16.0 7.7 %collective-permute-start.2 = (bf16[48,1792]{1,0:T(8,128)(2,1)S(1)}, bf16[48,1792]{1,0:T(8,128)(2,1)S(1)}, u32[]{:S(2)}, u32[]{:S(2)}) collective-permute-start(bf16[48,1792]{1,0:T(8,128)(2,1)S(1)} %collective-permute-done.1), channel_id=1, source_target_pairs={{0,1},{1,0},{2,3},{3,2},{4,5},{5,4},{6,7},{7,6},{8,9},{9,8},{10,11... | collective-permute-start | bytes 516104 | tf_op jit(solution)/shard_map/ppermute | solution.py:239
  20.3 6.4 %collective-permute-start.17 = (bf16[48,1792]{1,0:T(8,128)(2,1)S(1)}, bf16[48,1792]{1,0:T(8,128)(2,1)S(1)}, u32[]{:S(2)}, u32[]{:S(2)}) collective-permute-start(bf16[48,1792]{1,0:T(8,128)(2,1)S(1)} %collective-permute-done.16), channel_id=1, source_target_pairs={{0,2},{1,3},{2,0},{3,1},{4,6},{5,7},{6,4},{7,5},{8,10},{9,11},{10,... | collective-permute-start | bytes 516104 | tf_op jit(solution)/shard_map/ppermute | solution.py:239
  20.8 3.0 %collective-permute-start.13 = (bf16[48,1792]{1,0:T(8,128)(2,1)S(1)}, bf16[48,1792]{1,0:T(8,128)(2,1)S(1)}, u32[]{:S(2)}, u32[]{:S(2)}) collective-permute-start(bf16[48,1792]{1,0:T(8,128)(2,1)S(1)} %collective-permute-done.11), channel_id=1, source_target_pairs={{0,1},{1,0},{2,3},{3,2},{4,5},{5,4},{6,7},{7,6},{8,9},{9,8},{10,11... | collective-permute-start | bytes 516104 | tf_op jit(solution)/shard_map/ppermute | solution.py:239
  23.7 3.1 %collective-permute-start.4 = (bf16[48,1792]{1,0:T(8,128)(2,1)S(1)}, bf16[48,1792]{1,0:T(8,128)(2,1)S(1)}, u32[]{:S(2)}, u32[]{:S(2)}) collective-permute-start(bf16[48,1792]{1,0:T(8,128)(2,1)S(1)} %collective-permute-done.3), channel_id=1, source_target_pairs={{0,1},{1,0},{2,3},{3,2},{4,5},{5,4},{6,7},{7,6},{8,9},{9,8},{10,11... | collective-permute-start | bytes 516104 | tf_op jit(solution)/shard_map/ppermute | solution.py:239
  26.1 1.9 %collective-permute-start.14 = (bf16[96,1792]{1,0:T(8,128)(2,1)S(1)}, bf16[96,1792]{1,0:T(8,128)(2,1)S(1)}, u32[]{:S(2)}, u32[]{:S(2)}) collective-permute-start(bf16[96,1792]{1,0:T(8,128)(2,1)S(1)} %get-tuple-element.38), channel_id=1, source_target_pairs={{0,1},{1,0},{2,3},{3,2},{4,5},{5,4},{6,7},{7,6},{8,9},{9,8},{10,11... | collective-permute-start | bytes 1032200 | tf_op jit(solution)/shard_map/ppermute | solution.py:239
  26.7 3.9 %collective-permute-start.18 = (bf16[96,1792]{1,0:T(8,128)(2,1)S(1)}, bf16[96,1792]{1,0:T(8,128)(2,1)S(1)}, u32[]{:S(2)}, u32[]{:S(2)}) collective-permute-start(bf16[96,1792]{1,0:T(8,128)(2,1)S(1)} %constant_dynamic-update-slice_fusion.4.refs_0_), channel_id=1, source_target_pairs={{0,1},{1,0},{2,3},{3,2},{4,5},{5,4},{6,7},{7,6},{8,9},{9,8},{10,11... | collective-permute-start | bytes 1032200 | tf_op jit(solution)/shard_map/ppermute | solution.py:239
  26.8 6.3 %collective-permute-start.5 = (bf16[96,1792]{1,0:T(8,128)(2,1)S(1)}, bf16[96,1792]{1,0:T(8,128)(2,1)S(1)}, u32[]{:S(2)}, u32[]{:S(2)}) collective-permute-start(bf16[96,1792]{1,0:T(8,128)(2,1)S(1)} %constant_dynamic-update-slice_fusion.refs_0_), channel_id=1, source_target_pairs={{0,1},{1,0},{2,3},{3,2},{4,5},{5,4},{6,7},{7,6},{8,9},{9,8},{10,11... | collective-permute-start | bytes 1032200 | tf_op jit(solution)/shard_map/ppermute | solution.py:239
  28.0 8.5 %collective-permute-start.15 = (bf16[48,1792]{1,0:T(8,128)(2,1)S(1)}, bf16[48,1792]{1,0:T(8,128)(2,1)S(1)}, u32[]{:S(2)}, u32[]{:S(2)}) collective-permute-start(bf16[48,1792]{1,0:T(8,128)(2,1)S(1)} %fusion.4), channel_id=1, source_target_pairs={{0,2},{1,3},{2,0},{3,1},{4,6},{5,7},{6,4},{7,5},{8,10},{9,11},{10,... | collective-permute-start | bytes 516104 | tf_op jit(solution)/shard_map/ppermute | solution.py:239
  32.9 3.7 %collective-permute-start.19 = (bf16[96,1792]{1,0:T(8,128)(2,1)S(1)}, bf16[96,1792]{1,0:T(8,128)(2,1)S(1)}, u32[]{:S(2)}, u32[]{:S(2)}) collective-permute-start(bf16[96,1792]{1,0:T(8,128)(2,1)S(1)} %get-tuple-element.44), channel_id=1, source_target_pairs={{0,1},{1,0},{2,3},{3,2},{4,5},{5,4},{6,7},{7,6},{8,9},{9,8},{10,11... | collective-permute-start | bytes 1032200 | tf_op jit(solution)/shard_map/ppermute | solution.py:239
  35.9 3.4 %collective-permute-start.6 = (bf16[192,1792]{1,0:T(8,128)(2,1)S(1)}, bf16[192,1792]{1,0:T(8,128)(2,1)S(1)}, u32[]{:S(2)}, u32[]{:S(2)}) collective-permute-start(bf16[192,1792]{1,0:T(8,128)(2,1)S(1)} %get-tuple-element.34), channel_id=1, source_target_pairs={{0,1},{1,0},{2,3},{3,2},{4,5},{5,4},{6,7},{7,6},{8,9},{9,8},{10,11... | collective-permute-start | bytes 2064392 | tf_op jit(solution)/shard_map/ppermute | solution.py:239
  36.7 7.3 %collective-permute-start.21 = (bf16[48,1792]{1,0:T(8,128)(2,1)S(1)}, bf16[48,1792]{1,0:T(8,128)(2,1)S(1)}, u32[]{:S(2)}, u32[]{:S(2)}) collective-permute-start(bf16[48,1792]{1,0:T(8,128)(2,1)S(1)} %fusion.1), channel_id=1, source_target_pairs={{0,2},{1,3},{2,0},{3,1},{4,6},{5,7},{6,4},{7,5},{8,10},{9,11},{10,... | collective-permute-start | bytes 516104 | tf_op jit(solution)/shard_map/ppermute | solution.py:239
  37.5 15.6 %collective-permute-start.20 = (bf16[48,1792]{1,0:T(8,128)(2,1)S(1)}, bf16[48,1792]{1,0:T(8,128)(2,1)S(1)}, u32[]{:S(2)}, u32[]{:S(2)}) collective-permute-start(bf16[48,1792]{1,0:T(8,128)(2,1)S(1)} %fusion.6), channel_id=1, source_target_pairs={{0,8},{1,9},{2,10},{3,11},{4,12},{5,13},{6,14},{7,15},{8,0},{9,1},... | collective-permute-start | bytes 516104 | tf_op jit(solution)/shard_map/ppermute | solution.py:239
  39.6 10.0 %collective-permute-start.8 = (bf16[48,1792]{1,0:T(8,128)(2,1)S(1)}, bf16[48,1792]{1,0:T(8,128)(2,1)S(1)}, u32[]{:S(2)}, u32[]{:S(2)}) collective-permute-start(bf16[48,1792]{1,0:T(8,128)(2,1)S(1)} %get-tuple-element.51), channel_id=1, source_target_pairs={{0,2},{1,3},{2,0},{3,1},{4,6},{5,7},{6,4},{7,5},{8,10},{9,11},{10,... | collective-permute-start | bytes 516104 | tf_op jit(solution)/shard_map/ppermute | solution.py:239
  44.1 9.0 %collective-permute-start.22 = (bf16[48,1792]{1,0:T(8,128)(2,1)S(1)}, bf16[48,1792]{1,0:T(8,128)(2,1)S(1)}, u32[]{:S(2)}, u32[]{:S(2)}) collective-permute-start(bf16[48,1792]{1,0:T(8,128)(2,1)S(1)} %fusion.3), channel_id=1, source_target_pairs={{0,12},{1,13},{2,14},{3,15},{4,8},{5,9},{6,10},{7,11},{8,4},{9,5},... | collective-permute-start | bytes 516104 | tf_op jit(solution)/shard_map/ppermute | solution.py:239
  48.9 5.4 %collective-permute-start.7 = (bf16[48,1792]{1,0:T(8,128)(2,1)S(1)}, bf16[48,1792]{1,0:T(8,128)(2,1)S(1)}, u32[]{:S(2)}, u32[]{:S(2)}) collective-permute-start(bf16[48,1792]{1,0:T(8,128)(2,1)S(1)} %get-tuple-element.35), channel_id=1, source_target_pairs={{0,2},{1,3},{2,0},{3,1},{4,6},{5,7},{6,4},{7,5},{8,10},{9,11},{10,... | collective-permute-start | bytes 516104 | tf_op jit(solution)/shard_map/ppermute | solution.py:239
  49.7 6.5 %collective-permute-start.9 = (bf16[48,1792]{1,0:T(8,128)(2,1)S(1)}, bf16[48,1792]{1,0:T(8,128)(2,1)S(1)}, u32[]{:S(2)}, u32[]{:S(2)}) collective-permute-start(bf16[48,1792]{1,0:T(8,128)(2,1)S(1)} %get-tuple-element.49), channel_id=1, source_target_pairs={{0,4},{1,5},{2,6},{3,7},{4,0},{5,1},{6,2},{7,3},{8,12},{9,13},{10,... | collective-permute-start | bytes 516104 | tf_op jit(solution)/shard_map/ppermute | solution.py:239

commit v16 on v15

--- a/solution.py
+++ b/solution.py
@@ -15,13 +15,15 @@
 APART = ("own+near",)
 ORDER = {
     "z far": ("y own",),
-    "expert own+near": ("y own",),
+    "expert own+near": ("y own", "z mid",),
     "expert far": ("rc mid",),
+    "rz far": ("rc own+near",),
     "c own": ("c near",),
     "rz mid": ("rc far", "z near",),
     "c far": ("z near", "expert mid",),
-    "ry own+near": ("y near",),
     "y far": ("z near",),
+    "rz own+near": ("rc mid",),
+    "c near": ("expert mid",),
 }
 VMEM_BYTES = 16 * 1024 * 1024
 LOAD_VMEM_BYTES = 40 * 1024 * 1024

time: 57.3 us -> 57.5 us (level)
  waiting for transfers between devices: 15.7 us -> 16.4 us
    ppermute x23, waiting for transfers between devices: 15.7 us -> 16.4 us  [partner(): lax.ppermute(array, 'expert', [(i, i ^ distance) for i in range(devices)])]
where the time goes in v16:
time: 57.5 us; the launch traced here: 57.4 us
  starting transfers between devices  24.6 us (43%)
  waiting for transfers between devices  16.4 us (29%)
  Pallas kernels  15.1 us (26%)
  other arithmetic  0.9 us (2%)
    ppermute x23, starting transfers between devices, partner(): lax.ppermute(array, 'expert', [(i, i ^ distance) for i in range(devices)])  24.6 us
    ppermute x23, waiting for transfers between devices, partner(): lax.ppermute(array, 'expert', [(i, i ^ distance) for i in range(devices)])  16.4 us
    pallas_call x3, Pallas kernels, expert(): pl.pallas_call(functools.partial(expert_kernel, capacity, offsets), out_s...  7.39 us
    pallas_call x1, Pallas kernels, load(): pl.pallas_call(load_kernel, out_shape=[jax.ShapeDtypeStruct(w.shape, w.dt...  4.23 us
    pallas_call x1, Pallas kernels, shards(): pl.pallas_call(functools.partial(pack_kernel, capacity, planes), out_shap...  1.48 us
  transfers between devices with their start and end apart: 23, of which 8 were waited for; matrix products, arithmetic and copies ran while one was open for 2% of the time, Pallas kernels for 22%

profile of v16, /device:TPU:0, one launch (start us, length us, event | category | flops | bytes accessed | tf_op | source)
XLA Modules:
  0.0 57.4 jit_solution(11988112537016894084)
XLA Ops:
  0.0 1.5 %shard_map.73 = (bf16[48,1792]{1,0:T(8,128)(2,1)S(1)}, bf16[48,1792]{1,0:T(8,128)(2,1)S(1)}, bf16[48,1792]{1,0:T(8,128)(2,1)S(1)}, bf16[48,1792]{1,0:T(8,128)(2,1)S(1)}) custom-call(s32[2,16]{1,0:T(2,128)} %bitcast.2, bf16[16,7168]{1,0:T(8,128)(2,1)} %tok_hbm.1, f32[16,56]{1,0:T(8,128)} %scale_hbm.1), custom_call_target="tpu_custom_call" | custom-call | tf_op jit(solution)/shard_map/pallas_call | solution.py:244
  1.5 4.1 %collective-permute-start.1 = (bf16[48,1792]{1,0:T(8,128)(2,1)S(1)}, bf16[48,1792]{1,0:T(8,128)(2,1)S(1)}, u32[]{:S(2)}, u32[]{:S(2)}) collective-permute-start(bf16[48,1792]{1,0:T(8,128)(2,1)S(1)} %get-tuple-element.29), channel_id=1, source_target_pairs={{0,8},{1,9},{2,10},{3,11},{4,12},{5,13},{6,14},{7,15},{8,0},{9,1},... | collective-permute-start | bytes 516104 | tf_op jit(solution)/shard_map/ppermute | solution.py:241
  5.6 1.5 %collective-permute-start = (bf16[48,1792]{1,0:T(8,128)(2,1)S(1)}, bf16[48,1792]{1,0:T(8,128)(2,1)S(1)}, u32[]{:S(2)}, u32[]{:S(2)}) collective-permute-start(bf16[48,1792]{1,0:T(8,128)(2,1)S(1)} %get-tuple-element.28.unused), channel_id=1, source_target_pairs={{0,2},{1,3},{2,0},{3,1},{4,6},{5,7},{6,4},{7,5},{8,10},{9,11},{10,... | collective-permute-start | bytes 516104 | tf_op jit(solution)/shard_map/ppermute | solution.py:241
  7.1 1.6 %collective-permute-start.2 = (bf16[48,1792]{1,0:T(8,128)(2,1)S(1)}, bf16[48,1792]{1,0:T(8,128)(2,1)S(1)}, u32[]{:S(2)}, u32[]{:S(2)}) collective-permute-start(bf16[48,1792]{1,0:T(8,128)(2,1)S(1)} %get-tuple-element.31), channel_id=1, source_target_pairs={{0,4},{1,5},{2,6},{3,7},{4,0},{5,1},{6,2},{7,3},{8,12},{9,13},{10,... | collective-permute-start | bytes 516104 | tf_op jit(solution)/shard_map/ppermute | solution.py:241
  8.7 4.2 %shard_map.75 = (bf16[1,7168,256]{2,1,0:T(8,128)(2,1)S(1)}, bf16[1,7168,256]{2,1,0:T(8,128)(2,1)S(1)}, bf16[1,256,7168]{2,1,0:T(8,128)(2,1)S(1)}) custom-call(bf16[1,7168,256]{2,1,0:T(8,128)(2,1)} %gate_hbm.1, bf16[1,7168,256]{2,1,0:T(8,128)(2,1)} %up_hbm.1, bf16[1,256,7168]{2,1,0:T(8,128)(2,1)} %down_hbm.1, bf16[48,1792]{1,0:T(8,128)(2,1)S(1)} %get-tuple-element.28.unused), custom_call_target="tpu_custom_call" | custom-call | tf_op jit(solution)/shard_map/pallas_call | solution.py:286
  12.9 0.0 collective-permute-done
  13.0 0.3 collective-permute-start.16
  13.2 0.5 collective-permute-done.1
  13.8 1.6 %collective-permute-start.5 = (bf16[48,1792]{1,0:T(8,128)(2,1)S(1)}, bf16[48,1792]{1,0:T(8,128)(2,1)S(1)}, u32[]{:S(2)}, u32[]{:S(2)}) collective-permute-start(bf16[48,1792]{1,0:T(8,128)(2,1)S(1)} %collective-permute-done.1), channel_id=1, source_target_pairs={{0,2},{1,3},{2,0},{3,1},{4,6},{5,7},{6,4},{7,5},{8,10},{9,11},{10,... | collective-permute-start | bytes 516104 | tf_op jit(solution)/shard_map/ppermute | solution.py:241
  15.3 0.0 collective-permute-start.6
  15.3 0.0 collective-permute-done.2
  15.4 0.5 collective-permute-start.4
  15.9 0.2 collective-permute-start.3
  16.1 4.2 %collective-permute-done.16 = bf16[48,1792]{1,0:T(8,128)(2,1)S(1)} collective-permute-done((bf16[48,1792]{1,0:T(8,128)(2,1)S(1)}, bf16[48,1792]{1,0:T(8,128)(2,1)S(1)}, u32[]{:S(2)}, u32[]{:S(2)}) %collective-permute-start.16) | collective-permute-done | bytes 172064 | tf_op jit(solution)/shard_map/ppermute | solution.py:241
  20.3 0.5 collective-permute-start.17
  20.8 0.0 collective-permute-done.5
  20.8 0.0 collective-permute-start.7
  20.8 0.0 collective-permute-done.3
  20.9 2.8 %collective-permute-done.4 = bf16[48,1792]{1,0:T(8,128)(2,1)S(1)} collective-permute-done((bf16[48,1792]{1,0:T(8,128)(2,1)S(1)}, bf16[48,1792]{1,0:T(8,128)(2,1)S(1)}, u32[]{:S(2)}, u32[]{:S(2)}) %collective-permute-start.4) | collective-permute-done | bytes 172064 | tf_op jit(solution)/shard_map/ppermute | solution.py:241
  23.7 0.0 collective-permute-done.6
  23.7 0.0 collective-permute-done.7
  23.8 2.3 %shard_map.76 = (bf16[96,1792]{1,0:T(8,128)(2,1)S(1)}, bf16[96,1792]{1,0:T(8,128)(2,1)S(1)}) custom-call(bf16[96,1792]{1,0:T(8,128)(2,1)S(1)} %pad_maximum_fusion.refs_0_, bf16[96,1792]{1,0:T(8,128)(2,1)S(1)} %pad_maximum_fusion.1.refs_1_, bf16[1,7168,256]{2,1,0:T(8,128)(2,1)S(1)} %get-tuple-element.32.refs_2_.refs_4_, ...), custom_call_target="tpu_custom_call" | custom-call | flops 528482304 | tf_op jit(solution)/shard_map/pallas_call | solution.py:271
  26.1 0.1 collective-permute-start.13
  26.2 0.6 collective-permute-start.8
  26.7 0.0 collective-permute-done.17
  26.7 0.1 collective-permute-start.18
  26.9 1.1 %collective-permute-done.8 = bf16[48,1792]{1,0:T(8,128)(2,1)S(1)} collective-permute-done((bf16[48,1792]{1,0:T(8,128)(2,1)S(1)}, bf16[48,1792]{1,0:T(8,128)(2,1)S(1)}, u32[]{:S(2)}, u32[]{:S(2)}) %collective-permute-start.8) | collective-permute-done | bytes 172064 | tf_op jit(solution)/shard_map/ppermute | solution.py:241
  28.0 0.2 collective-permute-start.9
  28.2 0.0 collective-permute-done.13
  28.3 2.6 %collective-permute-start.15 = (bf16[48,1792]{1,0:T(8,128)(2,1)S(1)}, bf16[48,1792]{1,0:T(8,128)(2,1)S(1)}, u32[]{:S(2)}, u32[]{:S(2)}) collective-permute-start(bf16[48,1792]{1,0:T(8,128)(2,1)S(1)} %fusion.4), channel_id=1, source_target_pairs={{0,2},{1,3},{2,0},{3,1},{4,6},{5,7},{6,4},{7,5},{8,10},{9,11},{10,... | collective-permute-start | bytes 516104 | tf_op jit(solution)/shard_map/ppermute | solution.py:241
  30.9 0.0 collective-permute-done.18.refs_1_
  30.9 2.3 %shard_map.78 = (bf16[96,1792]{1,0:T(8,128)(2,1)S(1)}, bf16[96,1792]{1,0:T(8,128)(2,1)S(1)}) custom-call(bf16[96,1792]{1,0:T(8,128)(2,1)S(1)} %constant_dynamic-update-slice_fusion.6.refs_0_, bf16[96,1792]{1,0:T(8,128)(2,1)S(1)} %collective-permute-done.18.refs_1_, bf16[1,7168,256]{2,1,0:T(8,128)(2,1)S(1)} %get-tuple-element.32.refs_2_.refs_4_, ...), custom_call_target="tpu_custom_call" | custom-call | flops 528482304 | tf_op jit(solution)/shard_map/pallas_call | solution.py:271
  33.2 0.1 collective-permute-start.19
  33.4 0.0 collective-permute-done.9.refs_1_
  33.4 2.8 %shard_map.77 = (bf16[192,1792]{1,0:T(8,128)(2,1)S(1)}, bf16[192,1792]{1,0:T(8,128)(2,1)S(1)}) custom-call(bf16[96,1792]{1,0:T(8,128)(2,1)S(1)} %constant_dynamic-update-slice_fusion.refs_0_, bf16[96,1792]{1,0:T(8,128)(2,1)S(1)} %collective-permute-done.9.refs_1_, bf16[96,1792]{1,0:T(8,128)(2,1)S(1)} %constant_dynamic-update-slice_fusion.2.refs_2_, ...), custom_call_target="tpu_custom_call" | custom-call | flops 1056964608 | tf_op jit(solution)/shard_map/pallas_call | solution.py:271
  36.2 0.5 collective-permute-start.10
  36.7 0.0 collective-permute-done.15
  36.7 0.1 fusion.6
  36.8 0.1 convert_element_type.45
  36.9 0.0 collective-permute-done.19
  36.9 0.1 fusion.1
  37.0 0.9 %collective-permute-start.21 = (bf16[48,1792]{1,0:T(8,128)(2,1)S(1)}, bf16[48,1792]{1,0:T(8,128)(2,1)S(1)}, u32[]{:S(2)}, u32[]{:S(2)}) collective-permute-start(bf16[48,1792]{1,0:T(8,128)(2,1)S(1)} %fusion.1), channel_id=1, source_target_pairs={{0,2},{1,3},{2,0},{3,1},{4,6},{5,7},{6,4},{7,5},{8,10},{9,11},{10,... | collective-permute-start | bytes 516104 | tf_op jit(solution)/shard_map/ppermute | solution.py:241
  37.9 1.6 %collective-permute-start.20 = (bf16[48,1792]{1,0:T(8,128)(2,1)S(1)}, bf16[48,1792]{1,0:T(8,128)(2,1)S(1)}, u32[]{:S(2)}, u32[]{:S(2)}) collective-permute-start(bf16[48,1792]{1,0:T(8,128)(2,1)S(1)} %fusion.6), channel_id=1, source_target_pairs={{0,8},{1,9},{2,10},{3,11},{4,12},{5,13},{6,14},{7,15},{8,0},{9,1},... | collective-permute-start | bytes 516104 | tf_op jit(solution)/shard_map/ppermute | solution.py:241
  39.5 0.0 collective-permute-done.10
  39.5 0.1 convert_element_type.46
  39.6 0.2 fusion
  39.8 1.2 %collective-permute-start.12 = (bf16[48,1792]{1,0:T(8,128)(2,1)S(1)}, bf16[48,1792]{1,0:T(8,128)(2,1)S(1)}, u32[]{:S(2)}, u32[]{:S(2)}) collective-permute-start(bf16[48,1792]{1,0:T(8,128)(2,1)S(1)} %get-tuple-element.55), channel_id=1, source_target_pairs={{0,2},{1,3},{2,0},{3,1},{4,6},{5,7},{6,4},{7,5},{8,10},{9,11},{10,... | collective-permute-start | bytes 516104 | tf_op jit(solution)/shard_map/ppermute | solution.py:241
  41.0 3.3 %collective-permute-done.21 = bf16[48,1792]{1,0:T(8,128)(2,1)S(1)} collective-permute-done((bf16[48,1792]{1,0:T(8,128)(2,1)S(1)}, bf16[48,1792]{1,0:T(8,128)(2,1)S(1)}, u32[]{:S(2)}, u32[]{:S(2)}) %collective-permute-start.21) | collective-permute-done | bytes 172064 | tf_op jit(solution)/shard_map/ppermute | solution.py:241
  44.3 0.1 fusion.3
  44.3 4.8 %collective-permute-start.22 = (bf16[48,1792]{1,0:T(8,128)(2,1)S(1)}, bf16[48,1792]{1,0:T(8,128)(2,1)S(1)}, u32[]{:S(2)}, u32[]{:S(2)}) collective-permute-start(bf16[48,1792]{1,0:T(8,128)(2,1)S(1)} %fusion.3), channel_id=1, source_target_pairs={{0,12},{1,13},{2,14},{3,15},{4,8},{5,9},{6,10},{7,11},{8,4},{9,5},... | collective-permute-start | bytes 516104 | tf_op jit(solution)/shard_map/ppermute | solution.py:241
  49.1 0.9 %collective-permute-start.11 = (bf16[48,1792]{1,0:T(8,128)(2,1)S(1)}, bf16[48,1792]{1,0:T(8,128)(2,1)S(1)}, u32[]{:S(2)}, u32[]{:S(2)}) collective-permute-start(bf16[48,1792]{1,0:T(8,128)(2,1)S(1)} %get-tuple-element.56), channel_id=1, source_target_pairs={{0,2},{1,3},{2,0},{3,1},{4,6},{5,7},{6,4},{7,5},{8,10},{9,11},{10,... | collective-permute-start | bytes 516104 | tf_op jit(solution)/shard_map/ppermute | solution.py:241
  50.0 0.0 collective-permute-done.12
  50.1 0.1 fusion.7
  50.1 0.8 %collective-permute-start.14 = (bf16[48,1792]{1,0:T(8,128)(2,1)S(1)}, bf16[48,1792]{1,0:T(8,128)(2,1)S(1)}, u32[]{:S(2)}, u32[]{:S(2)}) collective-permute-start(bf16[48,1792]{1,0:T(8,128)(2,1)S(1)} %get-tuple-element.40), channel_id=1, source_target_pairs={{0,4},{1,5},{2,6},{3,7},{4,0},{5,1},{6,2},{7,3},{8,12},{9,13},{10,... | collective-permute-start | bytes 516104 | tf_op jit(solution)/shard_map/ppermute | solution.py:241
  50.9 1.0 %shard_map.74.plan_ref = bf16[4,128,48]{2,1,0:T(8,128)(2,1)S(1)} custom-call(s32[2,16]{1,0:T(2,128)} %bitcast.3, s32[2,16]{1,0:T(2,128)} %bitcast.4, bf16[48,1792]{1,0:T(8,128)(2,1)S(1)} %get-tuple-element.28.unused), custom_call_target="tpu_custom_call" | custom-call | tf_op jit(solution)/shard_map/pallas_call | solution.py:258
  52.0 1.2 %collective-permute-done.20.refs_3_ = bf16[48,1792]{1,0:T(8,128)(2,1)S(1)} collective-permute-done((bf16[48,1792]{1,0:T(8,128)(2,1)S(1)}, bf16[48,1792]{1,0:T(8,128)(2,1)S(1)}, u32[]{:S(2)}, u32[]{:S(2)}) %collective-permute-start.20) | collective-permute-done | bytes 172064 | tf_op jit(solution)/shard_map/ppermute | solution.py:241
  53.2 0.0 collective-permute-done.22.refs_4_
  53.2 1.3 %collective-permute-done.11.refs_1_ = bf16[48,1792]{1,0:T(8,128)(2,1)S(1)} collective-permute-done((bf16[48,1792]{1,0:T(8,128)(2,1)S(1)}, bf16[48,1792]{1,0:T(8,128)(2,1)S(1)}, u32[]{:S(2)}, u32[]{:S(2)}) %collective-permute-start.11) | collective-permute-done | bytes 172064 | tf_op jit(solution)/shard_map/ppermute | solution.py:241
  54.6 1.8 %collective-permute-done.14.refs_2_ = bf16[48,1792]{1,0:T(8,128)(2,1)S(1)} collective-permute-done((bf16[48,1792]{1,0:T(8,128)(2,1)S(1)}, bf16[48,1792]{1,0:T(8,128)(2,1)S(1)}, u32[]{:S(2)}, u32[]{:S(2)}) %collective-permute-start.14) | collective-permute-done | bytes 172064 | tf_op jit(solution)/shard_map/ppermute | solution.py:241
  56.4 1.0 %shard_map.79 = bf16[16,7168]{1,0:T(8,128)(2,1)} custom-call(bf16[4,128,48]{2,1,0:T(8,128)(2,1)S(1)} %shard_map.74.plan_ref, f32[48,1792]{1,0:T(8,128)S(1)} %get-tuple-element.54.refs_0_, bf16[48,1792]{1,0:T(8,128)(2,1)S(1)} %collective-permute-done.11.refs_1_, bf16[48,1792]{1,0:T(8,128)(2,1)S(1)} %collective-permute-done.14.refs_2_, ...), custom_call_target="tpu_custom_call" | custom-call | tf_op jit(solution)/shard_map/pallas_call | solution.py:389
  (17 shorter events, 0.4 us)
Async XLA Ops:
  1.5 12.3 %collective-permute-start.1 = (bf16[48,1792]{1,0:T(8,128)(2,1)S(1)}, bf16[48,1792]{1,0:T(8,128)(2,1)S(1)}, u32[]{:S(2)}, u32[]{:S(2)}) collective-permute-start(bf16[48,1792]{1,0:T(8,128)(2,1)S(1)} %get-tuple-element.29), channel_id=1, source_target_pairs={{0,8},{1,9},{2,10},{3,11},{4,12},{5,13},{6,14},{7,15},{8,0},{9,1},... | collective-permute-start | bytes 516104 | tf_op jit(solution)/shard_map/ppermute | solution.py:241
  5.6 7.4 %collective-permute-start = (bf16[48,1792]{1,0:T(8,128)(2,1)S(1)}, bf16[48,1792]{1,0:T(8,128)(2,1)S(1)}, u32[]{:S(2)}, u32[]{:S(2)}) collective-permute-start(bf16[48,1792]{1,0:T(8,128)(2,1)S(1)} %get-tuple-element.28.unused), channel_id=1, source_target_pairs={{0,2},{1,3},{2,0},{3,1},{4,6},{5,7},{6,4},{7,5},{8,10},{9,11},{10,... | collective-permute-start | bytes 516104 | tf_op jit(solution)/shard_map/ppermute | solution.py:241
  7.1 8.2 %collective-permute-start.2 = (bf16[48,1792]{1,0:T(8,128)(2,1)S(1)}, bf16[48,1792]{1,0:T(8,128)(2,1)S(1)}, u32[]{:S(2)}, u32[]{:S(2)}) collective-permute-start(bf16[48,1792]{1,0:T(8,128)(2,1)S(1)} %get-tuple-element.31), channel_id=1, source_target_pairs={{0,4},{1,5},{2,6},{3,7},{4,0},{5,1},{6,2},{7,3},{8,12},{9,13},{10,... | collective-permute-start | bytes 516104 | tf_op jit(solution)/shard_map/ppermute | solution.py:241
  13.0 7.3 %collective-permute-start.16 = (bf16[48,1792]{1,0:T(8,128)(2,1)S(1)}, bf16[48,1792]{1,0:T(8,128)(2,1)S(1)}, u32[]{:S(2)}, u32[]{:S(2)}) collective-permute-start(bf16[48,1792]{1,0:T(8,128)(2,1)S(1)} %get-tuple-element.43), channel_id=1, source_target_pairs={{0,12},{1,13},{2,14},{3,15},{4,8},{5,9},{6,10},{7,11},{8,4},{9,5},... | collective-permute-start | bytes 516104 | tf_op jit(solution)/shard_map/ppermute | solution.py:241
  13.8 7.0 %collective-permute-start.5 = (bf16[48,1792]{1,0:T(8,128)(2,1)S(1)}, bf16[48,1792]{1,0:T(8,128)(2,1)S(1)}, u32[]{:S(2)}, u32[]{:S(2)}) collective-permute-start(bf16[48,1792]{1,0:T(8,128)(2,1)S(1)} %collective-permute-done.1), channel_id=1, source_target_pairs={{0,2},{1,3},{2,0},{3,1},{4,6},{5,7},{6,4},{7,5},{8,10},{9,11},{10,... | collective-permute-start | bytes 516104 | tf_op jit(solution)/shard_map/ppermute | solution.py:241
  15.3 8.4 %collective-permute-start.6 = (bf16[48,1792]{1,0:T(8,128)(2,1)S(1)}, bf16[48,1792]{1,0:T(8,128)(2,1)S(1)}, u32[]{:S(2)}, u32[]{:S(2)}) collective-permute-start(bf16[48,1792]{1,0:T(8,128)(2,1)S(1)} %collective-permute-done.1), channel_id=1, source_target_pairs={{0,1},{1,0},{2,3},{3,2},{4,5},{5,4},{6,7},{7,6},{8,9},{9,8},{10,11... | collective-permute-start | bytes 516104 | tf_op jit(solution)/shard_map/ppermute | solution.py:241
  15.4 8.3 %collective-permute-start.4 = (bf16[48,1792]{1,0:T(8,128)(2,1)S(1)}, bf16[48,1792]{1,0:T(8,128)(2,1)S(1)}, u32[]{:S(2)}, u32[]{:S(2)}) collective-permute-start(bf16[48,1792]{1,0:T(8,128)(2,1)S(1)} %collective-permute-done.2), channel_id=1, source_target_pairs={{0,2},{1,3},{2,0},{3,1},{4,6},{5,7},{6,4},{7,5},{8,10},{9,11},{10,... | collective-permute-start | bytes 516104 | tf_op jit(solution)/shard_map/ppermute | solution.py:241
  15.9 5.0 %collective-permute-start.3 = (bf16[48,1792]{1,0:T(8,128)(2,1)S(1)}, bf16[48,1792]{1,0:T(8,128)(2,1)S(1)}, u32[]{:S(2)}, u32[]{:S(2)}) collective-permute-start(bf16[48,1792]{1,0:T(8,128)(2,1)S(1)} %collective-permute-done.2), channel_id=1, source_target_pairs={{0,1},{1,0},{2,3},{3,2},{4,5},{5,4},{6,7},{7,6},{8,9},{9,8},{10,11... | collective-permute-start | bytes 516104 | tf_op jit(solution)/shard_map/ppermute | solution.py:241
  20.3 6.4 %collective-permute-start.17 = (bf16[48,1792]{1,0:T(8,128)(2,1)S(1)}, bf16[48,1792]{1,0:T(8,128)(2,1)S(1)}, u32[]{:S(2)}, u32[]{:S(2)}) collective-permute-start(bf16[48,1792]{1,0:T(8,128)(2,1)S(1)} %collective-permute-done.16), channel_id=1, source_target_pairs={{0,2},{1,3},{2,0},{3,1},{4,6},{5,7},{6,4},{7,5},{8,10},{9,11},{10,... | collective-permute-start | bytes 516104 | tf_op jit(solution)/shard_map/ppermute | solution.py:241
  20.8 2.9 %collective-permute-start.7 = (bf16[48,1792]{1,0:T(8,128)(2,1)S(1)}, bf16[48,1792]{1,0:T(8,128)(2,1)S(1)}, u32[]{:S(2)}, u32[]{:S(2)}) collective-permute-start(bf16[48,1792]{1,0:T(8,128)(2,1)S(1)} %collective-permute-done.5), channel_id=1, source_target_pairs={{0,1},{1,0},{2,3},{3,2},{4,5},{5,4},{6,7},{7,6},{8,9},{9,8},{10,11... | collective-permute-start | bytes 516104 | tf_op jit(solution)/shard_map/ppermute | solution.py:241
  26.1 2.2 %collective-permute-start.13 = (bf16[96,1792]{1,0:T(8,128)(2,1)S(1)}, bf16[96,1792]{1,0:T(8,128)(2,1)S(1)}, u32[]{:S(2)}, u32[]{:S(2)}) collective-permute-start(bf16[96,1792]{1,0:T(8,128)(2,1)S(1)} %get-tuple-element.35), channel_id=1, source_target_pairs={{0,1},{1,0},{2,3},{3,2},{4,5},{5,4},{6,7},{7,6},{8,9},{9,8},{10,11... | collective-permute-start | bytes 1032200 | tf_op jit(solution)/shard_map/ppermute | solution.py:241
  26.2 1.9 %collective-permute-start.8 = (bf16[48,1792]{1,0:T(8,128)(2,1)S(1)}, bf16[48,1792]{1,0:T(8,128)(2,1)S(1)}, u32[]{:S(2)}, u32[]{:S(2)}) collective-permute-start(bf16[48,1792]{1,0:T(8,128)(2,1)S(1)} %split.15), channel_id=1, source_target_pairs={{0,1},{1,0},{2,3},{3,2},{4,5},{5,4},{6,7},{7,6},{8,9},{9,8},{10,11... | collective-permute-start | bytes 516104 | tf_op jit(solution)/shard_map/ppermute | solution.py:241
  26.7 4.2 %collective-permute-start.18 = (bf16[96,1792]{1,0:T(8,128)(2,1)S(1)}, bf16[96,1792]{1,0:T(8,128)(2,1)S(1)}, u32[]{:S(2)}, u32[]{:S(2)}) collective-permute-start(bf16[96,1792]{1,0:T(8,128)(2,1)S(1)} %constant_dynamic-update-slice_fusion.6.refs_0_), channel_id=1, source_target_pairs={{0,1},{1,0},{2,3},{3,2},{4,5},{5,4},{6,7},{7,6},{8,9},{9,8},{10,11... | collective-permute-start | bytes 1032200 | tf_op jit(solution)/shard_map/ppermute | solution.py:241
  28.0 5.4 %collective-permute-start.9 = (bf16[96,1792]{1,0:T(8,128)(2,1)S(1)}, bf16[96,1792]{1,0:T(8,128)(2,1)S(1)}, u32[]{:S(2)}, u32[]{:S(2)}) collective-permute-start(bf16[96,1792]{1,0:T(8,128)(2,1)S(1)} %constant_dynamic-update-slice_fusion.refs_0_), channel_id=1, source_target_pairs={{0,1},{1,0},{2,3},{3,2},{4,5},{5,4},{6,7},{7,6},{8,9},{9,8},{10,11... | collective-permute-start | bytes 1032200 | tf_op jit(solution)/shard_map/ppermute | solution.py:241
  28.3 8.4 %collective-permute-start.15 = (bf16[48,1792]{1,0:T(8,128)(2,1)S(1)}, bf16[48,1792]{1,0:T(8,128)(2,1)S(1)}, u32[]{:S(2)}, u32[]{:S(2)}) collective-permute-start(bf16[48,1792]{1,0:T(8,128)(2,1)S(1)} %fusion.4), channel_id=1, source_target_pairs={{0,2},{1,3},{2,0},{3,1},{4,6},{5,7},{6,4},{7,5},{8,10},{9,11},{10,... | collective-permute-start | bytes 516104 | tf_op jit(solution)/shard_map/ppermute | solution.py:241
  33.2 3.7 %collective-permute-start.19 = (bf16[96,1792]{1,0:T(8,128)(2,1)S(1)}, bf16[96,1792]{1,0:T(8,128)(2,1)S(1)}, u32[]{:S(2)}, u32[]{:S(2)}) collective-permute-start(bf16[96,1792]{1,0:T(8,128)(2,1)S(1)} %get-tuple-element.47), channel_id=1, source_target_pairs={{0,1},{1,0},{2,3},{3,2},{4,5},{5,4},{6,7},{7,6},{8,9},{9,8},{10,11... | collective-permute-start | bytes 1032200 | tf_op jit(solution)/shard_map/ppermute | solution.py:241
  36.2 3.2 %collective-permute-start.10 = (bf16[192,1792]{1,0:T(8,128)(2,1)S(1)}, bf16[192,1792]{1,0:T(8,128)(2,1)S(1)}, u32[]{:S(2)}, u32[]{:S(2)}) collective-permute-start(bf16[192,1792]{1,0:T(8,128)(2,1)S(1)} %get-tuple-element.39), channel_id=1, source_target_pairs={{0,1},{1,0},{2,3},{3,2},{4,5},{5,4},{6,7},{7,6},{8,9},{9,8},{10,11... | collective-permute-start | bytes 2064392 | tf_op jit(solution)/shard_map/ppermute | solution.py:241
  37.0 7.3 %collective-permute-start.21 = (bf16[48,1792]{1,0:T(8,128)(2,1)S(1)}, bf16[48,1792]{1,0:T(8,128)(2,1)S(1)}, u32[]{:S(2)}, u32[]{:S(2)}) collective-permute-start(bf16[48,1792]{1,0:T(8,128)(2,1)S(1)} %fusion.1), channel_id=1, source_target_pairs={{0,2},{1,3},{2,0},{3,1},{4,6},{5,7},{6,4},{7,5},{8,10},{9,11},{10,... | collective-permute-start | bytes 516104 | tf_op jit(solution)/shard_map/ppermute | solution.py:241
  37.9 15.3 %collective-permute-start.20 = (bf16[48,1792]{1,0:T(8,128)(2,1)S(1)}, bf16[48,1792]{1,0:T(8,128)(2,1)S(1)}, u32[]{:S(2)}, u32[]{:S(2)}) collective-permute-start(bf16[48,1792]{1,0:T(8,128)(2,1)S(1)} %fusion.6), channel_id=1, source_target_pairs={{0,8},{1,9},{2,10},{3,11},{4,12},{5,13},{6,14},{7,15},{8,0},{9,1},... | collective-permute-start | bytes 516104 | tf_op jit(solution)/shard_map/ppermute | solution.py:241
  39.8 10.2 %collective-permute-start.12 = (bf16[48,1792]{1,0:T(8,128)(2,1)S(1)}, bf16[48,1792]{1,0:T(8,128)(2,1)S(1)}, u32[]{:S(2)}, u32[]{:S(2)}) collective-permute-start(bf16[48,1792]{1,0:T(8,128)(2,1)S(1)} %get-tuple-element.55), channel_id=1, source_target_pairs={{0,2},{1,3},{2,0},{3,1},{4,6},{5,7},{6,4},{7,5},{8,10},{9,11},{10,... | collective-permute-start | bytes 516104 | tf_op jit(solution)/shard_map/ppermute | solution.py:241
  44.3 8.9 %collective-permute-start.22 = (bf16[48,1792]{1,0:T(8,128)(2,1)S(1)}, bf16[48,1792]{1,0:T(8,128)(2,1)S(1)}, u32[]{:S(2)}, u32[]{:S(2)}) collective-permute-start(bf16[48,1792]{1,0:T(8,128)(2,1)S(1)} %fusion.3), channel_id=1, source_target_pairs={{0,12},{1,13},{2,14},{3,15},{4,8},{5,9},{6,10},{7,11},{8,4},{9,5},... | collective-permute-start | bytes 516104 | tf_op jit(solution)/shard_map/ppermute | solution.py:241
  49.1 5.4 %collective-permute-start.11 = (bf16[48,1792]{1,0:T(8,128)(2,1)S(1)}, bf16[48,1792]{1,0:T(8,128)(2,1)S(1)}, u32[]{:S(2)}, u32[]{:S(2)}) collective-permute-start(bf16[48,1792]{1,0:T(8,128)(2,1)S(1)} %get-tuple-element.56), channel_id=1, source_target_pairs={{0,2},{1,3},{2,0},{3,1},{4,6},{5,7},{6,4},{7,5},{8,10},{9,11},{10,... | collective-permute-start | bytes 516104 | tf_op jit(solution)/shard_map/ppermute | solution.py:241
  50.1 6.3 %collective-permute-start.14 = (bf16[48,1792]{1,0:T(8,128)(2,1)S(1)}, bf16[48,1792]{1,0:T(8,128)(2,1)S(1)}, u32[]{:S(2)}, u32[]{:S(2)}) collective-permute-start(bf16[48,1792]{1,0:T(8,128)(2,1)S(1)} %get-tuple-element.40), channel_id=1, source_target_pairs={{0,4},{1,5},{2,6},{3,7},{4,0},{5,1},{6,2},{7,3},{8,12},{9,13},{10,... | collective-permute-start | bytes 516104 | tf_op jit(solution)/shard_map/ppermute | solution.py:241
